TPU v7x, 32 devices: a whole 2x2x4 slice. The times are simulated.
32 devices in a mesh: row: 8 (over y, x, core), col: 4 (over z).
Axes of the slice: x: 2, y: 2, z: 4, core: 2. Of those that a mesh axis runs over, the one named last changes fastest.
Arguments:
- tokens: bfloat16 [8192, 2048], P('row', 'col'), may hold values from -6 to 6
- cotangent: bfloat16 [8192, 2048], P('row', 'col'), may hold values from -6 to 6
- segments: int32 [8192], P('row'), may hold values from 0 to 20, never falling along the last dimension, each value on 1 to 800 neighbouring positions
- w_query: bfloat16 [2048, 2048], P('row', 'col'), may hold values from -0.125 to 0.125
- w_key: bfloat16 [2048, 2048], P('row', 'col'), may hold values from -0.125 to 0.125
- w_value: bfloat16 [2048, 2048], P('row', 'col'), may hold values from -0.125 to 0.125
- w_out: bfloat16 [2048, 2048], P('col', 'row'), may hold values from -1 to 1
- w_gate: bfloat16 [2048, 8192], P('row', 'col'), may hold values from -0.125 to 0.125
- w_up: bfloat16 [2048, 8192], P('row', 'col'), may hold values from -0.125 to 0.125
- w_down: bfloat16 [8192, 2048], P('col', 'row'), may hold values from -0.0625 to 0.0625
Outputs:
- output: bfloat16 [8192, 2048], P('row', 'col')
- grad_tokens: bfloat16 [8192, 2048], P('row', 'col')
- grad_query: float32 [2048, 2048], P('row', 'col')
- grad_key: float32 [2048, 2048], P('row', 'col')
- grad_value: float32 [2048, 2048], P('row', 'col')
- grad_out: float32 [2048, 2048], P('col', 'row')
- grad_gate: float32 [2048, 8192], P('row', 'col')
- grad_up: float32 [2048, 8192], P('row', 'col')
- grad_down: float32 [8192, 2048], P('col', 'row')
Inputs may be any that keep to these rules, and one draw needn't show every extreme that they name: `segments`: segment numbers never fall along the tokens; each segment covers 1 to 800 tokens, one exactly that many.
All inputs are finite; a program needn't handle non-finite values.
Results may differ from a plain program's by a relative error of at most 0.018.
Values may be sent and summed in bfloat16 or wider, within the bound.
A program may use at most 256 MiB of HBM per device.

v0:
```python
import jax
import jax.numpy as jnp
from jax import lax
from jax.sharding import PartitionSpec as P

HEAD_DIM = 128
SEQ = 1024


EPSILON = 1e-05
MASKED = -1e30


def matmul(left, right):
    return jnp.dot(left, right, preferred_element_type=jnp.float32)


def matmul_tn(left, right):
    return lax.dot_general(
        left, right, (((0,), (0,)), ((), ())), preferred_element_type=jnp.float32
    )


def matmul_nt(left, right):
    return lax.dot_general(
        left, right, (((1,), (1,)), ((), ())), preferred_element_type=jnp.float32
    )


def allowed_of(segment_ids):
    places = jnp.arange(segment_ids.shape[0], dtype=jnp.int32)
    causal = places[None, :] <= places[:, None]
    return (segment_ids[:, None] == segment_ids[None, :]) & causal


def count_seen(segment_ids):
    return jnp.sum(allowed_of(segment_ids).astype(jnp.int32), axis=1) - 1


def rope_tables(segments):
    positions = lax.map(count_seen, segments.reshape(-1, SEQ)).reshape(-1)
    halfway = HEAD_DIM // 2
    inverse = 10000.0 ** (-(jnp.arange(halfway, dtype=jnp.float32) * 2.0 / HEAD_DIM))
    angles = positions.astype(jnp.float32)[:, None] * inverse[None, :]
    return (jnp.cos(angles)[:, None, :], jnp.sin(angles)[:, None, :])


def rotate(values, cos_table, sin_table):
    shaped = values.reshape(values.shape[0], -1, HEAD_DIM)
    halfway = HEAD_DIM // 2
    first_half = shaped[..., :halfway]
    second_half = shaped[..., halfway:]
    turned = jnp.concatenate(
        [
            first_half * cos_table - second_half * sin_table,
            second_half * cos_table + first_half * sin_table,
        ],
        axis=-1,
    )
    return turned.reshape(values.shape)


def layer_norm(values):
    centre = jnp.mean(values, axis=-1, keepdims=True)
    spread = jnp.mean(values * values, axis=-1, keepdims=True) - centre * centre
    inverse_dev = lax.rsqrt(spread + EPSILON)
    return ((values - centre) * inverse_dev, inverse_dev)


def masked_scores(query_seq, key_seq, segment_ids):
    score_scale = HEAD_DIM ** (-0.5)
    scores = (
        jnp.einsum("qhd,khd->hqk", query_seq, key_seq, preferred_element_type=jnp.float32)
        * score_scale
    )
    return jnp.where(allowed_of(segment_ids)[None], scores, MASKED)


def attend_forward(query_r, key_r, value_r, segments):
    shaped = (query_r.shape[0] // SEQ, SEQ, -1, HEAD_DIM)

    def one_sequence(blocks_in):
        query_seq, key_seq, value_seq, segment_ids = blocks_in
        scores = masked_scores(query_seq, key_seq, segment_ids)
        row_peak = jnp.max(scores, axis=-1, keepdims=True)
        exponent = jnp.exp(scores - row_peak)
        row_total = jnp.sum(exponent, axis=-1, keepdims=True)
        weights = (exponent / row_total).astype(jnp.bfloat16)
        result = jnp.einsum("hqk,khd->qhd", weights, value_seq, preferred_element_type=jnp.float32)
        return (result, row_peak + jnp.log(row_total))

    result, log_total = lax.map(
        one_sequence,
        (
            query_r.reshape(shaped),
            key_r.reshape(shaped),
            value_r.reshape(shaped),
            segments.reshape(-1, SEQ),
        ),
    )
    return (result.reshape(query_r.shape), log_total)


def attend_backward(query_r, key_r, value_r, segments, log_total, grad_attn):
    shaped = (query_r.shape[0] // SEQ, SEQ, -1, HEAD_DIM)
    score_scale = HEAD_DIM ** (-0.5)

    def one_sequence(blocks_in):
        query_seq, key_seq, value_seq, segment_ids, seq_log, grad_seq = blocks_in
        probs = jnp.exp(masked_scores(query_seq, key_seq, segment_ids) - seq_log)
        weights = probs.astype(jnp.bfloat16)
        grad_vals = jnp.einsum(
            "hqk,qhd->khd", weights, grad_seq, preferred_element_type=jnp.float32
        )
        grad_probs = jnp.einsum(
            "qhd,khd->hqk", grad_seq, value_seq, preferred_element_type=jnp.float32
        )
        inner = jnp.sum(probs * grad_probs, axis=-1, keepdims=True)
        grad_scores = (probs * (grad_probs - inner)).astype(jnp.bfloat16)
        grad_quer = (
            jnp.einsum("hqk,khd->qhd", grad_scores, key_seq, preferred_element_type=jnp.float32)
            * score_scale
        )
        grad_keys = (
            jnp.einsum("hqk,qhd->khd", grad_scores, query_seq, preferred_element_type=jnp.float32)
            * score_scale
        )
        return (grad_quer, grad_keys, grad_vals)

    grad_quer, grad_keys, grad_vals = lax.map(
        one_sequence,
        (
            query_r.reshape(shaped),
            key_r.reshape(shaped),
            value_r.reshape(shaped),
            segments.reshape(-1, SEQ),
            log_total,
            grad_attn.reshape(shaped),
        ),
    )
    return (
        grad_quer.reshape(query_r.shape),
        grad_keys.reshape(query_r.shape),
        grad_vals.reshape(query_r.shape),
    )


def on_device(tokens, cotangent, segments, w_query, w_key, w_value, w_out, w_gate, w_up, w_down):
    width_here = tokens.shape[1]
    col_start = lax.axis_index("col") * width_here
    tokens_full, cotangent_full = (
        lax.all_gather(tokens, "col", axis=1, tiled=True),
        lax.all_gather(cotangent, "col", axis=1, tiled=True),
    )
    query_w, key_w, value_w, out_w, gate_w, up_w, down_w = (
        lax.all_gather(w_query, "row", axis=0, tiled=True),
        lax.all_gather(w_key, "row", axis=0, tiled=True),
        lax.all_gather(w_value, "row", axis=0, tiled=True),
        lax.all_gather(w_out, "row", axis=1, tiled=True),
        lax.all_gather(w_gate, "row", axis=0, tiled=True),
        lax.all_gather(w_up, "row", axis=0, tiled=True),
        lax.all_gather(w_down, "row", axis=1, tiled=True),
    )
    width_all = tokens_full.shape[1]
    inputs = tokens_full.astype(jnp.float32)
    normed_one, inverse_one = layer_norm(inputs)
    act_one = normed_one.astype(jnp.bfloat16)
    cos_table, sin_table = rope_tables(segments)
    query_r = rotate(matmul(act_one, query_w), cos_table, sin_table).astype(jnp.bfloat16)
    key_r = rotate(matmul(act_one, key_w), cos_table, sin_table).astype(jnp.bfloat16)
    value_r = matmul(act_one, value_w).astype(jnp.bfloat16)
    attended, log_total = attend_forward(query_r, key_r, value_r, segments)
    attended_r = attended.astype(jnp.bfloat16)
    attn_terms = matmul(attended_r, out_w)
    resid_full = inputs + lax.psum(attn_terms, "col")
    normed_two, inverse_two = layer_norm(resid_full)
    act_two = normed_two.astype(jnp.bfloat16)
    resid_local = lax.dynamic_slice_in_dim(resid_full, col_start, width_here, 1)
    gate = matmul(act_two, gate_w)
    upward = matmul(act_two, up_w)
    sigmoid_gate = jax.nn.sigmoid(gate)
    silu_gate = gate * sigmoid_gate
    hidden = (silu_gate * upward).astype(jnp.bfloat16)
    output = resid_local + lax.psum_scatter(
        matmul(hidden, down_w).astype(jnp.bfloat16), "col", scatter_dimension=1, tiled=True
    ).astype(jnp.float32)
    grad_down = matmul_tn(hidden, cotangent_full)
    grad_hidden = matmul_nt(cotangent_full, down_w)
    grad_gate_in = (
        grad_hidden * upward * sigmoid_gate * (1.0 + gate * (1.0 - sigmoid_gate))
    ).astype(jnp.bfloat16)
    grad_up_in = (grad_hidden * silu_gate).astype(jnp.bfloat16)
    grad_gate = matmul_tn(act_two, grad_gate_in)
    grad_up = matmul_tn(act_two, grad_up_in)
    norm_terms = matmul_nt(grad_gate_in, gate_w) + matmul_nt(grad_up_in, up_w)
    grad_norm = lax.psum(norm_terms, "col")
    first_mean = jnp.mean(grad_norm, axis=1, keepdims=True)
    second_mean = jnp.mean(grad_norm * normed_two, axis=1, keepdims=True)
    grad_resid_full = cotangent_full.astype(jnp.float32) + inverse_two * (
        grad_norm - first_mean - normed_two * second_mean
    )
    grad_resid_send = grad_resid_full.astype(jnp.bfloat16)
    grad_resid = lax.dynamic_slice_in_dim(grad_resid_full, col_start, width_here, 1)
    grad_out = matmul_tn(attended_r, grad_resid_send)
    grad_attn = matmul_nt(grad_resid_send, out_w).astype(jnp.bfloat16)
    grad_quer, grad_keys, grad_vals = attend_backward(
        query_r, key_r, value_r, segments, log_total, grad_attn
    )
    grad_quer = rotate(grad_quer, cos_table, -sin_table).astype(jnp.bfloat16)
    grad_keys = rotate(grad_keys, cos_table, -sin_table).astype(jnp.bfloat16)
    grad_vals = grad_vals.astype(jnp.bfloat16)
    grad_query = matmul_tn(act_one, grad_quer)
    grad_key = matmul_tn(act_one, grad_keys)
    grad_value = matmul_tn(act_one, grad_vals)
    input_terms = (
        matmul_nt(grad_quer, query_w) + matmul_nt(grad_keys, key_w) + matmul_nt(grad_vals, value_w)
    )
    grad_input = lax.psum_scatter(
        input_terms.astype(jnp.bfloat16), "col", scatter_dimension=1, tiled=True
    ).astype(jnp.float32)
    normed_local = lax.dynamic_slice_in_dim(normed_one, col_start, width_here, 1)
    first_sum, second_sum = lax.psum(
        (jnp.sum(grad_input, axis=1), jnp.sum(grad_input * normed_local, axis=1)), "col"
    )
    grad_tokens = grad_resid + inverse_one * (
        grad_input
        - (first_sum / width_all)[:, None]
        - normed_local * (second_sum / width_all)[:, None]
    )
    summed = (
        lax.psum_scatter(
            grad_query.astype(jnp.bfloat16), "row", scatter_dimension=0, tiled=True
        ).astype(jnp.float32),
        lax.psum_scatter(
            grad_key.astype(jnp.bfloat16), "row", scatter_dimension=0, tiled=True
        ).astype(jnp.float32),
        lax.psum_scatter(
            grad_value.astype(jnp.bfloat16), "row", scatter_dimension=0, tiled=True
        ).astype(jnp.float32),
        lax.psum_scatter(
            grad_out.astype(jnp.bfloat16), "row", scatter_dimension=1, tiled=True
        ).astype(jnp.float32),
        lax.psum_scatter(
            grad_gate.astype(jnp.bfloat16), "row", scatter_dimension=0, tiled=True
        ).astype(jnp.float32),
        lax.psum_scatter(
            grad_up.astype(jnp.bfloat16), "row", scatter_dimension=0, tiled=True
        ).astype(jnp.float32),
        lax.psum_scatter(
            grad_down.astype(jnp.bfloat16), "row", scatter_dimension=1, tiled=True
        ).astype(jnp.float32),
    )
    return (
        output.astype(jnp.bfloat16),
        grad_tokens.astype(jnp.bfloat16),
        summed[0],
        summed[1],
        summed[2],
        summed[3],
        summed[4],
        summed[5],
        summed[6],
    )


def solution(mesh):
    in_specs = (
        P("row", "col"),
        P("row", "col"),
        P("row"),
        P("row", "col"),
        P("row", "col"),
        P("row", "col"),
        P("col", "row"),
        P("row", "col"),
        P("row", "col"),
        P("col", "row"),
    )
    out_specs = (
        P("row", "col"),
        P("row", "col"),
        P("row", "col"),
        P("row", "col"),
        P("row", "col"),
        P("col", "row"),
        P("row", "col"),
        P("row", "col"),
        P("col", "row"),
    )
    return jax.shard_map(
        on_device, mesh=mesh, in_specs=in_specs, out_specs=out_specs, check_vma=False
    )
```

profile of v0, /device:TPU:8, one launch (start us, length us, event | category | flops | bytes accessed | tf_op | source)
XLA Modules:
  0.0 1682.7 jit_solution(3713300162968308138)
XLA Ops:
  17.2 71.7 %all-gather.10.cloned.1.call-done = bf16[1024,2048]{1,0:T(8,128)(2,1)} async-done(((bf16[1024,512]{1,0:T(8,128)(2,1)}), bf16[1024,2048]{1,0:T(8,128)(2,1)}) %all-gather.10.cloned.1.call-update) | async-done | bytes 4194320 | tf_op jit(solution)/shard_map/all_gather | solution.py:152
  93.1 5.2 fusion.4
  98.3 21.6 %all-gather.16.cloned.1.call-done = bf16[2048,512]{1,0:T(8,128)(2,1)} async-done(((bf16[256,512]{1,0:T(8,128)(2,1)}), bf16[2048,512]{1,0:T(8,128)(2,1)}) %all-gather.16.cloned.1.call-update) | async-done | bytes 2097168 | tf_op jit(solution)/shard_map/all_gather | solution.py:157
  119.9 5.2 fusion.37
  131.7 18.0 %all-gather.14.cloned.1.call-done = bf16[2048,512]{1,0:T(8,128)(2,1)} async-done(((bf16[256,512]{1,0:T(8,128)(2,1)}), bf16[2048,512]{1,0:T(8,128)(2,1)}) %all-gather.14.cloned.1.call-update) | async-done | bytes 2097168 | tf_op jit(solution)/shard_map/all_gather | solution.py:156
  149.7 5.2 fusion.36
  162.8 4.0 subtract_convert_fusion.3
  168.9 8.8 fusion.35
  179.4 5.2 convolution_convert_fusion.8
  184.6 8.7 fusion
  193.3 7.6 fusion.19
  200.9 8.4 all-gather.18.cloned.1.call-done
  209.3 7.2 fusion.38
  219.4 285.9 %all-reduce.4.cloned.1.call-done = f32[1024,2048]{1,0:T(8,128)} async-done(((f32[1024,2048]{1,0:T(8,128)}), f32[1024,2048]{1,0:T(8,128)}) %all-reduce.4.cloned.1.call-update) | async-done | bytes 8388624 | tf_op jit(solution)/shard_map/psum | solution.py:175
  505.4 5.6 fusion.32
  516.8 46.1 %all-gather.22.cloned.1.call-done = bf16[2048,2048]{1,0:T(8,128)(2,1)} async-done(((bf16[256,2048]{1,0:T(8,128)(2,1)}), bf16[2048,2048]{1,0:T(8,128)(2,1)}) %all-gather.22.cloned.1.call-update) | async-done | bytes 8388624 | tf_op jit(solution)/shard_map/all_gather | solution.py:161
  562.9 14.5 fusion.40
  577.4 41.8 %all-gather.20.cloned.1.call-done = bf16[2048,2048]{1,0:T(8,128)(2,1)} async-done(((bf16[256,2048]{1,0:T(8,128)(2,1)}), bf16[2048,2048]{1,0:T(8,128)(2,1)}) %all-gather.20.cloned.1.call-update) | async-done | bytes 8388624 | tf_op jit(solution)/shard_map/all_gather | solution.py:160
  619.2 14.5 fusion.39
  633.7 65.2 %all-gather.26.cloned.1.call-done = bf16[1024,2048]{1,0:T(8,128)(2,1)} async-done(((bf16[1024,512]{1,0:T(8,128)(2,1)}), bf16[1024,2048]{1,0:T(8,128)(2,1)}) %all-gather.26.cloned.1.call-update) | async-done | bytes 4194320 | tf_op jit(solution)/shard_map/all_gather | solution.py:153
  698.9 58.9 %all-gather.24.cloned.1.call-done = bf16[2048,2048]{1,0:T(8,128)(2,1)} async-done(((bf16[2048,256]{1,0:T(8,128)(2,1)}), bf16[2048,2048]{1,0:T(8,128)(2,1)}) %all-gather.24.cloned.1.call-update) | async-done | bytes 8388624 | tf_op jit(solution)/shard_map/all_gather | solution.py:162
  757.8 22.0 %multiply_convert_fusion.1 = (bf16[1024,2048]{1,0:T(8,128)(2,1)}, bf16[1024,2048]{1,0:T(8,128)(2,1)}, bf16[1024,2048]{1,0:T(8,128)(2,1)}) fusion(f32[1024,2048]{1,0:T(8,128)} %fusion.39, f32[1024,2048]{1,0:T(8,128)} %fusion.40, bf16[1024,2048]{1,0:T(8,128)(2,1)} %all-gather.26.cloned.1.call-done, bf16[2048,2048]{1,0:T(8,128)(2,1)} %all-gather.24.cloned.1.call-done), kind=kOutput, calls=%fused_computation.19 | convolution fusion | flops 8621391872 | bytes 41943040 | tf_op jit(solution)/shard_map/dot_general | solution.py:25
  779.8 12.7 fusion.41
  792.5 13.6 convolution_add_fusion
  806.3 14.1 convolution_convert_fusion.3
  820.5 274.5 %all-reduce.6.cloned.1.call-done = f32[1024,2048]{1,0:T(8,128)} async-done(((f32[1024,2048]{1,0:T(8,128)}), f32[1024,2048]{1,0:T(8,128)}) %all-reduce.6.cloned.1.call-update) | async-done | bytes 8388624 | tf_op jit(solution)/shard_map/psum | solution.py:196
  1095.0 7.0 fusion.31
  1104.4 5.3 multiply_add_fusion
  1117.3 6.4 fusion.20
  1123.7 8.9 fusion.23
  1137.5 10.8 multiply_reduce_fusion
  1148.5 12.5 multiply_convert_fusion
  1170.3 6.2 convolution_convert_fusion.7
  1177.9 6.3 convolution_convert_fusion.6
  1184.3 14.3 convolution_convert_fusion
  1199.1 14.4 convolution_convert_fusion.1
  1213.6 14.3 convolution_convert_fusion.2
  1229.1 4.3 fusion.43
  1235.8 6.1 add_convert_fusion
  1247.1 18.5 %reduce-scatter.18.cloned.1.call-done = bf16[256,512]{1,0:T(8,128)(2,1)} async-done(((bf16[2048,512]{1,0:T(8,128)(2,1)}), bf16[256,512]{1,0:T(8,128)(2,1)}) %reduce-scatter.18.cloned.1.call-update) | async-done | bytes 262160 | tf_op jit(solution)/shard_map/reduce_scatter | solution.py:237
  1267.4 43.5 %reduce-scatter.14.cloned.1.call-done = bf16[256,512]{1,0:T(8,128)(2,1)} async-done(((bf16[2048,512]{1,0:T(8,128)(2,1)}), bf16[256,512]{1,0:T(8,128)(2,1)}) %reduce-scatter.14.cloned.1.call-update) | async-done | bytes 262160 | tf_op jit(solution)/shard_map/reduce_scatter | solution.py:231
  1312.7 43.2 %reduce-scatter.16.cloned.1.call-done = bf16[256,512]{1,0:T(8,128)(2,1)} async-done(((bf16[2048,512]{1,0:T(8,128)(2,1)}), bf16[256,512]{1,0:T(8,128)(2,1)}) %reduce-scatter.16.cloned.1.call-update) | async-done | bytes 262160 | tf_op jit(solution)/shard_map/reduce_scatter | solution.py:234
  1357.7 73.2 %reduce-scatter.26.cloned.1.call-done = bf16[2048,256]{1,0:T(8,128)(2,1)} async-done(((bf16[2048,2048]{1,0:T(8,128)(2,1)}), bf16[2048,256]{1,0:T(8,128)(2,1)}) %reduce-scatter.26.cloned.1.call-update) | async-done | bytes 1048592 | tf_op jit(solution)/shard_map/reduce_scatter | solution.py:249
  1433.6 71.9 %reduce-scatter.24.cloned.1.call-done = bf16[256,2048]{1,0:T(8,128)(2,1)} async-done(((bf16[2048,2048]{1,0:T(8,128)(2,1)}), bf16[256,2048]{1,0:T(8,128)(2,1)}) %reduce-scatter.24.cloned.1.call-update) | async-done | bytes 1048592 | tf_op jit(solution)/shard_map/reduce_scatter | solution.py:246
  1508.3 72.4 %reduce-scatter.22.cloned.1.call-done = bf16[256,2048]{1,0:T(8,128)(2,1)} async-done(((bf16[2048,2048]{1,0:T(8,128)(2,1)}), bf16[256,2048]{1,0:T(8,128)(2,1)}) %reduce-scatter.22.cloned.1.call-update) | async-done | bytes 1048592 | tf_op jit(solution)/shard_map/reduce_scatter | solution.py:243
  1583.4 76.1 %reduce-scatter.12.cloned.1.call-done = bf16[1024,512]{1,0:T(8,128)(2,1)} async-done(((bf16[1024,2048]{1,0:T(8,128)(2,1)}), bf16[1024,512]{1,0:T(8,128)(2,1)}) %reduce-scatter.12.cloned.1.call-update) | async-done | bytes 1048592 | tf_op jit(solution)/shard_map/reduce_scatter | solution.py:218
  1662.0 9.6 all-reduce
  1671.6 4.1 fusion.14
  (139 shorter events, 91.7 us)
Async XLA Ops:
  7.2 81.7 %all-gather.10.cloned.1.call-start = ((), (), s32[]{:S(2)}) async-start(), calls=%async_computation.9 | async-start | bytes 5242880 | tf_op jit(solution)/shard_map/all_gather | solution.py:152
  7.9 112.0 %all-gather.16.cloned.1.call-start = ((), (), s32[]{:S(2)}) async-start(), calls=%async_computation.12 | async-start | bytes 2359296 | tf_op jit(solution)/shard_map/all_gather | solution.py:157
  8.7 141.0 %all-gather.14.cloned.1.call-start = ((), (), s32[]{:S(2)}) async-start(), calls=%async_computation.11 | async-start | bytes 2359296 | tf_op jit(solution)/shard_map/all_gather | solution.py:156
  9.4 170.0 %all-gather.12.cloned.1.call-start = ((), (), s32[]{:S(2)}) async-start(), calls=%async_computation.10 | async-start | bytes 2359296 | tf_op jit(solution)/shard_map/all_gather | solution.py:158
  10.0 199.4 %all-gather.18.cloned.1.call-start = ((), (), s32[]{:S(2)}) async-start(), calls=%async_computation.13 | async-start | bytes 2359296 | tf_op jit(solution)/shard_map/all_gather | solution.py:159
  10.6 494.8 %all-reduce.4.cloned.1.call-start = ((), (), s32[]{:S(2)}) async-start(), calls=%async_computation.14 | async-start | bytes 16777216 | tf_op jit(solution)/shard_map/psum | solution.py:175
  17.1 145.7 %copy-start.4 = (f32[1024,64]{1,0:T(8,128)}, f32[1024,64]{1,0:T(8,128)S(1)}, u32[]{:S(2)}) copy-start(f32[1024,64]{1,0:T(8,128)S(1)} %get-tuple-element.103) | copy-start | bytes 786436
  88.9 4.2 copy-start.1
  162.8 6.0 copy-start.18
  166.9 1.0 copy-start.8
  166.9 1.3 copy-start.10
  166.9 1.6 copy-start.21
  166.9 2.0 copy-start.23
  184.6 8.7 copy-start.14
  216.6 346.3 %all-gather.22.cloned.1.call-start = ((), (), s32[]{:S(2)}) async-start(), calls=%async_computation.16 | async-start | bytes 9437184 | tf_op jit(solution)/shard_map/all_gather | solution.py:161
  217.3 401.9 %all-gather.20.cloned.1.call-start = ((), (), s32[]{:S(2)}) async-start(), calls=%async_computation.15 | async-start | bytes 9437184 | tf_op jit(solution)/shard_map/all_gather | solution.py:160
  218.1 480.8 %all-gather.26.cloned.1.call-start = ((), (), s32[]{:S(2)}) async-start(), calls=%async_computation.19 | async-start | bytes 5242880 | tf_op jit(solution)/shard_map/all_gather | solution.py:153
  218.8 539.0 %all-gather.24.cloned.1.call-start = ((), (), s32[]{:S(2)}) async-start(), calls=%async_computation.17 | async-start | bytes 9437184 | tf_op jit(solution)/shard_map/all_gather | solution.py:162
  219.4 875.6 %all-reduce.6.cloned.1.call-start = ((), (), s32[]{:S(2)}) async-start(), calls=%async_computation.20 | async-start | bytes 16777216 | tf_op jit(solution)/shard_map/psum | solution.py:196
  511.0 3.2 copy-start
  779.8 12.7 copy-start.28
  806.2 435.8 %reduce-scatter.10.cloned.1.call-start = ((), (), s32[]{:S(2)}) async-start(), calls=%async_computation.18 | async-start | bytes 5242880 | tf_op jit(solution)/shard_map/reduce_scatter | solution.py:184
  820.4 424.8 %reduce-scatter.20.cloned.1.call-start = ((), (), s32[]{:S(2)}) async-start(), calls=%async_computation.25 | async-start | bytes 2359296 | tf_op jit(solution)/shard_map/reduce_scatter | solution.py:240
  1095.0 8.2 copy-start.2
  1095.0 9.4 copy-start.6
  1109.8 3.3 copy-start.3
  1116.8 148.8 %reduce-scatter.18.cloned.1.call-start = ((), (), s32[]{:S(2)}) async-start(), calls=%async_computation.24 | async-start | bytes 2359296 | tf_op jit(solution)/shard_map/reduce_scatter | solution.py:237
  1123.7 9.9 copy-start.7
  1132.7 1.0 copy-start.12
  1133.7 3.8 copy-start.15
  1148.3 162.6 %reduce-scatter.14.cloned.1.call-start = ((), (), s32[]{:S(2)}) async-start(), calls=%async_computation.22 | async-start | bytes 2359296 | tf_op jit(solution)/shard_map/reduce_scatter | solution.py:231
  1148.5 12.5 copy-start.9
  1148.5 12.5 copy-start.11
  1161.1 3.4 copy-start.22
  1161.1 3.4 copy-start.24
  1164.5 2.4 copy-start.5
  1164.6 2.4 copy-start.16
  1176.5 179.4 %reduce-scatter.16.cloned.1.call-start = ((), (), s32[]{:S(2)}) async-start(), calls=%async_computation.23 | async-start | bytes 2359296 | tf_op jit(solution)/shard_map/reduce_scatter | solution.py:234
  1177.9 6.3 copy-start.19
  1184.2 246.7 %reduce-scatter.26.cloned.1.call-start = ((), (), s32[]{:S(2)}) async-start(), calls=%async_computation.28 | async-start | bytes 9437184 | tf_op jit(solution)/shard_map/reduce_scatter | solution.py:249
  1198.6 306.8 %reduce-scatter.24.cloned.1.call-start = ((), (), s32[]{:S(2)}) async-start(), calls=%async_computation.27 | async-start | bytes 9437184 | tf_op jit(solution)/shard_map/reduce_scatter | solution.py:246
  1213.5 367.1 %reduce-scatter.22.cloned.1.call-start = ((), (), s32[]{:S(2)}) async-start(), calls=%async_computation.26 | async-start | bytes 9437184 | tf_op jit(solution)/shard_map/reduce_scatter | solution.py:243
  1227.8 1.2 copy-start.20
  1227.8 5.5 copy-start.17
  1227.9 431.7 %reduce-scatter.12.cloned.1.call-start = ((), (), s32[]{:S(2)}) async-start(), calls=%async_computation.21 | async-start | bytes 5242880 | tf_op jit(solution)/shard_map/reduce_scatter | solution.py:218
  1229.0 4.3 copy-start.27
  1233.4 2.4 copy-start.13
  1433.6 238.0 %copy-start.26 = (f32[1024]{0:T(1024)S(1)}, f32[1024]{0:T(1024)}, u32[]{:S(2)}) copy-start(f32[1024]{0:T(1024)} %copy-done.25) | copy-start | bytes 12292
  (1 other events, 0.6 us)
Sparse Core Ops, SparseCore 0:
  9.6 79.2 all-gather.9
  90.7 29.0 all-gather.15
  121.8 27.8 all-gather.13
  151.4 27.8 all-gather.11
  181.1 28.1 all-gather.17
  216.7 288.6 all-reduce.3
  507.3 55.5 all-gather.21
  564.8 54.3 all-gather.19
  620.8 78.0 all-gather.25
  700.6 57.1 all-gather.23
  806.3 288.6 all-reduce.5
  1097.2 77.9 reduce-scatter.9
  1178.8 41.7 reduce-scatter.19
  1224.3 41.2 reduce-scatter.17
  1269.6 41.2 reduce-scatter.13
  1314.6 41.2 reduce-scatter.15
  1359.6 71.2 reduce-scatter.25
  1434.2 71.2 reduce-scatter.23
  1509.3 71.2 reduce-scatter.21
  1582.8 76.7 reduce-scatter.11
where the time goes:
time: 1690 us; the launch traced here: 1680 us
  waiting for transfers between devices  1300 us (77%)
  matrix products  239 us (14%)
  other arithmetic  88.8 us (5%)
  local copies, waits for them, and re-layouts  29.7 us (2%)
    psum x1, waiting for transfers between devices, on_device(): resid_full = inputs + lax.psum(attn_terms, 'col')  286 us
    psum x1, waiting for transfers between devices, on_device(): grad_norm = lax.psum(norm_terms, 'col')  275 us
    reduce_scatter x1, waiting for transfers between devices, on_device(): lax.psum_scatter(input_terms.astype(jnp.bfloat16), 'col', scatter_dimensi...  76.1 us
    reduce_scatter x1, waiting for transfers between devices, on_device(): lax.psum_scatter(grad_down.astype(jnp.bfloat16), 'row', scatter_dimension...  73.2 us
    reduce_scatter x1, waiting for transfers between devices, on_device(): lax.psum_scatter(grad_gate.astype(jnp.bfloat16), 'row', scatter_dimension...  72.4 us
    reduce_scatter x1, waiting for transfers between devices, on_device(): lax.psum_scatter(grad_up.astype(jnp.bfloat16), 'row', scatter_dimension=0...  71.9 us
    all_gather x1, waiting for transfers between devices, on_device(): lax.all_gather(tokens, 'col', axis=1, tiled=True)  71.7 us
    dot_general x7, matrix products, matmul_nt(): lax.dot_general(left, right, (((1,), (1,)), ((), ())), preferred_element_...  67.6 us
  transfers between devices with their start and end apart: 20, of which 18 were waited for; matrix products, arithmetic and copies ran while one was open for 17% of the time, Pallas kernels for 0%

commit v1 on v0

v1 whole, which is shorter than its diff:
```python
import functools

import jax
import jax.numpy as jnp
from jax import lax
from jax.experimental import pallas as pl
from jax.experimental.pallas import tpu as pltpu
from jax.sharding import PartitionSpec as P

HEAD_DIM = 128
HALF = HEAD_DIM // 2
SEQ = 1024
EPSILON = 1e-05
MASKED = -1e30
SCALE = HEAD_DIM ** (-0.5)
BF = jnp.bfloat16
F32 = jnp.float32
MIB = 1 << 20
ANY = pl.BlockSpec(memory_space=pl.ANY)


def dot_nn(left, right):
    return jnp.dot(left, right, preferred_element_type=F32)


def dot_tn(left, right):
    return lax.dot_general(left, right, (((0,), (0,)), ((), ())), preferred_element_type=F32)


def dot_nt(left, right):
    return lax.dot_general(left, right, (((1,), (1,)), ((), ())), preferred_element_type=F32)


def struct(shape, dtype):
    return jax.ShapeDtypeStruct(shape, dtype)


def params(mib=60):
    return pltpu.CompilerParams(vmem_limit_bytes=mib * MIB)


def cost(flops, moved):
    return pl.CostEstimate(flops=int(flops), bytes_accessed=int(moved), transcendentals=0)


def count_seen(segment_ids):
    places = jnp.arange(segment_ids.shape[0], dtype=jnp.int32)
    causal = places[None, :] <= places[:, None]
    allowed = (segment_ids[:, None] == segment_ids[None, :]) & causal
    return jnp.sum(allowed.astype(jnp.int32), axis=1) - 1


def rope_tables(segments):
    positions = jax.vmap(count_seen)(segments.reshape(-1, SEQ)).reshape(-1)
    inverse = 10000.0 ** (-(jnp.arange(HALF, dtype=F32) * 2.0 / HEAD_DIM))
    angles = positions.astype(F32)[:, None] * inverse[None, :]
    cosine, sine = jnp.cos(angles), jnp.sin(angles)
    return jnp.concatenate([cosine, cosine], 1), jnp.concatenate([-sine, sine], 1)


def turn(values, cos_table, sin_table):
    return values * cos_table + pltpu.roll(values, HALF, 1) * sin_table


def norm_rows(x):
    centre = jnp.mean(x, axis=-1, keepdims=True)
    spread = jnp.mean(x * x, axis=-1, keepdims=True) - centre * centre
    inverse = lax.rsqrt(spread + EPSILON)
    return centre, inverse


def qkv_kernel(C, place, *refs):
    pieces = refs[:C]
    w_ref, cos_ref, sin_ref, x_ref, a_ref, q_ref, k_ref, v_ref, mu_ref, r_ref = refs[C:]
    width = pieces[0].shape[1]
    me = place[0]
    for k in range(C):
        owner = lax.rem(me - k + C, C)
        x_ref[:, pl.ds(pl.multiple_of(owner * width, width), width)] = pieces[k][...]
    x = x_ref[...].astype(F32)
    centre, inverse = norm_rows(x)
    a = ((x - centre) * inverse).astype(BF)
    a_ref[...] = a
    mu_ref[...] = centre
    r_ref[...] = inverse
    cosine, sine = cos_ref[...], sin_ref[...]
    for index, out in enumerate((q_ref, k_ref, v_ref)):
        product = dot_nn(a, w_ref[:, index * width : (index + 1) * width])
        if index == 2:
            out[...] = product.astype(BF)
            continue
        for start in range(0, width, HEAD_DIM):
            part = product[:, start : start + HEAD_DIM]
            out[:, start : start + HEAD_DIM] = turn(part, cosine, sine).astype(BF)


def norm_and_project(place, pieces, w_qkv, cos_table, sin_table):
    C = len(pieces)
    T, width = pieces[0].shape
    D = width * C
    bt = 256
    rows = lambda n: pl.BlockSpec((bt, n), lambda i, p: (i, 0))
    return pl.pallas_call(
        functools.partial(qkv_kernel, C),
        grid_spec=pltpu.PrefetchScalarGridSpec(
            num_scalar_prefetch=1,
            grid=(T // bt,),
            in_specs=[rows(width)] * C
            + [
                pl.BlockSpec(w_qkv.shape, lambda i, p: (0, 0), pipeline_mode=pl.Buffered(1)),
                rows(HEAD_DIM),
                rows(HEAD_DIM),
            ],
            out_specs=[rows(D), rows(D), rows(width), rows(width), rows(width), rows(1), rows(1)],
        ),
        out_shape=[
            struct((T, D), BF),
            struct((T, D), BF),
            struct((T, width), BF),
            struct((T, width), BF),
            struct((T, width), BF),
            struct((T, 1), F32),
            struct((T, 1), F32),
        ],
        compiler_params=params(),
        cost_estimate=cost(2 * T * D * 3 * width, 14 * MIB),
        name="norm_and_project",
    )(place, *pieces, w_qkv, cos_table, sin_table)


def allowed_block(seg_key, seg_query, first_query):
    shape = (seg_key.shape[0], seg_query.shape[1])
    keys = lax.broadcasted_iota(jnp.int32, shape, 0)
    queries = lax.broadcasted_iota(jnp.int32, shape, 1) + first_query
    return (seg_key == seg_query) & (keys <= queries)


def attend_kernel(bq, q_ref, k_ref, v_ref, segk_ref, segq_ref, o_ref, log_ref):
    length = q_ref.shape[0]
    for start in range(0, length, bq):
        stop = start + bq
        scores = dot_nt(k_ref[:stop], q_ref[start:stop]) * SCALE
        allowed = allowed_block(segk_ref[:stop], segq_ref[0, :, start:stop], start)
        scores = jnp.where(allowed, scores, MASKED)
        peak = jnp.max(scores, axis=0, keepdims=True)
        exponent = jnp.exp(scores - peak)
        total = jnp.sum(exponent, axis=0, keepdims=True)
        weights = (exponent * (1.0 / total)).astype(BF)
        o_ref[start:stop] = dot_tn(v_ref[:stop], weights).T.astype(BF)
        log_ref[0, 0, :, start:stop] = peak + jnp.log(total)


def attend(q, k, v, seg_column, seg_row):
    T, width = q.shape
    heads, sequences = width // HEAD_DIM, T // SEQ
    one = pl.BlockSpec((SEQ, HEAD_DIM), lambda s, h: (s, h))
    return pl.pallas_call(
        functools.partial(attend_kernel, 256),
        grid=(sequences, heads),
        in_specs=[
            one,
            one,
            one,
            pl.BlockSpec((SEQ, 1), lambda s, h: (s, 0)),
            pl.BlockSpec((1, 1, SEQ), lambda s, h: (s, 0, 0)),
        ],
        out_specs=[one, pl.BlockSpec((1, 1, 1, SEQ), lambda s, h: (s, h, 0, 0))],
        out_shape=[struct((T, width), BF), struct((sequences, heads, 1, SEQ), F32)],
        compiler_params=params(),
        cost_estimate=cost(4 * T * SEQ * width, 5 * MIB),
        name="attend",
    )(q, k, v, seg_column, seg_row)


def attend_back_kernel(
    bq, q_ref, k_ref, v_ref, do_ref, log_ref, segk_ref, segq_ref, cos_ref, sin_ref, dq_ref, dk_ref, dv_ref, dk_sum, dv_sum
):
    length = q_ref.shape[0]
    dk_sum[...] = jnp.zeros_like(dk_sum)
    dv_sum[...] = jnp.zeros_like(dv_sum)
    for start in range(0, length, bq):
        stop = start + bq
        keys, queries, grads = k_ref[:stop], q_ref[start:stop], do_ref[start:stop]
        scores = dot_nt(keys, queries) * SCALE
        allowed = allowed_block(segk_ref[:stop], segq_ref[0, :, start:stop], start)
        scores = jnp.where(allowed, scores, MASKED)
        probs = jnp.exp(scores - log_ref[0, 0, :, start:stop])
        dv_sum[:stop] += dot_nn(probs.astype(BF), grads)
        grad_probs = dot_nt(v_ref[:stop], grads)
        inner = jnp.sum(probs * grad_probs, axis=0, keepdims=True)
        grad_scores = (probs * (grad_probs - inner)).astype(BF)
        dk_sum[:stop] += dot_nn(grad_scores, queries)
        grad_query = dot_tn(keys, grad_scores).T * SCALE
        dq_ref[start:stop] = turn(grad_query, cos_ref[start:stop], -sin_ref[start:stop]).astype(BF)
    dk_ref[...] = turn(dk_sum[...] * SCALE, cos_ref[...], -sin_ref[...]).astype(BF)
    dv_ref[...] = dv_sum[...].astype(BF)


def attend_back(q, k, v, do, log_total, seg_column, seg_row, cos_table, sin_table):
    T, width = q.shape
    heads, sequences = width // HEAD_DIM, T // SEQ
    one = pl.BlockSpec((SEQ, HEAD_DIM), lambda s, h: (s, h))
    table = pl.BlockSpec((SEQ, HEAD_DIM), lambda s, h: (s, 0))
    return pl.pallas_call(
        functools.partial(attend_back_kernel, 256),
        grid=(sequences, heads),
        in_specs=[
            one,
            one,
            one,
            one,
            pl.BlockSpec((1, 1, 1, SEQ), lambda s, h: (s, h, 0, 0)),
            pl.BlockSpec((SEQ, 1), lambda s, h: (s, 0)),
            pl.BlockSpec((1, 1, SEQ), lambda s, h: (s, 0, 0)),
            table,
            table,
        ],
        out_specs=[one, one, one],
        out_shape=[struct((T, width), BF)] * 3,
        scratch_shapes=[pltpu.VMEM((SEQ, HEAD_DIM), F32), pltpu.VMEM((SEQ, HEAD_DIM), F32)],
        compiler_params=params(),
        cost_estimate=cost(10 * T * SEQ * width, 9 * MIB),
        name="attend_back",
    )(q, k, v, do, log_total, seg_column, seg_row, cos_table, sin_table)


def out_kernel(C, place, *refs):
    pieces = refs[:C]
    w_ref, x_ref, o_ref, h_ref, b_ref, mu_ref, r_ref = refs[C:]
    width = pieces[0].shape[1]
    blocks, part = w_ref.shape[0], w_ref.shape[2]
    me = place[0]
    for k in range(C):
        owner = lax.rem(me - k + C, C)
        o_ref[:, pl.ds(pl.multiple_of(owner * width, width), width)] = pieces[k][...]
    heads = o_ref[...]
    for n in range(blocks):
        columns = slice(n * part, (n + 1) * part)
        h_ref[:, columns] = x_ref[:, columns].astype(F32) + dot_nn(heads, w_ref[n])
    h = h_ref[...]
    centre, inverse = norm_rows(h)
    b_ref[...] = ((h - centre) * inverse).astype(BF)
    mu_ref[...] = centre
    r_ref[...] = inverse


def project_and_norm(place, pieces, w_out, x_full):
    C = len(pieces)
    T, D = x_full.shape
    width = D // C
    bt = 256
    rows = lambda n: pl.BlockSpec((bt, n), lambda i, p: (i, 0))
    return pl.pallas_call(
        functools.partial(out_kernel, C),
        grid_spec=pltpu.PrefetchScalarGridSpec(
            num_scalar_prefetch=1,
            grid=(T // bt,),
            in_specs=[rows(width)] * C
            + [pl.BlockSpec(w_out.shape, lambda i, p: (0, 0, 0), pipeline_mode=pl.Buffered(1)), rows(D)],
            out_specs=[rows(D), rows(D), rows(D), rows(1), rows(1)],
        ),
        out_shape=[
            struct((T, D), BF),
            struct((T, D), F32),
            struct((T, D), BF),
            struct((T, 1), F32),
            struct((T, 1), F32),
        ],
        compiler_params=params(),
        cost_estimate=cost(2 * T * D * D, 32 * MIB),
        name="project_and_norm",
    )(place, *pieces, w_out, x_full)


def hidden_kernel(b_ref, dy_ref, wg_ref, wu_ref, wd_ref, hm_ref, dg_ref, du_ref):
    b = b_ref[...]
    gate = dot_nn(b, wg_ref[...])
    upward = dot_nn(b, wu_ref[...])
    grad_hidden = dot_nn(dy_ref[...], wd_ref[...])
    sigmoid = jax.nn.sigmoid(gate)
    silu = gate * sigmoid
    hm_ref[...] = (silu * upward).astype(BF)
    dg_ref[...] = (grad_hidden * upward * sigmoid * (1.0 + gate * (1.0 - sigmoid))).astype(BF)
    du_ref[...] = (grad_hidden * silu).astype(BF)


def hidden_units(b, dy, w_gate, w_up, w_down):
    T, D = b.shape
    F = w_gate.shape[1]
    bt, bf = 512, 512
    left = pl.BlockSpec((bt, D), lambda j, i: (i, 0))
    right = pl.BlockSpec((D, bf), lambda j, i: (0, j))
    out = pl.BlockSpec((bt, bf), lambda j, i: (i, j))
    return pl.pallas_call(
        hidden_kernel,
        grid=(F // bf, T // bt),
        in_specs=[left, left, right, right, right],
        out_specs=[out, out, out],
        out_shape=[struct((T, F), BF)] * 3,
        compiler_params=params(),
        cost_estimate=cost(6 * T * D * F, 60 * MIB),
        name="hidden_units",
    )(b, dy, w_gate, w_up, w_down)


def sum_nt_kernel(pairs, *refs):
    total = dot_nt(refs[0][...], refs[pairs][...])
    for k in range(1, pairs):
        total += dot_nt(refs[k][...], refs[pairs + k][...])
    refs[-1][...] = total.astype(refs[-1].dtype)


def sum_nt(lefts, rights, name):
    T = lefts[0].shape[0]
    N = rights[0].shape[0]
    bt, bn = 512, 512
    deep = sum(left.shape[1] for left in lefts)
    return pl.pallas_call(
        functools.partial(sum_nt_kernel, len(lefts)),
        grid=(N // bn, T // bt),
        in_specs=[pl.BlockSpec((bt, left.shape[1]), lambda j, i: (i, 0)) for left in lefts]
        + [pl.BlockSpec((bn, right.shape[1]), lambda j, i: (j, 0)) for right in rights],
        out_specs=pl.BlockSpec((bt, bn), lambda j, i: (i, j)),
        out_shape=struct((T, N), BF),
        compiler_params=params(),
        cost_estimate=cost(2 * T * N * deep, 40 * MIB),
        name=name,
    )(*lefts, *rights)


def resid_back_kernel(C, place, *refs):
    terms = refs[:C]
    h_ref, mu_ref, r_ref, dy_ref, w_ref, dh_ref, do_ref = refs[C:]

    @pl.when(pl.program_id(0) == 0)
    def _():
        grad = terms[0][...].astype(F32)
        for k in range(1, C):
            grad += terms[k][...].astype(F32)
        inverse = r_ref[...]
        normed = (h_ref[...] - mu_ref[...]) * inverse
        first = jnp.mean(grad, axis=1, keepdims=True)
        second = jnp.mean(grad * normed, axis=1, keepdims=True)
        dh = dy_ref[...].astype(F32) + inverse * (grad - first - normed * second)
        dh_ref[...] = dh.astype(BF)

    part = w_ref.shape[2]
    total = dot_nt(dh_ref[:, :part], w_ref[0])
    for n in range(1, w_ref.shape[0]):
        total += dot_nt(dh_ref[:, n * part : (n + 1) * part], w_ref[n])
    do_ref[...] = total.astype(BF)


def resid_back(place, terms, h, mu, r, dy, w_out):
    C = len(terms)
    rows, D = terms[0].shape
    bn = 512
    whole = pl.BlockSpec((rows, D), lambda j, p: (0, 0))
    mine = lambda n: pl.BlockSpec((rows, n), lambda j, p: (p[0], 0))
    return pl.pallas_call(
        functools.partial(resid_back_kernel, C),
        grid_spec=pltpu.PrefetchScalarGridSpec(
            num_scalar_prefetch=1,
            grid=(D // bn,),
            in_specs=[whole] * C
            + [
                mine(D),
                mine(1),
                mine(1),
                mine(D),
                pl.BlockSpec((w_out.shape[0], bn, w_out.shape[2]), lambda j, p: (0, j, 0)),
            ],
            out_specs=[whole, pl.BlockSpec((rows, bn), lambda j, p: (0, j))],
        ),
        out_shape=[struct((rows, D), BF), struct((rows, D), BF)],
        compiler_params=params(),
        cost_estimate=cost(2 * rows * D * D, 20 * MIB),
        name="resid_back",
    )(place, *terms, h, mu, r, dy, w_out)


def on_device(R, C, tokens, cotangent, segments, w_query, w_key, w_value, w_out, w_gate, w_up, w_down):
    T, width = tokens.shape
    D = width * C
    rows = T // C
    me = lax.axis_index("col")
    place = me.astype(jnp.int32).reshape(1)

    def shift(values, k):
        return lax.ppermute(values, "col", [(i, (i + k) % C) for i in range(C)])

    def pieces_of(values):
        return [values] + [shift(values, k) for k in range(1, C)]

    def block(values, k, axis):
        size = values.shape[axis] // C
        return lax.dynamic_slice_in_dim(values, lax.rem(me + k, C) * size, size, axis)

    def scattered(values, axis):
        return [block(values, 0, axis)] + [shift(block(values, k, axis), k) for k in range(1, C)]

    def assembled(pieces, axis):
        shape = list(pieces[0].shape)
        size = shape[axis]
        shape[axis] = size * C
        whole = jnp.zeros(shape, pieces[0].dtype)
        for k, piece in enumerate(pieces):
            whole = lax.dynamic_update_slice_in_dim(whole, piece, lax.rem(me - k + C, C) * size, axis)
        return whole

    def total_of(terms):
        total = terms[0].astype(F32)
        for term in terms[1:]:
            total = total + term.astype(F32)
        return total

    gathered = lambda w: lax.all_gather(w, "row", axis=0, tiled=True)

    x_pieces = pieces_of(tokens)
    w_qkv = gathered(jnp.concatenate([w_query, w_key, w_value], axis=1))
    cos_table, sin_table = rope_tables(segments)
    seg_column, seg_row = segments.reshape(T, 1), segments.reshape(-1, 1, SEQ)
    x_full, act_one, q, k, v, mu_one, r_one = norm_and_project(place, x_pieces, w_qkv, cos_table, sin_table)
    out_w = lax.all_gather(assembled(pieces_of(w_out), 0), "row", axis=0, tiled=False)
    gate_w, up_w, down_w = gathered(w_gate), gathered(w_up), gathered(w_down.T)
    attended, log_total = attend(q, k, v, seg_column, seg_row)
    o_full, h_full, act_two, mu_two, r_two = project_and_norm(place, pieces_of(attended), out_w, x_full)
    dy_full = assembled(pieces_of(cotangent), 1)
    hidden, grad_gate_in, grad_up_in = hidden_units(act_two, dy_full, gate_w, up_w, down_w)
    norm_terms = sum_nt([grad_gate_in, grad_up_in], [gate_w, up_w], "norm_terms")
    term_list = scattered(norm_terms, 0)
    grad_down = dot_tn(dy_full, hidden).astype(BF)
    grad_gate = dot_tn(act_two, grad_gate_in).astype(BF)
    grad_up = dot_tn(act_two, grad_up_in).astype(BF)
    out_terms = sum_nt([hidden], [down_w], "out_terms")
    scatter = lambda g: lax.psum_scatter(g, "row", scatter_dimension=0, tiled=True)
    grad_down, grad_gate, grad_up = scatter(grad_down), scatter(grad_gate), scatter(grad_up)

    grad_resid_r, grad_attn = resid_back(place, term_list, h_full, mu_two, r_two, dy_full, out_w)
    both = scattered(jnp.stack([grad_attn, grad_resid_r]), 2)
    whole = assembled(both, 1)
    grad_heads, grad_resid = whole[0], whole[1]
    my_heads = lax.dynamic_slice_in_dim(o_full, me * rows, rows, 0)
    grad_out = scatter(dot_tn(grad_resid_r, my_heads).astype(BF))
    grad_out = total_of(scattered(grad_out, 1)).T

    out_sum = total_of(scattered(out_terms, 1))
    output = (lax.dynamic_slice_in_dim(h_full, me * width, width, 1) + out_sum).astype(BF)

    dq, dk, dv = attend_back(q, k, v, grad_heads, log_total, seg_column, seg_row, cos_table, sin_table)
    w_list = [w_qkv[:, i * width : (i + 1) * width] for i in range(3)]
    input_terms = sum_nt([dq, dk, dv], w_list, "input_terms")
    grad_input = total_of(scattered(input_terms, 1))
    grad_qkv = scatter(dot_tn(act_one, jnp.concatenate([dq, dk, dv], axis=1)).astype(BF)).astype(F32)
    normed = (tokens.astype(F32) - mu_one) * r_one
    sums = lax.psum(jnp.stack([jnp.sum(grad_input, axis=1), jnp.sum(grad_input * normed, axis=1)]), "col")
    grad_tokens = grad_resid.astype(F32) + r_one * (
        grad_input - (sums[0] / D)[:, None] - normed * (sums[1] / D)[:, None]
    )
    return (
        output,
        grad_tokens.astype(BF),
        grad_qkv[:, :width],
        grad_qkv[:, width : 2 * width],
        grad_qkv[:, 2 * width :],
        grad_out,
        grad_gate.astype(F32),
        grad_up.astype(F32),
        grad_down.astype(F32).T,
    )


def solution(mesh):
    here = P("row", "col")
    turned = P("col", "row")
    return jax.shard_map(
        functools.partial(on_device, mesh.shape["row"], mesh.shape["col"]),
        mesh=mesh,
        in_specs=(here, here, P("row"), here, here, here, turned, here, here, turned),
        out_specs=(here, here, here, here, here, turned, here, here, turned),
        check_vma=False,
    )
```

time: 1690 us -> 960 us (0.57)
  waiting for transfers between devices: 1300 us -> 585 us
  matrix products: 239 us -> 62.4 us
  Pallas kernels: 0 us -> 165 us
  other arithmetic: 88.8 us -> 30.3 us
  starting transfers between devices: 2.22 us -> 39.2 us
    psum x2 -> x0, waiting for transfers between devices: 560 us -> none  [the longest x1 286 us: on_device(): resid_full = inputs + lax.psum(attn_terms, 'col')]
    ppermute x0 -> x27, waiting for transfers between devices: none -> 510 us  [shift(): return lax.ppermute(values, 'col', [(i, (i + k) % C) for i in range(C)])]
    all_gather x9 -> x5, waiting for transfers between devices: 333 us -> 0.06 us  [the longest x4 0.06 us: on_device(): gathered = lambda w: lax.all_gather(w, 'row', axis=0, tiled=True)]
    reduce_scatter x9 -> x5, waiting for transfers between devices: 399 us -> 73 us  [on_device(): lax.psum_scatter(g, 'row', scatter_dimension=0, tiled=True)]
    dot_general x27 -> x5, matrix products: 239 us -> 62.4 us  [dot_tn(): lax.dot_general(left, right, (((0,), (0,)), ((), ())), preferred_element_...]
    pallas_call x0 -> x9, Pallas kernels: none -> 165 us  [the longest x3 60 us: sum_nt(): pl.pallas_call(functools.partial(sum_nt_kernel, len(lefts)), grid=(N // b...]
    ppermute x0 -> x27, starting transfers between devices: none -> 38.4 us  [shift(): return lax.ppermute(values, 'col', [(i, (i + k) % C) for i in range(C)])]
    reduce_sum x5 -> x1, other arithmetic: 26 us -> 0.53 us  [count_seen(): return jnp.sum(allowed.astype(jnp.int32), axis=1) - 1]
  transfers between devices with their start and end apart: 20 -> 37, of which waited for: 18 -> 23; matrix products, arithmetic and copies ran while one was open for 17% -> 12% of each run, Pallas kernels for 0% -> 8%
where the time goes in v1:
time: 960 us; the launch traced here: 951 us
  waiting for transfers between devices  585 us (61%)
  Pallas kernels  165 us (17%)
  matrix products  62.4 us (6%)
  local copies, waits for them, and re-layouts  45.2 us (5%)
  starting transfers between devices  39.2 us (4%)
  other arithmetic  30.3 us (3%)
  between operations  14.9 us (2%)
    ppermute x27, waiting for transfers between devices, shift(): return lax.ppermute(values, 'col', [(i, (i + k) % C) for i in range(C)])  510 us
    reduce_scatter x5, waiting for transfers between devices, on_device(): lax.psum_scatter(g, 'row', scatter_dimension=0, tiled=True)  73 us
    dot_general x5, matrix products, dot_tn(): lax.dot_general(left, right, (((0,), (0,)), ((), ())), preferred_element_...  62.4 us
    pallas_call x3, Pallas kernels, sum_nt(): pl.pallas_call(functools.partial(sum_nt_kernel, len(lefts)), grid=(N // b...  60 us
    ppermute x27, starting transfers between devices, shift(): return lax.ppermute(values, 'col', [(i, (i + k) % C) for i in range(C)])  38.4 us
    pallas_call x1, Pallas kernels, hidden_units(): pl.pallas_call(hidden_kernel, grid=(F // bf, T // bt), in_specs=[left, le...  37.3 us
  transfers between devices with their start and end apart: 37, of which 23 were waited for; matrix products, arithmetic and copies ran while one was open for 12% of the time, Pallas kernels for 8%

profile of v1, /device:TPU:8, one launch (start us, length us, event | category | flops | bytes accessed | tf_op | source)
XLA Modules:
  0.0 951.1 jit_solution(8792164440846208070)
XLA Ops:
  15.3 14.0 %collective-permute-done.6 = bf16[512,256]{1,0:T(8,128)(2,1)} collective-permute-done((bf16[512,256]{1,0:T(8,128)(2,1)}, bf16[512,256]{1,0:T(8,128)(2,1)}, u32[]{:S(2)}, u32[]{:S(2)}) %collective-permute-start.6) | collective-permute-done | bytes 262176 | tf_op jit(solution)/shard_map/ppermute | solution.py:390
  30.3 3.5 collective-permute-done.7
  39.4 2.7 collective-permute-start.1
  51.2 14.3 %collective-permute-done.refs_1_ = bf16[1024,512]{1,0:T(8,128)(2,1)} collective-permute-done((bf16[1024,512]{1,0:T(8,128)(2,1)S(1)}, bf16[1024,512]{1,0:T(8,128)(2,1)}, u32[]{:S(2)}, u32[]{:S(2)}) %collective-permute-start) | collective-permute-done | bytes 1048608 | tf_op jit(solution)/shard_map/ppermute | solution.py:390
  67.8 62.4 %collective-permute-done.1.refs_2_ = bf16[1024,512]{1,0:T(8,128)(2,1)} collective-permute-done((bf16[1024,512]{1,0:T(8,128)(2,1)S(1)}, bf16[1024,512]{1,0:T(8,128)(2,1)}, u32[]{:S(2)}, u32[]{:S(2)}) %collective-permute-start.1) | collective-permute-done | bytes 1048608 | tf_op jit(solution)/shard_map/ppermute | solution.py:390
  130.2 48.6 %collective-permute-done.2.refs_3_ = bf16[1024,512]{1,0:T(8,128)(2,1)} collective-permute-done((bf16[1024,512]{1,0:T(8,128)(2,1)S(1)}, bf16[1024,512]{1,0:T(8,128)(2,1)}, u32[]{:S(2)}, u32[]{:S(2)}) %collective-permute-start.2) | collective-permute-done | bytes 1048608 | tf_op jit(solution)/shard_map/ppermute | solution.py:390
  178.8 14.5 %norm_and_project.1 = (bf16[1024,2048]{1,0:T(8,128)(2,1)}, bf16[1024,2048]{1,0:T(8,128)(2,1)}, bf16[1024,512]{1,0:T(8,128)(2,1)}, bf16[1024,512]{1,0:T(8,128)(2,...) custom-call(s32[1]{0:T(128)} %bitcast.place, bf16[1024,512]{1,0:T(8,128)(2,1)} %refs_0_.1, ...), custom_call_target="tpu_custom_call" | custom-call | flops 6442450944 | bytes 14680064 | tf_op jit(solution)/shard_map/norm_and_project/pallas_call | solution.py:103
  193.2 10.9 %attend.1 = (bf16[1024,512]{1,0:T(8,128)(2,1)}, f32[1,4,1,1024]{3,2,1,0:T(1,128)}) custom-call(bf16[1024,512]{1,0:T(8,128)(2,1)} %get-tuple-element.31.q_ref, bf16[1024,512]{1,0:T(8,128)(2,1)} %get-tuple-element.32.k_ref, bf16[1024,512]{1,0:T(8,128)(2,1)} %get-tuple-element.33.v_ref, s32[1024,1]{1,0:T(8,128)} %copy.32.segk_ref, s32[1,1,1024]{2,1,0:T(1,128)} %bitcast.44), custom_call_target="tpu_custom_call" | custom-call | flops 2147483648 | bytes 5242880 | tf_op jit(solution)/shard_map/attend/pallas_call | solution.py:157
  204.2 2.4 collective-permute-start.5
  206.6 2.5 broadcast_in_dim.4
  213.7 6.6 collective-permute-done.10
  222.7 44.1 %collective-permute-done.11 = bf16[1024,512]{1,0:T(8,128)(2,1)S(1)} collective-permute-done((bf16[1024,512]{1,0:T(8,128)(2,1)}, bf16[1024,512]{1,0:T(8,128)(2,1)S(1)}, u32[]{:S(2)}, u32[]{:S(2)}) %collective-permute-start.11) | collective-permute-done | bytes 1048608 | tf_op jit(solution)/shard_map/ppermute | solution.py:390
  267.8 19.9 %collective-permute-done.3.refs_1_ = bf16[1024,512]{1,0:T(8,128)(2,1)S(1)} collective-permute-done((bf16[1024,512]{1,0:T(8,128)(2,1)}, bf16[1024,512]{1,0:T(8,128)(2,1)S(1)}, u32[]{:S(2)}, u32[]{:S(2)}) %collective-permute-start.3) | collective-permute-done | bytes 1048608 | tf_op jit(solution)/shard_map/ppermute | solution.py:390
  287.8 21.8 %collective-permute-done.4.refs_2_ = bf16[1024,512]{1,0:T(8,128)(2,1)S(1)} collective-permute-done((bf16[1024,512]{1,0:T(8,128)(2,1)}, bf16[1024,512]{1,0:T(8,128)(2,1)S(1)}, u32[]{:S(2)}, u32[]{:S(2)}) %collective-permute-start.4) | collective-permute-done | bytes 1048608 | tf_op jit(solution)/shard_map/ppermute | solution.py:390
  311.7 16.8 %project_and_norm.1 = (bf16[1024,2048]{1,0:T(8,128)(2,1)}, f32[1024,2048]{1,0:T(8,128)}, bf16[1024,2048]{1,0:T(8,128)(2,1)}, f32[1024,1]{1,0:T(8,128)}, f32[1024,1]{1,0:T(8,128)}) custom-call(s32[1]{0:T(128)} %bitcast.place, bf16[1024,512]{1,0:T(8,128)(2,1)} %get-tuple-element.34.refs_0_, bf16[1024,512]{1,0:T(8,128)(2,1)} %copy-done.9, ...), custom_call_target="tpu_custom_call" | custom-call | flops 8589934592 | bytes 33554432 | tf_op jit(solution)/shard_map/project_and_norm/pallas_call | solution.py:253
  328.5 37.3 %hidden_units.1 = (bf16[1024,2048]{1,0:T(8,128)(2,1)}, bf16[1024,2048]{1,0:T(8,128)(2,1)}, bf16[1024,2048]{1,0:T(8,128)(2,1)}) custom-call(bf16[1024,2048]{1,0:T(8,128)(2,1)} %get-tuple-element.37.b_ref, bf16[1024,2048]{1,0:T(8,128)(2,1)} %constant_dynamic-update-slice_fusion.3.dy_ref.refs_7_, ...), custom_call_target="tpu_custom_call" | custom-call | flops 25769803776 | bytes 62914560 | tf_op jit(solution)/shard_map/hidden_units/pallas_call | solution.py:294
  365.8 27.7 %norm_terms.1 = bf16[1024,2048]{1,0:T(8,128)(2,1)} custom-call(bf16[1024,2048]{1,0:T(8,128)(2,1)} %get-tuple-element.39.refs_0_, bf16[1024,2048]{1,0:T(8,128)(2,1)} %get-tuple-element.40.refs_1_, bf16[2048,2048]{1,0:T(8,128)(2,1)} %all-gather.10.cloned.1.call-done.wg_ref.refs_2_, bf16[2048,2048]{1,0:T(8,128)(2,1)} %all-gather.12.cloned.1.call-done.wu_ref.refs_3_), custom_call_target="tpu_custom_call" | custom-call | flops 17179869184 | bytes 41943040 | tf_op jit(solution)/shard_map/norm_terms/pallas_call | solution.py:318
  393.6 4.0 constant_dynamic-slice_fusion.6
  401.7 22.0 %collective-permute-done.15.refs_1_ = bf16[256,2048]{1,0:T(8,128)(2,1)S(1)} collective-permute-done((bf16[256,2048]{1,0:T(8,128)(2,1)}, bf16[256,2048]{1,0:T(8,128)(2,1)S(1)}, u32[]{:S(2)}, u32[]{:S(2)}) %collective-permute-start.15) | collective-permute-done | bytes 1048608 | tf_op jit(solution)/shard_map/ppermute | solution.py:390
  423.8 64.4 %collective-permute-done.16.refs_2_ = bf16[256,2048]{1,0:T(8,128)(2,1)S(1)} collective-permute-done((bf16[256,2048]{1,0:T(8,128)(2,1)}, bf16[256,2048]{1,0:T(8,128)(2,1)S(1)}, u32[]{:S(2)}, u32[]{:S(2)}) %collective-permute-start.16) | collective-permute-done | bytes 1048608 | tf_op jit(solution)/shard_map/ppermute | solution.py:390
  490.3 10.1 %resid_back.1 = (bf16[256,2048]{1,0:T(8,128)(2,1)}, bf16[256,2048]{1,0:T(8,128)(2,1)}) custom-call(s32[1]{0:T(128)} %bitcast.place, bf16[256,2048]{1,0:T(8,128)(2,1)} %get-tuple-element.101.refs_0_, bf16[256,2048]{1,0:T(8,128)(2,1)} %copy-done.4, bf16[256,2048]{1,0:T(8,128)(2,1)} %copy-done.5, bf16[256,2048]{1,0:T(8,128)(2,1)} %collective-permute-done.17.refs_3_, ...), custom_call_target="tpu_custom_call" | custom-call | flops 2147483648 | bytes 20971520 | tf_op jit(solution)/shard_map/resid_back/pallas_call | solution.py:360
  506.5 10.6 %collective-permute-done.18 = bf16[2,256,512]{2,1,0:T(8,128)(2,1)S(1)} collective-permute-done((bf16[2,256,512]{2,1,0:T(8,128)(2,1)S(1)}, bf16[2,256,512]{2,1,0:T(8,128)(2,1)S(1)}, u32[]{:S(2)}, u32[]{:S(2)}) %collective-permute-start.18) | collective-permute-done | bytes 524320 | tf_op jit(solution)/shard_map/ppermute | solution.py:390
  517.1 30.5 %collective-permute-done.19 = bf16[2,256,512]{2,1,0:T(8,128)(2,1)S(1)} collective-permute-done((bf16[2,256,512]{2,1,0:T(8,128)(2,1)S(1)}, bf16[2,256,512]{2,1,0:T(8,128)(2,1)S(1)}, u32[]{:S(2)}, u32[]{:S(2)}) %collective-permute-start.19) | collective-permute-done | bytes 524320 | tf_op jit(solution)/shard_map/ppermute | solution.py:390
  550.7 15.4 %attend_back.1 = (bf16[1024,512]{1,0:T(8,128)(2,1)}, bf16[1024,512]{1,0:T(8,128)(2,1)}, bf16[1024,512]{1,0:T(8,128)(2,1)}) custom-call(bf16[1024,512]{1,0:T(8,128)(2,1)} %get-tuple-element.31.q_ref, bf16[1024,512]{1,0:T(8,128)(2,1)} %get-tuple-element.32.k_ref, bf16[1024,512]{1,0:T(8,128)(2,1)} %get-tuple-element.33.v_ref, ...), custom_call_target="tpu_custom_call" | custom-call | flops 5368709120 | bytes 9437184 | tf_op jit(solution)/shard_map/attend_back/pallas_call | solution.py:204
  566.1 11.1 %convolution_convert_fusion.4 = bf16[2048,1536]{1,0:T(8,128)(2,1)} fusion(bf16[1024,2048]{1,0:T(8,128)(2,1)} %get-tuple-element.51, bf16[1024,512]{1,0:T(8,128)(2,1)} %get-tuple-element.49.refs_2_, bf16[1024,512]{1,0:T(8,128)(2,1)} %get-tuple-element.48.refs_1_, bf16[1024,512]{1,0:T(8,128)(2,1)} %get-tuple-element.47.refs_0_), kind=kOutput, calls=%fused_computation.4 | convolution fusion | flops 6455033856 | bytes 13631488 | tf_op jit(solution)/shard_map/dot_general | solution.py:27
  578.5 7.6 convolution_convert_fusion.3
  586.3 14.9 %convolution_convert_fusion = bf16[2048,2048]{1,0:T(8,128)(2,1)} fusion(bf16[1024,2048]{1,0:T(8,128)(2,1)} %constant_dynamic-update-slice_fusion.3.dy_ref.refs_7_, bf16[1024,2048]{1,0:T(8,128)(2,1)} %get-tuple-element.38.refs_0_), kind=kOutput, calls=%fused_computation | convolution fusion | flops 8594128896 | bytes 16777216 | tf_op jit(solution)/shard_map/dot_general | solution.py:27
  601.3 14.6 %convolution_convert_fusion.2 = bf16[2048,2048]{1,0:T(8,128)(2,1)} fusion(bf16[1024,2048]{1,0:T(8,128)(2,1)} %get-tuple-element.37.b_ref, bf16[1024,2048]{1,0:T(8,128)(2,1)} %get-tuple-element.39.refs_0_), kind=kOutput, calls=%fused_computation.2 | convolution fusion | flops 8594128896 | bytes 16777216 | tf_op jit(solution)/shard_map/dot_general | solution.py:27
  616.3 14.2 %convolution_convert_fusion.1 = bf16[2048,2048]{1,0:T(8,128)(2,1)} fusion(bf16[1024,2048]{1,0:T(8,128)(2,1)} %get-tuple-element.37.b_ref, bf16[1024,2048]{1,0:T(8,128)(2,1)} %get-tuple-element.40.refs_1_), kind=kOutput, calls=%fused_computation.1 | convolution fusion | flops 8594128896 | bytes 16777216 | tf_op jit(solution)/shard_map/dot_general | solution.py:27
  630.5 17.5 %out_terms.1 = bf16[1024,2048]{1,0:T(8,128)(2,1)} custom-call(bf16[1024,2048]{1,0:T(8,128)(2,1)} %get-tuple-element.38.refs_0_, bf16[2048,2048]{1,0:T(8,128)(2,1)} %all-gather.14.cloned.1.call-done.wd_ref.refs_1_), custom_call_target="tpu_custom_call" | custom-call | flops 8589934592 | bytes 41943040 | tf_op jit(solution)/shard_map/out_terms/pallas_call | solution.py:318
  648.0 4.3 constant_dynamic-slice_fusion.12
  652.3 7.0 fusion.17
  661.9 14.7 %input_terms.1 = bf16[1024,2048]{1,0:T(8,128)(2,1)} custom-call(bf16[1024,512]{1,0:T(8,128)(2,1)} %get-tuple-element.47.refs_0_, bf16[1024,512]{1,0:T(8,128)(2,1)} %get-tuple-element.48.refs_1_, bf16[1024,512]{1,0:T(8,128)(2,1)} %get-tuple-element.49.refs_2_, bf16[2048,512]{1,0:T(8,128)(2,1)} %get-tuple-element.94.refs_3_, ...), custom_call_target="tpu_custom_call" | custom-call | flops 6442450944 | bytes 41943040 | tf_op jit(solution)/shard_map/input_terms/pallas_call | solution.py:318
  676.6 3.9 constant_dynamic-slice_fusion.3
  681.5 2.5 collective-permute-start.22
  687.6 55.9 %collective-permute-done.13 = bf16[1024,512]{1,0:T(8,128)(2,1)} collective-permute-done((bf16[1024,512]{1,0:T(8,128)(2,1)}, bf16[1024,512]{1,0:T(8,128)(2,1)}, u32[]{:S(2)}, u32[]{:S(2)}) %collective-permute-start.13) | collective-permute-done | bytes 1048608 | tf_op jit(solution)/shard_map/ppermute | solution.py:390
  743.6 43.9 %collective-permute-done.14 = bf16[1024,512]{1,0:T(8,128)(2,1)} collective-permute-done((bf16[1024,512]{1,0:T(8,128)(2,1)}, bf16[1024,512]{1,0:T(8,128)(2,1)}, u32[]{:S(2)}, u32[]{:S(2)}) %collective-permute-start.14) | collective-permute-done | bytes 1048608 | tf_op jit(solution)/shard_map/ppermute | solution.py:390
  787.5 4.6 add_convert_fusion
  792.1 18.9 %collective-permute-done.21 = bf16[1024,512]{1,0:T(8,128)(2,1)} collective-permute-done((bf16[1024,512]{1,0:T(8,128)(2,1)}, bf16[1024,512]{1,0:T(8,128)(2,1)}, u32[]{:S(2)}, u32[]{:S(2)}) %collective-permute-start.21) | collective-permute-done | bytes 1048608 | tf_op jit(solution)/shard_map/ppermute | solution.py:390
  811.0 22.1 %collective-permute-done.22 = bf16[1024,512]{1,0:T(8,128)(2,1)} collective-permute-done((bf16[1024,512]{1,0:T(8,128)(2,1)}, bf16[1024,512]{1,0:T(8,128)(2,1)}, u32[]{:S(2)}, u32[]{:S(2)}) %collective-permute-start.22) | collective-permute-done | bytes 1048608 | tf_op jit(solution)/shard_map/ppermute | solution.py:390
  833.1 4.4 fusion.16
  837.5 9.5 %psum.7 = f32[2,1024]{1,0:T(2,128)S(1)} all-reduce(f32[2,1024]{1,0:T(2,128)S(1)} %pad_maximum_fusion.3), channel_id=1, replica_groups=mesh['row'=8,'col'=4] {'col'}, use_global_device_ids=true, to_apply=%region_3.0 | all-reduce | flops 2048 | bytes 16384 | tf_op jit(solution)/shard_map/psum | solution.py:456
  847.0 2.9 fusion.6
  849.9 2.3 fusion.18
  855.5 4.3 collective-permute-start.25
  864.2 2.8 convert_element_type.117
  867.0 71.8 %reduce-scatter.12.cloned.1.call-done = bf16[256,2048]{1,0:T(8,128)(2,1)} async-done(((bf16[2048,2048]{1,0:T(8,128)(2,1)}), bf16[256,2048]{1,0:T(8,128)(2,1)}) %reduce-scatter.12.cloned.1.call-update) | async-done | bytes 1048592 | tf_op jit(solution)/shard_map/reduce_scatter | solution.py:436
  938.9 2.8 convert_element_type.119
  (116 shorter events, 70.5 us)
Async XLA Ops:
  7.2 29.4 %copy-start.6 = (bf16[2048,256]{1,0:T(8,128)(2,1)S(1)}, bf16[2048,256]{1,0:T(8,128)(2,1)}, u32[]{:S(2)}) copy-start(bf16[2048,256]{1,0:T(8,128)(2,1)} %param.19) | copy-start | bytes 3145732
  7.2 171.6 %all-gather.6.cloned.1.call-start = ((), (), s32[]{:S(2)}) async-start(), calls=%async_computation.5 | async-start | bytes 7077888 | tf_op jit(solution)/shard_map/all_gather | solution.py:417
  9.4 302.3 %all-gather.8.cloned.1.call-start = ((), (), s32[]{:S(2)}) async-start(), calls=%async_computation.6 | async-start | bytes 9437184 | tf_op jit(solution)/shard_map/all_gather | solution.py:424
  9.4 19.9 %collective-permute-start.6 = (bf16[512,256]{1,0:T(8,128)(2,1)}, bf16[512,256]{1,0:T(8,128)(2,1)}, u32[]{:S(2)}, u32[]{:S(2)}) collective-permute-start(bf16[512,256]{1,0:T(8,128)(2,1)} %param.16), channel_id=1, source_target_pairs={{0,1},{1,2},{2,3},{3,0},{4,5},{5,6},{6,7},{7,4},{8,9},{9,10},{10,1... | collective-permute-start | bytes 786440 | tf_op jit(solution)/shard_map/ppermute | solution.py:390
  11.1 22.7 %collective-permute-start.7 = (bf16[512,256]{1,0:T(8,128)(2,1)}, bf16[512,256]{1,0:T(8,128)(2,1)}, u32[]{:S(2)}, u32[]{:S(2)}) collective-permute-start(bf16[512,256]{1,0:T(8,128)(2,1)} %param.16), channel_id=1, source_target_pairs={{0,2},{1,3},{2,0},{3,1},{4,6},{5,7},{6,4},{7,5},{8,10},{9,11},{10,... | collective-permute-start | bytes 786440 | tf_op jit(solution)/shard_map/ppermute | solution.py:390
  12.1 23.3 %collective-permute-start.8 = (bf16[512,256]{1,0:T(8,128)(2,1)}, bf16[512,256]{1,0:T(8,128)(2,1)S(1)}, u32[]{:S(2)}, u32[]{:S(2)}) collective-permute-start(bf16[512,256]{1,0:T(8,128)(2,1)} %param.16), channel_id=1, source_target_pairs={{0,3},{1,0},{2,1},{3,2},{4,7},{5,4},{6,5},{7,6},{8,11},{9,8},{10,9... | collective-permute-start | bytes 786440 | tf_op jit(solution)/shard_map/ppermute | solution.py:390
  14.2 25.1 %copy-start.2 = (bf16[1024,512]{1,0:T(8,128)(2,1)S(1)}, bf16[1024,512]{1,0:T(8,128)(2,1)}, u32[]{:S(2)}) copy-start(bf16[1024,512]{1,0:T(8,128)(2,1)} %refs_0_.1) | copy-start | bytes 3145732
  14.2 32.2 %copy-start.8 = (s32[1024]{0:T(1024)S(1)}, s32[1024]{0:T(1024)}, u32[]{:S(2)}) copy-start(s32[1024]{0:T(1024)} %param.12) | copy-start | bytes 12292
  35.5 1.0 copy-start.1
  36.5 291.9 %all-gather.14.cloned.1.call-start = ((), (), s32[]{:S(2)}) async-start(), calls=%async_computation.9 | async-start | bytes 9437184 | tf_op jit(solution)/shard_map/all_gather | solution.py:417
  38.1 290.4 %all-gather.10.cloned.1.call-start = ((), (), s32[]{:S(2)}) async-start(), calls=%async_computation.7 | async-start | bytes 9437184 | tf_op jit(solution)/shard_map/all_gather | solution.py:417
  38.7 289.9 %all-gather.12.cloned.1.call-start = ((), (), s32[]{:S(2)}) async-start(), calls=%async_computation.8 | async-start | bytes 9437184 | tf_op jit(solution)/shard_map/all_gather | solution.py:417
  39.2 810.7 %reduce-scatter.6.cloned.1.call-start = ((), (), s32[]{:S(2)}) async-start(), calls=%async_computation.10 | async-start | bytes 7077888 | tf_op jit(solution)/shard_map/reduce_scatter | solution.py:436
  39.3 26.2 %collective-permute-start = (bf16[1024,512]{1,0:T(8,128)(2,1)S(1)}, bf16[1024,512]{1,0:T(8,128)(2,1)}, u32[]{:S(2)}, u32[]{:S(2)}) collective-permute-start(bf16[1024,512]{1,0:T(8,128)(2,1)S(1)} %copy-done.2), channel_id=1, source_target_pairs={{0,1},{1,2},{2,3},{3,0},{4,5},{5,6},{6,7},{7,4},{8,9},{9,10},{10,1... | collective-permute-start | bytes 3145736 | tf_op jit(solution)/shard_map/ppermute | solution.py:390
  39.4 90.8 %collective-permute-start.1 = (bf16[1024,512]{1,0:T(8,128)(2,1)S(1)}, bf16[1024,512]{1,0:T(8,128)(2,1)}, u32[]{:S(2)}, u32[]{:S(2)}) collective-permute-start(bf16[1024,512]{1,0:T(8,128)(2,1)S(1)} %copy-done.2), channel_id=1, source_target_pairs={{0,2},{1,3},{2,0},{3,1},{4,6},{5,7},{6,4},{7,5},{8,10},{9,11},{10,... | collective-permute-start | bytes 3145736 | tf_op jit(solution)/shard_map/ppermute | solution.py:390
  42.1 136.6 %collective-permute-start.2 = (bf16[1024,512]{1,0:T(8,128)(2,1)S(1)}, bf16[1024,512]{1,0:T(8,128)(2,1)}, u32[]{:S(2)}, u32[]{:S(2)}) collective-permute-start(bf16[1024,512]{1,0:T(8,128)(2,1)S(1)} %copy-done.2), channel_id=1, source_target_pairs={{0,3},{1,0},{2,1},{3,2},{4,7},{5,4},{6,5},{7,6},{8,11},{9,8},{10,9... | collective-permute-start | bytes 3145736 | tf_op jit(solution)/shard_map/ppermute | solution.py:390
  44.0 160.2 %collective-permute-start.9 = (bf16[1024,512]{1,0:T(8,128)(2,1)}, bf16[1024,512]{1,0:T(8,128)(2,1)}, u32[]{:S(2)}, u32[]{:S(2)}) collective-permute-start(bf16[1024,512]{1,0:T(8,128)(2,1)} %param.11), channel_id=1, source_target_pairs={{0,1},{1,2},{2,3},{3,0},{4,5},{5,6},{6,7},{7,4},{8,9},{9,10},{10,1... | collective-permute-start | bytes 3145736 | tf_op jit(solution)/shard_map/ppermute | solution.py:390
  44.1 176.2 %collective-permute-start.10 = (bf16[1024,512]{1,0:T(8,128)(2,1)}, bf16[1024,512]{1,0:T(8,128)(2,1)}, u32[]{:S(2)}, u32[]{:S(2)}) collective-permute-start(bf16[1024,512]{1,0:T(8,128)(2,1)} %param.11), channel_id=1, source_target_pairs={{0,2},{1,3},{2,0},{3,1},{4,6},{5,7},{6,4},{7,5},{8,10},{9,11},{10,... | collective-permute-start | bytes 3145736 | tf_op jit(solution)/shard_map/ppermute | solution.py:390
  65.5 201.3 %collective-permute-start.11 = (bf16[1024,512]{1,0:T(8,128)(2,1)}, bf16[1024,512]{1,0:T(8,128)(2,1)S(1)}, u32[]{:S(2)}, u32[]{:S(2)}) collective-permute-start(bf16[1024,512]{1,0:T(8,128)(2,1)} %param.11), channel_id=1, source_target_pairs={{0,3},{1,0},{2,1},{3,2},{4,7},{5,4},{6,5},{7,6},{8,11},{9,8},{10,9... | collective-permute-start | bytes 3145736 | tf_op jit(solution)/shard_map/ppermute | solution.py:390
  204.1 83.6 %collective-permute-start.3 = (bf16[1024,512]{1,0:T(8,128)(2,1)}, bf16[1024,512]{1,0:T(8,128)(2,1)S(1)}, u32[]{:S(2)}, u32[]{:S(2)}) collective-permute-start(bf16[1024,512]{1,0:T(8,128)(2,1)} %get-tuple-element.34.refs_0_), channel_id=1, source_target_pairs={{0,1},{1,2},{2,3},{3,0},{4,5},{5,6},{6,7},{7,4},{8,9},{9,10},{10,1... | collective-permute-start | bytes 3145736 | tf_op jit(solution)/shard_map/ppermute | solution.py:390
  204.1 105.5 %collective-permute-start.4 = (bf16[1024,512]{1,0:T(8,128)(2,1)}, bf16[1024,512]{1,0:T(8,128)(2,1)S(1)}, u32[]{:S(2)}, u32[]{:S(2)}) collective-permute-start(bf16[1024,512]{1,0:T(8,128)(2,1)} %get-tuple-element.34.refs_0_), channel_id=1, source_target_pairs={{0,2},{1,3},{2,0},{3,1},{4,6},{5,7},{6,4},{7,5},{8,10},{9,11},{10,... | collective-permute-start | bytes 3145736 | tf_op jit(solution)/shard_map/ppermute | solution.py:390
  204.2 107.4 %collective-permute-start.5 = (bf16[1024,512]{1,0:T(8,128)(2,1)}, bf16[1024,512]{1,0:T(8,128)(2,1)}, u32[]{:S(2)}, u32[]{:S(2)}) collective-permute-start(bf16[1024,512]{1,0:T(8,128)(2,1)} %get-tuple-element.34.refs_0_), channel_id=1, source_target_pairs={{0,3},{1,0},{2,1},{3,2},{4,7},{5,4},{6,5},{7,6},{8,11},{9,8},{10,9... | collective-permute-start | bytes 3145736 | tf_op jit(solution)/shard_map/ppermute | solution.py:390
  287.8 23.9 %copy-start.9 = (bf16[1024,512]{1,0:T(8,128)(2,1)}, bf16[1024,512]{1,0:T(8,128)(2,1)S(1)}, u32[]{:S(2)}) copy-start(bf16[1024,512]{1,0:T(8,128)(2,1)S(1)} %collective-permute-done.3.refs_1_) | copy-start | bytes 3145732
  309.6 2.1 copy-start.10
  397.5 26.2 %collective-permute-start.15 = (bf16[256,2048]{1,0:T(8,128)(2,1)}, bf16[256,2048]{1,0:T(8,128)(2,1)S(1)}, u32[]{:S(2)}, u32[]{:S(2)}) collective-permute-start(bf16[256,2048]{1,0:T(8,128)(2,1)} %get-tuple-element.100), channel_id=1, source_target_pairs={{0,1},{1,2},{2,3},{3,0},{4,5},{5,6},{6,7},{7,4},{8,9},{9,10},{10,1... | collective-permute-start | bytes 3145736 | tf_op jit(solution)/shard_map/ppermute | solution.py:390
  397.5 90.6 %collective-permute-start.16 = (bf16[256,2048]{1,0:T(8,128)(2,1)}, bf16[256,2048]{1,0:T(8,128)(2,1)S(1)}, u32[]{:S(2)}, u32[]{:S(2)}) collective-permute-start(bf16[256,2048]{1,0:T(8,128)(2,1)} %get-tuple-element.99), channel_id=1, source_target_pairs={{0,2},{1,3},{2,0},{3,1},{4,6},{5,7},{6,4},{7,5},{8,10},{9,11},{10,... | collective-permute-start | bytes 3145736 | tf_op jit(solution)/shard_map/ppermute | solution.py:390
  399.7 90.6 %collective-permute-start.17 = (bf16[256,2048]{1,0:T(8,128)(2,1)S(1)}, bf16[256,2048]{1,0:T(8,128)(2,1)}, u32[]{:S(2)}, u32[]{:S(2)}) collective-permute-start(bf16[256,2048]{1,0:T(8,128)(2,1)S(1)} %get-tuple-element.98), channel_id=1, source_target_pairs={{0,3},{1,0},{2,1},{3,2},{4,7},{5,4},{6,5},{7,6},{8,11},{9,8},{10,9... | collective-permute-start | bytes 3145736 | tf_op jit(solution)/shard_map/ppermute | solution.py:390
  423.8 66.5 %copy-start.4 = (bf16[256,2048]{1,0:T(8,128)(2,1)}, bf16[256,2048]{1,0:T(8,128)(2,1)S(1)}, u32[]{:S(2)}) copy-start(bf16[256,2048]{1,0:T(8,128)(2,1)S(1)} %collective-permute-done.15.refs_1_) | copy-start | bytes 3145732
  488.1 2.2 copy-start.5
  502.2 14.8 %collective-permute-start.18 = (bf16[2,256,512]{2,1,0:T(8,128)(2,1)S(1)}, bf16[2,256,512]{2,1,0:T(8,128)(2,1)S(1)}, u32[]{:S(2)}, u32[]{:S(2)}) collective-permute-start(bf16[2,256,512]{2,1,0:T(8,128)(2,1)S(1)} %get-tuple-element.107), channel_id=1, source_target_pairs={{0,1},{1,2},{2,3},{3,0},{4,5},{5,6},{6,7},{7,4},{8,9},{9,10},{10,1... | collective-permute-start | bytes 1572872 | tf_op jit(solution)/shard_map/ppermute | solution.py:390
  502.3 45.3 %collective-permute-start.19 = (bf16[2,256,512]{2,1,0:T(8,128)(2,1)S(1)}, bf16[2,256,512]{2,1,0:T(8,128)(2,1)S(1)}, u32[]{:S(2)}, u32[]{:S(2)}) collective-permute-start(bf16[2,256,512]{2,1,0:T(8,128)(2,1)S(1)} %get-tuple-element.108), channel_id=1, source_target_pairs={{0,2},{1,3},{2,0},{3,1},{4,6},{5,7},{6,4},{7,5},{8,10},{9,11},{10,... | collective-permute-start | bytes 1572872 | tf_op jit(solution)/shard_map/ppermute | solution.py:390
  504.4 45.2 %collective-permute-start.20 = (bf16[2,256,512]{2,1,0:T(8,128)(2,1)S(1)}, bf16[2,256,512]{2,1,0:T(8,128)(2,1)S(1)}, u32[]{:S(2)}, u32[]{:S(2)}) collective-permute-start(bf16[2,256,512]{2,1,0:T(8,128)(2,1)S(1)} %get-tuple-element.105), channel_id=1, source_target_pairs={{0,3},{1,0},{2,1},{3,2},{4,7},{5,4},{6,5},{7,6},{8,11},{9,8},{10,9... | collective-permute-start | bytes 1572872 | tf_op jit(solution)/shard_map/ppermute | solution.py:390
  577.3 1.2 copy-start
  577.3 275.0 %reduce-scatter.8.cloned.1.call-start = ((), (), s32[]{:S(2)}) async-start(), calls=%async_computation.11 | async-start | bytes 9437184 | tf_op jit(solution)/shard_map/reduce_scatter | solution.py:436
  586.1 273.8 %reduce-scatter.14.cloned.1.call-start = ((), (), s32[]{:S(2)}) async-start(), calls=%async_computation.14 | async-start | bytes 9437184 | tf_op jit(solution)/shard_map/reduce_scatter | solution.py:436
  601.2 263.0 %reduce-scatter.10.cloned.1.call-start = ((), (), s32[]{:S(2)}) async-start(), calls=%async_computation.12 | async-start | bytes 9437184 | tf_op jit(solution)/shard_map/reduce_scatter | solution.py:436
  616.0 322.9 %reduce-scatter.12.cloned.1.call-start = ((), (), s32[]{:S(2)}) async-start(), calls=%async_computation.13 | async-start | bytes 9437184 | tf_op jit(solution)/shard_map/reduce_scatter | solution.py:436
  652.3 31.7 %collective-permute-start.12 = (bf16[1024,512]{1,0:T(8,128)(2,1)}, bf16[1024,512]{1,0:T(8,128)(2,1)S(1)}, u32[]{:S(2)}, u32[]{:S(2)}) collective-permute-start(bf16[1024,512]{1,0:T(8,128)(2,1)} %get-tuple-element.102), channel_id=1, source_target_pairs={{0,1},{1,2},{2,3},{3,0},{4,5},{5,6},{6,7},{7,4},{8,9},{9,10},{10,1... | collective-permute-start | bytes 3145736 | tf_op jit(solution)/shard_map/ppermute | solution.py:390
  659.4 84.2 %collective-permute-start.13 = (bf16[1024,512]{1,0:T(8,128)(2,1)}, bf16[1024,512]{1,0:T(8,128)(2,1)}, u32[]{:S(2)}, u32[]{:S(2)}) collective-permute-start(bf16[1024,512]{1,0:T(8,128)(2,1)} %get-tuple-element.104), channel_id=1, source_target_pairs={{0,2},{1,3},{2,0},{3,1},{4,6},{5,7},{6,4},{7,5},{8,10},{9,11},{10,... | collective-permute-start | bytes 3145736 | tf_op jit(solution)/shard_map/ppermute | solution.py:390
  660.4 127.1 %collective-permute-start.14 = (bf16[1024,512]{1,0:T(8,128)(2,1)}, bf16[1024,512]{1,0:T(8,128)(2,1)}, u32[]{:S(2)}, u32[]{:S(2)}) collective-permute-start(bf16[1024,512]{1,0:T(8,128)(2,1)} %get-tuple-element.103), channel_id=1, source_target_pairs={{0,3},{1,0},{2,1},{3,2},{4,7},{5,4},{6,5},{7,6},{8,11},{9,8},{10,9... | collective-permute-start | bytes 3145736 | tf_op jit(solution)/shard_map/ppermute | solution.py:390
  680.5 130.5 %collective-permute-start.21 = (bf16[1024,512]{1,0:T(8,128)(2,1)}, bf16[1024,512]{1,0:T(8,128)(2,1)}, u32[]{:S(2)}, u32[]{:S(2)}) collective-permute-start(bf16[1024,512]{1,0:T(8,128)(2,1)} %get-tuple-element.95), channel_id=1, source_target_pairs={{0,1},{1,2},{2,3},{3,0},{4,5},{5,6},{6,7},{7,4},{8,9},{9,10},{10,1... | collective-permute-start | bytes 3145736 | tf_op jit(solution)/shard_map/ppermute | solution.py:390
  681.5 151.6 %collective-permute-start.22 = (bf16[1024,512]{1,0:T(8,128)(2,1)}, bf16[1024,512]{1,0:T(8,128)(2,1)}, u32[]{:S(2)}, u32[]{:S(2)}) collective-permute-start(bf16[1024,512]{1,0:T(8,128)(2,1)} %get-tuple-element.97), channel_id=1, source_target_pairs={{0,2},{1,3},{2,0},{3,1},{4,6},{5,7},{6,4},{7,5},{8,10},{9,11},{10,... | collective-permute-start | bytes 3145736 | tf_op jit(solution)/shard_map/ppermute | solution.py:390
  684.0 1.0 copy-start.7
  684.1 149.0 %collective-permute-start.23 = (bf16[1024,512]{1,0:T(8,128)(2,1)}, bf16[1024,512]{1,0:T(8,128)(2,1)}, u32[]{:S(2)}, u32[]{:S(2)}) collective-permute-start(bf16[1024,512]{1,0:T(8,128)(2,1)} %get-tuple-element.96), channel_id=1, source_target_pairs={{0,3},{1,0},{2,1},{3,2},{4,7},{5,4},{6,5},{7,6},{8,11},{9,8},{10,9... | collective-permute-start | bytes 3145736 | tf_op jit(solution)/shard_map/ppermute | solution.py:390
  685.0 148.0 %copy-start.3 = (bf16[1024,512]{1,0:T(8,128)(2,1)S(1)}, bf16[1024,512]{1,0:T(8,128)(2,1)}, u32[]{:S(2)}) copy-start(bf16[1024,512]{1,0:T(8,128)(2,1)} %refs_0_.1) | copy-start | bytes 3145732
  853.5 88.2 %collective-permute-start.24 = (bf16[256,512]{1,0:T(8,128)(2,1)S(1)}, bf16[256,512]{1,0:T(8,128)(2,1)S(1)}, u32[]{:S(2)}, u32[]{:S(2)}) collective-permute-start(bf16[256,512]{1,0:T(8,128)(2,1)S(1)} %get-tuple-element.109), channel_id=1, source_target_pairs={{0,1},{1,2},{2,3},{3,0},{4,5},{5,6},{6,7},{7,4},{8,9},{9,10},{10,1... | collective-permute-start | bytes 786440 | tf_op jit(solution)/shard_map/ppermute | solution.py:390
  855.5 86.2 %collective-permute-start.25 = (bf16[256,512]{1,0:T(8,128)(2,1)S(1)}, bf16[256,512]{1,0:T(8,128)(2,1)S(1)}, u32[]{:S(2)}, u32[]{:S(2)}) collective-permute-start(bf16[256,512]{1,0:T(8,128)(2,1)S(1)} %get-tuple-element.111), channel_id=1, source_target_pairs={{0,2},{1,3},{2,0},{3,1},{4,6},{5,7},{6,4},{7,5},{8,10},{9,11},{10,... | collective-permute-start | bytes 786440 | tf_op jit(solution)/shard_map/ppermute | solution.py:390
  859.8 81.8 %collective-permute-start.26 = (bf16[256,512]{1,0:T(8,128)(2,1)S(1)}, bf16[256,512]{1,0:T(8,128)(2,1)}, u32[]{:S(2)}, u32[]{:S(2)}) collective-permute-start(bf16[256,512]{1,0:T(8,128)(2,1)S(1)} %get-tuple-element.110), channel_id=1, source_target_pairs={{0,3},{1,0},{2,1},{3,2},{4,7},{5,4},{6,5},{7,6},{8,11},{9,8},{10,9... | collective-permute-start | bytes 786440 | tf_op jit(solution)/shard_map/ppermute | solution.py:390
Sparse Core Ops, SparseCore 0:
  10.5 46.6 all-gather.5
  59.1 54.3 all-gather.7
  115.4 54.3 all-gather.13
  171.6 54.4 all-gather.9
  227.8 54.3 all-gather.11
  577.4 61.7 reduce-scatter.5
  643.0 71.2 reduce-scatter.7
  717.8 71.2 reduce-scatter.13
  793.0 71.2 reduce-scatter.9
  867.5 71.2 reduce-scatter.11

commit v2 on v1

v2 whole, which is shorter than its diff:
```python
import functools

import jax
import jax.numpy as jnp
from jax import lax
from jax.experimental import pallas as pl
from jax.experimental.pallas import tpu as pltpu
from jax.sharding import PartitionSpec as P

HEAD_DIM = 128
HALF = HEAD_DIM // 2
SEQ = 1024
EPSILON = 1e-05
MASKED = -1e30
SCALE = HEAD_DIM ** (-0.5)
BF = jnp.bfloat16
F32 = jnp.float32
MIB = 1 << 20
ANY = pl.BlockSpec(memory_space=pl.ANY)


def dot_nn(left, right):
    return jnp.dot(left, right, preferred_element_type=F32)


def dot_tn(left, right):
    return lax.dot_general(left, right, (((0,), (0,)), ((), ())), preferred_element_type=F32)


def dot_nt(left, right):
    return lax.dot_general(left, right, (((1,), (1,)), ((), ())), preferred_element_type=F32)


def struct(shape, dtype):
    return jax.ShapeDtypeStruct(shape, dtype)


def params(mib=60):
    return pltpu.CompilerParams(vmem_limit_bytes=mib * MIB)


def cost(flops, moved):
    return pl.CostEstimate(flops=int(flops), bytes_accessed=int(moved), transcendentals=0)


def count_seen(segment_ids):
    places = jnp.arange(segment_ids.shape[0], dtype=jnp.int32)
    causal = places[None, :] <= places[:, None]
    allowed = (segment_ids[:, None] == segment_ids[None, :]) & causal
    return jnp.sum(allowed.astype(jnp.int32), axis=1) - 1


def rope_tables(segments):
    positions = jax.vmap(count_seen)(segments.reshape(-1, SEQ)).reshape(-1)
    inverse = 10000.0 ** (-(jnp.arange(HALF, dtype=F32) * 2.0 / HEAD_DIM))
    angles = positions.astype(F32)[:, None] * inverse[None, :]
    cosine, sine = jnp.cos(angles), jnp.sin(angles)
    return jnp.concatenate([cosine, cosine], 1), jnp.concatenate([-sine, sine], 1)


def turn(values, cos_table, sin_table):
    return values * cos_table + pltpu.roll(values, HALF, 1) * sin_table


MESH = pl.DeviceIdType.MESH
VMEM_SPEC = pl.BlockSpec(memory_space=pltpu.VMEM)
DMA = pltpu.SemaphoreType.DMA


def comm_params(number, mib=60):
    return pltpu.CompilerParams(vmem_limit_bytes=mib * MIB, collective_id=number, has_side_effects=True)


def remote(source, target, send, recv, **device):
    return pltpu.make_async_remote_copy(
        src_ref=source, dst_ref=target, send_sem=send, recv_sem=recv, device_id=device, device_id_type=MESH
    )


def greet(senders, targets):
    semaphore = pltpu.get_barrier_semaphore()
    for device in senders:
        pl.semaphore_signal(semaphore, inc=1, device_id=device, device_id_type=MESH)
    pl.semaphore_wait(semaphore, targets)


def ring_places(C):
    me = lax.axis_index("col")
    return me, lax.rem(me + 1, C), lax.rem(me + C - 1, C)


def row_places(R):
    row = lax.axis_index("row")
    ahead = [lax.rem(row + 2 * k, R) for k in range(R // 2)]
    behind = [lax.rem(row + R - 2 * k, R) for k in range(R // 2)]
    other = row + 1 - 2 * lax.rem(row, 2)
    return row, ahead, behind, other


def gather_kernel(
    R, C, x_ref, wo_ref, wq_ref, wk_ref, wv_ref, xs_ref, wos_ref, w_ref,
    local, x_send, x_recv, o_send, o_recv, w_send, w_recv, f_send, f_recv,
):
    me, right, left = ring_places(C)
    row, ahead, behind, other = row_places(R)
    weights = (wq_ref, wk_ref, wv_ref)
    mine = [
        pltpu.make_async_copy(x_ref, xs_ref.at[me], local.at[0]),
        pltpu.make_async_copy(wo_ref, wos_ref.at[me], local.at[1]),
    ] + [pltpu.make_async_copy(w, w_ref.at[i, row], local.at[2 + i]) for i, w in enumerate(weights)]
    for copy in mine:
        copy.start()
    greet(
        [{"col": left}, {"row": other}] + [{"row": r} for r in behind[1:]],
        1 + R // 2,
    )

    def ring(source, whole, send, recv, step):
        owner = lax.rem(me - step + C, C)
        piece = source if step == 0 else whole.at[owner]
        return remote(piece, whole.at[owner], send.at[step], recv.at[step], col=right)

    x_copies = [ring(x_ref, xs_ref, x_send, x_recv, s) for s in range(C - 1)]
    o_copies = [ring(wo_ref, wos_ref, o_send, o_recv, s) for s in range(C - 1)]
    x_copies[0].start()
    o_copies[0].start()
    spread, forward = [], []
    for i, w in enumerate(weights):
        for k in range(1, R // 2):
            copy = remote(w, w_ref.at[i, row], w_send.at[i, k], w_recv.at[i, k], row=ahead[k])
            copy.start()
            spread.append(copy)
        copy = remote(w, w_ref.at[i, row], f_send.at[i, 0], f_recv.at[i, 0], row=other)
        copy.start()
        forward.append(copy)
    for s in range(1, C - 1):
        x_copies[s - 1].wait_recv()
        x_copies[s].start()
        o_copies[s - 1].wait_recv()
        o_copies[s].start()
    for i in range(3):
        for k in range(1, R // 2):
            spread[i * (R // 2 - 1) + k - 1].wait_recv()
            block = w_ref.at[i, behind[k]]
            copy = remote(block, block, f_send.at[i, k], f_recv.at[i, k], row=other)
            copy.start()
            forward.append(copy)
    x_copies[-1].wait_recv()
    o_copies[-1].wait_recv()
    for copy in forward:
        copy.wait_recv()
    for copy in x_copies + o_copies + spread + forward:
        copy.wait_send()
    for copy in mine:
        copy.wait()


def first_gather(R, C, tokens, w_out, w_query, w_key, w_value):
    depth, width = w_query.shape
    half = R // 2
    return pl.pallas_call(
        functools.partial(gather_kernel, R, C),
        in_specs=[ANY] * 5,
        out_specs=[ANY] * 3,
        out_shape=[
            struct((C,) + tokens.shape, BF),
            struct((C,) + w_out.shape, BF),
            struct((3, R, depth, width), BF),
        ],
        scratch_shapes=[
            DMA((5,)),
            DMA((C - 1,)),
            DMA((C - 1,)),
            DMA((C - 1,)),
            DMA((C - 1,)),
            DMA((3, half)),
            DMA((3, half)),
            DMA((3, half)),
            DMA((3, half)),
        ],
        compiler_params=comm_params(0),
        cost_estimate=cost(6e10, 14 * MIB),
        name="first_gather",
    )(tokens, w_out, w_query, w_key, w_value)


def norm_rows(x):
    centre = jnp.mean(x, axis=-1, keepdims=True)
    spread = jnp.mean(x * x, axis=-1, keepdims=True) - centre * centre
    inverse = lax.rsqrt(spread + EPSILON)
    return centre, inverse


def beside(ref):
    return jnp.concatenate([ref[j] for j in range(ref.shape[0])], axis=1)


def qkv_kernel(xs_ref, w_ref, cos_ref, sin_ref, a_ref, q_ref, k_ref, v_ref, mu_ref, r_ref):
    x = beside(xs_ref).astype(F32)
    centre, inverse = norm_rows(x)
    a = ((x - centre) * inverse).astype(BF)
    a_ref[...] = a
    mu_ref[...] = centre
    r_ref[...] = inverse
    cosine, sine = cos_ref[...], sin_ref[...]
    for index, out in enumerate((q_ref, k_ref, v_ref)):
        product = dot_nn(a, w_ref[index])
        if index == 2:
            out[...] = product.astype(BF)
            continue
        for start in range(0, out.shape[1], HEAD_DIM):
            part = product[:, start : start + HEAD_DIM]
            out[:, start : start + HEAD_DIM] = turn(part, cosine, sine).astype(BF)


def norm_and_project(xs, w_qkv, cos_table, sin_table):
    C, T, width = xs.shape
    D = width * C
    bt = 256
    rows = lambda n: pl.BlockSpec((bt, n), lambda i: (i, 0))
    return pl.pallas_call(
        qkv_kernel,
        grid=(T // bt,),
        in_specs=[
            pl.BlockSpec((C, bt, width), lambda i: (0, i, 0)),
            pl.BlockSpec(w_qkv.shape, lambda i: (0, 0, 0), pipeline_mode=pl.Buffered(1)),
            rows(HEAD_DIM),
            rows(HEAD_DIM),
        ],
        out_specs=[rows(D), rows(width), rows(width), rows(width), rows(1), rows(1)],
        out_shape=[
            struct((T, D), BF),
            struct((T, width), BF),
            struct((T, width), BF),
            struct((T, width), BF),
            struct((T, 1), F32),
            struct((T, 1), F32),
        ],
        compiler_params=params(),
        cost_estimate=cost(2 * T * D * 3 * width, 14 * MIB),
        name="norm_and_project",
    )(xs, w_qkv, cos_table, sin_table)


def allowed_block(seg_key, seg_query, first_query):
    shape = (seg_key.shape[0], seg_query.shape[1])
    keys = lax.broadcasted_iota(jnp.int32, shape, 0)
    queries = lax.broadcasted_iota(jnp.int32, shape, 1) + first_query
    return (seg_key == seg_query) & (keys <= queries)


def attend_kernel(
    R, C, q_ref, k_ref, v_ref, segk_ref, segq_ref, wos_ref, os_ref, log_ref, w_ref,
    o_buf, local, o_send, o_recv, w_send, w_recv, f_send, f_recv,
):
    me, right, left = ring_places(C)
    row, ahead, behind, other = row_places(R)
    T, width = q_ref.shape
    heads, bq = width // HEAD_DIM, 256
    greet([{"col": left}, {"row": other}] + [{"row": r} for r in behind[1:]], 1 + R // 2)
    mine = pltpu.make_async_copy(wos_ref, w_ref.at[row], local.at[0])
    mine.start()
    spread, forward = [], []
    for k in range(1, R // 2):
        copy = remote(wos_ref, w_ref.at[row], w_send.at[k], w_recv.at[k], row=ahead[k])
        copy.start()
        spread.append(copy)
    copy = remote(wos_ref, w_ref.at[row], f_send.at[0], f_recv.at[0], row=other)
    copy.start()
    forward.append(copy)

    def ring(step, head):
        owner = lax.rem(me - step + C, C)
        piece = o_buf.at[head] if step == 0 else os_ref.at[owner, head]
        return remote(piece, os_ref.at[owner, head], o_send.at[step, head], o_recv.at[step, head], col=right)

    def one_head(head, carry):
        columns = pl.ds(pl.multiple_of(head * HEAD_DIM, HEAD_DIM), HEAD_DIM)
        for first in range(0, T, SEQ):
            for start in range(first, first + SEQ, bq):
                stop = start + bq
                scores = dot_nt(k_ref[first:stop, columns], q_ref[start:stop, columns]) * SCALE
                allowed = allowed_block(segk_ref[first:stop], segq_ref[:, start:stop], start - first)
                scores = jnp.where(allowed, scores, MASKED)
                peak = jnp.max(scores, axis=0, keepdims=True)
                exponent = jnp.exp(scores - peak)
                total = jnp.sum(exponent, axis=0, keepdims=True)
                weights = (exponent * (1.0 / total)).astype(BF)
                o_buf[head, start:stop] = dot_tn(v_ref[first:stop, columns], weights).T.astype(BF)
                log_ref[head, :, start:stop] = peak + jnp.log(total)
        ring(0, head).start()
        pltpu.make_async_copy(o_buf.at[head], os_ref.at[me, head], local.at[1 + head]).start()
        return carry

    lax.fori_loop(0, heads, one_head, 0)
    for step in range(1, C - 1):
        for head in range(heads):
            ring(step - 1, head).wait_recv()
            ring(step, head).start()
    for k in range(1, R // 2):
        spread[k - 1].wait_recv()
        block = w_ref.at[behind[k]]
        copy = remote(block, block, f_send.at[k], f_recv.at[k], row=other)
        copy.start()
        forward.append(copy)
    for head in range(heads):
        ring(C - 2, head).wait_recv()
        pltpu.make_async_copy(o_buf.at[head], os_ref.at[me, head], local.at[1 + head]).wait()
        for step in range(C - 1):
            ring(step, head).wait_send()
    for copy in forward:
        copy.wait_recv()
    for copy in spread + forward:
        copy.wait_send()
    mine.wait()


def attend(R, C, q, k, v, seg_column, seg_row, w_part):
    T, width = q.shape
    heads, half = width // HEAD_DIM, R // 2
    return pl.pallas_call(
        functools.partial(attend_kernel, R, C),
        in_specs=[VMEM_SPEC] * 5 + [ANY],
        out_specs=[ANY, VMEM_SPEC, ANY],
        out_shape=[
            struct((C, heads, T, HEAD_DIM), BF),
            struct((heads, 1, T), F32),
            struct((R,) + w_part.shape, BF),
        ],
        scratch_shapes=[
            pltpu.VMEM((heads, T, HEAD_DIM), BF),
            DMA((1 + heads,)),
            DMA((C - 1, heads)),
            DMA((C - 1, heads)),
            DMA((half,)),
            DMA((half,)),
            DMA((half,)),
            DMA((half,)),
        ],
        compiler_params=comm_params(1),
        cost_estimate=cost(7e10, 14 * MIB),
        name="attend",
    )(q, k, v, seg_column, seg_row, w_part)


def feed_kernel(
    C, tiles, os_ref, w_ref, xs_ref, wg_ref, wu_ref, dy_ref,
    h_ref, b_ref, mu_ref, r_ref, hm_ref, slope_ref, silu_ref, dys_ref, normed, local, send, recv,
):
    step = pl.program_id(0)
    me, right, left = ring_places(C)

    def ring(s):
        owner = lax.rem(me - s + C, C)
        piece = dy_ref if s == 0 else dys_ref.at[owner]
        return remote(piece, dys_ref.at[owner], send.at[s], recv.at[s], col=right)

    mine = pltpu.make_async_copy(dy_ref, dys_ref.at[me], local.at[0])
    steps = pl.num_programs(0)

    @pl.when(step == 0)
    def _():
        mine.start()
        greet([{"col": left}], 1)
        ring(0).start()

    for s in range(1, C - 1):

        @pl.when(step == min(tiles + s, tiles + 3))
        def _():
            ring(s - 1).wait_recv()
            ring(s).start()

    @pl.when(step < tiles)
    def _():
        size = h_ref.shape[0]
        blocks, part = w_ref.shape[0], w_ref.shape[2]
        heads = jnp.concatenate(
            [os_ref[j, h] for j in range(os_ref.shape[0]) for h in range(os_ref.shape[1])], axis=1
        )
        x = beside(xs_ref)
        for n in range(blocks):
            columns = slice(n * part, (n + 1) * part)
            h_ref[:, columns] = x[:, columns].astype(F32) + dot_nn(heads, w_ref[n])
        h = h_ref[...]
        centre, inverse = norm_rows(h)
        b = ((h - centre) * inverse).astype(BF)
        b_ref[...] = b
        normed[pl.ds(pl.multiple_of(step * size, size), size), :] = b
        mu_ref[...] = centre
        r_ref[...] = inverse

    @pl.when(step >= tiles)
    def _():
        b = normed[...]
        gate = dot_nn(b, wg_ref[...])
        upward = dot_nn(b, wu_ref[...])
        sigmoid = jax.nn.sigmoid(gate)
        silu = gate * sigmoid
        hm_ref[...] = (silu * upward).astype(BF)
        slope_ref[...] = (upward * sigmoid * (1.0 + gate * (1.0 - sigmoid))).astype(BF)
        silu_ref[...] = silu.astype(BF)

    @pl.when(step == steps - 1)
    def _():
        ring(C - 2).wait_recv()
        for s in range(C - 1):
            ring(s).wait_send()
        mine.wait()


def feed_forward(C, os, w_out, xs, w_gate, w_up, cotangent):
    heads, T = os.shape[1], os.shape[2]
    width = xs.shape[2]
    D, F = w_gate.shape
    bt = 256
    bf = F // 4
    tiles = T // bt
    early = lambda i: jnp.minimum(i, tiles - 1)
    late = lambda i: jnp.maximum(i - tiles, 0)
    rows = lambda n: pl.BlockSpec((bt, n), lambda i: (early(i), 0))
    tile = pl.BlockSpec((T, bf), lambda i: (0, late(i)))
    weight = pl.BlockSpec((D, bf), lambda i: (0, late(i)))
    return pl.pallas_call(
        functools.partial(feed_kernel, C, tiles),
        grid=(tiles + F // bf,),
        in_specs=[
            pl.BlockSpec((C, heads, bt, HEAD_DIM), lambda i: (0, 0, early(i), 0)),
            pl.BlockSpec(w_out.shape, lambda i: (0, 0, 0), pipeline_mode=pl.Buffered(1)),
            pl.BlockSpec((C, bt, width), lambda i: (0, early(i), 0)),
            weight,
            weight,
            ANY,
        ],
        out_specs=[rows(D), rows(D), rows(1), rows(1), tile, tile, tile, ANY],
        out_shape=[
            struct((T, D), F32),
            struct((T, D), BF),
            struct((T, 1), F32),
            struct((T, 1), F32),
            struct((T, F), BF),
            struct((T, F), BF),
            struct((T, F), BF),
            struct((C, T, width), BF),
        ],
        scratch_shapes=[pltpu.VMEM((T, D), BF), DMA((1,)), DMA((C - 1,)), DMA((C - 1,))],
        compiler_params=comm_params(2),
        cost_estimate=cost(7e10, 60 * MIB),
        name="feed_forward",
    )(os, w_out, xs, w_gate, w_up, cotangent)


def hidden_back_kernel(dys_ref, wd_ref, slope_ref, silu_ref, dg_ref, du_ref, dy):
    @pl.when(pl.program_id(0) == 0)
    def _():
        width = dys_ref.shape[2]
        for j in range(dys_ref.shape[0]):
            dy[:, j * width : (j + 1) * width] = dys_ref[j]

    grad_hidden = dot_nn(dy[...], wd_ref[...])
    dg_ref[...] = (grad_hidden * slope_ref[...].astype(F32)).astype(BF)
    du_ref[...] = (grad_hidden * silu_ref[...].astype(F32)).astype(BF)


def hidden_back(dys, w_down, slope, silu):
    C, T, width = dys.shape
    D, F = w_down.shape
    bf = F // 4
    tile = pl.BlockSpec((T, bf), lambda j: (0, j))
    return pl.pallas_call(
        hidden_back_kernel,
        grid=(F // bf,),
        in_specs=[
            pl.BlockSpec(dys.shape, lambda j: (0, 0, 0), pipeline_mode=pl.Buffered(1)),
            pl.BlockSpec((D, bf), lambda j: (0, j)),
            tile,
            tile,
        ],
        out_specs=[tile, tile],
        out_shape=[struct((T, F), BF)] * 2,
        scratch_shapes=[pltpu.VMEM((T, D), BF)],
        compiler_params=params(),
        cost_estimate=cost(2 * T * D * F, 28 * MIB),
        name="hidden_back",
    )(dys, w_down, slope, silu)


def ring_step(step, C, right, first, held, send, recv):
    source = first if step == 0 else held.at[step - 1]
    return remote(source, held.at[step], send.at[step], recv.at[step], col=right)


def add_into(held, terms):
    size = 64

    def body(i, carry):
        rows = pl.ds(pl.multiple_of(i * size, size), size)
        held[rows, :] = (held[rows, :].astype(F32) + terms[rows, :].astype(F32)).astype(BF)
        return carry

    lax.fori_loop(0, held.shape[0] // size, body, 0)


def norm_terms_kernel(
    C, dg_hbm, du_hbm, hm_hbm, wg_hbm, wu_hbm, wd_hbm, b_hbm, dys_hbm,
    sum_ref, gate_hbm, up_hbm, down_hbm, out_hbm,
    dg, du, hm, wg, wu, b, dys, terms, held, stage, load, tile_load, store, send, recv,
):
    me, right, left = ring_places(C)
    D, F = wg.shape
    T = dg.shape[0]
    rows = T // C
    width = D // C
    loads = []

    def fetch(source, target, semaphore):
        copy = pltpu.make_async_copy(source, target, semaphore)
        copy.start()
        return copy

    def chunk(s):
        return pl.ds(pl.multiple_of(lax.rem(me + 2 * C - 1 - s, C) * rows, rows), rows)

    grads_in = []
    for s in range(C):
        part = chunk(s)
        grads_in.append(
            (fetch(dg_hbm.at[part, :], dg.at[part, :], load.at[2 * s]), fetch(du_hbm.at[part, :], du.at[part, :], load.at[2 * s + 1]))
        )
        if s == 0:
            weights_in = []
            for n in range(C):
                cut = pl.ds(n * width, width)
                weights_in.append(
                    (fetch(wg_hbm.at[cut, :], wg.at[cut, :], tile_load.at[2 * n]), fetch(wu_hbm.at[cut, :], wu.at[cut, :], tile_load.at[2 * n + 1]))
                )
    late = [
        fetch(b_hbm, b, load.at[2 * C]),
        fetch(hm_hbm, hm, load.at[2 * C + 1]),
        fetch(dys_hbm, dys, load.at[2 * C + 2]),
    ]
    greet([{"col": left}], 1)

    def term_tile(s, part, n):
        cut = pl.ds(pl.multiple_of(n * width, width), width)
        total = dot_nt(dg[part, :], wg[cut, :]) + dot_nt(du[part, :], wu[cut, :])
        terms[s, :, cut] = total.astype(BF)

    def moves(step):
        return ring_step(step, C, right, terms.at[0], held, send, recv)

    def pass_on(step):
        moves(step - 1).wait_recv()
        add_into(held.at[step - 1], terms.at[step])
        moves(step).start()

    for s in range(C):
        part = chunk(s)
        for copy in grads_in[s]:
            copy.wait()
        if s == 0:
            for n in range(C):
                for copy in weights_in[n]:
                    copy.wait()
                term_tile(s, part, n)
            moves(0).start()
        else:

            def body(n, carry):
                term_tile(s, part, n)
                return carry

            lax.fori_loop(0, C, body, 0)
    down_in = fetch(wd_hbm, wg, tile_load.at[0])
    for copy in late:
        copy.wait()

    def stored(target, t, slot):
        cut = pl.ds(pl.multiple_of(t * width, width), width)
        return pltpu.make_async_copy(stage.at[slot], target.at[cut, :], store.at[slot])

    def product(left_of, right_ref, target):
        def body(t, carry):
            slot = lax.rem(t, 2)

            @pl.when(t >= 2)
            def _():
                stored(target, t, slot).wait()

            stage[slot] = dot_tn(left_of(t), right_ref[...]).astype(BF)
            stored(target, t, slot).start()
            return carry

        lax.fori_loop(0, C, body, 0)
        for slot in range(2):
            stored(target, slot, slot).wait()

    def b_tile(t):
        return b[:, pl.ds(pl.multiple_of(t * width, width), width)]

    middle = max(1, (C - 1) // 2)
    product(b_tile, dg, gate_hbm)
    for step in range(1, middle + 1):
        if step < C - 1:
            pass_on(step)
    product(b_tile, du, up_hbm)
    product(lambda t: dys[t], hm, down_hbm)
    for step in range(middle + 1, C - 1):
        pass_on(step)
    down_in.wait()

    def out_tile(n, carry):
        cut = pl.ds(pl.multiple_of(n * width, width), width)
        terms_out = dot_nt(hm[...], wg[cut, :]).astype(BF)
        dys[0] = terms_out
        copy = pltpu.make_async_copy(dys.at[0], out_hbm.at[n], store.at[0])
        copy.start()
        copy.wait()
        return carry

    lax.fori_loop(0, C, out_tile, 0)
    moves(C - 2).wait_recv()
    sum_ref[...] = held[C - 2].astype(F32) + terms[C - 1].astype(F32)
    for step in range(C - 1):
        moves(step).wait_send()


def norm_terms(C, dg, du, hm, w_gate, w_up, w_down, b, dys):
    T, F = dg.shape
    D = w_gate.shape[0]
    rows, width = T // C, D // C
    return pl.pallas_call(
        functools.partial(norm_terms_kernel, C),
        in_specs=[ANY] * 8,
        out_specs=[VMEM_SPEC, ANY, ANY, ANY, ANY],
        out_shape=[
            struct((rows, D), F32),
            struct((D, F), BF),
            struct((D, F), BF),
            struct((D, F), BF),
            struct((C, T, width), BF),
        ],
        scratch_shapes=[
            pltpu.VMEM((T, F), BF),
            pltpu.VMEM((T, F), BF),
            pltpu.VMEM((T, F), BF),
            pltpu.VMEM((D, F), BF),
            pltpu.VMEM((D, F), BF),
            pltpu.VMEM((T, D), BF),
            pltpu.VMEM((C, T, width), BF),
            pltpu.VMEM((C, rows, D), BF),
            pltpu.VMEM((C - 1, rows, D), BF),
            pltpu.VMEM((2, width, F), BF),
            DMA((2 * C + 3,)),
            DMA((2 * C,)),
            DMA((2,)),
            DMA((C - 1,)),
            DMA((C - 1,)),
        ],
        compiler_params=comm_params(3, 62),
        cost_estimate=cost(9e10, 70 * MIB),
        name="norm_terms",
    )(dg, du, hm, w_gate, w_up, w_down, b, dys)


def resid_back_kernel(
    C, sum_ref, h_ref, mu_ref, r_ref, dys_ref, w_hbm, dh_ref, do_hbm, dhs_hbm,
    w, out, load, local, h_send, h_recv, o_send, o_recv,
):
    me, right, left = ring_places(C)
    blocks, D, part = w.shape
    rows = sum_ref.shape[0]
    width = D // C
    order = [lax.rem(me + k, C) for k in range(1, C)] + [me]
    loads = []
    for k in range(C):
        cut = pl.ds(pl.multiple_of(order[k] * width, width), width)
        copy = pltpu.make_async_copy(w_hbm.at[:, cut, :], w.at[:, cut, :], load.at[k])
        copy.start()
        loads.append(copy)
    greet([{"col": lax.rem(me + k, C)} for k in range(1, C)], C - 1)
    grad = sum_ref[...]
    inverse = r_ref[...]
    normed = (h_ref[...] - mu_ref[...]) * inverse
    first = jnp.mean(grad, axis=1, keepdims=True)
    second = jnp.mean(grad * normed, axis=1, keepdims=True)
    dh = beside(dys_ref).astype(F32) + inverse * (grad - first - normed * second)
    dh_ref[...] = dh.astype(BF)
    mine = pl.ds(pl.multiple_of(me * rows, rows), rows)
    copies = []
    for k in range(C):
        cut = pl.ds(pl.multiple_of(order[k] * width, width), width)
        loads[k].wait()
        total = dot_nt(dh_ref[:, :part], w[0, cut, :])
        for n in range(1, blocks):
            total += dot_nt(dh_ref[:, n * part : (n + 1) * part], w[n, cut, :])
        out[k] = total.astype(BF)
        if k < C - 1:
            copy = remote(out.at[k], do_hbm.at[mine, :], o_send.at[k], o_recv.at[k], col=order[k])
        else:
            copy = pltpu.make_async_copy(out.at[k], do_hbm.at[mine, :], local.at[0])
        copy.start()
        copies.append(copy)
    for k in range(C):
        cut = pl.ds(pl.multiple_of(order[k] * width, width), width)
        if k < C - 1:
            copy = remote(dh_ref.at[:, cut], dhs_hbm.at[mine, :], h_send.at[k], h_recv.at[k], col=order[k])
        else:
            copy = pltpu.make_async_copy(dh_ref.at[:, cut], dhs_hbm.at[mine, :], local.at[1])
        copy.start()
        copies.append(copy)
    for copy in copies:
        copy.wait()


def resid_back(total, h, mu, r, dys, w_out):
    C, rows, width = dys.shape
    T, D = rows * C, width * C
    return pl.pallas_call(
        functools.partial(resid_back_kernel, C),
        in_specs=[VMEM_SPEC] * 5 + [ANY],
        out_specs=[VMEM_SPEC, ANY, ANY],
        out_shape=[struct((rows, D), BF), struct((T, width), BF), struct((T, width), BF)],
        scratch_shapes=[
            pltpu.VMEM(w_out.shape, BF),
            pltpu.VMEM((C, rows, width), BF),
            DMA((C,)),
            DMA((2,)),
            DMA((C - 1,)),
            DMA((C - 1,)),
            DMA((C - 1,)),
            DMA((C - 1,)),
        ],
        compiler_params=comm_params(4),
        cost_estimate=cost(4e10, 20 * MIB),
        name="resid_back",
    )(total, h, mu, r, dys, w_out)


def attend_back_kernel(
    C, q_ref, k_ref, v_ref, do_ref, log_ref, segk_ref, segq_ref, cos_ref, sin_ref, h_ref, terms,
    dq_ref, dk_ref, dv_ref, y_ref, dk_sum, dv_sum, held, send, recv,
):
    me, right, left = ring_places(C)
    T, width = q_ref.shape
    heads, bq = width // HEAD_DIM, 256
    greet([{"col": left}], 1)

    def chunk(s):
        return lax.rem(me + 2 * C - 1 - s, C)

    def moves(step):
        return ring_step(step, C, right, terms.at[chunk(0)], held, send, recv)

    moves(0).start()

    def one_head(head, carry):
        columns = pl.ds(pl.multiple_of(head * HEAD_DIM, HEAD_DIM), HEAD_DIM)
        dk_sum[...] = jnp.zeros_like(dk_sum)
        dv_sum[...] = jnp.zeros_like(dv_sum)
        for first in range(0, T, SEQ):
            for start in range(first, first + SEQ, bq):
                stop = start + bq
                keys = k_ref[first:stop, columns]
                queries = q_ref[start:stop, columns]
                grads = do_ref[start:stop, columns]
                scores = dot_nt(keys, queries) * SCALE
                allowed = allowed_block(segk_ref[first:stop], segq_ref[:, start:stop], start - first)
                scores = jnp.where(allowed, scores, MASKED)
                probs = jnp.exp(scores - log_ref[head, :, start:stop])
                dv_sum[first:stop] += dot_nn(probs.astype(BF), grads)
                grad_probs = dot_nt(v_ref[first:stop, columns], grads)
                inner = jnp.sum(probs * grad_probs, axis=0, keepdims=True)
                grad_scores = (probs * (grad_probs - inner)).astype(BF)
                dk_sum[first:stop] += dot_nn(grad_scores, queries)
                grad_query = dot_tn(keys, grad_scores).T * SCALE
                dq_ref[start:stop, columns] = turn(grad_query, cos_ref[start:stop], -sin_ref[start:stop]).astype(BF)
        dk_ref[:, columns] = turn(dk_sum[...] * SCALE, cos_ref[...], -sin_ref[...]).astype(BF)
        dv_ref[:, columns] = dv_sum[...].astype(BF)
        return carry

    lax.fori_loop(0, heads, one_head, 0)
    for step in range(1, C - 1):
        moves(step - 1).wait_recv()
        add_into(held.at[step - 1], terms.at[chunk(step)])
        moves(step).start()
    moves(C - 2).wait_recv()
    y_ref[...] = (h_ref[...] + held[C - 2].astype(F32) + terms[me].astype(F32)).astype(BF)
    for step in range(C - 1):
        moves(step).wait_send()


def attend_back(q, k, v, do, log_total, seg_column, seg_row, cos_table, sin_table, h_mine, out_terms):
    C = out_terms.shape[0]
    T, width = q.shape
    return pl.pallas_call(
        functools.partial(attend_back_kernel, C),
        in_specs=[VMEM_SPEC] * 11,
        out_specs=[VMEM_SPEC] * 4,
        out_shape=[struct((T, width), BF)] * 4,
        scratch_shapes=[
            pltpu.VMEM((T, HEAD_DIM), F32),
            pltpu.VMEM((T, HEAD_DIM), F32),
            pltpu.VMEM((C - 1, T, width), BF),
            DMA((C - 1,)),
            DMA((C - 1,)),
        ],
        compiler_params=comm_params(5),
        cost_estimate=cost(7e10, 14 * MIB),
        name="attend_back",
    )(q, k, v, do, log_total, seg_column, seg_row, cos_table, sin_table, h_mine, out_terms)


def input_terms_kernel(
    C, dq_ref, dk_ref, dv_ref, w_ref, a_ref, sum_ref, grad_hbm, terms, held, stage, store, send, recv
):
    me, right, left = ring_places(C)
    T, width = dq_ref.shape
    greet([{"col": left}], 1)
    heads = (dq_ref, dk_ref, dv_ref)

    def moves(step):
        return ring_step(step, C, right, terms.at[0], held, send, recv)

    def compute(s):
        cut = pl.ds(pl.multiple_of(lax.rem(me + 2 * C - 1 - s, C) * width, width), width)
        total = dot_nt(dq_ref[...], w_ref[0, cut, :])
        total += dot_nt(dk_ref[...], w_ref[1, cut, :])
        total += dot_nt(dv_ref[...], w_ref[2, cut, :])
        terms[s] = total.astype(BF)

    compute(0)
    moves(0).start()

    def body(s, carry):
        compute(s)
        return carry

    lax.fori_loop(1, C, body, 0)

    def stored(t, slot):
        cut = pl.ds(pl.multiple_of(t * width, width), width)
        return pltpu.make_async_copy(stage.at[slot], grad_hbm.at[cut, :], store.at[slot])

    def grad_tile(t, carry):
        slot = lax.rem(t, 2)

        @pl.when(t >= 2)
        def _():
            stored(t, slot).wait()

        left_tile = a_ref[:, pl.ds(pl.multiple_of(t * width, width), width)]
        for i in range(3):
            stage[slot, :, i * width : (i + 1) * width] = dot_tn(left_tile, heads[i][...]).astype(BF)
        stored(t, slot).start()
        return carry

    lax.fori_loop(0, C, grad_tile, 0)
    for slot in range(2):
        stored(slot, slot).wait()
    for step in range(1, C - 1):
        moves(step - 1).wait_recv()
        add_into(held.at[step - 1], terms.at[step])
        moves(step).start()
    moves(C - 2).wait_recv()
    sum_ref[...] = held[C - 2].astype(F32) + terms[C - 1].astype(F32)
    for step in range(C - 1):
        moves(step).wait_send()


def input_terms(C, dq, dk, dv, w_qkv, a):
    T, width = dq.shape
    D = w_qkv.shape[1]
    return pl.pallas_call(
        functools.partial(input_terms_kernel, C),
        in_specs=[VMEM_SPEC] * 5,
        out_specs=[VMEM_SPEC, ANY],
        out_shape=[struct((T, width), F32), struct((D, 3 * width), BF)],
        scratch_shapes=[
            pltpu.VMEM((C, T, width), BF),
            pltpu.VMEM((C - 1, T, width), BF),
            pltpu.VMEM((2, width, 3 * width), BF),
            DMA((2,)),
            DMA((C - 1,)),
            DMA((C - 1,)),
        ],
        compiler_params=comm_params(6),
        cost_estimate=cost(8e10, 20 * MIB),
        name="input_terms",
    )(dq, dk, dv, w_qkv, a)


def on_device(R, C, tokens, cotangent, segments, w_query, w_key, w_value, w_out, w_gate, w_up, w_down):
    T, width = tokens.shape
    D = width * C
    rows = T // C
    me = lax.axis_index("col")

    def shift(values, k):
        return lax.ppermute(values, "col", [(i, (i + k) % C) for i in range(C)])

    def block(values, k, axis):
        size = values.shape[axis] // C
        return lax.dynamic_slice_in_dim(values, lax.rem(me + k, C) * size, size, axis)

    def scattered(values, axis):
        return [block(values, 0, axis)] + [shift(block(values, k, axis), k) for k in range(1, C)]

    def total_of(terms):
        total = terms[0].astype(F32)
        for term in terms[1:]:
            total = total + term.astype(F32)
        return total

    gathered = lambda w: lax.all_gather(w, "row", axis=0, tiled=True)
    scatter = lambda g: lax.psum_scatter(g, "row", scatter_dimension=0, tiled=True)

    gate_w, up_w, down_w = gathered(w_gate), gathered(w_up), gathered(w_down.T)
    cos_table, sin_table = rope_tables(segments)
    seg_column, seg_row = segments.reshape(T, 1), segments.reshape(1, T)
    xs, out_part, w_qkv = first_gather(R, C, tokens, w_out, w_query, w_key, w_value)
    w_qkv = w_qkv.reshape(3, D, width)
    act_one, q, k, v, mu_one, r_one = norm_and_project(xs, w_qkv, cos_table, sin_table)
    os, log_total, out_w = attend(R, C, q, k, v, seg_column, seg_row, out_part.reshape(D, -1))
    h_full, act_two, mu_two, r_two, hidden, slope, silu, dys = feed_forward(
        C, os, out_w, xs, gate_w, up_w, cotangent
    )
    dg, du = hidden_back(dys, down_w, slope, silu)
    total, grad_gate, grad_up, grad_down, out_terms = norm_terms(
        C, dg, du, hidden, gate_w, up_w, down_w, act_two, dys
    )
    grad_down, grad_gate, grad_up = scatter(grad_down), scatter(grad_gate), scatter(grad_up)
    mine = lambda values, axis: lax.dynamic_slice_in_dim(values, me * rows, rows, axis)
    dh_rows, grad_heads, grad_resid = resid_back(
        total, mine(h_full, 0), mine(mu_two, 0), mine(r_two, 0), mine(dys, 1), out_w
    )
    my_heads = mine(os, 2).transpose(2, 0, 1, 3).reshape(rows, D)
    grad_out = scatter(dot_tn(dh_rows, my_heads).astype(BF))
    h_mine = lax.dynamic_slice_in_dim(h_full, me * width, width, 1)
    dq, dk, dv, output = attend_back(
        q, k, v, grad_heads, log_total, seg_column, seg_row, cos_table, sin_table, h_mine, out_terms
    )
    grad_input, grad_qkv = input_terms(C, dq, dk, dv, w_qkv, act_one)
    grad_qkv = scatter(grad_qkv).astype(F32)
    grad_out = total_of(scattered(grad_out, 1)).T
    normed = (tokens.astype(F32) - mu_one) * r_one
    sums = lax.psum(jnp.stack([jnp.sum(grad_input, axis=1), jnp.sum(grad_input * normed, axis=1)]), "col")
    grad_tokens = grad_resid.astype(F32) + r_one * (
        grad_input - (sums[0] / D)[:, None] - normed * (sums[1] / D)[:, None]
    )
    return (
        output,
        grad_tokens.astype(BF),
        grad_qkv[:, :width],
        grad_qkv[:, width : 2 * width],
        grad_qkv[:, 2 * width :],
        grad_out,
        grad_gate.astype(F32),
        grad_up.astype(F32),
        grad_down.astype(F32).T,
    )


def solution(mesh):
    here = P("row", "col")
    turned = P("col", "row")
    return jax.shard_map(
        functools.partial(on_device, mesh.shape["row"], mesh.shape["col"]),
        mesh=mesh,
        in_specs=(here, here, P("row"), here, here, here, turned, here, here, turned),
        out_specs=(here, here, here, here, here, turned, here, here, turned),
        check_vma=False,
    )
```

time: 960 us -> 976 us (1.017)
  Pallas kernels: 165 us -> 568 us
  waiting for transfers between devices: 585 us -> 323 us
  matrix products: 62.4 us -> 5.99 us
  starting transfers between devices: 39.2 us -> 4.81 us
  local copies, waits for them, and re-layouts: 45.2 us -> 24.3 us
  other arithmetic: 30.3 us -> 18.9 us
    ppermute x27 -> x3, waiting for transfers between devices: 510 us -> 0.01 us  [shift(): return lax.ppermute(values, 'col', [(i, (i + k) % C) for i in range(C)])]
    pallas_call x9, Pallas kernels: 165 us -> 568 us  [the longest x1 88.6 us: first_gather(): pl.pallas_call(functools.partial(gather_kernel, R, C), in_specs=[ANY] * 5...]
    reduce_scatter x5, waiting for transfers between devices: 73 us -> 320 us  [on_device(): lax.psum_scatter(g, 'row', scatter_dimension=0, tiled=True)]
    dot_general x5 -> x1, matrix products: 62.4 us -> 5.99 us  [dot_tn(): lax.dot_general(left, right, (((0,), (0,)), ((), ())), preferred_element_...]
    ppermute x27 -> x3, starting transfers between devices: 38.4 us -> 4.5 us  [shift(): return lax.ppermute(values, 'col', [(i, (i + k) % C) for i in range(C)])]
    dynamic_slice x4 -> x1, local copies, waits for them, and re-layouts: 13.3 us -> 1.16 us  [block(): lax.dynamic_slice_in_dim(values, lax.rem(me + k, C) * size, size, axis)]
    dynamic_slice x0 -> x5, local copies, waits for them, and re-layouts: none -> 11.6 us  [the longest x4 8.52 us: on_device(): lax.dynamic_slice_in_dim(values, me * rows, rows, axis)]
    dynamic_update_slice x11 -> x0, local copies, waits for them, and re-layouts: 11.2 us -> none  [assembled(): lax.dynamic_update_slice_in_dim(whole, piece, lax.rem(me - k + C, C) * si...]
  transfers between devices with their start and end apart: 37 -> 11, of which waited for: 23 -> 5; matrix products, arithmetic and copies ran while one was open for 12% -> 5% of each run, Pallas kernels for 8% -> 27%
where the time goes in v2:
time: 976 us; the launch traced here: 971 us
  Pallas kernels  568 us (58%)
  waiting for transfers between devices  323 us (33%)
  local copies, waits for them, and re-layouts  24.3 us (2%)
  other arithmetic  18.9 us (2%)
  between operations  14.6 us (1%)
  blocking collectives  10.4 us (1%)
    reduce_scatter x5, waiting for transfers between devices, on_device(): lax.psum_scatter(g, 'row', scatter_dimension=0, tiled=True)  320 us
    pallas_call x1, Pallas kernels, first_gather(): pl.pallas_call(functools.partial(gather_kernel, R, C), in_specs=[ANY] * 5...  88.6 us
    pallas_call x1, Pallas kernels, norm_terms(): pl.pallas_call(functools.partial(norm_terms_kernel, C), in_specs=[ANY] *...  84.5 us
    pallas_call x1, Pallas kernels, feed_forward(): pl.pallas_call(functools.partial(feed_kernel, C, tiles), grid=(tiles + F...  80 us
    pallas_call x1, Pallas kernels, input_terms(): pl.pallas_call(functools.partial(input_terms_kernel, C), in_specs=[VMEM_S...  79.8 us
    pallas_call x1, Pallas kernels, attend(): pl.pallas_call(functools.partial(attend_kernel, R, C), in_specs=[VMEM_SPE...  77.7 us
    pallas_call x1, Pallas kernels, attend_back(): pl.pallas_call(functools.partial(attend_back_kernel, C), in_specs=[VMEM_S...  77 us
    pallas_call x1, Pallas kernels, resid_back(): pl.pallas_call(functools.partial(resid_back_kernel, C), in_specs=[VMEM_SP...  51.7 us
  transfers between devices with their start and end apart: 11, of which 5 were waited for; matrix products, arithmetic and copies ran while one was open for 5% of the time, Pallas kernels for 27%

profile of v2, /device:TPU:8, one launch (start us, length us, event | category | flops | bytes accessed | tf_op | source)
XLA Modules:
  0.0 970.9 jit_solution(6187690685439118244)
XLA Ops:
  7.2 0.7 all-gather.4.cloned.1.call-update
  8.0 0.7 all-gather.6.cloned.1.call-update
  8.7 2.3 copy.29
  11.6 88.6 %first_gather.1 = (bf16[4,1024,512]{2,1,0:T(8,128)(2,1)}, bf16[4,512,256]{2,1,0:T(8,128)(2,1)}, bf16[3,8,256,512]{3,2,1,0:T(8,128)(2,1)}) custom-call(bf16[1024,512]{1,0:T(8,128)(2,1)} %x_ref.1, bf16[512,256]{1,0:T(8,128)(2,1)} %wo_ref.1, bf16[256,512]{1,0:T(8,128)(2,1)} %wq_ref.1, bf16[256,512]{1,0:T(8,128)(2,1)} %wk_ref.1, bf16[256,512]{1,0:T(8,128)(2,1)} %wv_ref.1), custom_call_target="tpu_custom_call" | custom-call | flops 60000002048 | bytes 14680064 | tf_op jit(solution)/shard_map/first_gather/pallas_call | solution.py:161
  100.3 1.9 fusion.1
  102.2 1.0 copy.28.segk_ref
  103.2 1.3 pad_maximum_fusion
  104.5 12.5 %norm_and_project.1 = (bf16[1024,2048]{1,0:T(8,128)(2,1)}, bf16[1024,512]{1,0:T(8,128)(2,1)}, bf16[1024,512]{1,0:T(8,128)(2,1)}, bf16[1024,512]{1,0:T(8,128)(2,1...) custom-call(bf16[4,1024,512]{2,1,0:T(8,128)(2,1)} %get-tuple-element.45.xs_ref, bf16[3,2048,512]{2,1,0:T(8,128)(2,1)} %bitcast.27, ...), custom_call_target="tpu_custom_call" | custom-call | flops 6442450944 | bytes 14680064 | tf_op jit(solution)/shard_map/norm_and_project/pallas_call | solution.py:221
  117.0 77.7 %attend.1 = (bf16[4,4,1024,128]{3,2,1,0:T(8,128)(2,1)}, f32[4,1,1024]{2,1,0:T(1,128)}, bf16[8,2048,256]{2,1,0:T(8,128)(2,1)}) custom-call(bf16[1024,512]{1,0:T(8,128)(2,1)} %get-tuple-element.47.q_ref, bf16[1024,512]{1,0:T(8,128)(2,1)} %get-tuple-element.48.k_ref, bf16[1024,512]{1,0:T(8,128)(2,1)} %get-tuple-element.49.v_ref, s32[1024,1]{1,0:T(8,128)} %copy.28.segk_ref, ...), custom_call_target="tpu_custom_call" | custom-call | flops 70000001024 | bytes 14680064 | tf_op jit(solution)/shard_map/attend/pallas_call | solution.py:321
  194.8 80.0 %feed_forward.1 = (f32[1024,2048]{1,0:T(8,128)}, bf16[1024,2048]{1,0:T(8,128)(2,1)}, f32[1024,1]{1,0:T(8,128)}, f32[1024,1]{1,0:T(8,128)}, bf16[1024,2048]{1,0:T...) custom-call(bf16[4,4,1024,128]{3,2,1,0:T(8,128)(2,1)} %get-tuple-element.51.os_r, ...), custom_call_target="tpu_custom_call" | custom-call | flops 70000001024 | bytes 62914560 | tf_op jit(solution)/shard_map/feed_forward/pallas_call | solution.py:424
  274.8 1.6 constant_dynamic-slice_fusion.6.mu_ref
  276.3 1.6 constant_dynamic-slice_fusion.5.r_ref
  277.9 2.3 constant_dynamic-slice_fusion.4.dys_ref
  280.2 3.1 constant_dynamic-slice_fusion.3.h_ref
  283.2 3.1 constant_dynamic-slice_fusion.7.h_ref
  286.4 16.7 %hidden_back.1 = (bf16[1024,2048]{1,0:T(8,128)(2,1)}, bf16[1024,2048]{1,0:T(8,128)(2,1)}) custom-call(bf16[4,1024,512]{2,1,0:T(8,128)(2,1)} %get-tuple-element.53.dys_ref.dys_hbm, bf16[2048,2048]{1,0:T(8,128)(2,1)} %all-gather.8.cloned.1.call-done.wd_ref.wd_hbm, bf16[1024,2048]{1,0:T(8,128)(2,1)} %get-tuple-element.54.slope_ref, ...), custom_call_target="tpu_custom_call" | custom-call | flops 8589934592 | bytes 29360128 | tf_op jit(solution)/shard_map/hidden_back/pallas_call | solution.py:470
  303.1 84.5 %norm_terms.1 = (f32[256,2048]{1,0:T(8,128)}, bf16[2048,2048]{1,0:T(8,128)(2,1)}, bf16[2048,2048]{1,0:T(8,128)(2,1)}, bf16[2048,2048]{1,0:T(8,128)(2,1)}, bf16[4,1024,512]{2,1,0:T(8,128)(2,1)}) custom-call(bf16[1024,2048]{1,0:T(8,128)(2,1)} %get-tuple-element.56.dg_hbm, bf16[1024,2048]{1,0:T(8,128)(2,1)} %get-tuple-element.57.du_hbm, ...), custom_call_target="tpu_custom_call" | custom-call | flops 89999998976 | bytes 73400320 | tf_op jit(solution)/shard_map/norm_terms/pallas_call | solution.py:632
  387.6 51.7 %resid_back.1 = (bf16[256,2048]{1,0:T(8,128)(2,1)}, bf16[1024,512]{1,0:T(8,128)(2,1)}, bf16[1024,512]{1,0:T(8,128)(2,1)}) custom-call(f32[256,2048]{1,0:T(8,128)} %get-tuple-element.60.sum_ref, f32[256,2048]{1,0:T(8,128)} %constant_dynamic-slice_fusion.7.h_ref, f32[256,1]{1,0:T(8,128)} %constant_dynamic-slice_fusion.6.mu_ref, ...), custom_call_target="tpu_custom_call" | custom-call | flops 40000000000 | bytes 20971520 | tf_op jit(solution)/shard_map/resid_back/pallas_call | solution.py:719
  439.3 77.0 %attend_back.1 = (bf16[1024,512]{1,0:T(8,128)(2,1)}, bf16[1024,512]{1,0:T(8,128)(2,1)}, bf16[1024,512]{1,0:T(8,128)(2,1)}, bf16[1024,512]{1,0:T(8,128)(2,1)}) custom-call(bf16[1024,512]{1,0:T(8,128)(2,1)} %get-tuple-element.47.q_ref, bf16[1024,512]{1,0:T(8,128)(2,1)} %get-tuple-element.48.k_ref, bf16[1024,512]{1,0:T(8,128)(2,1)} %get-tuple-element.49.v_ref, ...), custom_call_target="tpu_custom_call" | custom-call | flops 70000001024 | bytes 14680064 | tf_op jit(solution)/shard_map/attend_back/pallas_call | solution.py:796
  516.3 79.8 %input_terms.1 = (f32[1024,512]{1,0:T(8,128)}, bf16[2048,1536]{1,0:T(8,128)(2,1)}) custom-call(bf16[1024,512]{1,0:T(8,128)(2,1)} %get-tuple-element.70.dq_ref, bf16[1024,512]{1,0:T(8,128)(2,1)} %get-tuple-element.71.dk_ref, bf16[1024,512]{1,0:T(8,128)(2,1)} %get-tuple-element.72.dv_ref, bf16[3,2048,512]{2,1,0:T(8,128)(2,1)} %bitcast.28, ...), custom_call_target="tpu_custom_call" | custom-call | flops 80000000000 | bytes 20971520 | tf_op jit(solution)/shard_map/input_terms/pallas_call | solution.py:874
  596.2 1.4 dynamic-slice_bitcast_fusion
  597.6 0.7 copy.31
  598.3 6.0 convolution_convert_fusion
  604.3 0.5 reduce-scatter.14.cloned.1.call-update
  604.9 0.7 reduce-scatter.12.cloned.1.call-update
  605.7 0.7 reduce-scatter.10.cloned.1.call-update
  606.4 1.9 reduce.1
  608.3 1.3 reduce.2
  609.7 0.9 fusion.2
  610.6 10.4 %psum.7 = f32[2,1024]{1,0:T(2,128)S(1)} all-reduce(f32[2,1024]{1,0:T(2,128)S(1)} %pad_maximum_fusion.2), channel_id=1, replica_groups=mesh['row'=8,'col'=4] {'col'}, use_global_device_ids=true, to_apply=%region_3.0 | all-reduce | flops 2048 | bytes 16384 | tf_op jit(solution)/shard_map/psum | solution.py:947
  621.0 2.8 add_convert_fusion
  623.9 34.5 %reduce-scatter.6.cloned.1.call-done = bf16[256,1536]{1,0:T(8,128)(2,1)} async-done(((bf16[2048,1536]{1,0:T(8,128)(2,1)}), bf16[256,1536]{1,0:T(8,128)(2,1)}) %reduce-scatter.6.cloned.1.call-update) | async-done | bytes 786448 | tf_op jit(solution)/shard_map/reduce_scatter | solution.py:916
  658.4 2.3 fusion.3
  660.7 72.7 %reduce-scatter.8.cloned.1.call-done = bf16[256,2048]{1,0:T(8,128)(2,1)} async-done(((bf16[2048,2048]{1,0:T(8,128)(2,1)}), bf16[256,2048]{1,0:T(8,128)(2,1)}) %reduce-scatter.8.cloned.1.call-update) | async-done | bytes 1048592 | tf_op jit(solution)/shard_map/reduce_scatter | solution.py:916
  733.4 1.2 constant_dynamic-slice_fusion.2
  734.5 1.5 collective-permute-start
  736.1 0.5 collective-permute-start.2
  736.6 2.4 collective-permute-start.1
  739.0 69.0 %reduce-scatter.14.cloned.1.call-done = bf16[256,2048]{1,0:T(8,128)(2,1)} async-done(((bf16[2048,2048]{1,0:T(8,128)(2,1)}), bf16[256,2048]{1,0:T(8,128)(2,1)}) %reduce-scatter.14.cloned.1.call-update) | async-done | bytes 1048592 | tf_op jit(solution)/shard_map/reduce_scatter | solution.py:916
  808.0 1.5 convert_bitcast_fusion
  809.5 1.8 copy.33
  811.3 71.8 %reduce-scatter.12.cloned.1.call-done = bf16[256,2048]{1,0:T(8,128)(2,1)} async-done(((bf16[2048,2048]{1,0:T(8,128)(2,1)}), bf16[256,2048]{1,0:T(8,128)(2,1)}) %reduce-scatter.12.cloned.1.call-update) | async-done | bytes 1048592 | tf_op jit(solution)/shard_map/reduce_scatter | solution.py:916
  883.2 2.8 convert_element_type.64
  885.9 72.0 %reduce-scatter.10.cloned.1.call-done = bf16[256,2048]{1,0:T(8,128)(2,1)} async-done(((bf16[2048,2048]{1,0:T(8,128)(2,1)}), bf16[256,2048]{1,0:T(8,128)(2,1)}) %reduce-scatter.10.cloned.1.call-update) | async-done | bytes 1048592 | tf_op jit(solution)/shard_map/reduce_scatter | solution.py:916
  957.9 2.8 convert_element_type.63
  960.7 1.2 add_bitcast_fusion
  961.9 1.0 copy.32
  962.9 1.0 copy.35
  (32 shorter events, 1.0 us)
Async XLA Ops:
  7.2 3.9 copy-start.4
  7.2 187.6 %all-gather.4.cloned.1.call-start = ((), (), s32[]{:S(2)}) async-start(), calls=%async_computation.5 | async-start | bytes 9437184 | tf_op jit(solution)/shard_map/all_gather | solution.py:915
  7.9 186.9 %all-gather.6.cloned.1.call-start = ((), (), s32[]{:S(2)}) async-start(), calls=%async_computation.6 | async-start | bytes 9437184 | tf_op jit(solution)/shard_map/all_gather | solution.py:915
  8.7 277.7 %all-gather.8.cloned.1.call-start = ((), (), s32[]{:S(2)}) async-start(), calls=%async_computation.7 | async-start | bytes 9437184 | tf_op jit(solution)/shard_map/all_gather | solution.py:915
  11.0 647.3 %reduce-scatter.6.cloned.1.call-start = ((), (), s32[]{:S(2)}) async-start(), calls=%async_computation.8 | async-start | bytes 7077888 | tf_op jit(solution)/shard_map/reduce_scatter | solution.py:916
  596.1 2.2 copy-start.2
  596.1 137.3 %reduce-scatter.8.cloned.1.call-start = ((), (), s32[]{:S(2)}) async-start(), calls=%async_computation.9 | async-start | bytes 9437184 | tf_op jit(solution)/shard_map/reduce_scatter | solution.py:916
  604.3 203.8 %reduce-scatter.14.cloned.1.call-start = ((), (), s32[]{:S(2)}) async-start(), calls=%async_computation.12 | async-start | bytes 9437184 | tf_op jit(solution)/shard_map/reduce_scatter | solution.py:916
  604.9 278.3 %reduce-scatter.12.cloned.1.call-start = ((), (), s32[]{:S(2)}) async-start(), calls=%async_computation.11 | async-start | bytes 9437184 | tf_op jit(solution)/shard_map/reduce_scatter | solution.py:916
  605.6 352.3 %reduce-scatter.10.cloned.1.call-start = ((), (), s32[]{:S(2)}) async-start(), calls=%async_computation.10 | async-start | bytes 9437184 | tf_op jit(solution)/shard_map/reduce_scatter | solution.py:916
  605.7 4.0 copy-start
  605.7 4.0 copy-start.1
  734.5 226.2 %collective-permute-start = (bf16[256,512]{1,0:T(8,128)(2,1)S(1)}, bf16[256,512]{1,0:T(8,128)(2,1)S(1)}, u32[]{:S(2)}, u32[]{:S(2)}) collective-permute-start(bf16[256,512]{1,0:T(8,128)(2,1)S(1)} %get-tuple-element.110), channel_id=1, source_target_pairs={{0,1},{1,2},{2,3},{3,0},{4,5},{5,6},{6,7},{7,4},{8,9},{9,10},{10,1... | collective-permute-start | bytes 786440 | tf_op jit(solution)/shard_map/ppermute | solution.py:900
  736.1 224.6 %collective-permute-start.2 = (bf16[256,512]{1,0:T(8,128)(2,1)S(1)}, bf16[256,512]{1,0:T(8,128)(2,1)S(1)}, u32[]{:S(2)}, u32[]{:S(2)}) collective-permute-start(bf16[256,512]{1,0:T(8,128)(2,1)S(1)} %get-tuple-element.111), channel_id=1, source_target_pairs={{0,3},{1,0},{2,1},{3,2},{4,7},{5,4},{6,5},{7,6},{8,11},{9,8},{10,9... | collective-permute-start | bytes 786440 | tf_op jit(solution)/shard_map/ppermute | solution.py:900
  736.6 224.1 %collective-permute-start.1 = (bf16[256,512]{1,0:T(8,128)(2,1)S(1)}, bf16[256,512]{1,0:T(8,128)(2,1)}, u32[]{:S(2)}, u32[]{:S(2)}) collective-permute-start(bf16[256,512]{1,0:T(8,128)(2,1)S(1)} %get-tuple-element.112), channel_id=1, source_target_pairs={{0,2},{1,3},{2,0},{3,1},{4,6},{5,7},{6,4},{7,5},{8,10},{9,11},{10,... | collective-permute-start | bytes 786440 | tf_op jit(solution)/shard_map/ppermute | solution.py:900
  811.3 151.6 %copy-start.3 = (bf16[1024,512]{1,0:T(8,128)(2,1)S(1)}, bf16[1024,512]{1,0:T(8,128)(2,1)}, u32[]{:S(2)}) copy-start(bf16[1024,512]{1,0:T(8,128)(2,1)} %get-tuple-element.132) | copy-start | bytes 3145732
Sparse Core Ops, SparseCore 0:
  9.9 77.0 all-gather.3
  88.9 95.6 all-gather.5
  186.5 52.4 all-gather.7
  596.2 62.0 reduce-scatter.5
  662.1 71.2 reduce-scatter.7
  736.7 71.2 reduce-scatter.13
  811.9 71.2 reduce-scatter.11
  886.6 71.2 reduce-scatter.9

commit v3 on v2

--- a/solution.py
+++ b/solution.py
@@ -345,7 +345,7 @@
 
 def feed_kernel(
     C, tiles, os_ref, w_ref, xs_ref, wg_ref, wu_ref, dy_ref,
-    h_ref, b_ref, mu_ref, r_ref, hm_ref, slope_ref, silu_ref, dys_ref, normed, local, send, recv,
+    h_ref, b_ref, hm_ref, slope_ref, silu_ref, dys_ref, normed, local, send, recv,
 ):
     step = pl.program_id(0)
     me, right, left = ring_places(C)
@@ -387,8 +387,6 @@
         b = ((h - centre) * inverse).astype(BF)
         b_ref[...] = b
         normed[pl.ds(pl.multiple_of(step * size, size), size), :] = b
-        mu_ref[...] = centre
-        r_ref[...] = inverse
 
     @pl.when(step >= tiles)
     def _():
@@ -432,12 +430,10 @@
             weight,
             ANY,
         ],
-        out_specs=[rows(D), rows(D), rows(1), rows(1), tile, tile, tile, ANY],
+        out_specs=[rows(D), rows(D), tile, tile, tile, ANY],
         out_shape=[
             struct((T, D), F32),
             struct((T, D), BF),
-            struct((T, 1), F32),
-            struct((T, 1), F32),
             struct((T, F), BF),
             struct((T, F), BF),
             struct((T, F), BF),
@@ -499,6 +495,62 @@
         return carry
 
     lax.fori_loop(0, held.shape[0] // size, body, 0)
+
+
+class RowSum:
+    def __init__(self, R, own, twin, exchanged, arrived, semaphores):
+        self.R, self.own, self.twin = R, own, twin
+        self.exchanged, self.arrived = exchanged, arrived
+        self.row, self.ahead, self.behind, self.other = row_places(R)
+        self.x_send, self.x_recv, self.y_send, self.y_recv = semaphores
+
+    def exchange(self, k):
+        return remote(self.twin(k), self.exchanged.at[k], self.x_send.at[k], self.x_recv.at[k], row=self.other)
+
+    def spread(self, k):
+        return remote(self.own(k), self.arrived.at[k - 1], self.y_send.at[k], self.y_recv.at[k], row=self.ahead[k])
+
+    def order(self):
+        return list(range(1, self.R // 2)) + [0]
+
+    def relay(self, before=None):
+        for k in self.order():
+            if before is not None:
+                before(k)
+            self.exchange(k).wait_recv()
+            add_into(self.own(k), self.exchanged.at[k])
+            if k:
+                self.spread(k).start()
+
+    def finish(self, target):
+        for k in range(1, self.R // 2):
+            self.spread(k).wait_recv()
+        size = min(64, target.shape[0])
+
+        def body(i, carry):
+            rows = pl.ds(pl.multiple_of(i * size, size), size)
+            total = self.own(0)[rows, :].astype(F32)
+            for k in range(1, self.R // 2):
+                total += self.arrived[k - 1, rows, :].astype(F32)
+            target[rows, :] = total.astype(target.dtype)
+            return carry
+
+        lax.fori_loop(0, target.shape[0] // size, body, 0)
+        for k in range(self.R // 2):
+            self.exchange(k).wait_send()
+            if k:
+                self.spread(k).wait_send()
+
+
+def row_sum_semaphores(R):
+    return [DMA((R // 2,)) for _ in range(4)]
+
+
+def held_row_sum(R, grad_hbm, own, exchanged, arrived, load, semaphores):
+    row, ahead, behind, other = row_places(R)
+    sums = RowSum(R, lambda k: own.at[k], lambda k: grad_hbm.at[lax.rem(other + 2 * k, R)], exchanged, arrived, semaphores)
+    loads = [pltpu.make_async_copy(grad_hbm.at[ahead[k]], own.at[k], load.at[k]) for k in range(R // 2)]
+    return sums, loads
 
 
 def norm_terms_kernel(
@@ -664,36 +716,45 @@
 
 
 def resid_back_kernel(
-    C, sum_ref, h_ref, mu_ref, r_ref, dys_ref, w_hbm, dh_ref, do_hbm, dhs_hbm,
-    w, out, load, local, h_send, h_recv, o_send, o_recv,
+    R, C, sum_ref, h_hbm, dys_hbm, os_hbm, w_hbm, do_hbm, dhs_hbm, grad_hbm,
+    h, dy, heads, w, dh, out, stage, load, w_load, local, store, h_send, h_recv, o_send, o_recv,
 ):
     me, right, left = ring_places(C)
     blocks, D, part = w.shape
     rows = sum_ref.shape[0]
     width = D // C
+    mine = pl.ds(pl.multiple_of(me * rows, rows), rows)
+    first_in = [
+        pltpu.make_async_copy(h_hbm.at[mine, :], h, load.at[0]),
+        pltpu.make_async_copy(dys_hbm.at[:, mine, :], dy, load.at[1]),
+    ]
+    heads_in = pltpu.make_async_copy(os_hbm.at[:, :, mine, :], heads, load.at[2])
+    for copy in first_in:
+        copy.start()
     order = [lax.rem(me + k, C) for k in range(1, C)] + [me]
     loads = []
     for k in range(C):
         cut = pl.ds(pl.multiple_of(order[k] * width, width), width)
-        copy = pltpu.make_async_copy(w_hbm.at[:, cut, :], w.at[:, cut, :], load.at[k])
+        copy = pltpu.make_async_copy(w_hbm.at[:, cut, :], w.at[:, cut, :], w_load.at[k])
         copy.start()
         loads.append(copy)
+    heads_in.start()
     greet([{"col": lax.rem(me + k, C)} for k in range(1, C)], C - 1)
+    for copy in first_in:
+        copy.wait()
     grad = sum_ref[...]
-    inverse = r_ref[...]
-    normed = (h_ref[...] - mu_ref[...]) * inverse
+    centre, inverse = norm_rows(h[...])
+    normed = (h[...] - centre) * inverse
     first = jnp.mean(grad, axis=1, keepdims=True)
     second = jnp.mean(grad * normed, axis=1, keepdims=True)
-    dh = beside(dys_ref).astype(F32) + inverse * (grad - first - normed * second)
-    dh_ref[...] = dh.astype(BF)
-    mine = pl.ds(pl.multiple_of(me * rows, rows), rows)
+    dh[...] = (beside(dy).astype(F32) + inverse * (grad - first - normed * second)).astype(BF)
     copies = []
     for k in range(C):
         cut = pl.ds(pl.multiple_of(order[k] * width, width), width)
         loads[k].wait()
-        total = dot_nt(dh_ref[:, :part], w[0, cut, :])
+        total = dot_nt(dh[:, :part], w[0, cut, :])
         for n in range(1, blocks):
-            total += dot_nt(dh_ref[:, n * part : (n + 1) * part], w[n, cut, :])
+            total += dot_nt(dh[:, n * part : (n + 1) * part], w[n, cut, :])
         out[k] = total.astype(BF)
         if k < C - 1:
             copy = remote(out.at[k], do_hbm.at[mine, :], o_send.at[k], o_recv.at[k], col=order[k])
@@ -704,27 +765,44 @@
     for k in range(C):
         cut = pl.ds(pl.multiple_of(order[k] * width, width), width)
         if k < C - 1:
-            copy = remote(dh_ref.at[:, cut], dhs_hbm.at[mine, :], h_send.at[k], h_recv.at[k], col=order[k])
+            copy = remote(dh.at[:, cut], dhs_hbm.at[mine, :], h_send.at[k], h_recv.at[k], col=order[k])
         else:
-            copy = pltpu.make_async_copy(dh_ref.at[:, cut], dhs_hbm.at[mine, :], local.at[1])
+            copy = pltpu.make_async_copy(dh.at[:, cut], dhs_hbm.at[mine, :], local.at[1])
         copy.start()
         copies.append(copy)
-    for copy in copies:
+    heads_in.wait()
+    right_side = jnp.concatenate([heads[j, i] for j in range(C) for i in range(heads.shape[1])], axis=1)
+    stores = []
+    for t in range(C):
+        if t >= 2:
+            stores[t - 2].wait()
+        stage[t % 2] = dot_tn(dh[:, t * width : (t + 1) * width], right_side).astype(BF)
+        copy = pltpu.make_async_copy(stage.at[t % 2], grad_hbm.at[pl.ds(t * width, width), :], store.at[t % 2])
+        copy.start()
+        stores.append(copy)
+    for copy in copies + stores[-2:]:
         copy.wait()
 
 
-def resid_back(total, h, mu, r, dys, w_out):
-    C, rows, width = dys.shape
-    T, D = rows * C, width * C
+def resid_back(R, total, h, dys, os, w_out):
+    C, T, width = dys.shape
+    rows, D = total.shape
     return pl.pallas_call(
-        functools.partial(resid_back_kernel, C),
-        in_specs=[VMEM_SPEC] * 5 + [ANY],
-        out_specs=[VMEM_SPEC, ANY, ANY],
-        out_shape=[struct((rows, D), BF), struct((T, width), BF), struct((T, width), BF)],
+        functools.partial(resid_back_kernel, R, C),
+        in_specs=[VMEM_SPEC] + [ANY] * 4,
+        out_specs=[ANY, ANY, ANY],
+        out_shape=[struct((T, width), BF), struct((T, width), BF), struct((D, D), BF)],
         scratch_shapes=[
+            pltpu.VMEM((rows, D), F32),
+            pltpu.VMEM((C, rows, width), BF),
+            pltpu.VMEM((C, os.shape[1], rows, HEAD_DIM), BF),
             pltpu.VMEM(w_out.shape, BF),
+            pltpu.VMEM((rows, D), BF),
             pltpu.VMEM((C, rows, width), BF),
+            pltpu.VMEM((2, width, D), BF),
+            DMA((3,)),
             DMA((C,)),
+            DMA((2,)),
             DMA((2,)),
             DMA((C - 1,)),
             DMA((C - 1,)),
@@ -734,17 +812,27 @@
         compiler_params=comm_params(4),
         cost_estimate=cost(4e10, 20 * MIB),
         name="resid_back",
-    )(total, h, mu, r, dys, w_out)
+    )(total, h, dys, os, w_out)
 
 
 def attend_back_kernel(
-    C, q_ref, k_ref, v_ref, do_ref, log_ref, segk_ref, segq_ref, cos_ref, sin_ref, h_ref, terms,
-    dq_ref, dk_ref, dv_ref, y_ref, dk_sum, dv_sum, held, send, recv,
+    R, C, q_ref, k_ref, v_ref, do_ref, log_ref, segk_ref, segq_ref, cos_ref, sin_ref, terms, h_hbm, grad_hbm,
+    dq_ref, dk_ref, dv_ref, y_ref, total_ref, dk_sum, dv_sum, held, h, own, exchanged, arrived,
+    send, recv, h_load, load, *semaphores,
 ):
     me, right, left = ring_places(C)
+    row, ahead, behind, other = row_places(R)
     T, width = q_ref.shape
     heads, bq = width // HEAD_DIM, 256
-    greet([{"col": left}], 1)
+    cut = pl.ds(pl.multiple_of(me * width, width), width)
+    h_in = pltpu.make_async_copy(h_hbm.at[:, cut], h, h_load.at[0])
+    sums, loads = held_row_sum(R, grad_hbm, own, exchanged, arrived, load, semaphores)
+    for copy in loads:
+        copy.start()
+    h_in.start()
+    greet([{"col": left}, {"row": other}] + [{"row": r} for r in behind[1:]], 1 + R // 2)
+    for k in sums.order():
+        sums.exchange(k).start()
 
     def chunk(s):
         return lax.rem(me + 2 * C - 1 - s, C)
@@ -779,48 +867,83 @@
         dv_ref[:, columns] = dv_sum[...].astype(BF)
         return carry
 
-    lax.fori_loop(0, heads, one_head, 0)
+    lax.fori_loop(0, 1, one_head, 0)
+    sums.relay(lambda k: loads[k].wait())
+    lax.fori_loop(1, heads, one_head, 0)
     for step in range(1, C - 1):
         moves(step - 1).wait_recv()
         add_into(held.at[step - 1], terms.at[chunk(step)])
         moves(step).start()
+    sums.finish(total_ref)
+    h_in.wait()
     moves(C - 2).wait_recv()
-    y_ref[...] = (h_ref[...] + held[C - 2].astype(F32) + terms[me].astype(F32)).astype(BF)
+    y_ref[...] = (h[...] + held[C - 2].astype(F32) + terms[me].astype(F32)).astype(BF)
     for step in range(C - 1):
         moves(step).wait_send()
 
 
-def attend_back(q, k, v, do, log_total, seg_column, seg_row, cos_table, sin_table, h_mine, out_terms):
+def attend_back(R, q, k, v, do, log_total, seg_column, seg_row, cos_table, sin_table, out_terms, h, grad_out):
     C = out_terms.shape[0]
     T, width = q.shape
+    depth, columns = grad_out.shape[1:]
     return pl.pallas_call(
-        functools.partial(attend_back_kernel, C),
-        in_specs=[VMEM_SPEC] * 11,
-        out_specs=[VMEM_SPEC] * 4,
-        out_shape=[struct((T, width), BF)] * 4,
+        functools.partial(attend_back_kernel, R, C),
+        in_specs=[VMEM_SPEC] * 10 + [ANY] * 2,
+        out_specs=[VMEM_SPEC] * 5,
+        out_shape=[struct((T, width), BF)] * 4 + [struct((depth, columns), BF)],
         scratch_shapes=[
             pltpu.VMEM((T, HEAD_DIM), F32),
             pltpu.VMEM((T, HEAD_DIM), F32),
             pltpu.VMEM((C - 1, T, width), BF),
-            DMA((C - 1,)),
-            DMA((C - 1,)),
-        ],
+            pltpu.VMEM((T, width), F32),
+            pltpu.VMEM((R // 2, depth, columns), BF),
+            pltpu.VMEM((R // 2, depth, columns), BF),
+            pltpu.VMEM((R // 2 - 1, depth, columns), BF),
+            DMA((C - 1,)),
+            DMA((C - 1,)),
+            DMA((1,)),
+            DMA((R // 2,)),
+        ]
+        + row_sum_semaphores(R),
         compiler_params=comm_params(5),
         cost_estimate=cost(7e10, 14 * MIB),
         name="attend_back",
-    )(q, k, v, do, log_total, seg_column, seg_row, cos_table, sin_table, h_mine, out_terms)
+    )(q, k, v, do, log_total, seg_column, seg_row, cos_table, sin_table, out_terms, h, grad_out)
 
 
 def input_terms_kernel(
-    C, dq_ref, dk_ref, dv_ref, w_ref, a_ref, sum_ref, grad_hbm, terms, held, stage, store, send, recv
+    R, C, dq_ref, dk_ref, dv_ref, w_ref, a_ref, x_ref, dh_ref, mu_ref, r_ref, grad_hbm,
+    y_ref, qkv_ref, total_ref,
+    terms, held, da, stats, stats_in, own, exchanged, arrived, tiles, q_exchanged, q_arrived,
+    send, recv, s_send, s_recv, load, *semaphores,
 ):
     me, right, left = ring_places(C)
+    row, ahead, behind, other = row_places(R)
     T, width = dq_ref.shape
-    greet([{"col": left}], 1)
+    D = width * C
     heads = (dq_ref, dk_ref, dv_ref)
+    half, depth = R // 2, tiles.shape[2]
+    sums, loads = held_row_sum(R, grad_hbm, own, exchanged, arrived, load, semaphores[:4])
+    side = lax.rem(row, 2)
+    q_sums = RowSum(
+        R, lambda k: tiles.at[k, side], lambda k: tiles.at[k, 1 - side], q_exchanged, q_arrived, semaphores[4:]
+    )
+    for copy in loads:
+        copy.start()
+    greet(
+        [{"col": lax.rem(me + k, C)} for k in range(1, C)] + [{"row": other}] + [{"row": r} for r in behind[1:]],
+        C - 1 + half,
+    )
+    for k in sums.order():
+        sums.exchange(k).start()
 
     def moves(step):
         return ring_step(step, C, right, terms.at[0], held, send, recv)
+
+    def pass_on(step):
+        moves(step - 1).wait_recv()
+        add_into(held.at[step - 1], terms.at[step])
+        moves(step).start()
 
     def compute(s):
         cut = pl.ds(pl.multiple_of(lax.rem(me + 2 * C - 1 - s, C) * width, width), width)
@@ -837,63 +960,108 @@
         return carry
 
     lax.fori_loop(1, C, body, 0)
-
-    def stored(t, slot):
-        cut = pl.ds(pl.multiple_of(t * width, width), width)
-        return pltpu.make_async_copy(stage.at[slot], grad_hbm.at[cut, :], store.at[slot])
-
-    def grad_tile(t, carry):
-        slot = lax.rem(t, 2)
-
-        @pl.when(t >= 2)
-        def _():
-            stored(t, slot).wait()
-
-        left_tile = a_ref[:, pl.ds(pl.multiple_of(t * width, width), width)]
-        for i in range(3):
-            stage[slot, :, i * width : (i + 1) * width] = dot_tn(left_tile, heads[i][...]).astype(BF)
-        stored(t, slot).start()
+    sums.relay(lambda k: loads[k].wait())
+
+    def grad_tile(i, carry):
+        k = lax.rem(i + 1, half)
+        chip = lax.rem(lax.div(row, 2) + k, half)
+        left_tile = a_ref[:, pl.ds(pl.multiple_of(chip * 2 * depth, 2 * depth), 2 * depth)]
+        for i, right_side in enumerate(heads):
+            product = dot_tn(left_tile, right_side[...]).astype(BF)
+            tiles[k, 0, :, i * width : (i + 1) * width] = product[:depth]
+            tiles[k, 1, :, i * width : (i + 1) * width] = product[depth:]
+        q_sums.exchange(k).start()
         return carry
 
-    lax.fori_loop(0, C, grad_tile, 0)
-    for slot in range(2):
-        stored(slot, slot).wait()
-    for step in range(1, C - 1):
-        moves(step - 1).wait_recv()
-        add_into(held.at[step - 1], terms.at[step])
-        moves(step).start()
+    lax.fori_loop(0, half, grad_tile, 0)
+    pass_on(1)
+    q_sums.relay()
+    for step in range(2, C - 1):
+        pass_on(step)
+    sums.finish(total_ref)
     moves(C - 2).wait_recv()
-    sum_ref[...] = held[C - 2].astype(F32) + terms[C - 1].astype(F32)
+    size = 128
+
+    def normed_of(rows):
+        return (x_ref[rows, :].astype(F32) - mu_ref[rows, :]) * r_ref[rows, :]
+
+    def sum_rows(i, carry):
+        rows = pl.ds(pl.multiple_of(i * size, size), size)
+        grad = held[C - 2, rows, :].astype(F32) + terms[C - 1, rows, :].astype(F32)
+        da[rows, :] = grad
+        lane = lax.broadcasted_iota(jnp.int32, (size, 128), 1)
+        first = jnp.sum(grad, axis=1, keepdims=True)
+        second = jnp.sum(grad * normed_of(rows), axis=1, keepdims=True)
+        packed = jnp.where(lane == 0, first, jnp.where(lane == 1, second, 0.0))
+        stats[:, rows] = packed.T[:8]
+        return carry
+
+    lax.fori_loop(0, T // size, sum_rows, 0)
+    exchanges = [
+        remote(stats, stats_in.at[k - 1], s_send.at[k - 1], s_recv.at[k - 1], col=lax.rem(me + k, C)) for k in range(1, C)
+    ]
+    for copy in exchanges:
+        copy.start()
+    for copy in exchanges:
+        copy.wait_recv()
+
+    def last_rows(i, carry):
+        rows = pl.ds(pl.multiple_of(i * size, size), size)
+        both = stats[:, rows]
+        for k in range(C - 1):
+            both += stats_in[k, :, rows]
+        columns = jnp.concatenate([both, jnp.zeros((120, size), F32)], axis=0).T * (1.0 / D)
+        grad = da[rows, :] - columns[:, 0:1] - normed_of(rows) * columns[:, 1:2]
+        y_ref[rows, :] = (dh_ref[rows, :].astype(F32) + r_ref[rows, :] * grad).astype(BF)
+        return carry
+
+    lax.fori_loop(0, T // size, last_rows, 0)
+    q_sums.finish(qkv_ref)
+    for copy in exchanges:
+        copy.wait_send()
     for step in range(C - 1):
         moves(step).wait_send()
 
 
-def input_terms(C, dq, dk, dv, w_qkv, a):
+def input_terms(R, C, dq, dk, dv, w_qkv, a, tokens, dh, mu, r, grad):
     T, width = dq.shape
     D = w_qkv.shape[1]
+    half = R // 2
+    depth, columns = grad.shape[1:]
     return pl.pallas_call(
-        functools.partial(input_terms_kernel, C),
-        in_specs=[VMEM_SPEC] * 5,
-        out_specs=[VMEM_SPEC, ANY],
-        out_shape=[struct((T, width), F32), struct((D, 3 * width), BF)],
+        functools.partial(input_terms_kernel, R, C),
+        in_specs=[VMEM_SPEC] * 9 + [ANY],
+        out_specs=[VMEM_SPEC] * 3,
+        out_shape=[struct((T, width), BF), struct((D // R, 3 * width), F32), struct((depth, columns), F32)],
         scratch_shapes=[
             pltpu.VMEM((C, T, width), BF),
             pltpu.VMEM((C - 1, T, width), BF),
-            pltpu.VMEM((2, width, 3 * width), BF),
-            DMA((2,)),
-            DMA((C - 1,)),
-            DMA((C - 1,)),
-        ],
-        compiler_params=comm_params(6),
+            pltpu.VMEM((T, width), F32),
+            pltpu.VMEM((8, T), F32),
+            pltpu.VMEM((C - 1, 8, T), F32),
+            pltpu.VMEM((half, depth, columns), BF),
+            pltpu.VMEM((half, depth, columns), BF),
+            pltpu.VMEM((half - 1, depth, columns), BF),
+            pltpu.VMEM((half, 2, D // R, 3 * width), BF),
+            pltpu.VMEM((half, D // R, 3 * width), BF),
+            pltpu.VMEM((half - 1, D // R, 3 * width), BF),
+            DMA((C - 1,)),
+            DMA((C - 1,)),
+            DMA((C - 1,)),
+            DMA((C - 1,)),
+            DMA((half,)),
+        ]
+        + row_sum_semaphores(R)
+        + row_sum_semaphores(R),
+        compiler_params=comm_params(6, 63),
         cost_estimate=cost(8e10, 20 * MIB),
         name="input_terms",
-    )(dq, dk, dv, w_qkv, a)
+    )(dq, dk, dv, w_qkv, a, tokens, dh, mu, r, grad)
 
 
 def on_device(R, C, tokens, cotangent, segments, w_query, w_key, w_value, w_out, w_gate, w_up, w_down):
     T, width = tokens.shape
     D = width * C
-    rows = T // C
     me = lax.axis_index("col")
 
     def shift(values, k):
@@ -922,40 +1090,31 @@
     w_qkv = w_qkv.reshape(3, D, width)
     act_one, q, k, v, mu_one, r_one = norm_and_project(xs, w_qkv, cos_table, sin_table)
     os, log_total, out_w = attend(R, C, q, k, v, seg_column, seg_row, out_part.reshape(D, -1))
-    h_full, act_two, mu_two, r_two, hidden, slope, silu, dys = feed_forward(
+    h_full, act_two, hidden, slope, silu, dys = feed_forward(
         C, os, out_w, xs, gate_w, up_w, cotangent
     )
     dg, du = hidden_back(dys, down_w, slope, silu)
     total, grad_gate, grad_up, grad_down, out_terms = norm_terms(
         C, dg, du, hidden, gate_w, up_w, down_w, act_two, dys
     )
-    grad_down, grad_gate, grad_up = scatter(grad_down), scatter(grad_gate), scatter(grad_up)
-    mine = lambda values, axis: lax.dynamic_slice_in_dim(values, me * rows, rows, axis)
-    dh_rows, grad_heads, grad_resid = resid_back(
-        total, mine(h_full, 0), mine(mu_two, 0), mine(r_two, 0), mine(dys, 1), out_w
+    grad_down, grad_up = scatter(grad_down), scatter(grad_up)
+    by_row = lambda values: values.reshape(R, D // R, -1)
+    grad_heads, grad_resid, grad_out = resid_back(R, total, h_full, dys, os, out_w)
+    dq, dk, dv, output, grad_out = attend_back(
+        R, q, k, v, grad_heads, log_total, seg_column, seg_row, cos_table, sin_table, out_terms, h_full, by_row(grad_out)
     )
-    my_heads = mine(os, 2).transpose(2, 0, 1, 3).reshape(rows, D)
-    grad_out = scatter(dot_tn(dh_rows, my_heads).astype(BF))
-    h_mine = lax.dynamic_slice_in_dim(h_full, me * width, width, 1)
-    dq, dk, dv, output = attend_back(
-        q, k, v, grad_heads, log_total, seg_column, seg_row, cos_table, sin_table, h_mine, out_terms
-    )
-    grad_input, grad_qkv = input_terms(C, dq, dk, dv, w_qkv, act_one)
-    grad_qkv = scatter(grad_qkv).astype(F32)
     grad_out = total_of(scattered(grad_out, 1)).T
-    normed = (tokens.astype(F32) - mu_one) * r_one
-    sums = lax.psum(jnp.stack([jnp.sum(grad_input, axis=1), jnp.sum(grad_input * normed, axis=1)]), "col")
-    grad_tokens = grad_resid.astype(F32) + r_one * (
-        grad_input - (sums[0] / D)[:, None] - normed * (sums[1] / D)[:, None]
+    grad_tokens, grad_qkv, grad_gate = input_terms(
+        R, C, dq, dk, dv, w_qkv, act_one, tokens, grad_resid, mu_one, r_one, by_row(grad_gate)
     )
     return (
         output,
-        grad_tokens.astype(BF),
+        grad_tokens,
         grad_qkv[:, :width],
         grad_qkv[:, width : 2 * width],
         grad_qkv[:, 2 * width :],
         grad_out,
-        grad_gate.astype(F32),
+        grad_gate,
         grad_up.astype(F32),
         grad_down.astype(F32).T,
     )

time: 976 us -> 650 us (0.67)
  waiting for transfers between devices: 323 us -> 1.5 us
  Pallas kernels: 568 us -> 600 us
  local copies, waits for them, and re-layouts: 24.3 us -> 13.1 us
  blocking collectives: 10.4 us -> 0 us
    reduce_scatter x5 -> x2, waiting for transfers between devices: 320 us -> 0.01 us  [on_device(): lax.psum_scatter(g, 'row', scatter_dimension=0, tiled=True)]
    pallas_call x3, Pallas kernels: 208 us -> 239 us  [the longest x1 109 us: input_terms(): pl.pallas_call(functools.partial(input_terms_kernel, R, C), in_specs=[VME...]
    dynamic_slice x5 -> x0, local copies, waits for them, and re-layouts: 11.6 us -> none  [the longest x4 8.52 us: on_device(): lax.dynamic_slice_in_dim(values, me * rows, rows, axis)]
    psum x1 -> x0, blocking collectives: 10.4 us -> none  [on_device(): lax.psum(jnp.stack([jnp.sum(grad_input, axis=1), jnp.sum(grad_input * nor...]
  transfers between devices with their start and end apart: 11 -> 8, of which waited for: 5 -> 0; matrix products, arithmetic and copies ran while one was open for 5% -> 3% of each run, Pallas kernels for 27% -> 78%
where the time goes in v3:
time: 650 us; the launch traced here: 643 us
  Pallas kernels  600 us (92%)
  between operations  14.2 us (2%)
  local copies, waits for them, and re-layouts  13.1 us (2%)
  other arithmetic  9.47 us (1%)
    pallas_call x1, Pallas kernels, input_terms(): pl.pallas_call(functools.partial(input_terms_kernel, R, C), in_specs=[VME...  109 us
    pallas_call x1, Pallas kernels, first_gather(): pl.pallas_call(functools.partial(gather_kernel, R, C), in_specs=[ANY] * 5...  88.6 us
    pallas_call x1, Pallas kernels, norm_terms(): pl.pallas_call(functools.partial(norm_terms_kernel, C), in_specs=[ANY] *...  84.5 us
    pallas_call x1, Pallas kernels, attend_back(): pl.pallas_call(functools.partial(attend_back_kernel, R, C), in_specs=[VME...  80.1 us
    pallas_call x1, Pallas kernels, feed_forward(): pl.pallas_call(functools.partial(feed_kernel, C, tiles), grid=(tiles + F...  80.1 us
    pallas_call x1, Pallas kernels, attend(): pl.pallas_call(functools.partial(attend_kernel, R, C), in_specs=[VMEM_SPE...  77.8 us
    pallas_call x1, Pallas kernels, resid_back(): pl.pallas_call(functools.partial(resid_back_kernel, R, C), in_specs=[VMEM...  50.1 us
    pallas_call x1, Pallas kernels, hidden_back(): pl.pallas_call(hidden_back_kernel, grid=(F // bf,), in_specs=[pl.BlockSpe...  16.9 us
  transfers between devices with their start and end apart: 8, of which 0 were waited for; matrix products, arithmetic and copies ran while one was open for 3% of the time, Pallas kernels for 78%

profile of v3, /device:TPU:8, one launch (start us, length us, event | category | flops | bytes accessed | tf_op | source)
XLA Modules:
  0.0 643.2 jit_solution(4245180199780108870)
XLA Ops:
  7.2 0.0 all-gather.4.cloned.1.call-start
  7.2 0.7 all-gather.4.cloned.1.call-update
  7.9 0.0 all-gather.6.cloned.1.call-start
  8.0 0.7 all-gather.6.cloned.1.call-update
  8.7 0.0 all-gather.8.cloned.1.call-start
  8.7 2.3 copy.28
  11.0 0.0 all-gather.8.cloned.1.call-update
  11.0 0.0 copy-start.3
  11.0 0.0 reduce-scatter.5.cloned.1.call-start
  11.1 88.6 %first_gather.1 = (bf16[4,1024,512]{2,1,0:T(8,128)(2,1)}, bf16[4,512,256]{2,1,0:T(8,128)(2,1)}, bf16[3,8,256,512]{3,2,1,0:T(8,128)(2,1)}) custom-call(bf16[1024,512]{1,0:T(8,128)(2,1)} %x_ref.3, bf16[512,256]{1,0:T(8,128)(2,1)} %wo_ref.1, bf16[256,512]{1,0:T(8,128)(2,1)} %wq_ref.1, bf16[256,512]{1,0:T(8,128)(2,1)} %wk_ref.1, bf16[256,512]{1,0:T(8,128)(2,1)} %wv_ref.1), custom_call_target="tpu_custom_call" | custom-call | flops 60000002048 | bytes 14680064 | tf_op jit(solution)/shard_map/first_gather/pallas_call | solution.py:161
  99.7 0.0 copy-done.3
  99.7 1.0 copy.27.segk_ref
  100.7 0.5 convert_reduce_fusion
  101.3 1.9 fusion.1
  103.2 1.3 pad_maximum_fusion
  104.5 12.6 %norm_and_project.1 = (bf16[1024,2048]{1,0:T(8,128)(2,1)}, bf16[1024,512]{1,0:T(8,128)(2,1)}, bf16[1024,512]{1,0:T(8,128)(2,1)}, bf16[1024,512]{1,0:T(8,128)(2,1...) custom-call(bf16[4,1024,512]{2,1,0:T(8,128)(2,1)} %get-tuple-element.45.xs_ref, bf16[3,2048,512]{2,1,0:T(8,128)(2,1)} %bitcast.17, ...), custom_call_target="tpu_custom_call" | custom-call | flops 6442450944 | bytes 14680064 | tf_op jit(solution)/shard_map/norm_and_project/pallas_call | solution.py:221
  117.1 77.8 %attend.1 = (bf16[4,4,1024,128]{3,2,1,0:T(8,128)(2,1)}, f32[4,1,1024]{2,1,0:T(1,128)}, bf16[8,2048,256]{2,1,0:T(8,128)(2,1)}) custom-call(bf16[1024,512]{1,0:T(8,128)(2,1)} %get-tuple-element.47.q_ref, bf16[1024,512]{1,0:T(8,128)(2,1)} %get-tuple-element.48.k_ref, bf16[1024,512]{1,0:T(8,128)(2,1)} %get-tuple-element.49.v_ref, s32[1024,1]{1,0:T(8,128)} %copy.27.segk_ref, ...), custom_call_target="tpu_custom_call" | custom-call | flops 70000001024 | bytes 14680064 | tf_op jit(solution)/shard_map/attend/pallas_call | solution.py:321
  194.8 0.0 all-gather.4.cloned.1.call-done.wg_ref.wg_hbm
  194.9 0.0 all-gather.6.cloned.1.call-done.wu_ref.wu_hbm
  194.9 80.1 %feed_forward.1 = (f32[1024,2048]{1,0:T(8,128)}, bf16[1024,2048]{1,0:T(8,128)(2,1)}, bf16[1024,2048]{1,0:T(8,128)(2,1)}, bf16[1024,2048]{1,0:T(8,128)(2,1)}, bf1...) custom-call(bf16[4,4,1024,128]{3,2,1,0:T(8,128)(2,1)} %get-tuple-element.51.os_ref.os_hbm, ...), custom_call_target="tpu_custom_call" | custom-call | flops 70000001024 | bytes 62914560 | tf_op jit(solution)/shard_map/feed_forward/pallas_call | solution.py:422
  275.0 0.0 all-gather.8.cloned.1.call-done.wd_ref.wd_hbm
  275.0 16.9 %hidden_back.1 = (bf16[1024,2048]{1,0:T(8,128)(2,1)}, bf16[1024,2048]{1,0:T(8,128)(2,1)}) custom-call(bf16[4,1024,512]{2,1,0:T(8,128)(2,1)} %get-tuple-element.53.dys_ref.dys_hbm, bf16[2048,2048]{1,0:T(8,128)(2,1)} %all-gather.8.cloned.1.call-done.wd_ref.wd_hbm, bf16[1024,2048]{1,0:T(8,128)(2,1)} %get-tuple-element.54.slope_ref, ...), custom_call_target="tpu_custom_call" | custom-call | flops 8589934592 | bytes 29360128 | tf_op jit(solution)/shard_map/hidden_back/pallas_call | solution.py:466
  292.0 84.5 %norm_terms.1 = (f32[256,2048]{1,0:T(8,128)}, bf16[2048,2048]{1,0:T(8,128)(2,1)}, bf16[2048,2048]{1,0:T(8,128)(2,1)}, bf16[2048,2048]{1,0:T(8,128)(2,1)}, bf16[4,1024,512]{2,1,0:T(8,128)(2,1)}) custom-call(bf16[1024,2048]{1,0:T(8,128)(2,1)} %get-tuple-element.56.dg_hbm, bf16[1024,2048]{1,0:T(8,128)(2,1)} %get-tuple-element.57.du_hbm, ...), custom_call_target="tpu_custom_call" | custom-call | flops 89999998976 | bytes 73400320 | tf_op jit(solution)/shard_map/norm_terms/pallas_call | solution.py:684
  376.5 0.0 reduce-scatter.5.cloned.1.call-update
  376.5 0.0 reduce-scatter.3.cloned.1.call-start
  376.6 50.1 %resid_back.1 = (bf16[1024,512]{1,0:T(8,128)(2,1)}, bf16[1024,512]{1,0:T(8,128)(2,1)}, bf16[2048,2048]{1,0:T(8,128)(2,1)}) custom-call(f32[256,2048]{1,0:T(8,128)} %get-tuple-element.60.sum_ref, f32[1024,2048]{1,0:T(8,128)} %get-tuple-element.61.h_hbm, bf16[4,1024,512]{2,1,0:T(8,128)(2,1)} %get-tuple-element.53.dys_ref.dys_hbm, ...), custom_call_target="tpu_custom_call" | custom-call | flops 40000000000 | bytes 20971520 | tf_op jit(solution)/shard_map/resid_back/pallas_call | solution.py:790
  426.7 0.0 reduce-scatter.3.cloned.1.call-update
  426.8 80.1 %attend_back.1 = (bf16[1024,512]{1,0:T(8,128)(2,1)}, bf16[1024,512]{1,0:T(8,128)(2,1)}, bf16[1024,512]{1,0:T(8,128)(2,1)}, bf16[1024,512]{1,0:T(8,128)(2,1)}, bf16[256,2048]{1,0:T(8,128)(2,1)}) custom-call(bf16[1024,512]{1,0:T(8,128)(2,1)} %get-tuple-element.47.q_ref, bf16[1024,512]{1,0:T(8,128)(2,1)} %get-tuple-element.48.k_ref, ...), custom_call_target="tpu_custom_call" | custom-call | flops 70000001024 | bytes 14680064 | tf_op jit(solution)/shard_map/attend_back/pallas_call | solution.py:889
  506.9 1.2 constant_dynamic-slice_fusion.2
  508.1 0.1 collective-permute-start
  508.1 4.7 collective-permute-start.1
  512.8 0.0 collective-permute-start.2
  512.8 109.2 %input_terms.1 = (bf16[1024,512]{1,0:T(8,128)(2,1)}, f32[256,1536]{1,0:T(8,128)}, f32[256,2048]{1,0:T(8,128)}) custom-call(bf16[1024,512]{1,0:T(8,128)(2,1)} %get-tuple-element.67.dq_ref, bf16[1024,512]{1,0:T(8,128)(2,1)} %get-tuple-element.68.dk_ref, bf16[1024,512]{1,0:T(8,128)(2,1)} %get-tuple-element.69.dv_ref, bf16[3,2048,512]{2,1,0:T(8,128)(2,1)} %bitcast.18, ...), custom_call_target="tpu_custom_call" | custom-call | flops 80000000000 | bytes 20971520 | tf_op jit(solution)/shard_map/input_terms/pallas_call | solution.py:1031
  622.0 2.5 fusion.2
  624.6 0.0 collective-permute-done
  624.6 0.0 collective-permute-done.1
  624.6 0.0 collective-permute-done.2
  624.6 1.3 add_bitcast_fusion
  625.9 1.0 copy.30
  626.9 1.5 convert_bitcast_fusion
  628.4 0.0 copy-start.1
  628.4 1.8 copy.31
  630.2 2.9 convert_element_type.40
  633.1 0.0 copy-done.1
  633.1 1.0 copy.35
  634.1 0.0 copy-done.2
  634.1 1.0 copy.36
  635.1 1.3 copy.37
  (7 shorter events, 0.0 us)
Async XLA Ops:
  7.2 187.7 %all-gather.4.cloned.1.call-start = ((), (), s32[]{:S(2)}) async-start(), calls=%async_computation.2 | async-start | bytes 9437184 | tf_op jit(solution)/shard_map/all_gather | solution.py:1083
  7.9 187.0 %all-gather.6.cloned.1.call-start = ((), (), s32[]{:S(2)}) async-start(), calls=%async_computation.3 | async-start | bytes 9437184 | tf_op jit(solution)/shard_map/all_gather | solution.py:1083
  8.7 266.4 %all-gather.8.cloned.1.call-start = ((), (), s32[]{:S(2)}) async-start(), calls=%async_computation.4 | async-start | bytes 9437184 | tf_op jit(solution)/shard_map/all_gather | solution.py:1083
  11.0 88.7 %copy-start.3 = (s32[1024]{0:T(1024)S(1)}, s32[1024]{0:T(1024)}, u32[]{:S(2)}) copy-start(s32[1024]{0:T(1024)} %param.12) | copy-start | bytes 12292
  11.0 615.9 %reduce-scatter.5.cloned.1.call-start = ((), (), s32[]{:S(2)}) async-start(), calls=%async_computation.6 | async-start | bytes 9437184 | tf_op jit(solution)/shard_map/reduce_scatter | solution.py:1084
  376.5 253.7 %reduce-scatter.3.cloned.1.call-start = ((), (), s32[]{:S(2)}) async-start(), calls=%async_computation.5 | async-start | bytes 9437184 | tf_op jit(solution)/shard_map/reduce_scatter | solution.py:1084
  508.1 116.5 %collective-permute-start = (bf16[256,512]{1,0:T(8,128)(2,1)S(1)}, bf16[256,512]{1,0:T(8,128)(2,1)}, u32[]{:S(2)}, u32[]{:S(2)}) collective-permute-start(bf16[256,512]{1,0:T(8,128)(2,1)S(1)} %get-tuple-element.111), channel_id=1, source_target_pairs={{0,1},{1,2},{2,3},{3,0},{4,5},{5,6},{6,7},{7,4},{8,9},{9,10},{10,1... | collective-permute-start | bytes 786440 | tf_op jit(solution)/shard_map/ppermute | solution.py:1068
  508.1 116.4 %collective-permute-start.1 = (bf16[256,512]{1,0:T(8,128)(2,1)S(1)}, bf16[256,512]{1,0:T(8,128)(2,1)}, u32[]{:S(2)}, u32[]{:S(2)}) collective-permute-start(bf16[256,512]{1,0:T(8,128)(2,1)S(1)} %get-tuple-element.113), channel_id=1, source_target_pairs={{0,2},{1,3},{2,0},{3,1},{4,6},{5,7},{6,4},{7,5},{8,10},{9,11},{10,... | collective-permute-start | bytes 786440 | tf_op jit(solution)/shard_map/ppermute | solution.py:1068
  512.8 111.8 %collective-permute-start.2 = (bf16[256,512]{1,0:T(8,128)(2,1)S(1)}, bf16[256,512]{1,0:T(8,128)(2,1)}, u32[]{:S(2)}, u32[]{:S(2)}) collective-permute-start(bf16[256,512]{1,0:T(8,128)(2,1)S(1)} %get-tuple-element.112), channel_id=1, source_target_pairs={{0,3},{1,0},{2,1},{3,2},{4,7},{5,4},{6,5},{7,6},{8,11},{9,8},{10,9... | collective-permute-start | bytes 786440 | tf_op jit(solution)/shard_map/ppermute | solution.py:1068
  628.4 4.8 copy-start.1
  630.2 4.9 copy-start
  630.2 3.9 copy-start.2
Sparse Core Ops, SparseCore 0:
  9.9 77.2 all-gather.3
  89.1 96.0 all-gather.5
  187.7 52.3 all-gather.7
  376.7 100.4 reduce-scatter.4
  480.8 96.7 reduce-scatter.2

commit v4 on v3

--- a/solution.py
+++ b/solution.py
@@ -499,57 +499,134 @@
 
 class RowSum:
     def __init__(self, R, own, twin, exchanged, arrived, semaphores):
-        self.R, self.own, self.twin = R, own, twin
-        self.exchanged, self.arrived = exchanged, arrived
-        self.row, self.ahead, self.behind, self.other = row_places(R)
+        self.P = R // 4
+        self.own, self.twin, self.exchanged, self.arrived = own, twin, exchanged, arrived
         self.x_send, self.x_recv, self.y_send, self.y_recv = semaphores
-
-    def exchange(self, k):
-        return remote(self.twin(k), self.exchanged.at[k], self.x_send.at[k], self.x_recv.at[k], row=self.other)
-
-    def spread(self, k):
-        return remote(self.own(k), self.arrived.at[k - 1], self.y_send.at[k], self.y_recv.at[k], row=self.ahead[k])
+        self.width = arrived.shape[2]
+        self.places = row_of(R)
+        self.peers = row_peers(R)
+
+    def part(self, ref, side):
+        return ref.at[:, pl.ds(side * self.width, self.width)]
+
+    def exchange(self, slot):
+        return remote(
+            self.twin(slot), self.exchanged.at[slot], self.x_send.at[slot], self.x_recv.at[slot], row=self.places(0, True)
+        )
+
+    def send(self, slot, side, index, target):
+        return remote(
+            self.part(self.own(slot), side), self.arrived.at[index], self.y_send.at[index], self.y_recv.at[index],
+            row=self.places(target),
+        )
+
+    def left_one(self, dp):
+        return self.send(2 * dp + 1, 0, dp, 1)
+
+    def left_two(self, dp):
+        return self.send(2 * dp, 0, self.P + dp - 1, 2 * dp)
+
+    def right_one(self, dp, dq):
+        return self.send(2 * dp + dq, 1, 2 * self.P - 1 + 2 * (dp - 1) + dq, 2 * dp)
+
+    def right_two(self):
+        return self.send(1, 1, 4 * self.P - 3, 1)
 
     def order(self):
-        return list(range(1, self.R // 2)) + [0]
+        return (
+            [2 * dp + 1 for dp in range(1, self.P)] + [1] + [2 * dp for dp in range(1, self.P)] + [0]
+        )
 
     def relay(self, before=None):
-        for k in self.order():
+        for slot in self.order():
             if before is not None:
-                before(k)
-            self.exchange(k).wait_recv()
-            add_into(self.own(k), self.exchanged.at[k])
-            if k:
-                self.spread(k).start()
-
-    def finish(self, target):
-        for k in range(1, self.R // 2):
-            self.spread(k).wait_recv()
-        size = min(64, target.shape[0])
+                before(slot)
+            self.exchange(slot).wait_recv()
+            add_into(self.own(slot), self.exchanged.at[slot])
+            dp, dq = divmod(slot, 2)
+            if dq:
+                self.left_one(dp).start()
+            if dp:
+                self.right_one(dp, dq).start()
+
+    def relay_again(self):
+        for dp in range(1, self.P):
+            self.left_one(dp).wait_recv()
+            add_into(self.part(self.own(2 * dp), 0), self.arrived.at[dp])
+            self.left_two(dp).start()
+        for dp in range(1, self.P):
+            copy = self.right_one(dp, 1)
+            copy.wait_recv()
+            add_into(self.part(self.own(1), 1), self.arrived.at[2 * self.P - 1 + 2 * (dp - 1) + 1])
+        self.right_two().start()
+
+    def finish(self, write, size=64):
+        P, width = self.P, self.width
+        self.left_one(0).wait_recv()
+        self.right_two().wait_recv()
+        for dp in range(1, P):
+            self.left_two(dp).wait_recv()
+            self.right_one(dp, 0).wait_recv()
+        lefts = [0] + [P + dp - 1 for dp in range(1, P)]
+        rights = [4 * P - 3] + [2 * P - 1 + 2 * (dp - 1) for dp in range(1, P)]
 
         def body(i, carry):
             rows = pl.ds(pl.multiple_of(i * size, size), size)
             total = self.own(0)[rows, :].astype(F32)
-            for k in range(1, self.R // 2):
-                total += self.arrived[k - 1, rows, :].astype(F32)
-            target[rows, :] = total.astype(target.dtype)
+            halves = []
+            for side, places in enumerate((lefts, rights)):
+                half = total[:, side * width : (side + 1) * width]
+                for index in places:
+                    half += self.arrived[index, rows, :].astype(F32)
+                halves.append(half)
+            write(rows, jnp.concatenate(halves, axis=1))
             return carry
 
-        lax.fori_loop(0, target.shape[0] // size, body, 0)
-        for k in range(self.R // 2):
-            self.exchange(k).wait_send()
-            if k:
-                self.spread(k).wait_send()
+        lax.fori_loop(0, self.exchanged.shape[1] // size, body, 0)
+        for slot in range(2 * P):
+            self.exchange(slot).wait_send()
+        self.left_one(0).wait_send()
+        self.right_two().wait_send()
+        for dp in range(1, P):
+            self.left_one(dp).wait_send()
+            self.left_two(dp).wait_send()
+            self.right_one(dp, 0).wait_send()
+            self.right_one(dp, 1).wait_send()
+
+
+def row_of(R):
+    row = lax.axis_index("row")
+    side, chip = lax.rem(row, 2), lax.div(row, 2)
+    p, q = lax.div(chip, 2), lax.rem(chip, 2)
+
+    def place(slot, twin=False):
+        dp, dq = divmod(slot, 2)
+        chip_there = 2 * lax.rem(p + dp, R // 4) + lax.rem(q + dq, 2)
+        return 2 * chip_there + (1 - side if twin else side)
+
+    return place
+
+
+def row_peers(R):
+    place = row_of(R)
+    return [{"row": place(0, True)}, {"row": place(1)}] + [{"row": place(2 * dp)} for dp in range(1, R // 4)]
 
 
 def row_sum_semaphores(R):
-    return [DMA((R // 2,)) for _ in range(4)]
+    return [DMA((R // 2,)), DMA((R // 2,)), DMA((R - 2,)), DMA((R - 2,))]
+
+
+def row_sum_buffers(R, depth, columns):
+    return [
+        pltpu.VMEM((R // 2, depth, columns), BF),
+        pltpu.VMEM((R - 2, depth, columns // 2), BF),
+    ]
 
 
 def held_row_sum(R, grad_hbm, own, exchanged, arrived, load, semaphores):
-    row, ahead, behind, other = row_places(R)
-    sums = RowSum(R, lambda k: own.at[k], lambda k: grad_hbm.at[lax.rem(other + 2 * k, R)], exchanged, arrived, semaphores)
-    loads = [pltpu.make_async_copy(grad_hbm.at[ahead[k]], own.at[k], load.at[k]) for k in range(R // 2)]
+    place = row_of(R)
+    sums = RowSum(R, lambda i: own.at[i], lambda i: grad_hbm.at[place(i, True)], exchanged, arrived, semaphores)
+    loads = [pltpu.make_async_copy(grad_hbm.at[place(i)], own.at[i], load.at[i]) for i in range(R // 2)]
     return sums, loads
 
 
@@ -716,8 +793,9 @@
 
 
 def resid_back_kernel(
-    R, C, sum_ref, h_hbm, dys_hbm, os_hbm, w_hbm, do_hbm, dhs_hbm, grad_hbm,
-    h, dy, heads, w, dh, out, stage, load, w_load, local, store, h_send, h_recv, o_send, o_recv,
+    R, C, sum_ref, h_hbm, dys_hbm, os_hbm, w_hbm, down_hbm, do_hbm, dhs_hbm, grad_hbm, down_ref,
+    h, dy, heads, w, dh, out, stage, own, exchanged, arrived,
+    load, w_load, local, store, h_send, h_recv, o_send, o_recv, own_load, *semaphores,
 ):
     me, right, left = ring_places(C)
     blocks, D, part = w.shape
@@ -738,8 +816,13 @@
         copy = pltpu.make_async_copy(w_hbm.at[:, cut, :], w.at[:, cut, :], w_load.at[k])
         copy.start()
         loads.append(copy)
+    sums, own_loads = held_row_sum(R, down_hbm, own, exchanged, arrived, own_load, semaphores)
+    for copy in own_loads:
+        copy.start()
     heads_in.start()
-    greet([{"col": lax.rem(me + k, C)} for k in range(1, C)], C - 1)
+    greet([{"col": lax.rem(me + k, C)} for k in range(1, C)] + sums.peers, C - 1 + len(sums.peers))
+    for slot in sums.order():
+        sums.exchange(slot).start()
     for copy in first_in:
         copy.wait()
     grad = sum_ref[...]
@@ -770,6 +853,7 @@
             copy = pltpu.make_async_copy(dh.at[:, cut], dhs_hbm.at[mine, :], local.at[1])
         copy.start()
         copies.append(copy)
+    sums.relay(lambda slot: own_loads[slot].wait())
     heads_in.wait()
     right_side = jnp.concatenate([heads[j, i] for j in range(C) for i in range(heads.shape[1])], axis=1)
     stores = []
@@ -780,18 +864,30 @@
         copy = pltpu.make_async_copy(stage.at[t % 2], grad_hbm.at[pl.ds(t * width, width), :], store.at[t % 2])
         copy.start()
         stores.append(copy)
+    sums.relay_again()
+
+    def write(part, values):
+        down_ref[:, part] = values.T
+
+    sums.finish(write, 128)
     for copy in copies + stores[-2:]:
         copy.wait()
 
 
-def resid_back(R, total, h, dys, os, w_out):
+def resid_back(R, total, h, dys, os, w_out, grad_down):
     C, T, width = dys.shape
     rows, D = total.shape
+    depth, columns = grad_down.shape[1:]
     return pl.pallas_call(
         functools.partial(resid_back_kernel, R, C),
-        in_specs=[VMEM_SPEC] + [ANY] * 4,
-        out_specs=[ANY, ANY, ANY],
-        out_shape=[struct((T, width), BF), struct((T, width), BF), struct((D, D), BF)],
+        in_specs=[VMEM_SPEC] + [ANY] * 5,
+        out_specs=[ANY, ANY, ANY, VMEM_SPEC],
+        out_shape=[
+            struct((T, width), BF),
+            struct((T, width), BF),
+            struct((D, D), BF),
+            struct((columns, depth), F32),
+        ],
         scratch_shapes=[
             pltpu.VMEM((rows, D), F32),
             pltpu.VMEM((C, rows, width), BF),
@@ -800,6 +896,10 @@
             pltpu.VMEM((rows, D), BF),
             pltpu.VMEM((C, rows, width), BF),
             pltpu.VMEM((2, width, D), BF),
+            pltpu.VMEM((R // 2, depth, columns), BF),
+        ]
+        + row_sum_buffers(R, depth, columns)
+        + [
             DMA((3,)),
             DMA((C,)),
             DMA((2,)),
@@ -808,31 +908,35 @@
             DMA((C - 1,)),
             DMA((C - 1,)),
             DMA((C - 1,)),
-        ],
+            DMA((R // 2,)),
+        ]
+        + row_sum_semaphores(R),
         compiler_params=comm_params(4),
         cost_estimate=cost(4e10, 20 * MIB),
         name="resid_back",
-    )(total, h, dys, os, w_out)
+    )(total, h, dys, os, w_out, grad_down)
 
 
 def attend_back_kernel(
-    R, C, q_ref, k_ref, v_ref, do_ref, log_ref, segk_ref, segq_ref, cos_ref, sin_ref, terms, h_hbm, grad_hbm,
-    dq_ref, dk_ref, dv_ref, y_ref, total_ref, dk_sum, dv_sum, held, h, own, exchanged, arrived,
-    send, recv, h_load, load, *semaphores,
+    R, C, q_ref, k_ref, v_ref, do_ref, log_ref, segk_ref, segq_ref, cos_ref, sin_ref, terms, h_hbm, out_hbm, up_hbm,
+    dq_ref, dk_ref, dv_ref, y_ref, out_ref, up_ref, dk_sum, dv_sum, held, h,
+    out_own, out_exchanged, out_arrived, up_own, up_exchanged, up_arrived,
+    send, recv, h_load, out_load, up_load, *semaphores,
 ):
     me, right, left = ring_places(C)
-    row, ahead, behind, other = row_places(R)
     T, width = q_ref.shape
     heads, bq = width // HEAD_DIM, 256
     cut = pl.ds(pl.multiple_of(me * width, width), width)
     h_in = pltpu.make_async_copy(h_hbm.at[:, cut], h, h_load.at[0])
-    sums, loads = held_row_sum(R, grad_hbm, own, exchanged, arrived, load, semaphores)
-    for copy in loads:
+    up_sums, up_loads = held_row_sum(R, up_hbm, up_own, up_exchanged, up_arrived, up_load, semaphores[:4])
+    out_sums, out_loads = held_row_sum(R, out_hbm, out_own, out_exchanged, out_arrived, out_load, semaphores[4:])
+    for copy in up_loads + out_loads:
         copy.start()
     h_in.start()
-    greet([{"col": left}, {"row": other}] + [{"row": r} for r in behind[1:]], 1 + R // 2)
-    for k in sums.order():
-        sums.exchange(k).start()
+    greet([{"col": left}] + up_sums.peers, 1 + len(up_sums.peers))
+    for sums in (up_sums, out_sums):
+        for slot in sums.order():
+            sums.exchange(slot).start()
 
     def chunk(s):
         return lax.rem(me + 2 * C - 1 - s, C)
@@ -867,14 +971,26 @@
         dv_ref[:, columns] = dv_sum[...].astype(BF)
         return carry
 
-    lax.fori_loop(0, 1, one_head, 0)
-    sums.relay(lambda k: loads[k].wait())
-    lax.fori_loop(1, heads, one_head, 0)
+    lax.fori_loop(0, heads // 2, one_head, 0)
+    up_sums.relay(lambda slot: up_loads[slot].wait())
+    lax.fori_loop(heads // 2, heads, one_head, 0)
+    out_sums.relay(lambda slot: out_loads[slot].wait())
     for step in range(1, C - 1):
         moves(step - 1).wait_recv()
         add_into(held.at[step - 1], terms.at[chunk(step)])
         moves(step).start()
-    sums.finish(total_ref)
+        if step == 1:
+            up_sums.relay_again()
+    out_sums.relay_again()
+
+    def write_up(part, values):
+        up_ref[part, :] = values
+
+    def write_out(part, values):
+        out_ref[part, :] = values.astype(BF)
+
+    up_sums.finish(write_up)
+    out_sums.finish(write_out)
     h_in.wait()
     moves(C - 2).wait_recv()
     y_ref[...] = (h[...] + held[C - 2].astype(F32) + terms[me].astype(F32)).astype(BF)
@@ -882,60 +998,70 @@
         moves(step).wait_send()
 
 
-def attend_back(R, q, k, v, do, log_total, seg_column, seg_row, cos_table, sin_table, out_terms, h, grad_out):
+def attend_back(R, q, k, v, do, log_total, seg_column, seg_row, cos_table, sin_table, out_terms, h, grad_out, grad_up):
     C = out_terms.shape[0]
     T, width = q.shape
-    depth, columns = grad_out.shape[1:]
+    shapes = (grad_out.shape[1:], grad_up.shape[1:])
     return pl.pallas_call(
         functools.partial(attend_back_kernel, R, C),
-        in_specs=[VMEM_SPEC] * 10 + [ANY] * 2,
-        out_specs=[VMEM_SPEC] * 5,
-        out_shape=[struct((T, width), BF)] * 4 + [struct((depth, columns), BF)],
+        in_specs=[VMEM_SPEC] * 10 + [ANY] * 3,
+        out_specs=[VMEM_SPEC] * 6,
+        out_shape=[struct((T, width), BF)] * 4 + [struct(shapes[0], BF), struct(shapes[1], F32)],
         scratch_shapes=[
             pltpu.VMEM((T, HEAD_DIM), F32),
             pltpu.VMEM((T, HEAD_DIM), F32),
             pltpu.VMEM((C - 1, T, width), BF),
             pltpu.VMEM((T, width), F32),
-            pltpu.VMEM((R // 2, depth, columns), BF),
-            pltpu.VMEM((R // 2, depth, columns), BF),
-            pltpu.VMEM((R // 2 - 1, depth, columns), BF),
+        ]
+        + [
+            buffer
+            for shape in shapes
+            for buffer in [pltpu.VMEM((R // 2,) + shape, BF)] + row_sum_buffers(R, *shape)
+        ]
+        + [
             DMA((C - 1,)),
             DMA((C - 1,)),
             DMA((1,)),
             DMA((R // 2,)),
+            DMA((R // 2,)),
         ]
+        + row_sum_semaphores(R)
         + row_sum_semaphores(R),
         compiler_params=comm_params(5),
         cost_estimate=cost(7e10, 14 * MIB),
         name="attend_back",
-    )(q, k, v, do, log_total, seg_column, seg_row, cos_table, sin_table, out_terms, h, grad_out)
+    )(q, k, v, do, log_total, seg_column, seg_row, cos_table, sin_table, out_terms, h, grad_out, grad_up)
 
 
 def input_terms_kernel(
-    R, C, dq_ref, dk_ref, dv_ref, w_ref, a_ref, x_ref, dh_ref, mu_ref, r_ref, grad_hbm,
-    y_ref, qkv_ref, total_ref,
-    terms, held, da, stats, stats_in, own, exchanged, arrived, tiles, q_exchanged, q_arrived,
-    send, recv, s_send, s_recv, load, *semaphores,
+    R, C, dq_ref, dk_ref, dv_ref, w_ref, a_ref, x_ref, dh_ref, mu_ref, r_ref, out_ref, grad_hbm,
+    y_ref, gq_ref, gk_ref, gv_ref, total_ref, gout_ref,
+    terms, held, da, stats, stats_in, out_in, own, exchanged, arrived, tiles, q_exchanged, q_arrived,
+    send, recv, s_send, s_recv, o_send, o_recv, load, *semaphores,
 ):
     me, right, left = ring_places(C)
-    row, ahead, behind, other = row_places(R)
     T, width = dq_ref.shape
     D = width * C
     heads = (dq_ref, dk_ref, dv_ref)
-    half, depth = R // 2, tiles.shape[2]
+    depth = tiles.shape[2]
     sums, loads = held_row_sum(R, grad_hbm, own, exchanged, arrived, load, semaphores[:4])
-    side = lax.rem(row, 2)
+    side = lax.rem(lax.axis_index("row"), 2)
     q_sums = RowSum(
-        R, lambda k: tiles.at[k, side], lambda k: tiles.at[k, 1 - side], q_exchanged, q_arrived, semaphores[4:]
+        R, lambda i: tiles.at[i, side], lambda i: tiles.at[i, 1 - side], q_exchanged, q_arrived, semaphores[4:]
     )
     for copy in loads:
         copy.start()
-    greet(
-        [{"col": lax.rem(me + k, C)} for k in range(1, C)] + [{"row": other}] + [{"row": r} for r in behind[1:]],
-        C - 1 + half,
-    )
-    for k in sums.order():
-        sums.exchange(k).start()
+    greet([{"col": lax.rem(me + k, C)} for k in range(1, C)] + sums.peers, C - 1 + len(sums.peers))
+    for slot in sums.order():
+        sums.exchange(slot).start()
+
+    def block_of(k):
+        return out_ref.at[:, pl.ds(pl.multiple_of(lax.rem(me + k, C) * width, width), width)]
+
+    out_copies = [
+        remote(block_of(k), out_in.at[k - 1], o_send.at[k - 1], o_recv.at[k - 1], col=lax.rem(me + k, C))
+        for k in range(1, C)
+    ]
 
     def moves(step):
         return ring_step(step, C, right, terms.at[0], held, send, recv)
@@ -960,25 +1086,39 @@
         return carry
 
     lax.fori_loop(1, C, body, 0)
-    sums.relay(lambda k: loads[k].wait())
-
-    def grad_tile(i, carry):
-        k = lax.rem(i + 1, half)
-        chip = lax.rem(lax.div(row, 2) + k, half)
-        left_tile = a_ref[:, pl.ds(pl.multiple_of(chip * 2 * depth, 2 * depth), 2 * depth)]
+    for copy in out_copies:
+        copy.start()
+    sums.relay(lambda slot: loads[slot].wait())
+    for slot in q_sums.order():
+        start = pl.multiple_of(lax.div(q_sums.places(slot), 2) * 2 * depth, 2 * depth)
+        left_tile = a_ref[:, pl.ds(start, 2 * depth)]
         for i, right_side in enumerate(heads):
             product = dot_tn(left_tile, right_side[...]).astype(BF)
-            tiles[k, 0, :, i * width : (i + 1) * width] = product[:depth]
-            tiles[k, 1, :, i * width : (i + 1) * width] = product[depth:]
-        q_sums.exchange(k).start()
-        return carry
-
-    lax.fori_loop(0, half, grad_tile, 0)
+            tiles[slot, 0, :, i * width : (i + 1) * width] = product[:depth]
+            tiles[slot, 1, :, i * width : (i + 1) * width] = product[depth:]
+        q_sums.exchange(slot).start()
+    q_sums.relay()
     pass_on(1)
-    q_sums.relay()
+    sums.relay_again()
+    q_sums.relay_again()
+    for copy in out_copies:
+        copy.wait_recv()
+    out_total = block_of(0)[...].astype(F32)
+    for k in range(C - 1):
+        out_total += out_in[k].astype(F32)
+    gout_ref[...] = out_total.T
     for step in range(2, C - 1):
         pass_on(step)
-    sums.finish(total_ref)
+
+    def write(part, values):
+        total_ref[part, :] = values
+
+    def write_qkv(part, values):
+        for i, target in enumerate((gq_ref, gk_ref, gv_ref)):
+            target[part, :] = values[:, i * width : (i + 1) * width]
+
+    sums.finish(write)
+    q_sums.finish(write_qkv)
     moves(C - 2).wait_recv()
     size = 128
 
@@ -1016,35 +1156,39 @@
         return carry
 
     lax.fori_loop(0, T // size, last_rows, 0)
-    q_sums.finish(qkv_ref)
-    for copy in exchanges:
+    for copy in exchanges + out_copies:
         copy.wait_send()
     for step in range(C - 1):
         moves(step).wait_send()
 
 
-def input_terms(R, C, dq, dk, dv, w_qkv, a, tokens, dh, mu, r, grad):
+def input_terms(R, C, dq, dk, dv, w_qkv, a, tokens, dh, mu, r, grad_out, grad):
     T, width = dq.shape
     D = w_qkv.shape[1]
-    half = R // 2
+    half, low = R // 2, D // R
     depth, columns = grad.shape[1:]
     return pl.pallas_call(
         functools.partial(input_terms_kernel, R, C),
-        in_specs=[VMEM_SPEC] * 9 + [ANY],
-        out_specs=[VMEM_SPEC] * 3,
-        out_shape=[struct((T, width), BF), struct((D // R, 3 * width), F32), struct((depth, columns), F32)],
+        in_specs=[VMEM_SPEC] * 10 + [ANY],
+        out_specs=[VMEM_SPEC] * 6,
+        out_shape=[struct((T, width), BF)]
+        + [struct((low, width), F32)] * 3
+        + [struct((depth, columns), F32), struct((width, low), F32)],
         scratch_shapes=[
             pltpu.VMEM((C, T, width), BF),
             pltpu.VMEM((C - 1, T, width), BF),
             pltpu.VMEM((T, width), F32),
             pltpu.VMEM((8, T), F32),
             pltpu.VMEM((C - 1, 8, T), F32),
+            pltpu.VMEM((C - 1, low, width), BF),
             pltpu.VMEM((half, depth, columns), BF),
-            pltpu.VMEM((half, depth, columns), BF),
-            pltpu.VMEM((half - 1, depth, columns), BF),
-            pltpu.VMEM((half, 2, D // R, 3 * width), BF),
-            pltpu.VMEM((half, D // R, 3 * width), BF),
-            pltpu.VMEM((half - 1, D // R, 3 * width), BF),
+        ]
+        + row_sum_buffers(R, depth, columns)
+        + [pltpu.VMEM((half, 2, low, 3 * width), BF)]
+        + row_sum_buffers(R, low, 3 * width)
+        + [
+            DMA((C - 1,)),
+            DMA((C - 1,)),
             DMA((C - 1,)),
             DMA((C - 1,)),
             DMA((C - 1,)),
@@ -1056,32 +1200,13 @@
         compiler_params=comm_params(6, 63),
         cost_estimate=cost(8e10, 20 * MIB),
         name="input_terms",
-    )(dq, dk, dv, w_qkv, a, tokens, dh, mu, r, grad)
+    )(dq, dk, dv, w_qkv, a, tokens, dh, mu, r, grad_out, grad)
 
 
 def on_device(R, C, tokens, cotangent, segments, w_query, w_key, w_value, w_out, w_gate, w_up, w_down):
     T, width = tokens.shape
     D = width * C
-    me = lax.axis_index("col")
-
-    def shift(values, k):
-        return lax.ppermute(values, "col", [(i, (i + k) % C) for i in range(C)])
-
-    def block(values, k, axis):
-        size = values.shape[axis] // C
-        return lax.dynamic_slice_in_dim(values, lax.rem(me + k, C) * size, size, axis)
-
-    def scattered(values, axis):
-        return [block(values, 0, axis)] + [shift(block(values, k, axis), k) for k in range(1, C)]
-
-    def total_of(terms):
-        total = terms[0].astype(F32)
-        for term in terms[1:]:
-            total = total + term.astype(F32)
-        return total
-
     gathered = lambda w: lax.all_gather(w, "row", axis=0, tiled=True)
-    scatter = lambda g: lax.psum_scatter(g, "row", scatter_dimension=0, tiled=True)
 
     gate_w, up_w, down_w = gathered(w_gate), gathered(w_up), gathered(w_down.T)
     cos_table, sin_table = rope_tables(segments)
@@ -1097,27 +1222,16 @@
     total, grad_gate, grad_up, grad_down, out_terms = norm_terms(
         C, dg, du, hidden, gate_w, up_w, down_w, act_two, dys
     )
-    grad_down, grad_up = scatter(grad_down), scatter(grad_up)
     by_row = lambda values: values.reshape(R, D // R, -1)
-    grad_heads, grad_resid, grad_out = resid_back(R, total, h_full, dys, os, out_w)
-    dq, dk, dv, output, grad_out = attend_back(
-        R, q, k, v, grad_heads, log_total, seg_column, seg_row, cos_table, sin_table, out_terms, h_full, by_row(grad_out)
+    grad_heads, grad_resid, grad_out, grad_down = resid_back(R, total, h_full, dys, os, out_w, by_row(grad_down))
+    dq, dk, dv, output, grad_out, grad_up = attend_back(
+        R, q, k, v, grad_heads, log_total, seg_column, seg_row, cos_table, sin_table, out_terms, h_full,
+        by_row(grad_out), by_row(grad_up),
     )
-    grad_out = total_of(scattered(grad_out, 1)).T
-    grad_tokens, grad_qkv, grad_gate = input_terms(
-        R, C, dq, dk, dv, w_qkv, act_one, tokens, grad_resid, mu_one, r_one, by_row(grad_gate)
+    grad_tokens, grad_query, grad_key, grad_value, grad_gate, grad_out = input_terms(
+        R, C, dq, dk, dv, w_qkv, act_one, tokens, grad_resid, mu_one, r_one, grad_out, by_row(grad_gate)
     )
-    return (
-        output,
-        grad_tokens,
-        grad_qkv[:, :width],
-        grad_qkv[:, width : 2 * width],
-        grad_qkv[:, 2 * width :],
-        grad_out,
-        grad_gate,
-        grad_up.astype(F32),
-        grad_down.astype(F32).T,
-    )
+    return (output, grad_tokens, grad_query, grad_key, grad_value, grad_out, grad_gate, grad_up, grad_down)
 
 
 def solution(mesh):

time: 650 us -> 681 us (1.048)
  Pallas kernels: 600 us -> 638 us
    pallas_call x1, Pallas kernels: 109 us -> 139 us  [input_terms(): pl.pallas_call(functools.partial(input_terms_kernel, R, C), in_specs=[VME...]
    unnamed x14 -> x26, local copies, waits for them, and re-layouts: 8.36 us -> 14.1 us
  transfers between devices with their start and end apart: 8 -> 3, of which waited for: 0 -> 0; matrix products, arithmetic and copies ran while one was open for 3% -> 1% of each run, Pallas kernels for 78% -> 39%
where the time goes in v4:
time: 681 us; the launch traced here: 673 us
  Pallas kernels  638 us (94%)
  local copies, waits for them, and re-layouts  15.1 us (2%)
  between operations  14.4 us (2%)
    pallas_call x1, Pallas kernels, input_terms(): pl.pallas_call(functools.partial(input_terms_kernel, R, C), in_specs=[VME...  139 us
    pallas_call x1, Pallas kernels, first_gather(): pl.pallas_call(functools.partial(gather_kernel, R, C), in_specs=[ANY] * 5...  88.6 us
    pallas_call x1, Pallas kernels, attend_back(): pl.pallas_call(functools.partial(attend_back_kernel, R, C), in_specs=[VME...  86.3 us
    pallas_call x1, Pallas kernels, norm_terms(): pl.pallas_call(functools.partial(norm_terms_kernel, C), in_specs=[ANY] *...  84.2 us
    pallas_call x1, Pallas kernels, feed_forward(): pl.pallas_call(functools.partial(feed_kernel, C, tiles), grid=(tiles + F...  80.5 us
    pallas_call x1, Pallas kernels, attend(): pl.pallas_call(functools.partial(attend_kernel, R, C), in_specs=[VMEM_SPE...  77.7 us
    pallas_call x1, Pallas kernels, resid_back(): pl.pallas_call(functools.partial(resid_back_kernel, R, C), in_specs=[VMEM...  52.5 us
    pallas_call x1, Pallas kernels, hidden_back(): pl.pallas_call(hidden_back_kernel, grid=(F // bf,), in_specs=[pl.BlockSpe...  16.6 us
  transfers between devices with their start and end apart: 3, of which 0 were waited for; matrix products, arithmetic and copies ran while one was open for 1% of the time, Pallas kernels for 39%

profile of v4, /device:TPU:8, one launch (start us, length us, event | category | flops | bytes accessed | tf_op | source)
XLA Modules:
  0.0 672.7 jit_solution(16593870849110550423)
XLA Ops:
  7.2 0.0 all-gather.4.cloned.1.call-start
  7.2 0.7 all-gather.4.cloned.1.call-update
  7.9 0.0 all-gather.6.cloned.1.call-start
  8.0 0.7 all-gather.6.cloned.1.call-update
  8.7 0.0 all-gather.8.cloned.1.call-start
  8.7 2.3 copy.24
  11.0 0.0 all-gather.8.cloned.1.call-update
  11.0 0.0 copy-start.7
  11.0 88.6 %first_gather.1 = (bf16[4,1024,512]{2,1,0:T(8,128)(2,1)}, bf16[4,512,256]{2,1,0:T(8,128)(2,1)}, bf16[3,8,256,512]{3,2,1,0:T(8,128)(2,1)}) custom-call(bf16[1024,512]{1,0:T(8,128)(2,1)} %x_ref.3, bf16[512,256]{1,0:T(8,128)(2,1)} %wo_ref.1, bf16[256,512]{1,0:T(8,128)(2,1)} %wq_ref.1, bf16[256,512]{1,0:T(8,128)(2,1)} %wk_ref.1, bf16[256,512]{1,0:T(8,128)(2,1)} %wv_ref.1), custom_call_target="tpu_custom_call" | custom-call | flops 60000002048 | bytes 14680064 | tf_op jit(solution)/shard_map/first_gather/pallas_call | solution.py:161
  99.7 0.0 copy-done.7
  99.7 1.0 copy.23.segk_ref
  100.7 0.5 convert_reduce_fusion
  101.2 1.9 fusion.1
  103.2 1.3 pad_maximum_fusion
  104.5 12.4 %norm_and_project.1 = (bf16[1024,2048]{1,0:T(8,128)(2,1)}, bf16[1024,512]{1,0:T(8,128)(2,1)}, bf16[1024,512]{1,0:T(8,128)(2,1)}, bf16[1024,512]{1,0:T(8,128)(2,1...) custom-call(bf16[4,1024,512]{2,1,0:T(8,128)(2,1)} %get-tuple-element.50.xs_ref, bf16[3,2048,512]{2,1,0:T(8,128)(2,1)} %bitcast.17, ...), custom_call_target="tpu_custom_call" | custom-call | flops 6442450944 | bytes 14680064 | tf_op jit(solution)/shard_map/norm_and_project/pallas_call | solution.py:221
  116.8 77.7 %attend.1 = (bf16[4,4,1024,128]{3,2,1,0:T(8,128)(2,1)}, f32[4,1,1024]{2,1,0:T(1,128)}, bf16[8,2048,256]{2,1,0:T(8,128)(2,1)}) custom-call(bf16[1024,512]{1,0:T(8,128)(2,1)} %get-tuple-element.52.q_ref, bf16[1024,512]{1,0:T(8,128)(2,1)} %get-tuple-element.53.k_ref, bf16[1024,512]{1,0:T(8,128)(2,1)} %get-tuple-element.54.v_ref, s32[1024,1]{1,0:T(8,128)} %copy.23.segk_ref, ...), custom_call_target="tpu_custom_call" | custom-call | flops 70000001024 | bytes 14680064 | tf_op jit(solution)/shard_map/attend/pallas_call | solution.py:321
  194.6 0.0 all-gather.4.cloned.1.call-done.wg_ref.wg_hbm
  194.6 0.0 all-gather.6.cloned.1.call-done.wu_ref.wu_hbm
  194.6 80.5 %feed_forward.1 = (f32[1024,2048]{1,0:T(8,128)}, bf16[1024,2048]{1,0:T(8,128)(2,1)}, bf16[1024,2048]{1,0:T(8,128)(2,1)}, bf16[1024,2048]{1,0:T(8,128)(2,1)}, bf1...) custom-call(bf16[4,4,1024,128]{3,2,1,0:T(8,128)(2,1)} %get-tuple-element.56.os_ref.os_hbm, ...), custom_call_target="tpu_custom_call" | custom-call | flops 70000001024 | bytes 62914560 | tf_op jit(solution)/shard_map/feed_forward/pallas_call | solution.py:422
  275.1 0.0 all-gather.8.cloned.1.call-done.wd_ref.wd_hbm
  275.1 16.6 %hidden_back.1 = (bf16[1024,2048]{1,0:T(8,128)(2,1)}, bf16[1024,2048]{1,0:T(8,128)(2,1)}) custom-call(bf16[4,1024,512]{2,1,0:T(8,128)(2,1)} %get-tuple-element.58.dys_ref.dys_hbm, bf16[2048,2048]{1,0:T(8,128)(2,1)} %all-gather.8.cloned.1.call-done.wd_ref.wd_hbm, bf16[1024,2048]{1,0:T(8,128)(2,1)} %get-tuple-element.59.slope_ref, ...), custom_call_target="tpu_custom_call" | custom-call | flops 8589934592 | bytes 29360128 | tf_op jit(solution)/shard_map/hidden_back/pallas_call | solution.py:466
  291.7 84.2 %norm_terms.1 = (f32[256,2048]{1,0:T(8,128)}, bf16[2048,2048]{1,0:T(8,128)(2,1)}, bf16[2048,2048]{1,0:T(8,128)(2,1)}, bf16[2048,2048]{1,0:T(8,128)(2,1)}, bf16[4,1024,512]{2,1,0:T(8,128)(2,1)}) custom-call(bf16[1024,2048]{1,0:T(8,128)(2,1)} %get-tuple-element.61.dg_hbm, bf16[1024,2048]{1,0:T(8,128)(2,1)} %get-tuple-element.62.du_hbm, ...), custom_call_target="tpu_custom_call" | custom-call | flops 89999998976 | bytes 73400320 | tf_op jit(solution)/shard_map/norm_terms/pallas_call | solution.py:761
  376.0 52.5 %resid_back.1 = (bf16[1024,512]{1,0:T(8,128)(2,1)}, bf16[1024,512]{1,0:T(8,128)(2,1)}, bf16[2048,2048]{1,0:T(8,128)(2,1)}, f32[2048,256]{1,0:T(8,128)}) custom-call(f32[256,2048]{1,0:T(8,128)} %get-tuple-element.65.sum_ref, f32[1024,2048]{1,0:T(8,128)} %get-tuple-element.66.h_hbm, bf16[4,1024,512]{2,1,0:T(8,128)(2,1)} %get-tuple-element.58.dys_ref.dys_hbm, ...), custom_call_target="tpu_custom_call" | custom-call | flops 40000000000 | bytes 20971520 | tf_op jit(solution)/shard_map/resid_back/pallas_call | solution.py:881
  428.4 86.3 %attend_back.1 = (bf16[1024,512]{1,0:T(8,128)(2,1)}, bf16[1024,512]{1,0:T(8,128)(2,1)}, bf16[1024,512]{1,0:T(8,128)(2,1)}, bf16[1024,512]{1,0:T(8,128)(2,1)}, bf...) custom-call(bf16[1024,512]{1,0:T(8,128)(2,1)} %get-tuple-element.52.q_ref, bf16[1024,512]{1,0:T(8,128)(2,1)} %get-tuple-element.53.k_ref, ...), custom_call_target="tpu_custom_call" | custom-call | flops 70000001024 | bytes 14680064 | tf_op jit(solution)/shard_map/attend_back/pallas_call | solution.py:1005
  514.7 139.1 %input_terms.1 = (bf16[1024,512]{1,0:T(8,128)(2,1)}, f32[256,512]{1,0:T(8,128)}, f32[256,512]{1,0:T(8,128)}, f32[256,512]{1,0:T(8,128)}, f32[256,2048]{1,0:T(8,128)}, /*index=5*/f32[512,256]{1,0:T(8,128)}) custom-call(bf16[1024,512]{1,0:T(8,128)(2,1)} %get-tuple-element.74.dq_ref, bf16[1024,512]{1,0:T(8,128)(2,1)} %get-tuple-element.75.dk_ref, ...), custom_call_target="tpu_custom_call" | custom-call | flops 80000000000 | bytes 20971520 | tf_op jit(solution)/shard_map/input_terms/pallas_call | solution.py:1170
  653.8 0.0 copy-start.6
  653.8 0.0 copy-start.5
  653.8 0.0 copy-start.4
  653.8 0.0 copy-start.3
  653.9 0.0 copy-start.2
  653.9 2.4 copy.35
  656.3 2.3 copy.36
  658.5 0.0 copy-done.6
  658.5 0.0 copy-start.1
  658.5 0.8 copy.37
  659.3 0.0 copy-done.5
  659.3 0.8 copy.38
  660.1 0.0 copy-done.4
  660.1 0.8 copy.39
  660.9 0.0 copy-done.3
  660.9 0.8 copy.40
  661.7 0.0 copy-done.2
  661.7 0.0 copy-start
  661.7 1.3 copy.41
  663.0 0.0 copy-done.1
  663.0 1.3 copy.42
  664.4 0.0 copy-done
  664.4 1.3 copy.43
  (2 shorter events, 0.0 us)
Async XLA Ops:
  7.2 187.4 %all-gather.4.cloned.1.call-start = ((), (), s32[]{:S(2)}) async-start(), calls=%async_computation | async-start | bytes 9437184 | tf_op jit(solution)/shard_map/all_gather | solution.py:1209
  7.9 186.7 %all-gather.6.cloned.1.call-start = ((), (), s32[]{:S(2)}) async-start(), calls=%async_computation.1 | async-start | bytes 9437184 | tf_op jit(solution)/shard_map/all_gather | solution.py:1209
  8.7 266.5 %all-gather.8.cloned.1.call-start = ((), (), s32[]{:S(2)}) async-start(), calls=%async_computation.2 | async-start | bytes 9437184 | tf_op jit(solution)/shard_map/all_gather | solution.py:1209
  11.0 88.7 %copy-start.7 = (s32[1024]{0:T(1024)S(1)}, s32[1024]{0:T(1024)}, u32[]{:S(2)}) copy-start(s32[1024]{0:T(1024)} %param.12) | copy-start | bytes 12292
  653.8 4.7 copy-start.6
  653.8 5.5 copy-start.5
  653.8 6.3 copy-start.4
  653.8 7.1 %copy-start.3 = (f32[512,256]{1,0:T(8,128)S(1)}, f32[512,256]{1,0:T(8,128)}, u32[]{:S(2)}) copy-start(f32[512,256]{1,0:T(8,128)} %get-tuple-element.110) | copy-start | bytes 1572868
  653.9 7.9 %copy-start.2 = (f32[256,2048]{1,0:T(8,128)S(1)}, f32[256,2048]{1,0:T(8,128)}, u32[]{:S(2)}) copy-start(f32[256,2048]{1,0:T(8,128)} %get-tuple-element.111) | copy-start | bytes 6291460
  658.5 4.5 copy-start.1
  661.7 2.6 copy-start
Sparse Core Ops, SparseCore 0:
  9.9 77.2 all-gather.3
  89.1 96.4 all-gather.5
  188.1 52.4 all-gather.7

commit v5 on v4

--- a/solution.py
+++ b/solution.py
@@ -43,21 +43,6 @@
     return pl.CostEstimate(flops=int(flops), bytes_accessed=int(moved), transcendentals=0)
 
 
-def count_seen(segment_ids):
-    places = jnp.arange(segment_ids.shape[0], dtype=jnp.int32)
-    causal = places[None, :] <= places[:, None]
-    allowed = (segment_ids[:, None] == segment_ids[None, :]) & causal
-    return jnp.sum(allowed.astype(jnp.int32), axis=1) - 1
-
-
-def rope_tables(segments):
-    positions = jax.vmap(count_seen)(segments.reshape(-1, SEQ)).reshape(-1)
-    inverse = 10000.0 ** (-(jnp.arange(HALF, dtype=F32) * 2.0 / HEAD_DIM))
-    angles = positions.astype(F32)[:, None] * inverse[None, :]
-    cosine, sine = jnp.cos(angles), jnp.sin(angles)
-    return jnp.concatenate([cosine, cosine], 1), jnp.concatenate([-sine, sine], 1)
-
-
 def turn(values, cos_table, sin_table):
     return values * cos_table + pltpu.roll(values, HALF, 1) * sin_table
 
@@ -97,17 +82,26 @@
     return row, ahead, behind, other
 
 
+def gather_ring(C, source, whole, send, recv):
+    me, right, left = ring_places(C)
+    copies = []
+    for step in range(C - 1):
+        owner = lax.rem(me - step + C, C)
+        piece = source if step == 0 else whole.at[owner]
+        copies.append(remote(piece, whole.at[owner], send.at[step], recv.at[step], col=right))
+    return copies
+
+
 def gather_kernel(
-    R, C, x_ref, wo_ref, wq_ref, wk_ref, wv_ref, xs_ref, wos_ref, w_ref,
-    local, x_send, x_recv, o_send, o_recv, w_send, w_recv, f_send, f_recv,
+    R, C, segk_ref, segq_ref, rate_ref, x_ref, wq_ref, wk_ref, wv_ref, xs_ref, w_ref, cos_ref, sin_ref,
+    local, x_send, x_recv, w_send, w_recv, f_send, f_recv,
 ):
     me, right, left = ring_places(C)
     row, ahead, behind, other = row_places(R)
     weights = (wq_ref, wk_ref, wv_ref)
     mine = [
         pltpu.make_async_copy(x_ref, xs_ref.at[me], local.at[0]),
-        pltpu.make_async_copy(wo_ref, wos_ref.at[me], local.at[1]),
-    ] + [pltpu.make_async_copy(w, w_ref.at[i, row], local.at[2 + i]) for i, w in enumerate(weights)]
+    ] + [pltpu.make_async_copy(w, w_ref.at[i, row], local.at[1 + i]) for i, w in enumerate(weights)]
     for copy in mine:
         copy.start()
     greet(
@@ -115,15 +109,8 @@
         1 + R // 2,
     )
 
-    def ring(source, whole, send, recv, step):
-        owner = lax.rem(me - step + C, C)
-        piece = source if step == 0 else whole.at[owner]
-        return remote(piece, whole.at[owner], send.at[step], recv.at[step], col=right)
-
-    x_copies = [ring(x_ref, xs_ref, x_send, x_recv, s) for s in range(C - 1)]
-    o_copies = [ring(wo_ref, wos_ref, o_send, o_recv, s) for s in range(C - 1)]
+    x_copies = gather_ring(C, x_ref, xs_ref, x_send, x_recv)
     x_copies[0].start()
-    o_copies[0].start()
     spread, forward = [], []
     for i, w in enumerate(weights):
         for k in range(1, R // 2):
@@ -133,11 +120,28 @@
         copy = remote(w, w_ref.at[i, row], f_send.at[i, 0], f_recv.at[i, 0], row=other)
         copy.start()
         forward.append(copy)
+    T = cos_ref.shape[0]
+    size = 128
+
+    def table_rows(i, carry):
+        rows = pl.ds(pl.multiple_of(i * size, size), size)
+        first = SEQ * lax.div(i * size, SEQ)
+        shape = (size, T)
+        queries = lax.broadcasted_iota(jnp.int32, shape, 0) + i * size
+        keys = lax.broadcasted_iota(jnp.int32, shape, 1)
+        seen = (segk_ref[rows, :] == segq_ref[...]) & (keys <= queries) & (keys >= first)
+        place = jnp.sum(jnp.where(seen, 1.0, 0.0), axis=1, keepdims=True) - 1.0
+        angles = place * rate_ref[...]
+        lane = lax.broadcasted_iota(jnp.int32, angles.shape, 1)
+        sine = jnp.sin(angles)
+        cos_ref[rows, :] = jnp.cos(angles)
+        sin_ref[rows, :] = jnp.where(lane < HALF, -sine, sine)
+        return carry
+
+    lax.fori_loop(0, T // size, table_rows, 0)
     for s in range(1, C - 1):
         x_copies[s - 1].wait_recv()
         x_copies[s].start()
-        o_copies[s - 1].wait_recv()
-        o_copies[s].start()
     for i in range(3):
         for k in range(1, R // 2):
             spread[i * (R // 2 - 1) + k - 1].wait_recv()
@@ -146,31 +150,32 @@
             copy.start()
             forward.append(copy)
     x_copies[-1].wait_recv()
-    o_copies[-1].wait_recv()
     for copy in forward:
         copy.wait_recv()
-    for copy in x_copies + o_copies + spread + forward:
+    for copy in x_copies + spread + forward:
         copy.wait_send()
     for copy in mine:
         copy.wait()
 
 
-def first_gather(R, C, tokens, w_out, w_query, w_key, w_value):
+def first_gather(R, C, seg_column, seg_row, tokens, w_query, w_key, w_value):
     depth, width = w_query.shape
+    T = tokens.shape[0]
     half = R // 2
+    rate = 10000.0 ** (-(jnp.arange(HALF, dtype=F32) * 2.0 / HEAD_DIM))
+    rate = jnp.concatenate([rate, rate]).reshape(1, HEAD_DIM)
     return pl.pallas_call(
         functools.partial(gather_kernel, R, C),
-        in_specs=[ANY] * 5,
-        out_specs=[ANY] * 3,
+        in_specs=[VMEM_SPEC] * 3 + [ANY] * 4,
+        out_specs=[ANY] * 2 + [VMEM_SPEC] * 2,
         out_shape=[
             struct((C,) + tokens.shape, BF),
-            struct((C,) + w_out.shape, BF),
             struct((3, R, depth, width), BF),
+            struct((T, HEAD_DIM), F32),
+            struct((T, HEAD_DIM), F32),
         ],
         scratch_shapes=[
-            DMA((5,)),
-            DMA((C - 1,)),
-            DMA((C - 1,)),
+            DMA((4,)),
             DMA((C - 1,)),
             DMA((C - 1,)),
             DMA((3, half)),
@@ -181,7 +186,7 @@
         compiler_params=comm_params(0),
         cost_estimate=cost(6e10, 14 * MIB),
         name="first_gather",
-    )(tokens, w_out, w_query, w_key, w_value)
+    )(seg_column, seg_row, rate, tokens, w_query, w_key, w_value)
 
 
 def norm_rows(x):
@@ -195,7 +200,27 @@
     return jnp.concatenate([ref[j] for j in range(ref.shape[0])], axis=1)
 
 
-def qkv_kernel(xs_ref, w_ref, cos_ref, sin_ref, a_ref, q_ref, k_ref, v_ref, mu_ref, r_ref):
+def qkv_kernel(
+    C, xs_ref, w_ref, cos_ref, sin_ref, wo_ref, a_ref, q_ref, k_ref, v_ref, mu_ref, r_ref, wos_ref, local, send, recv
+):
+    step, steps = pl.program_id(0), pl.num_programs(0)
+    me, right, left = ring_places(C)
+    copies = gather_ring(C, wo_ref, wos_ref, send, recv)
+    mine = pltpu.make_async_copy(wo_ref, wos_ref.at[me], local.at[0])
+
+    @pl.when(step == 0)
+    def _():
+        mine.start()
+        greet([{"col": left}], 1)
+        copies[0].start()
+
+    for s in range(1, C - 1):
+
+        @pl.when(step == jnp.minimum(2 * s, steps - 1))
+        def _():
+            copies[s - 1].wait_recv()
+            copies[s].start()
+
     x = beside(xs_ref).astype(F32)
     centre, inverse = norm_rows(x)
     a = ((x - centre) * inverse).astype(BF)
@@ -212,22 +237,30 @@
             part = product[:, start : start + HEAD_DIM]
             out[:, start : start + HEAD_DIM] = turn(part, cosine, sine).astype(BF)
 
-
-def norm_and_project(xs, w_qkv, cos_table, sin_table):
+    @pl.when(step == steps - 1)
+    def _():
+        copies[-1].wait_recv()
+        for copy in copies:
+            copy.wait_send()
+        mine.wait()
+
+
+def norm_and_project(xs, w_qkv, cos_table, sin_table, w_out):
     C, T, width = xs.shape
     D = width * C
     bt = 256
     rows = lambda n: pl.BlockSpec((bt, n), lambda i: (i, 0))
     return pl.pallas_call(
-        qkv_kernel,
+        functools.partial(qkv_kernel, C),
         grid=(T // bt,),
         in_specs=[
             pl.BlockSpec((C, bt, width), lambda i: (0, i, 0)),
             pl.BlockSpec(w_qkv.shape, lambda i: (0, 0, 0), pipeline_mode=pl.Buffered(1)),
             rows(HEAD_DIM),
             rows(HEAD_DIM),
+            ANY,
         ],
-        out_specs=[rows(D), rows(width), rows(width), rows(width), rows(1), rows(1)],
+        out_specs=[rows(D), rows(width), rows(width), rows(width), rows(1), rows(1), ANY],
         out_shape=[
             struct((T, D), BF),
             struct((T, width), BF),
@@ -235,11 +268,13 @@
             struct((T, width), BF),
             struct((T, 1), F32),
             struct((T, 1), F32),
+            struct((C,) + w_out.shape, BF),
         ],
-        compiler_params=params(),
-        cost_estimate=cost(2 * T * D * 3 * width, 14 * MIB),
+        scratch_shapes=[DMA((1,)), DMA((C - 1,)), DMA((C - 1,))],
+        compiler_params=comm_params(7),
+        cost_estimate=cost(2e10, 14 * MIB),
         name="norm_and_project",
-    )(xs, w_qkv, cos_table, sin_table)
+    )(xs, w_qkv, cos_table, sin_table, w_out)
 
 
 def allowed_block(seg_key, seg_query, first_query):
@@ -793,9 +828,9 @@
 
 
 def resid_back_kernel(
-    R, C, sum_ref, h_hbm, dys_hbm, os_hbm, w_hbm, down_hbm, do_hbm, dhs_hbm, grad_hbm, down_ref,
-    h, dy, heads, w, dh, out, stage, own, exchanged, arrived,
-    load, w_load, local, store, h_send, h_recv, o_send, o_recv, own_load, *semaphores,
+    R, C, sum_ref, h_hbm, dys_hbm, w_hbm, down_hbm, do_hbm, dhs_hbm, down_ref,
+    h, dy, w, dh, out, own, exchanged, arrived,
+    load, w_load, local, h_send, h_recv, o_send, o_recv, own_load, *semaphores,
 ):
     me, right, left = ring_places(C)
     blocks, D, part = w.shape
@@ -806,7 +841,6 @@
         pltpu.make_async_copy(h_hbm.at[mine, :], h, load.at[0]),
         pltpu.make_async_copy(dys_hbm.at[:, mine, :], dy, load.at[1]),
     ]
-    heads_in = pltpu.make_async_copy(os_hbm.at[:, :, mine, :], heads, load.at[2])
     for copy in first_in:
         copy.start()
     order = [lax.rem(me + k, C) for k in range(1, C)] + [me]
@@ -819,7 +853,6 @@
     sums, own_loads = held_row_sum(R, down_hbm, own, exchanged, arrived, own_load, semaphores)
     for copy in own_loads:
         copy.start()
-    heads_in.start()
     greet([{"col": lax.rem(me + k, C)} for k in range(1, C)] + sums.peers, C - 1 + len(sums.peers))
     for slot in sums.order():
         sums.exchange(slot).start()
@@ -854,55 +887,41 @@
         copy.start()
         copies.append(copy)
     sums.relay(lambda slot: own_loads[slot].wait())
-    heads_in.wait()
-    right_side = jnp.concatenate([heads[j, i] for j in range(C) for i in range(heads.shape[1])], axis=1)
-    stores = []
-    for t in range(C):
-        if t >= 2:
-            stores[t - 2].wait()
-        stage[t % 2] = dot_tn(dh[:, t * width : (t + 1) * width], right_side).astype(BF)
-        copy = pltpu.make_async_copy(stage.at[t % 2], grad_hbm.at[pl.ds(t * width, width), :], store.at[t % 2])
-        copy.start()
-        stores.append(copy)
     sums.relay_again()
 
     def write(part, values):
         down_ref[:, part] = values.T
 
     sums.finish(write, 128)
-    for copy in copies + stores[-2:]:
+    for copy in copies:
         copy.wait()
 
 
-def resid_back(R, total, h, dys, os, w_out, grad_down):
+def resid_back(R, total, h, dys, w_out, grad_down):
     C, T, width = dys.shape
     rows, D = total.shape
     depth, columns = grad_down.shape[1:]
     return pl.pallas_call(
         functools.partial(resid_back_kernel, R, C),
-        in_specs=[VMEM_SPEC] + [ANY] * 5,
-        out_specs=[ANY, ANY, ANY, VMEM_SPEC],
+        in_specs=[VMEM_SPEC] + [ANY] * 4,
+        out_specs=[ANY, ANY, VMEM_SPEC],
         out_shape=[
             struct((T, width), BF),
             struct((T, width), BF),
-            struct((D, D), BF),
             struct((columns, depth), F32),
         ],
         scratch_shapes=[
             pltpu.VMEM((rows, D), F32),
             pltpu.VMEM((C, rows, width), BF),
-            pltpu.VMEM((C, os.shape[1], rows, HEAD_DIM), BF),
             pltpu.VMEM(w_out.shape, BF),
             pltpu.VMEM((rows, D), BF),
             pltpu.VMEM((C, rows, width), BF),
-            pltpu.VMEM((2, width, D), BF),
             pltpu.VMEM((R // 2, depth, columns), BF),
         ]
         + row_sum_buffers(R, depth, columns)
         + [
-            DMA((3,)),
+            DMA((2,)),
             DMA((C,)),
-            DMA((2,)),
             DMA((2,)),
             DMA((C - 1,)),
             DMA((C - 1,)),
@@ -914,37 +933,68 @@
         compiler_params=comm_params(4),
         cost_estimate=cost(4e10, 20 * MIB),
         name="resid_back",
-    )(total, h, dys, os, w_out, grad_down)
+    )(total, h, dys, w_out, grad_down)
 
 
 def attend_back_kernel(
-    R, C, q_ref, k_ref, v_ref, do_ref, log_ref, segk_ref, segq_ref, cos_ref, sin_ref, terms, h_hbm, out_hbm, up_hbm,
-    dq_ref, dk_ref, dv_ref, y_ref, out_ref, up_ref, dk_sum, dv_sum, held, h,
-    out_own, out_exchanged, out_arrived, up_own, up_exchanged, up_arrived,
-    send, recv, h_load, out_load, up_load, *semaphores,
+    R, C, log_ref, segk_ref, segq_ref, cos_ref, sin_ref,
+    q_hbm, k_hbm, v_hbm, do_hbm, terms_hbm, h_hbm, up_hbm, dh_hbm, os_hbm,
+    dq_ref, dk_ref, dv_ref, y_ref, up_ref, out_ref,
+    q_ref, k_ref, v_ref, do_ref, terms, dk_sum, dv_sum, held, h, dh, os, mine, theirs,
+    up_own, up_exchanged, up_arrived, tiles, o_exchanged, o_arrived,
+    send, recv, term_load, head_load, out_load, h_load, up_load, own_send, own_recv, *semaphores,
 ):
     me, right, left = ring_places(C)
     T, width = q_ref.shape
     heads, bq = width // HEAD_DIM, 256
+    row = lax.axis_index("row")
+    side, partner_row, partner_col = lax.rem(row, 2), 2 * me + lax.rem(row, 2), lax.div(row, 2)
+    apart = partner_col != me
+
+    def term_in(s):
+        return pltpu.make_async_copy(terms_hbm.at[chunk(s)], terms.at[s], term_load.at[s])
+
+    def chunk(s):
+        return lax.rem(me + 2 * C - 1 - s, C)
+
     cut = pl.ds(pl.multiple_of(me * width, width), width)
+    head_loads = [
+        pltpu.make_async_copy(source, target, head_load.at[i])
+        for i, (source, target) in enumerate(((q_hbm, q_ref), (k_hbm, k_ref), (v_hbm, v_ref), (do_hbm, do_ref)))
+    ]
+    out_loads = [
+        pltpu.make_async_copy(dh_hbm, dh, out_load.at[0]),
+        pltpu.make_async_copy(os_hbm, os, out_load.at[1]),
+    ]
     h_in = pltpu.make_async_copy(h_hbm.at[:, cut], h, h_load.at[0])
     up_sums, up_loads = held_row_sum(R, up_hbm, up_own, up_exchanged, up_arrived, up_load, semaphores[:4])
-    out_sums, out_loads = held_row_sum(R, out_hbm, out_own, out_exchanged, out_arrived, out_load, semaphores[4:])
-    for copy in up_loads + out_loads:
-        copy.start()
+    out_sums = RowSum(
+        R, lambda i: tiles.at[i, side], lambda i: tiles.at[i, 1 - side], o_exchanged, o_arrived, semaphores[4:]
+    )
+    term_in(0).start()
+    for copy in head_loads + up_loads + out_loads:
+        copy.start()
+    for s in range(1, C):
+        term_in(s).start()
     h_in.start()
-    greet([{"col": left}] + up_sums.peers, 1 + len(up_sums.peers))
-    for sums in (up_sums, out_sums):
-        for slot in sums.order():
-            sums.exchange(slot).start()
-
-    def chunk(s):
-        return lax.rem(me + 2 * C - 1 - s, C)
+    @pl.when(apart)
+    def _():
+        greet([{"col": left}, {"row": partner_row, "col": partner_col}] + up_sums.peers, 2 + len(up_sums.peers))
+
+    @pl.when(jnp.logical_not(apart))
+    def _():
+        greet([{"col": left}] + up_sums.peers, 1 + len(up_sums.peers))
+
+    for slot in up_sums.order():
+        up_sums.exchange(slot).start()
+    term_in(0).wait()
 
     def moves(step):
-        return ring_step(step, C, right, terms.at[chunk(0)], held, send, recv)
+        return ring_step(step, C, right, terms.at[0], held, send, recv)
 
     moves(0).start()
+    for copy in head_loads:
+        copy.wait()
 
     def one_head(head, carry):
         columns = pl.ds(pl.multiple_of(head * HEAD_DIM, HEAD_DIM), HEAD_DIM)
@@ -971,78 +1021,138 @@
         dv_ref[:, columns] = dv_sum[...].astype(BF)
         return carry
 
-    lax.fori_loop(0, heads // 2, one_head, 0)
+    lax.fori_loop(0, 1, one_head, 0)
     up_sums.relay(lambda slot: up_loads[slot].wait())
-    lax.fori_loop(heads // 2, heads, one_head, 0)
-    out_sums.relay(lambda slot: out_loads[slot].wait())
+    for copy in out_loads:
+        copy.wait()
+    depth = tiles.shape[2]
+    for slot in out_sums.order():
+        chip = lax.div(out_sums.places(slot), 2)
+        right_side = jnp.concatenate([os[chip, i] for i in range(heads)], axis=1)
+        product = dot_tn(dh[...], right_side).astype(BF)
+        tiles[slot, 0] = product[:depth]
+        tiles[slot, 1] = product[depth:]
+        out_sums.exchange(slot).start()
+    lax.fori_loop(1, heads, one_head, 0)
+    out_sums.relay()
+    for s in range(1, C):
+        term_in(s).wait()
     for step in range(1, C - 1):
         moves(step - 1).wait_recv()
-        add_into(held.at[step - 1], terms.at[chunk(step)])
+        add_into(held.at[step - 1], terms.at[step])
         moves(step).start()
         if step == 1:
+            out_sums.relay_again()
             up_sums.relay_again()
-    out_sums.relay_again()
 
     def write_up(part, values):
         up_ref[part, :] = values
 
     def write_out(part, values):
-        out_ref[part, :] = values.astype(BF)
+        mine[part, :] = values.astype(BF)
+
+    out_sums.finish(write_out)
+    handed = remote(mine, theirs, own_send.at[0], own_recv.at[0], row=partner_row, col=partner_col)
+
+    @pl.when(apart)
+    def _():
+        handed.start()
 
     up_sums.finish(write_up)
-    out_sums.finish(write_out)
     h_in.wait()
     moves(C - 2).wait_recv()
-    y_ref[...] = (h[...] + held[C - 2].astype(F32) + terms[me].astype(F32)).astype(BF)
+    y_ref[...] = (h[...] + held[C - 2].astype(F32) + terms[C - 1].astype(F32)).astype(BF)
+
+    @pl.when(apart)
+    def _():
+        handed.wait()
+        out_ref[...] = theirs[...].astype(F32).T
+
+    @pl.when(jnp.logical_not(apart))
+    def _():
+        out_ref[...] = mine[...].astype(F32).T
+
     for step in range(C - 1):
         moves(step).wait_send()
 
 
-def attend_back(R, q, k, v, do, log_total, seg_column, seg_row, cos_table, sin_table, out_terms, h, grad_out, grad_up):
+def attend_back(R, q, k, v, do, log_total, seg_column, seg_row, cos_table, sin_table, out_terms, h, grad_up, dh, os):
     C = out_terms.shape[0]
     T, width = q.shape
-    shapes = (grad_out.shape[1:], grad_up.shape[1:])
+    assert R == 2 * C
+    depth, columns = grad_up.shape[1:]
+    one = pltpu.VMEM((T, width), BF)
     return pl.pallas_call(
         functools.partial(attend_back_kernel, R, C),
-        in_specs=[VMEM_SPEC] * 10 + [ANY] * 3,
+        in_specs=[VMEM_SPEC] * 5 + [ANY] * 9,
         out_specs=[VMEM_SPEC] * 6,
-        out_shape=[struct((T, width), BF)] * 4 + [struct(shapes[0], BF), struct(shapes[1], F32)],
+        out_shape=[struct((T, width), BF)] * 4 + [struct((depth, columns), F32), struct((width, depth), F32)],
         scratch_shapes=[
+            one,
+            one,
+            one,
+            one,
+            pltpu.VMEM((C, T, width), BF),
             pltpu.VMEM((T, HEAD_DIM), F32),
             pltpu.VMEM((T, HEAD_DIM), F32),
             pltpu.VMEM((C - 1, T, width), BF),
             pltpu.VMEM((T, width), F32),
+            one,
+            pltpu.VMEM(os.shape, BF),
+            pltpu.VMEM((depth, width), BF),
+            pltpu.VMEM((depth, width), BF),
+            pltpu.VMEM((R // 2, depth, columns), BF),
         ]
-        + [
-            buffer
-            for shape in shapes
-            for buffer in [pltpu.VMEM((R // 2,) + shape, BF)] + row_sum_buffers(R, *shape)
-        ]
+        + row_sum_buffers(R, depth, columns)
+        + [pltpu.VMEM((R // 2, 2, depth, width), BF)]
+        + row_sum_buffers(R, depth, width)
         + [
             DMA((C - 1,)),
             DMA((C - 1,)),
+            DMA((C,)),
+            DMA((4,)),
+            DMA((2,)),
             DMA((1,)),
             DMA((R // 2,)),
-            DMA((R // 2,)),
+            DMA((1,)),
+            DMA((1,)),
         ]
         + row_sum_semaphores(R)
         + row_sum_semaphores(R),
         compiler_params=comm_params(5),
         cost_estimate=cost(7e10, 14 * MIB),
         name="attend_back",
-    )(q, k, v, do, log_total, seg_column, seg_row, cos_table, sin_table, out_terms, h, grad_out, grad_up)
+    )(log_total, seg_column, seg_row, cos_table, sin_table, q, k, v, do, out_terms, h, grad_up, dh, os)
 
 
 def input_terms_kernel(
-    R, C, dq_ref, dk_ref, dv_ref, w_ref, a_ref, x_ref, dh_ref, mu_ref, r_ref, out_ref, grad_hbm,
-    y_ref, gq_ref, gk_ref, gv_ref, total_ref, gout_ref,
-    terms, held, da, stats, stats_in, out_in, own, exchanged, arrived, tiles, q_exchanged, q_arrived,
-    send, recv, s_send, s_recv, o_send, o_recv, load, *semaphores,
+    R, C, dq_ref, dk_ref, dv_ref, mu_hbm, r_hbm, w_hbm, a_hbm, x_hbm, dh_hbm, grad_hbm,
+    y_ref, gq_ref, gk_ref, gv_ref, total_ref,
+    mu_ref, r_ref, w_ref, a_ref, x_ref, dh_ref,
+    terms, held, da, stats, stats_in, own, exchanged, arrived, tiles, q_exchanged, q_arrived,
+    send, recv, s_send, s_recv, w_load, late_load, load, *semaphores,
 ):
     me, right, left = ring_places(C)
     T, width = dq_ref.shape
     D = width * C
     heads = (dq_ref, dk_ref, dv_ref)
+
+    def cut_of(s):
+        return pl.ds(pl.multiple_of(lax.rem(me + 2 * C - 1 - s, C) * width, width), width)
+
+    def weight_in(s):
+        return pltpu.make_async_copy(w_hbm.at[:, cut_of(s), :], w_ref.at[:, cut_of(s), :], w_load.at[s])
+
+    for s in range(C):
+        weight_in(s).start()
+    late = [
+        pltpu.make_async_copy(source, target, late_load.at[i])
+        for i, (source, target) in enumerate(
+            ((a_hbm, a_ref), (x_hbm, x_ref), (dh_hbm, dh_ref), (mu_hbm, mu_ref), (r_hbm, r_ref))
+        )
+    ]
+    for copy in late:
+        copy.start()
     depth = tiles.shape[2]
     sums, loads = held_row_sum(R, grad_hbm, own, exchanged, arrived, load, semaphores[:4])
     side = lax.rem(lax.axis_index("row"), 2)
@@ -1055,14 +1165,6 @@
     for slot in sums.order():
         sums.exchange(slot).start()
 
-    def block_of(k):
-        return out_ref.at[:, pl.ds(pl.multiple_of(lax.rem(me + k, C) * width, width), width)]
-
-    out_copies = [
-        remote(block_of(k), out_in.at[k - 1], o_send.at[k - 1], o_recv.at[k - 1], col=lax.rem(me + k, C))
-        for k in range(1, C)
-    ]
-
     def moves(step):
         return ring_step(step, C, right, terms.at[0], held, send, recv)
 
@@ -1072,7 +1174,8 @@
         moves(step).start()
 
     def compute(s):
-        cut = pl.ds(pl.multiple_of(lax.rem(me + 2 * C - 1 - s, C) * width, width), width)
+        cut = cut_of(s)
+        weight_in(s).wait()
         total = dot_nt(dq_ref[...], w_ref[0, cut, :])
         total += dot_nt(dk_ref[...], w_ref[1, cut, :])
         total += dot_nt(dv_ref[...], w_ref[2, cut, :])
@@ -1086,8 +1189,8 @@
         return carry
 
     lax.fori_loop(1, C, body, 0)
-    for copy in out_copies:
-        copy.start()
+    for copy in late:
+        copy.wait()
     sums.relay(lambda slot: loads[slot].wait())
     for slot in q_sums.order():
         start = pl.multiple_of(lax.div(q_sums.places(slot), 2) * 2 * depth, 2 * depth)
@@ -1101,12 +1204,6 @@
     pass_on(1)
     sums.relay_again()
     q_sums.relay_again()
-    for copy in out_copies:
-        copy.wait_recv()
-    out_total = block_of(0)[...].astype(F32)
-    for k in range(C - 1):
-        out_total += out_in[k].astype(F32)
-    gout_ref[...] = out_total.T
     for step in range(2, C - 1):
         pass_on(step)
 
@@ -1156,31 +1253,36 @@
         return carry
 
     lax.fori_loop(0, T // size, last_rows, 0)
-    for copy in exchanges + out_copies:
+    for copy in exchanges:
         copy.wait_send()
     for step in range(C - 1):
         moves(step).wait_send()
 
 
-def input_terms(R, C, dq, dk, dv, w_qkv, a, tokens, dh, mu, r, grad_out, grad):
+def input_terms(R, C, dq, dk, dv, w_qkv, a, tokens, dh, mu, r, grad):
     T, width = dq.shape
     D = w_qkv.shape[1]
     half, low = R // 2, D // R
     depth, columns = grad.shape[1:]
     return pl.pallas_call(
         functools.partial(input_terms_kernel, R, C),
-        in_specs=[VMEM_SPEC] * 10 + [ANY],
-        out_specs=[VMEM_SPEC] * 6,
+        in_specs=[VMEM_SPEC] * 3 + [ANY] * 7,
+        out_specs=[VMEM_SPEC] * 5,
         out_shape=[struct((T, width), BF)]
         + [struct((low, width), F32)] * 3
-        + [struct((depth, columns), F32), struct((width, low), F32)],
+        + [struct((depth, columns), F32)],
         scratch_shapes=[
+            pltpu.VMEM((T, 1), F32),
+            pltpu.VMEM((T, 1), F32),
+            pltpu.VMEM((3, D, width), BF),
+            pltpu.VMEM((T, D), BF),
+            pltpu.VMEM((T, width), BF),
+            pltpu.VMEM((T, width), BF),
             pltpu.VMEM((C, T, width), BF),
             pltpu.VMEM((C - 1, T, width), BF),
             pltpu.VMEM((T, width), F32),
             pltpu.VMEM((8, T), F32),
             pltpu.VMEM((C - 1, 8, T), F32),
-            pltpu.VMEM((C - 1, low, width), BF),
             pltpu.VMEM((half, depth, columns), BF),
         ]
         + row_sum_buffers(R, depth, columns)
@@ -1191,8 +1293,8 @@
             DMA((C - 1,)),
             DMA((C - 1,)),
             DMA((C - 1,)),
-            DMA((C - 1,)),
-            DMA((C - 1,)),
+            DMA((C,)),
+            DMA((5,)),
             DMA((half,)),
         ]
         + row_sum_semaphores(R)
@@ -1200,7 +1302,7 @@
         compiler_params=comm_params(6, 63),
         cost_estimate=cost(8e10, 20 * MIB),
         name="input_terms",
-    )(dq, dk, dv, w_qkv, a, tokens, dh, mu, r, grad_out, grad)
+    )(dq, dk, dv, mu, r, w_qkv, a, tokens, dh, grad)
 
 
 def on_device(R, C, tokens, cotangent, segments, w_query, w_key, w_value, w_out, w_gate, w_up, w_down):
@@ -1209,11 +1311,10 @@
     gathered = lambda w: lax.all_gather(w, "row", axis=0, tiled=True)
 
     gate_w, up_w, down_w = gathered(w_gate), gathered(w_up), gathered(w_down.T)
-    cos_table, sin_table = rope_tables(segments)
     seg_column, seg_row = segments.reshape(T, 1), segments.reshape(1, T)
-    xs, out_part, w_qkv = first_gather(R, C, tokens, w_out, w_query, w_key, w_value)
+    xs, w_qkv, cos_table, sin_table = first_gather(R, C, seg_column, seg_row, tokens, w_query, w_key, w_value)
     w_qkv = w_qkv.reshape(3, D, width)
-    act_one, q, k, v, mu_one, r_one = norm_and_project(xs, w_qkv, cos_table, sin_table)
+    act_one, q, k, v, mu_one, r_one, out_part = norm_and_project(xs, w_qkv, cos_table, sin_table, w_out)
     os, log_total, out_w = attend(R, C, q, k, v, seg_column, seg_row, out_part.reshape(D, -1))
     h_full, act_two, hidden, slope, silu, dys = feed_forward(
         C, os, out_w, xs, gate_w, up_w, cotangent
@@ -1223,13 +1324,13 @@
         C, dg, du, hidden, gate_w, up_w, down_w, act_two, dys
     )
     by_row = lambda values: values.reshape(R, D // R, -1)
-    grad_heads, grad_resid, grad_out, grad_down = resid_back(R, total, h_full, dys, os, out_w, by_row(grad_down))
-    dq, dk, dv, output, grad_out, grad_up = attend_back(
+    grad_heads, grad_resid, grad_down = resid_back(R, total, h_full, dys, out_w, by_row(grad_down))
+    dq, dk, dv, output, grad_up, grad_out = attend_back(
         R, q, k, v, grad_heads, log_total, seg_column, seg_row, cos_table, sin_table, out_terms, h_full,
-        by_row(grad_out), by_row(grad_up),
+        by_row(grad_up), grad_resid, os,
     )
-    grad_tokens, grad_query, grad_key, grad_value, grad_gate, grad_out = input_terms(
-        R, C, dq, dk, dv, w_qkv, act_one, tokens, grad_resid, mu_one, r_one, grad_out, by_row(grad_gate)
+    grad_tokens, grad_query, grad_key, grad_value, grad_gate = input_terms(
+        R, C, dq, dk, dv, w_qkv, act_one, tokens, grad_resid, mu_one, r_one, by_row(grad_gate)
     )
     return (output, grad_tokens, grad_query, grad_key, grad_value, grad_out, grad_gate, grad_up, grad_down)
 

time: 681 us -> 642 us (0.943)
  Pallas kernels: 638 us -> 601 us
    pallas_call x1, Pallas kernels: 139 us -> 90 us  [input_terms(): pl.pallas_call(functools.partial(input_terms_kernel, R, C), in_specs=[VME...]
  transfers between devices with their start and end apart: 3 -> 3, of which waited for: 0 -> 0; matrix products, arithmetic and copies ran while one was open for 1% -> 1% of each run, Pallas kernels for 39% -> 41%
where the time goes in v5:
time: 642 us; the launch traced here: 633 us
  Pallas kernels  601 us (94%)
  local copies, waits for them, and re-layouts  15.1 us (2%)
  between operations  14.3 us (2%)
    pallas_call x1, Pallas kernels, attend_back(): pl.pallas_call(functools.partial(attend_back_kernel, R, C), in_specs=[VME...  91.5 us
    pallas_call x1, Pallas kernels, input_terms(): pl.pallas_call(functools.partial(input_terms_kernel, R, C), in_specs=[VME...  90 us
    pallas_call x1, Pallas kernels, norm_terms(): pl.pallas_call(functools.partial(norm_terms_kernel, C), in_specs=[ANY] *...  86.4 us
    pallas_call x1, Pallas kernels, feed_forward(): pl.pallas_call(functools.partial(feed_kernel, C, tiles), grid=(tiles + F...  81 us
    pallas_call x1, Pallas kernels, attend(): pl.pallas_call(functools.partial(attend_kernel, R, C), in_specs=[VMEM_SPE...  77.7 us
    pallas_call x1, Pallas kernels, first_gather(): pl.pallas_call(functools.partial(gather_kernel, R, C), in_specs=[VMEM_SPE...  77.4 us
    pallas_call x1, Pallas kernels, resid_back(): pl.pallas_call(functools.partial(resid_back_kernel, R, C), in_specs=[VMEM...  54.1 us
    pallas_call x1, Pallas kernels, norm_and_project(): pl.pallas_call(functools.partial(qkv_kernel, C), grid=(T // bt,), in_spec...  25.9 us
  transfers between devices with their start and end apart: 3, of which 0 were waited for; matrix products, arithmetic and copies ran while one was open for 1% of the time, Pallas kernels for 41%

profile of v5, /device:TPU:8, one launch (start us, length us, event | category | flops | bytes accessed | tf_op | source)
XLA Modules:
  0.0 632.7 jit_solution(2199068728071709310)
XLA Ops:
  7.2 0.0 copy-start.7
  7.2 0.0 all-gather.4.cloned.1.call-start
  7.2 0.7 all-gather.4.cloned.1.call-update
  7.9 0.0 all-gather.6.cloned.1.call-start
  8.0 0.7 all-gather.6.cloned.1.call-update
  8.7 0.0 all-gather.8.cloned.1.call-start
  8.7 2.3 copy.22
  11.0 0.0 all-gather.8.cloned.1.call-update
  11.0 0.6 maximum_bitcast_fusion.rate_ref
  11.6 0.0 copy-done.7
  11.6 1.0 copy.20.segk_ref
  12.6 77.4 %first_gather.1 = (bf16[4,1024,512]{2,1,0:T(8,128)(2,1)}, bf16[3,8,256,512]{3,2,1,0:T(8,128)(2,1)}, f32[1024,128]{1,0:T(8,128)}, f32[1024,128]{1,0:T(8,128)}) custom-call(s32[1024,1]{1,0:T(8,128)} %copy.20.segk_ref, s32[1,1024]{1,0:T(1,128)} %bitcast.11, f32[1,128]{1,0:T(1,128)} %maximum_bitcast_fusion.rate_ref, bf16[1024,512]{1,0:T(8,128)(2,1)} %x_hbm.1, ...), custom_call_target="tpu_custom_call" | custom-call | flops 60000002048 | bytes 14680064 | tf_op jit(solution)/shard_map/first_gather/pallas_call | solution.py:167
  90.0 25.9 %norm_and_project.1 = (bf16[1024,2048]{1,0:T(8,128)(2,1)}, bf16[1024,512]{1,0:T(8,128)(2,1)}, bf16[1024,512]{1,0:T(8,128)(2,1)}, bf16[1024,512]{1,0:T(8,128)(2,1...) custom-call(bf16[4,1024,512]{2,1,0:T(8,128)(2,1)} %get-tuple-element.50.xs_ref, ...), custom_call_target="tpu_custom_call" | custom-call | flops 20000000000 | bytes 14680064 | tf_op jit(solution)/shard_map/norm_and_project/pallas_call | solution.py:253
  115.9 77.7 %attend.1 = (bf16[4,4,1024,128]{3,2,1,0:T(8,128)(2,1)}, f32[4,1,1024]{2,1,0:T(1,128)}, bf16[8,2048,256]{2,1,0:T(8,128)(2,1)}) custom-call(bf16[1024,512]{1,0:T(8,128)(2,1)} %get-tuple-element.54.q_ref.q_hbm, bf16[1024,512]{1,0:T(8,128)(2,1)} %get-tuple-element.55.k_ref.k_hbm, bf16[1024,512]{1,0:T(8,128)(2,1)} %get-tuple-element.56.v_ref.v_hbm, ...), custom_call_target="tpu_custom_call" | custom-call | flops 70000001024 | bytes 14680064 | tf_op jit(solution)/shard_map/attend/pallas_call | solution.py:356
  193.6 0.0 all-gather.4.cloned.1.call-done.wg_ref.wg_hbm
  193.6 0.0 all-gather.6.cloned.1.call-done.wu_ref.wu_hbm
  193.6 81.0 %feed_forward.1 = (f32[1024,2048]{1,0:T(8,128)}, bf16[1024,2048]{1,0:T(8,128)(2,1)}, bf16[1024,2048]{1,0:T(8,128)(2,1)}, bf16[1024,2048]{1,0:T(8,128)(2,1)}, bf1...) custom-call(bf16[4,4,1024,128]{3,2,1,0:T(8,128)(2,1)} %get-tuple-element.59.os_ref.os_hbm, ...), custom_call_target="tpu_custom_call" | custom-call | flops 70000001024 | bytes 62914560 | tf_op jit(solution)/shard_map/feed_forward/pallas_call | solution.py:457
  274.7 0.0 all-gather.8.cloned.1.call-done.wd_ref.wd_hbm
  274.7 17.0 %hidden_back.1 = (bf16[1024,2048]{1,0:T(8,128)(2,1)}, bf16[1024,2048]{1,0:T(8,128)(2,1)}) custom-call(bf16[4,1024,512]{2,1,0:T(8,128)(2,1)} %get-tuple-element.61.dys_ref.dys_hbm, bf16[2048,2048]{1,0:T(8,128)(2,1)} %all-gather.8.cloned.1.call-done.wd_ref.wd_hbm, bf16[1024,2048]{1,0:T(8,128)(2,1)} %get-tuple-element.62.slope_ref, ...), custom_call_target="tpu_custom_call" | custom-call | flops 8589934592 | bytes 29360128 | tf_op jit(solution)/shard_map/hidden_back/pallas_call | solution.py:501
  291.7 86.4 %norm_terms.1 = (f32[256,2048]{1,0:T(8,128)}, bf16[2048,2048]{1,0:T(8,128)(2,1)}, bf16[2048,2048]{1,0:T(8,128)(2,1)}, bf16[2048,2048]{1,0:T(8,128)(2,1)}, bf16[4,1024,512]{2,1,0:T(8,128)(2,1)}) custom-call(bf16[1024,2048]{1,0:T(8,128)(2,1)} %get-tuple-element.64.dg_hbm, bf16[1024,2048]{1,0:T(8,128)(2,1)} %get-tuple-element.65.du_hbm, ...), custom_call_target="tpu_custom_call" | custom-call | flops 89999998976 | bytes 73400320 | tf_op jit(solution)/shard_map/norm_terms/pallas_call | solution.py:796
  378.2 54.1 %resid_back.1 = (bf16[1024,512]{1,0:T(8,128)(2,1)}, bf16[1024,512]{1,0:T(8,128)(2,1)}, f32[2048,256]{1,0:T(8,128)}) custom-call(f32[256,2048]{1,0:T(8,128)} %get-tuple-element.68.sum_ref, f32[1024,2048]{1,0:T(8,128)} %get-tuple-element.69.h_hbm, bf16[4,1024,512]{2,1,0:T(8,128)(2,1)} %get-tuple-element.61.dys_ref.dys_hbm, ...), custom_call_target="tpu_custom_call" | custom-call | flops 40000000000 | bytes 20971520 | tf_op jit(solution)/shard_map/resid_back/pallas_call | solution.py:904
  432.3 91.5 %attend_back.1 = (bf16[1024,512]{1,0:T(8,128)(2,1)}, bf16[1024,512]{1,0:T(8,128)(2,1)}, bf16[1024,512]{1,0:T(8,128)(2,1)}, bf16[1024,512]{1,0:T(8,128)(2,1)}, f32[256,2048]{1,0:T(8,128)}, /*index=5*/f32[512,256]{1,0:T(8,128)}) custom-call(f32[4,1,1024]{2,1,0:T(1,128)} %get-tuple-element.58.log_ref, s32[1024,1]{1,0:T(8,128)} %copy.20.segk_ref, ...), custom_call_target="tpu_custom_call" | custom-call | flops 70000001024 | bytes 14680064 | tf_op jit(solution)/shard_map/attend_back/pallas_call | solution.py:1085
  523.8 90.0 %input_terms.1 = (bf16[1024,512]{1,0:T(8,128)(2,1)}, f32[256,512]{1,0:T(8,128)}, f32[256,512]{1,0:T(8,128)}, f32[256,512]{1,0:T(8,128)}, f32[256,2048]{1,0:T(8,128)}) custom-call(bf16[1024,512]{1,0:T(8,128)(2,1)} %get-tuple-element.76.dq_ref, bf16[1024,512]{1,0:T(8,128)(2,1)} %get-tuple-element.77.dk_ref, bf16[1024,512]{1,0:T(8,128)(2,1)} %get-tuple-element.78.dv_ref, ...), custom_call_target="tpu_custom_call" | custom-call | flops 80000000000 | bytes 20971520 | tf_op jit(solution)/shard_map/input_terms/pallas_call | solution.py:1267
  613.9 0.0 copy-start.6
  613.9 0.0 copy-start.5
  613.9 0.0 copy-start.4
  613.9 0.0 copy-start.3
  613.9 0.0 copy-start.2
  613.9 2.4 copy.33
  616.3 2.3 copy.34
  618.6 0.0 copy-done.6
  618.6 0.0 copy-start.1
  618.6 0.8 copy.35
  619.4 0.0 copy-done.5
  619.4 0.8 copy.36
  620.2 0.0 copy-done.4
  620.2 0.8 copy.37
  621.0 0.0 copy-done.3
  621.0 0.8 copy.38
  621.8 0.0 copy-done.2
  621.8 0.0 copy-start
  621.8 1.3 copy.39
  623.1 0.0 copy-done.1
  623.1 1.3 copy.40
  624.4 0.0 copy-done
  624.4 1.3 copy.41
  (1 shorter events, 0.0 us)
Async XLA Ops:
  7.2 4.4 copy-start.7
  7.2 186.4 %all-gather.4.cloned.1.call-start = ((), (), s32[]{:S(2)}) async-start(), calls=%async_computation | async-start | bytes 9437184 | tf_op jit(solution)/shard_map/all_gather | solution.py:1311
  7.9 185.7 %all-gather.6.cloned.1.call-start = ((), (), s32[]{:S(2)}) async-start(), calls=%async_computation.1 | async-start | bytes 9437184 | tf_op jit(solution)/shard_map/all_gather | solution.py:1311
  8.7 266.0 %all-gather.8.cloned.1.call-start = ((), (), s32[]{:S(2)}) async-start(), calls=%async_computation.2 | async-start | bytes 9437184 | tf_op jit(solution)/shard_map/all_gather | solution.py:1311
  613.9 4.7 copy-start.6
  613.9 5.5 copy-start.5
  613.9 6.3 copy-start.4
  613.9 7.1 %copy-start.3 = (f32[512,256]{1,0:T(8,128)S(1)}, f32[512,256]{1,0:T(8,128)}, u32[]{:S(2)}) copy-start(f32[512,256]{1,0:T(8,128)} %get-tuple-element.105) | copy-start | bytes 1572868
  613.9 7.9 %copy-start.2 = (f32[256,2048]{1,0:T(8,128)S(1)}, f32[256,2048]{1,0:T(8,128)}, u32[]{:S(2)}) copy-start(f32[256,2048]{1,0:T(8,128)} %get-tuple-element.106) | copy-start | bytes 6291460
  618.6 4.5 copy-start.1
  621.8 2.6 copy-start
Sparse Core Ops, SparseCore 0:
  9.9 78.0 all-gather.3
  89.9 100.3 all-gather.5
  192.8 52.5 all-gather.7

commit v6 on v5

--- a/solution.py
+++ b/solution.py
@@ -378,144 +378,6 @@
     )(q, k, v, seg_column, seg_row, w_part)
 
 
-def feed_kernel(
-    C, tiles, os_ref, w_ref, xs_ref, wg_ref, wu_ref, dy_ref,
-    h_ref, b_ref, hm_ref, slope_ref, silu_ref, dys_ref, normed, local, send, recv,
-):
-    step = pl.program_id(0)
-    me, right, left = ring_places(C)
-
-    def ring(s):
-        owner = lax.rem(me - s + C, C)
-        piece = dy_ref if s == 0 else dys_ref.at[owner]
-        return remote(piece, dys_ref.at[owner], send.at[s], recv.at[s], col=right)
-
-    mine = pltpu.make_async_copy(dy_ref, dys_ref.at[me], local.at[0])
-    steps = pl.num_programs(0)
-
-    @pl.when(step == 0)
-    def _():
-        mine.start()
-        greet([{"col": left}], 1)
-        ring(0).start()
-
-    for s in range(1, C - 1):
-
-        @pl.when(step == min(tiles + s, tiles + 3))
-        def _():
-            ring(s - 1).wait_recv()
-            ring(s).start()
-
-    @pl.when(step < tiles)
-    def _():
-        size = h_ref.shape[0]
-        blocks, part = w_ref.shape[0], w_ref.shape[2]
-        heads = jnp.concatenate(
-            [os_ref[j, h] for j in range(os_ref.shape[0]) for h in range(os_ref.shape[1])], axis=1
-        )
-        x = beside(xs_ref)
-        for n in range(blocks):
-            columns = slice(n * part, (n + 1) * part)
-            h_ref[:, columns] = x[:, columns].astype(F32) + dot_nn(heads, w_ref[n])
-        h = h_ref[...]
-        centre, inverse = norm_rows(h)
-        b = ((h - centre) * inverse).astype(BF)
-        b_ref[...] = b
-        normed[pl.ds(pl.multiple_of(step * size, size), size), :] = b
-
-    @pl.when(step >= tiles)
-    def _():
-        b = normed[...]
-        gate = dot_nn(b, wg_ref[...])
-        upward = dot_nn(b, wu_ref[...])
-        sigmoid = jax.nn.sigmoid(gate)
-        silu = gate * sigmoid
-        hm_ref[...] = (silu * upward).astype(BF)
-        slope_ref[...] = (upward * sigmoid * (1.0 + gate * (1.0 - sigmoid))).astype(BF)
-        silu_ref[...] = silu.astype(BF)
-
-    @pl.when(step == steps - 1)
-    def _():
-        ring(C - 2).wait_recv()
-        for s in range(C - 1):
-            ring(s).wait_send()
-        mine.wait()
-
-
-def feed_forward(C, os, w_out, xs, w_gate, w_up, cotangent):
-    heads, T = os.shape[1], os.shape[2]
-    width = xs.shape[2]
-    D, F = w_gate.shape
-    bt = 256
-    bf = F // 4
-    tiles = T // bt
-    early = lambda i: jnp.minimum(i, tiles - 1)
-    late = lambda i: jnp.maximum(i - tiles, 0)
-    rows = lambda n: pl.BlockSpec((bt, n), lambda i: (early(i), 0))
-    tile = pl.BlockSpec((T, bf), lambda i: (0, late(i)))
-    weight = pl.BlockSpec((D, bf), lambda i: (0, late(i)))
-    return pl.pallas_call(
-        functools.partial(feed_kernel, C, tiles),
-        grid=(tiles + F // bf,),
-        in_specs=[
-            pl.BlockSpec((C, heads, bt, HEAD_DIM), lambda i: (0, 0, early(i), 0)),
-            pl.BlockSpec(w_out.shape, lambda i: (0, 0, 0), pipeline_mode=pl.Buffered(1)),
-            pl.BlockSpec((C, bt, width), lambda i: (0, early(i), 0)),
-            weight,
-            weight,
-            ANY,
-        ],
-        out_specs=[rows(D), rows(D), tile, tile, tile, ANY],
-        out_shape=[
-            struct((T, D), F32),
-            struct((T, D), BF),
-            struct((T, F), BF),
-            struct((T, F), BF),
-            struct((T, F), BF),
-            struct((C, T, width), BF),
-        ],
-        scratch_shapes=[pltpu.VMEM((T, D), BF), DMA((1,)), DMA((C - 1,)), DMA((C - 1,))],
-        compiler_params=comm_params(2),
-        cost_estimate=cost(7e10, 60 * MIB),
-        name="feed_forward",
-    )(os, w_out, xs, w_gate, w_up, cotangent)
-
-
-def hidden_back_kernel(dys_ref, wd_ref, slope_ref, silu_ref, dg_ref, du_ref, dy):
-    @pl.when(pl.program_id(0) == 0)
-    def _():
-        width = dys_ref.shape[2]
-        for j in range(dys_ref.shape[0]):
-            dy[:, j * width : (j + 1) * width] = dys_ref[j]
-
-    grad_hidden = dot_nn(dy[...], wd_ref[...])
-    dg_ref[...] = (grad_hidden * slope_ref[...].astype(F32)).astype(BF)
-    du_ref[...] = (grad_hidden * silu_ref[...].astype(F32)).astype(BF)
-
-
-def hidden_back(dys, w_down, slope, silu):
-    C, T, width = dys.shape
-    D, F = w_down.shape
-    bf = F // 4
-    tile = pl.BlockSpec((T, bf), lambda j: (0, j))
-    return pl.pallas_call(
-        hidden_back_kernel,
-        grid=(F // bf,),
-        in_specs=[
-            pl.BlockSpec(dys.shape, lambda j: (0, 0, 0), pipeline_mode=pl.Buffered(1)),
-            pl.BlockSpec((D, bf), lambda j: (0, j)),
-            tile,
-            tile,
-        ],
-        out_specs=[tile, tile],
-        out_shape=[struct((T, F), BF)] * 2,
-        scratch_shapes=[pltpu.VMEM((T, D), BF)],
-        compiler_params=params(),
-        cost_estimate=cost(2 * T * D * F, 28 * MIB),
-        name="hidden_back",
-    )(dys, w_down, slope, silu)
-
-
 def ring_step(step, C, right, first, held, send, recv):
     source = first if step == 0 else held.at[step - 1]
     return remote(source, held.at[step], send.at[step], recv.at[step], col=right)
@@ -665,17 +527,401 @@
     return sums, loads
 
 
+class LineGather:
+    def __init__(self, C, source, whole, up, down):
+        self.C, self.source, self.whole, self.up, self.down = C, source, whole, up, down
+        self.me = lax.axis_index("col")
+
+    def upward(self, step):
+        owner = self.me - step
+        piece = self.source if step == 0 else self.whole.at[owner]
+        return remote(piece, self.whole.at[owner], self.up[0].at[step], self.up[1].at[step], col=self.me + 1)
+
+    def downward(self, step):
+        owner = self.me + step
+        piece = self.source if step == 0 else self.whole.at[owner]
+        return remote(piece, self.whole.at[owner], self.down[0].at[step], self.down[1].at[step], col=self.me - 1)
+
+    def arrival(self, step, rises):
+        sender = self.me - 1 if rises else self.me + 1
+        send, recv = self.up if rises else self.down
+        target = self.whole.at[sender - step if rises else sender + step]
+        return remote(target, target, send.at[step], recv.at[step], col=sender)
+
+    def event(self, step):
+        me, last = self.me, self.C - 1
+        if step:
+
+            @pl.when(me >= step)
+            def _():
+                self.arrival(step - 1, True).wait_recv()
+
+            @pl.when(me + step <= last)
+            def _():
+                self.arrival(step - 1, False).wait_recv()
+
+        if step < last:
+
+            @pl.when((me >= step) & (me < last))
+            def _():
+                self.upward(step).start()
+
+            @pl.when((me + step <= last) & (me > 0))
+            def _():
+                self.downward(step).start()
+
+    def finish(self):
+        me, last = self.me, self.C - 1
+        for step in range(last):
+
+            @pl.when((me >= step) & (me < last))
+            def _():
+                self.upward(step).wait_send()
+
+            @pl.when((me + step <= last) & (me > 0))
+            def _():
+                self.downward(step).wait_send()
+
+
+class LineSum:
+    def __init__(self, C, terms, rising, falling, up, down):
+        self.C, self.terms, self.rising, self.falling, self.up, self.down = C, terms, rising, falling, up, down
+        self.me = lax.axis_index("col")
+
+    def upward(self, m, alone):
+        source = self.terms.at[self.C - 1 - m] if alone else self.rising.at[m]
+        return remote(source, self.rising.at[m], self.up[0].at[m], self.up[1].at[m], col=lax.rem(self.me + 1, self.C))
+
+    def downward(self, m, alone):
+        source = self.terms.at[m] if alone else self.falling.at[m]
+        return remote(
+            source, self.falling.at[m], self.down[0].at[m], self.down[1].at[m], col=lax.rem(self.me + self.C - 1, self.C)
+        )
+
+    def level(self, t):
+        me, last = self.me, self.C - 1
+        rise, fall = t - me, t - (last - me)
+        if t < last:
+
+            @pl.when(me == 0)
+            def _():
+                if t:
+                    self.upward(t - 1, True).wait_send()
+                self.upward(t, True).start()
+
+            @pl.when(me == last)
+            def _():
+                if t:
+                    self.downward(t - 1, True).wait_send()
+                self.downward(t, True).start()
+
+        if t:
+
+            @pl.when((me > 0) & (rise >= 0))
+            def _():
+                self.upward(rise, False).wait_recv()
+                if t < last:
+                    add_into(self.rising.at[rise], self.terms.at[last - rise])
+                    self.upward(rise, False).start()
+
+            @pl.when((me < last) & (fall >= 0))
+            def _():
+                self.downward(fall, False).wait_recv()
+                if t < last:
+                    add_into(self.falling.at[fall], self.terms.at[fall])
+                    self.downward(fall, False).start()
+
+    def finish(self):
+        me, last = self.me, self.C - 1
+
+        @pl.when(me == 0)
+        def _():
+            self.upward(last - 1, True).wait_send()
+
+        @pl.when(me == last)
+        def _():
+            self.downward(last - 1, True).wait_send()
+
+        for m in range(last):
+
+            @pl.when((me > 0) & (m < last - me))
+            def _():
+                self.upward(m, False).wait_send()
+
+            @pl.when((me < last) & (m < me))
+            def _():
+                self.downward(m, False).wait_send()
+
+
+def line_semaphores(C):
+    return [DMA((C,)) for _ in range(4)]
+
+
+def greet_line(C, others):
+    me, last = lax.axis_index("col"), C - 1
+    above, below = {"col": me + 1}, {"col": me - 1}
+
+    @pl.when(me == 0)
+    def _():
+        greet([above] + others, 1 + len(others))
+
+    @pl.when(me == last)
+    def _():
+        greet([below] + others, 1 + len(others))
+
+    @pl.when((me > 0) & (me < last))
+    def _():
+        greet([above, below] + others, 2 + len(others))
+
+
+def feed_kernel(
+    R, C, os_hbm, w_hbm, xs_hbm, wg_hbm, wu_hbm, wd_hbm, dy_hbm,
+    h_hbm, b_hbm, dg_hbm, du_hbm, dys_hbm, grad_hbm, down_hbm, y_ref,
+    big, hidden, slope, silu, b, gates, ups, terms, rising, falling, dys, stage, h, h_mine,
+    load, block_load, tile_load, store, w_send, w_recv, f_send, f_recv, *semaphores,
+):
+    me = lax.axis_index("col")
+    row, ahead, behind, other = row_places(R)
+    parts, heads, T = os_hbm.shape[0], os_hbm.shape[1], os_hbm.shape[2]
+    D, F = wg_hbm.shape
+    width, depth = D // C, D // R
+    size, tiles, group = 256, 8, R // C
+    bf = F // tiles
+    up, down = semaphores[:2], semaphores[2:4]
+    gather = LineGather(C, dy_hbm, dys, up, down)
+    sums = LineSum(C, terms, rising, falling, semaphores[4:6], semaphores[6:8])
+
+    def began(source, target, semaphore):
+        copy = pltpu.make_async_copy(source, target, semaphore)
+        copy.start()
+        return copy
+
+    def block_in(i):
+        rows = pl.ds(i * size, size)
+        copies = [
+            pltpu.make_async_copy(
+                os_hbm.at[j, n, rows, :], hidden.at[rows, pl.ds((j * heads + n) * HEAD_DIM, HEAD_DIM)], block_load.at[i, j * heads + n]
+            )
+            for j in range(parts)
+            for n in range(heads)
+        ]
+        return copies + [
+            pltpu.make_async_copy(
+                xs_hbm.at[j, rows, :], slope.at[rows, pl.ds(j * width, width)], block_load.at[i, parts * heads + j]
+            )
+            for j in range(C)
+        ]
+
+    def tile_in(i):
+        cut = pl.ds(i * bf, bf)
+        return [
+            pltpu.make_async_copy(wg_hbm.at[:, cut], gates.at[i % 2], tile_load.at[0, i % 2]),
+            pltpu.make_async_copy(wu_hbm.at[:, cut], ups.at[i % 2], tile_load.at[1, i % 2]),
+        ]
+
+    blocks = [block_in(i) for i in range(T // size)]
+    for copy in blocks[0]:
+        copy.start()
+    out_w = [
+        began(w_hbm.at[:, j], big.at[:, :, pl.ds(j * width, width)], load.at[j]) for j in range(C)
+    ]
+    dy_mine = began(dy_hbm, dys.at[me], load.at[R])
+    down_mine = began(wd_hbm, down_hbm.at[row], load.at[R + 1])
+    for copies in blocks[1:] + [tile_in(0), tile_in(1)]:
+        for copy in copies:
+            copy.start()
+    greet_line(C, [{"row": other}] + [{"row": ahead[k]} for k in range(1, R // 2)])
+    gather.event(0)
+    spread = [
+        remote(wd_hbm, down_hbm.at[row], w_send.at[k], w_recv.at[k], row=ahead[k]) for k in range(1, R // 2)
+    ]
+    forward = [remote(wd_hbm, down_hbm.at[row], f_send.at[0], f_recv.at[0], row=other)]
+    for copy in spread + forward:
+        copy.start()
+
+    stores = []
+    mine = pl.ds(pl.multiple_of(me * width, width), width)
+    for copy in out_w:
+        copy.wait()
+    for i in range(T // size):
+        rows = pl.ds(i * size, size)
+        for copy in blocks[i]:
+            copy.wait()
+        if i:
+            stores[-1].wait()
+        left = hidden[rows, :D]
+        for j in range(C):
+            columns = slice(j * width, (j + 1) * width)
+            right = big[j * group : (j + 1) * group, :, :D].reshape(width, D)
+            h[:, columns] = slope[rows, columns].astype(F32) + dot_nt(left, right)
+        h_mine[rows, :] = h[:, mine]
+        values = h[...]
+        centre, inverse = norm_rows(values)
+        b[rows, :] = ((values - centre) * inverse).astype(BF)
+        stores.append(began(h, h_hbm.at[rows, :], store.at[0]))
+    stores[-1].wait()
+    b_out = began(b, b_hbm, store.at[1])
+    for i in range(tiles):
+        cut = slice(i * bf, (i + 1) * bf)
+        for copy in tile_in(i):
+            copy.wait()
+        values = b[...]
+        gate = dot_nn(values, gates[i % 2])
+        upward = dot_nn(values, ups[i % 2])
+        sigmoid = jax.nn.sigmoid(gate)
+        silued = gate * sigmoid
+        hidden[:, cut] = (silued * upward).astype(BF)
+        slope[:, cut] = (upward * sigmoid * (1.0 + gate * (1.0 - sigmoid))).astype(BF)
+        silu[:, cut] = silued.astype(BF)
+        if i + 2 < tiles:
+            for copy in tile_in(i + 2):
+                copy.start()
+        if i == 3:
+            gather.event(1)
+    for k in range(1, R // 2):
+        spread[k - 1].wait_recv()
+        block = down_hbm.at[behind[k]]
+        copy = remote(block, block, f_send.at[k], f_recv.at[k], row=other)
+        copy.start()
+        forward.append(copy)
+    for step in range(2, max(3, C - 1)):
+        if step < C:
+            gather.event(step)
+    for copy in forward:
+        copy.wait_recv()
+    down_mine.wait()
+    began(down_hbm, big.at[:, :, pl.ds(0, F)], load.at[0]).wait()
+    half = lax.div(me, C // 2)
+
+    def out_tile(k):
+        j = (C - 1 - k) * (1 - half) + k * half
+        right = big[pl.ds(j * group, group), :, :F].reshape(width, F)
+        terms[j] = dot_nt(hidden[:, :F], right).astype(BF)
+
+    out_tile(0)
+    sums.level(0)
+    for k in range(1, C):
+        out_tile(k)
+    for step in range(max(3, C - 1), C):
+        gather.event(step)
+    dy_mine.wait()
+    b_out.wait()
+    joined = [began(dys.at[j], b.at[:, pl.ds(j * width, width)], load.at[j]) for j in range(C)]
+    saved = [began(dys, dys_hbm, store.at[1])]
+    for copy in joined:
+        copy.wait()
+    sums.level(1)
+    for i in range(tiles):
+        cut = slice(i * bf, (i + 1) * bf)
+        grad_hidden = dot_nn(b[...], big[:, :, cut].reshape(D, bf))
+        slope[:, cut] = (grad_hidden * slope[:, cut].astype(F32)).astype(BF)
+        silu[:, cut] = (grad_hidden * silu[:, cut].astype(F32)).astype(BF)
+    saved.append(began(slope.at[:, pl.ds(0, F)], dg_hbm, store.at[2]))
+    saved.append(began(silu.at[:, pl.ds(0, F)], du_hbm, store.at[3]))
+
+    def grads(first, stop):
+        copies = []
+        for j in range(first, stop):
+            if len(copies) >= 2:
+                copies[-2].wait()
+            stage[j % 2] = dot_tn(dys[j], hidden[:, :F]).astype(BF)
+            copies.append(began(stage.at[j % 2], grad_hbm.at[pl.ds(j * width, width), :], load.at[j % 2]))
+        for copy in copies[-2:]:
+            copy.wait()
+
+    grads(0, C // 2)
+    for t in range(2, C - 1):
+        sums.level(t)
+    grads(C // 2, C)
+    sums.level(C - 1)
+    last = C - 1
+    y_ref[...] = terms[me]
+
+    @pl.when(me == 0)
+    def _():
+        y_ref[...] = (h_mine[...] + terms[me].astype(F32) + falling[0].astype(F32)).astype(BF)
+
+    @pl.when(me == last)
+    def _():
+        y_ref[...] = (h_mine[...] + terms[me].astype(F32) + rising[0].astype(F32)).astype(BF)
+
+    @pl.when((me > 0) & (me < last))
+    def _():
+        y_ref[...] = (
+            h_mine[...] + terms[me].astype(F32) + rising[last - me].astype(F32) + falling[me].astype(F32)
+        ).astype(BF)
+
+    sums.finish()
+    gather.finish()
+    for copy in spread + forward:
+        copy.wait_send()
+    for copy in saved:
+        copy.wait()
+
+
+def feed_forward(R, C, os, w_out, xs, w_gate, w_up, w_down, cotangent):
+    heads, T = os.shape[1], os.shape[2]
+    width = xs.shape[2]
+    D, F = w_gate.shape
+    most = max(D, F)
+    flat = pltpu.VMEM((T, most), BF)
+    return pl.pallas_call(
+        functools.partial(feed_kernel, R, C),
+        in_specs=[ANY] * 7,
+        out_specs=[ANY] * 7 + [VMEM_SPEC],
+        out_shape=[
+            struct((T, D), F32),
+            struct((T, D), BF),
+            struct((T, F), BF),
+            struct((T, F), BF),
+            struct((C, T, width), BF),
+            struct((D, F), BF),
+            struct((R, D // R, F), BF),
+            struct((T, width), BF),
+        ],
+        scratch_shapes=[
+            pltpu.VMEM((R, D // R, most), BF),
+            flat,
+            flat,
+            pltpu.VMEM((T, F), BF),
+            pltpu.VMEM((T, D), BF),
+            pltpu.VMEM((2, D, F // 8), BF),
+            pltpu.VMEM((2, D, F // 8), BF),
+            pltpu.VMEM((C, T, width), BF),
+            pltpu.VMEM((C - 1, T, width), BF),
+            pltpu.VMEM((C - 1, T, width), BF),
+            pltpu.VMEM((C, T, width), BF),
+            pltpu.VMEM((2, width, F), BF),
+            pltpu.VMEM((256, D), F32),
+            pltpu.VMEM((T, width), F32),
+            DMA((R + 2,)),
+            DMA((T // 256, C * heads + C)),
+            DMA((2, 2)),
+            DMA((4,)),
+            DMA((R // 2,)),
+            DMA((R // 2,)),
+            DMA((R // 2,)),
+            DMA((R // 2,)),
+        ]
+        + line_semaphores(C)
+        + line_semaphores(C),
+        compiler_params=comm_params(2, 63),
+        cost_estimate=cost(1.2e11, 90 * MIB),
+        name="feed_forward",
+    )(os, w_out, xs, w_gate, w_up, w_down, cotangent)
+
+
 def norm_terms_kernel(
-    C, dg_hbm, du_hbm, hm_hbm, wg_hbm, wu_hbm, wd_hbm, b_hbm, dys_hbm,
-    sum_ref, gate_hbm, up_hbm, down_hbm, out_hbm,
-    dg, du, hm, wg, wu, b, dys, terms, held, stage, load, tile_load, store, send, recv,
+    R, C, dg_hbm, du_hbm, wg_hbm, wu_hbm, b_hbm, down_hbm,
+    sum_ref, gate_hbm, up_hbm, down_ref,
+    dg, du, wg, wu, b, terms, held, stage, own, exchanged, arrived,
+    load, tile_load, store, own_load, send, recv, *semaphores,
 ):
     me, right, left = ring_places(C)
     D, F = wg.shape
     T = dg.shape[0]
     rows = T // C
     width = D // C
-    loads = []
 
     def fetch(source, target, semaphore):
         copy = pltpu.make_async_copy(source, target, semaphore)
@@ -698,12 +944,13 @@
                 weights_in.append(
                     (fetch(wg_hbm.at[cut, :], wg.at[cut, :], tile_load.at[2 * n]), fetch(wu_hbm.at[cut, :], wu.at[cut, :], tile_load.at[2 * n + 1]))
                 )
-    late = [
-        fetch(b_hbm, b, load.at[2 * C]),
-        fetch(hm_hbm, hm, load.at[2 * C + 1]),
-        fetch(dys_hbm, dys, load.at[2 * C + 2]),
-    ]
-    greet([{"col": left}], 1)
+    b_in = fetch(b_hbm, b, load.at[2 * C])
+    sums, own_loads = held_row_sum(R, down_hbm, own, exchanged, arrived, own_load, semaphores)
+    for copy in own_loads:
+        copy.start()
+    greet([{"col": left}] + sums.peers, 1 + len(sums.peers))
+    for slot in sums.order():
+        sums.exchange(slot).start()
 
     def term_tile(s, part, n):
         cut = pl.ds(pl.multiple_of(n * width, width), width)
@@ -728,6 +975,7 @@
                     copy.wait()
                 term_tile(s, part, n)
             moves(0).start()
+            sums.relay(lambda slot: own_loads[slot].wait())
         else:
 
             def body(n, carry):
@@ -735,15 +983,13 @@
                 return carry
 
             lax.fori_loop(0, C, body, 0)
-    down_in = fetch(wd_hbm, wg, tile_load.at[0])
-    for copy in late:
-        copy.wait()
+    b_in.wait()
 
     def stored(target, t, slot):
         cut = pl.ds(pl.multiple_of(t * width, width), width)
         return pltpu.make_async_copy(stage.at[slot], target.at[cut, :], store.at[slot])
 
-    def product(left_of, right_ref, target):
+    def product(right_ref, target):
         def body(t, carry):
             slot = lax.rem(t, 2)
 
@@ -751,7 +997,8 @@
             def _():
                 stored(target, t, slot).wait()
 
-            stage[slot] = dot_tn(left_of(t), right_ref[...]).astype(BF)
+            left_tile = b[:, pl.ds(pl.multiple_of(t * width, width), width)]
+            stage[slot] = dot_tn(left_tile, right_ref[...]).astype(BF)
             stored(target, t, slot).start()
             return carry
 
@@ -759,99 +1006,90 @@
         for slot in range(2):
             stored(target, slot, slot).wait()
 
-    def b_tile(t):
-        return b[:, pl.ds(pl.multiple_of(t * width, width), width)]
-
     middle = max(1, (C - 1) // 2)
-    product(b_tile, dg, gate_hbm)
     for step in range(1, middle + 1):
         if step < C - 1:
             pass_on(step)
-    product(b_tile, du, up_hbm)
-    product(lambda t: dys[t], hm, down_hbm)
+    product(dg, gate_hbm)
+    sums.relay_again()
+    product(du, up_hbm)
     for step in range(middle + 1, C - 1):
         pass_on(step)
-    down_in.wait()
-
-    def out_tile(n, carry):
-        cut = pl.ds(pl.multiple_of(n * width, width), width)
-        terms_out = dot_nt(hm[...], wg[cut, :]).astype(BF)
-        dys[0] = terms_out
-        copy = pltpu.make_async_copy(dys.at[0], out_hbm.at[n], store.at[0])
-        copy.start()
-        copy.wait()
-        return carry
-
-    lax.fori_loop(0, C, out_tile, 0)
+
+    def write(part, values):
+        down_ref[:, part] = values.T
+
+    sums.finish(write, 128)
     moves(C - 2).wait_recv()
     sum_ref[...] = held[C - 2].astype(F32) + terms[C - 1].astype(F32)
     for step in range(C - 1):
         moves(step).wait_send()
 
 
-def norm_terms(C, dg, du, hm, w_gate, w_up, w_down, b, dys):
+def norm_terms(R, C, dg, du, w_gate, w_up, b, grad_down):
     T, F = dg.shape
     D = w_gate.shape[0]
     rows, width = T // C, D // C
+    depth, columns = grad_down.shape[1:]
     return pl.pallas_call(
-        functools.partial(norm_terms_kernel, C),
-        in_specs=[ANY] * 8,
-        out_specs=[VMEM_SPEC, ANY, ANY, ANY, ANY],
-        out_shape=[
-            struct((rows, D), F32),
-            struct((D, F), BF),
-            struct((D, F), BF),
-            struct((D, F), BF),
-            struct((C, T, width), BF),
-        ],
+        functools.partial(norm_terms_kernel, R, C),
+        in_specs=[ANY] * 6,
+        out_specs=[VMEM_SPEC, ANY, ANY, VMEM_SPEC],
+        out_shape=[struct((rows, D), F32), struct((D, F), BF), struct((D, F), BF), struct((columns, depth), F32)],
         scratch_shapes=[
-            pltpu.VMEM((T, F), BF),
             pltpu.VMEM((T, F), BF),
             pltpu.VMEM((T, F), BF),
             pltpu.VMEM((D, F), BF),
             pltpu.VMEM((D, F), BF),
             pltpu.VMEM((T, D), BF),
-            pltpu.VMEM((C, T, width), BF),
             pltpu.VMEM((C, rows, D), BF),
             pltpu.VMEM((C - 1, rows, D), BF),
             pltpu.VMEM((2, width, F), BF),
-            DMA((2 * C + 3,)),
+            pltpu.VMEM((R // 2, depth, columns), BF),
+        ]
+        + row_sum_buffers(R, depth, columns)
+        + [
+            DMA((2 * C + 1,)),
             DMA((2 * C,)),
             DMA((2,)),
+            DMA((R // 2,)),
             DMA((C - 1,)),
             DMA((C - 1,)),
-        ],
-        compiler_params=comm_params(3, 62),
+        ]
+        + row_sum_semaphores(R),
+        compiler_params=comm_params(3, 63),
         cost_estimate=cost(9e10, 70 * MIB),
         name="norm_terms",
-    )(dg, du, hm, w_gate, w_up, w_down, b, dys)
-
-
-def resid_back_kernel(
-    R, C, sum_ref, h_hbm, dys_hbm, w_hbm, down_hbm, do_hbm, dhs_hbm, down_ref,
-    h, dy, w, dh, out, own, exchanged, arrived,
+    )(dg, du, w_gate, w_up, b, grad_down)
+
+
+def attend_back_kernel(
+    R, C, sum_ref, log_ref, segk_ref, segq_ref, cos_ref, sin_ref,
+    q_hbm, k_hbm, v_hbm, h_hbm, dys_hbm, w_hbm, gate_hbm,
+    dq_ref, dk_ref, dv_ref, gate_ref, dhs_hbm,
+    h, dy, w, dh, out, q_ref, k_ref, v_ref, do_ref, dk_sum, dv_sum, own, exchanged, arrived,
     load, w_load, local, h_send, h_recv, o_send, o_recv, own_load, *semaphores,
 ):
     me, right, left = ring_places(C)
-    blocks, D, part = w.shape
-    rows = sum_ref.shape[0]
-    width = D // C
+    rows, D = sum_ref.shape
+    T, width = q_ref.shape
+    heads, bq = width // HEAD_DIM, 256
     mine = pl.ds(pl.multiple_of(me * rows, rows), rows)
     first_in = [
         pltpu.make_async_copy(h_hbm.at[mine, :], h, load.at[0]),
         pltpu.make_async_copy(dys_hbm.at[:, mine, :], dy, load.at[1]),
     ]
+    head_loads = [
+        pltpu.make_async_copy(source, target, load.at[2 + i])
+        for i, (source, target) in enumerate(((q_hbm, q_ref), (k_hbm, k_ref), (v_hbm, v_ref)))
+    ]
     for copy in first_in:
         copy.start()
     order = [lax.rem(me + k, C) for k in range(1, C)] + [me]
-    loads = []
-    for k in range(C):
-        cut = pl.ds(pl.multiple_of(order[k] * width, width), width)
-        copy = pltpu.make_async_copy(w_hbm.at[:, cut, :], w.at[:, cut, :], w_load.at[k])
-        copy.start()
-        loads.append(copy)
-    sums, own_loads = held_row_sum(R, down_hbm, own, exchanged, arrived, own_load, semaphores)
-    for copy in own_loads:
+    cuts = [pl.ds(pl.multiple_of(place * width, width), width) for place in order]
+    loads = [pltpu.make_async_copy(w_hbm.at[:, order[k]], w.at[k], w_load.at[k]) for k in range(C)]
+    sums, own_loads = held_row_sum(R, gate_hbm, own, exchanged, arrived, own_load, semaphores)
+    for copy in loads + own_loads + head_loads:
         copy.start()
     greet([{"col": lax.rem(me + k, C)} for k in range(1, C)] + sums.peers, C - 1 + len(sums.peers))
     for slot in sums.order():
@@ -864,135 +1102,27 @@
     first = jnp.mean(grad, axis=1, keepdims=True)
     second = jnp.mean(grad * normed, axis=1, keepdims=True)
     dh[...] = (beside(dy).astype(F32) + inverse * (grad - first - normed * second)).astype(BF)
-    copies = []
+    do_copies, dh_copies = [], []
     for k in range(C):
-        cut = pl.ds(pl.multiple_of(order[k] * width, width), width)
         loads[k].wait()
-        total = dot_nt(dh[:, :part], w[0, cut, :])
-        for n in range(1, blocks):
-            total += dot_nt(dh[:, n * part : (n + 1) * part], w[n, cut, :])
-        out[k] = total.astype(BF)
+        out[k] = dot_nn(dh[...], w[k].reshape(D, width)).astype(BF)
         if k < C - 1:
-            copy = remote(out.at[k], do_hbm.at[mine, :], o_send.at[k], o_recv.at[k], col=order[k])
+            copy = remote(out.at[k], do_ref.at[mine, :], o_send.at[k], o_recv.at[k], col=order[k])
         else:
-            copy = pltpu.make_async_copy(out.at[k], do_hbm.at[mine, :], local.at[0])
-        copy.start()
-        copies.append(copy)
+            copy = pltpu.make_async_copy(out.at[k], do_ref.at[mine, :], local.at[0])
+        copy.start()
+        do_copies.append(copy)
+    sums.relay(lambda slot: own_loads[slot].wait())
+    for copy in do_copies[:-1]:
+        copy.wait_recv()
+    do_copies[-1].wait()
     for k in range(C):
-        cut = pl.ds(pl.multiple_of(order[k] * width, width), width)
         if k < C - 1:
-            copy = remote(dh.at[:, cut], dhs_hbm.at[mine, :], h_send.at[k], h_recv.at[k], col=order[k])
+            copy = remote(dh.at[:, cuts[k]], dhs_hbm.at[mine, :], h_send.at[k], h_recv.at[k], col=order[k])
         else:
-            copy = pltpu.make_async_copy(dh.at[:, cut], dhs_hbm.at[mine, :], local.at[1])
-        copy.start()
-        copies.append(copy)
-    sums.relay(lambda slot: own_loads[slot].wait())
-    sums.relay_again()
-
-    def write(part, values):
-        down_ref[:, part] = values.T
-
-    sums.finish(write, 128)
-    for copy in copies:
-        copy.wait()
-
-
-def resid_back(R, total, h, dys, w_out, grad_down):
-    C, T, width = dys.shape
-    rows, D = total.shape
-    depth, columns = grad_down.shape[1:]
-    return pl.pallas_call(
-        functools.partial(resid_back_kernel, R, C),
-        in_specs=[VMEM_SPEC] + [ANY] * 4,
-        out_specs=[ANY, ANY, VMEM_SPEC],
-        out_shape=[
-            struct((T, width), BF),
-            struct((T, width), BF),
-            struct((columns, depth), F32),
-        ],
-        scratch_shapes=[
-            pltpu.VMEM((rows, D), F32),
-            pltpu.VMEM((C, rows, width), BF),
-            pltpu.VMEM(w_out.shape, BF),
-            pltpu.VMEM((rows, D), BF),
-            pltpu.VMEM((C, rows, width), BF),
-            pltpu.VMEM((R // 2, depth, columns), BF),
-        ]
-        + row_sum_buffers(R, depth, columns)
-        + [
-            DMA((2,)),
-            DMA((C,)),
-            DMA((2,)),
-            DMA((C - 1,)),
-            DMA((C - 1,)),
-            DMA((C - 1,)),
-            DMA((C - 1,)),
-            DMA((R // 2,)),
-        ]
-        + row_sum_semaphores(R),
-        compiler_params=comm_params(4),
-        cost_estimate=cost(4e10, 20 * MIB),
-        name="resid_back",
-    )(total, h, dys, w_out, grad_down)
-
-
-def attend_back_kernel(
-    R, C, log_ref, segk_ref, segq_ref, cos_ref, sin_ref,
-    q_hbm, k_hbm, v_hbm, do_hbm, terms_hbm, h_hbm, up_hbm, dh_hbm, os_hbm,
-    dq_ref, dk_ref, dv_ref, y_ref, up_ref, out_ref,
-    q_ref, k_ref, v_ref, do_ref, terms, dk_sum, dv_sum, held, h, dh, os, mine, theirs,
-    up_own, up_exchanged, up_arrived, tiles, o_exchanged, o_arrived,
-    send, recv, term_load, head_load, out_load, h_load, up_load, own_send, own_recv, *semaphores,
-):
-    me, right, left = ring_places(C)
-    T, width = q_ref.shape
-    heads, bq = width // HEAD_DIM, 256
-    row = lax.axis_index("row")
-    side, partner_row, partner_col = lax.rem(row, 2), 2 * me + lax.rem(row, 2), lax.div(row, 2)
-    apart = partner_col != me
-
-    def term_in(s):
-        return pltpu.make_async_copy(terms_hbm.at[chunk(s)], terms.at[s], term_load.at[s])
-
-    def chunk(s):
-        return lax.rem(me + 2 * C - 1 - s, C)
-
-    cut = pl.ds(pl.multiple_of(me * width, width), width)
-    head_loads = [
-        pltpu.make_async_copy(source, target, head_load.at[i])
-        for i, (source, target) in enumerate(((q_hbm, q_ref), (k_hbm, k_ref), (v_hbm, v_ref), (do_hbm, do_ref)))
-    ]
-    out_loads = [
-        pltpu.make_async_copy(dh_hbm, dh, out_load.at[0]),
-        pltpu.make_async_copy(os_hbm, os, out_load.at[1]),
-    ]
-    h_in = pltpu.make_async_copy(h_hbm.at[:, cut], h, h_load.at[0])
-    up_sums, up_loads = held_row_sum(R, up_hbm, up_own, up_exchanged, up_arrived, up_load, semaphores[:4])
-    out_sums = RowSum(
-        R, lambda i: tiles.at[i, side], lambda i: tiles.at[i, 1 - side], o_exchanged, o_arrived, semaphores[4:]
-    )
-    term_in(0).start()
-    for copy in head_loads + up_loads + out_loads:
-        copy.start()
-    for s in range(1, C):
-        term_in(s).start()
-    h_in.start()
-    @pl.when(apart)
-    def _():
-        greet([{"col": left}, {"row": partner_row, "col": partner_col}] + up_sums.peers, 2 + len(up_sums.peers))
-
-    @pl.when(jnp.logical_not(apart))
-    def _():
-        greet([{"col": left}] + up_sums.peers, 1 + len(up_sums.peers))
-
-    for slot in up_sums.order():
-        up_sums.exchange(slot).start()
-    term_in(0).wait()
-
-    def moves(step):
-        return ring_step(step, C, right, terms.at[0], held, send, recv)
-
-    moves(0).start()
+            copy = pltpu.make_async_copy(dh.at[:, cuts[k]], dhs_hbm.at[mine, :], local.at[1])
+        copy.start()
+        dh_copies.append(copy)
     for copy in head_loads:
         copy.wait()
 
@@ -1021,121 +1151,77 @@
         dv_ref[:, columns] = dv_sum[...].astype(BF)
         return carry
 
-    lax.fori_loop(0, 1, one_head, 0)
-    up_sums.relay(lambda slot: up_loads[slot].wait())
-    for copy in out_loads:
+    lax.fori_loop(0, heads // 2, one_head, 0)
+    sums.relay_again()
+    lax.fori_loop(heads // 2, heads, one_head, 0)
+
+    def write(part, values):
+        gate_ref[part, :] = values
+
+    sums.finish(write)
+    for copy in do_copies[:-1]:
+        copy.wait_send()
+    for copy in dh_copies:
         copy.wait()
-    depth = tiles.shape[2]
-    for slot in out_sums.order():
-        chip = lax.div(out_sums.places(slot), 2)
-        right_side = jnp.concatenate([os[chip, i] for i in range(heads)], axis=1)
-        product = dot_tn(dh[...], right_side).astype(BF)
-        tiles[slot, 0] = product[:depth]
-        tiles[slot, 1] = product[depth:]
-        out_sums.exchange(slot).start()
-    lax.fori_loop(1, heads, one_head, 0)
-    out_sums.relay()
-    for s in range(1, C):
-        term_in(s).wait()
-    for step in range(1, C - 1):
-        moves(step - 1).wait_recv()
-        add_into(held.at[step - 1], terms.at[step])
-        moves(step).start()
-        if step == 1:
-            out_sums.relay_again()
-            up_sums.relay_again()
-
-    def write_up(part, values):
-        up_ref[part, :] = values
-
-    def write_out(part, values):
-        mine[part, :] = values.astype(BF)
-
-    out_sums.finish(write_out)
-    handed = remote(mine, theirs, own_send.at[0], own_recv.at[0], row=partner_row, col=partner_col)
-
-    @pl.when(apart)
-    def _():
-        handed.start()
-
-    up_sums.finish(write_up)
-    h_in.wait()
-    moves(C - 2).wait_recv()
-    y_ref[...] = (h[...] + held[C - 2].astype(F32) + terms[C - 1].astype(F32)).astype(BF)
-
-    @pl.when(apart)
-    def _():
-        handed.wait()
-        out_ref[...] = theirs[...].astype(F32).T
-
-    @pl.when(jnp.logical_not(apart))
-    def _():
-        out_ref[...] = mine[...].astype(F32).T
-
-    for step in range(C - 1):
-        moves(step).wait_send()
-
-
-def attend_back(R, q, k, v, do, log_total, seg_column, seg_row, cos_table, sin_table, out_terms, h, grad_up, dh, os):
-    C = out_terms.shape[0]
-    T, width = q.shape
-    assert R == 2 * C
-    depth, columns = grad_up.shape[1:]
+
+
+def attend_back(R, total, log_total, seg_column, seg_row, cos_table, sin_table, q, k, v, h, dys, w_out, grad_gate):
+    C, T, width = dys.shape
+    rows, D = total.shape
+    depth, columns = grad_gate.shape[1:]
     one = pltpu.VMEM((T, width), BF)
     return pl.pallas_call(
         functools.partial(attend_back_kernel, R, C),
-        in_specs=[VMEM_SPEC] * 5 + [ANY] * 9,
-        out_specs=[VMEM_SPEC] * 6,
-        out_shape=[struct((T, width), BF)] * 4 + [struct((depth, columns), F32), struct((width, depth), F32)],
+        in_specs=[VMEM_SPEC] * 6 + [ANY] * 7,
+        out_specs=[VMEM_SPEC] * 4 + [ANY],
+        out_shape=[struct((T, width), BF)] * 3 + [struct((depth, columns), F32), struct((T, width), BF)],
         scratch_shapes=[
+            pltpu.VMEM((rows, D), F32),
+            pltpu.VMEM((C, rows, width), BF),
+            pltpu.VMEM((C, R, D // R, width), BF),
+            pltpu.VMEM((rows, D), BF),
+            pltpu.VMEM((C, rows, width), BF),
             one,
             one,
             one,
             one,
-            pltpu.VMEM((C, T, width), BF),
             pltpu.VMEM((T, HEAD_DIM), F32),
             pltpu.VMEM((T, HEAD_DIM), F32),
-            pltpu.VMEM((C - 1, T, width), BF),
-            pltpu.VMEM((T, width), F32),
-            one,
-            pltpu.VMEM(os.shape, BF),
-            pltpu.VMEM((depth, width), BF),
-            pltpu.VMEM((depth, width), BF),
             pltpu.VMEM((R // 2, depth, columns), BF),
         ]
         + row_sum_buffers(R, depth, columns)
-        + [pltpu.VMEM((R // 2, 2, depth, width), BF)]
-        + row_sum_buffers(R, depth, width)
         + [
+            DMA((5,)),
+            DMA((C,)),
+            DMA((2,)),
             DMA((C - 1,)),
             DMA((C - 1,)),
-            DMA((C,)),
-            DMA((4,)),
-            DMA((2,)),
-            DMA((1,)),
+            DMA((C - 1,)),
+            DMA((C - 1,)),
             DMA((R // 2,)),
-            DMA((1,)),
-            DMA((1,)),
         ]
-        + row_sum_semaphores(R)
         + row_sum_semaphores(R),
         compiler_params=comm_params(5),
-        cost_estimate=cost(7e10, 14 * MIB),
+        cost_estimate=cost(5e10, 30 * MIB),
         name="attend_back",
-    )(log_total, seg_column, seg_row, cos_table, sin_table, q, k, v, do, out_terms, h, grad_up, dh, os)
+    )(total, log_total, seg_column, seg_row, cos_table, sin_table, q, k, v, h, dys, w_out, grad_gate)
 
 
 def input_terms_kernel(
-    R, C, dq_ref, dk_ref, dv_ref, mu_hbm, r_hbm, w_hbm, a_hbm, x_hbm, dh_hbm, grad_hbm,
-    y_ref, gq_ref, gk_ref, gv_ref, total_ref,
-    mu_ref, r_ref, w_ref, a_ref, x_ref, dh_ref,
-    terms, held, da, stats, stats_in, own, exchanged, arrived, tiles, q_exchanged, q_arrived,
-    send, recv, s_send, s_recv, w_load, late_load, load, *semaphores,
+    R, C, dq_ref, dk_ref, dv_ref, mu_hbm, r_hbm, w_hbm, a_hbm, x_hbm, dh_hbm, grad_hbm, os_hbm,
+    y_ref, gq_ref, gk_ref, gv_ref, total_ref, out_ref,
+    mu_ref, r_ref, w_ref, a_ref, x_ref, dh_ref, block, mine, theirs,
+    terms, held, stats, stats_in, own, exchanged, arrived, tiles, q_exchanged, q_arrived, o_tiles, o_exchanged, o_arrived,
+    send, recv, s_send, s_recv, w_load, late_load, load, block_load, own_send, own_recv, *semaphores,
 ):
     me, right, left = ring_places(C)
     T, width = dq_ref.shape
     D = width * C
     heads = (dq_ref, dk_ref, dv_ref)
+    side_row = lax.rem(lax.axis_index("row"), 2)
+    partner = {"row": 2 * me + side_row, "col": lax.div(lax.axis_index("row"), 2)}
+    direct = [{"col": lax.rem(me + k, C)} for k in range(1, C)]
+    apart = partner["col"] != me
 
     def cut_of(s):
         return pl.ds(pl.multiple_of(lax.rem(me + 2 * C - 1 - s, C) * width, width), width)
@@ -1157,11 +1243,32 @@
     sums, loads = held_row_sum(R, grad_hbm, own, exchanged, arrived, load, semaphores[:4])
     side = lax.rem(lax.axis_index("row"), 2)
     q_sums = RowSum(
-        R, lambda i: tiles.at[i, side], lambda i: tiles.at[i, 1 - side], q_exchanged, q_arrived, semaphores[4:]
+        R, lambda i: tiles.at[i, side], lambda i: tiles.at[i, 1 - side], q_exchanged, q_arrived, semaphores[4:8]
     )
-    for copy in loads:
-        copy.start()
-    greet([{"col": lax.rem(me + k, C)} for k in range(1, C)] + sums.peers, C - 1 + len(sums.peers))
+    o_sums = RowSum(
+        R, lambda i: o_tiles.at[i, side], lambda i: o_tiles.at[i, 1 - side], o_exchanged, o_arrived, semaphores[8:]
+    )
+
+    def block_in(i):
+        chip = lax.div(o_sums.places(o_sums.order()[i]), 2)
+        return [
+            pltpu.make_async_copy(
+                os_hbm.at[chip, n], block.at[i % 2, :, pl.ds(n * HEAD_DIM, HEAD_DIM)], block_load.at[i % 2, n]
+            )
+            for n in range(os_hbm.shape[1])
+        ]
+
+    for copy in loads + block_in(0) + block_in(1):
+        copy.start()
+
+    @pl.when(apart)
+    def _():
+        greet(direct + sums.peers + [partner], C + len(sums.peers))
+
+    @pl.when(jnp.logical_not(apart))
+    def _():
+        greet(direct + sums.peers, C - 1 + len(sums.peers))
+
     for slot in sums.order():
         sums.exchange(slot).start()
 
@@ -1200,9 +1307,20 @@
             tiles[slot, 0, :, i * width : (i + 1) * width] = product[:depth]
             tiles[slot, 1, :, i * width : (i + 1) * width] = product[depth:]
         q_sums.exchange(slot).start()
+    pass_on(1)
     q_sums.relay()
-    pass_on(1)
+    for i, slot in enumerate(o_sums.order()):
+        for copy in block_in(i):
+            copy.wait()
+        product = dot_tn(dh_ref[...], block[i % 2]).astype(BF)
+        o_tiles[slot, 0] = product[:depth]
+        o_tiles[slot, 1] = product[depth:]
+        o_sums.exchange(slot).start()
+        if i + 2 < R // 2:
+            for copy in block_in(i + 2):
+                copy.start()
     sums.relay_again()
+    o_sums.relay()
     q_sums.relay_again()
     for step in range(2, C - 1):
         pass_on(step)
@@ -1214,18 +1332,41 @@
         for i, target in enumerate((gq_ref, gk_ref, gv_ref)):
             target[part, :] = values[:, i * width : (i + 1) * width]
 
+    def write_out(part, values):
+        mine[part, :] = values.astype(BF)
+
+    o_sums.relay_again()
+    o_sums.finish(write_out)
+    handed = remote(mine, theirs, own_send.at[0], own_recv.at[0], **partner)
+
+    @pl.when(apart)
+    def _():
+        handed.start()
+
     sums.finish(write)
     q_sums.finish(write_qkv)
+
+    @pl.when(apart)
+    def _():
+        handed.wait()
+        out_ref[...] = theirs[...].astype(F32).T
+
+    @pl.when(jnp.logical_not(apart))
+    def _():
+        out_ref[...] = mine[...].astype(F32).T
+
     moves(C - 2).wait_recv()
     size = 128
 
+    def grad_of(rows):
+        return held[C - 2, rows, :].astype(F32) + terms[C - 1, rows, :].astype(F32)
+
     def normed_of(rows):
         return (x_ref[rows, :].astype(F32) - mu_ref[rows, :]) * r_ref[rows, :]
 
     def sum_rows(i, carry):
         rows = pl.ds(pl.multiple_of(i * size, size), size)
-        grad = held[C - 2, rows, :].astype(F32) + terms[C - 1, rows, :].astype(F32)
-        da[rows, :] = grad
+        grad = grad_of(rows)
         lane = lax.broadcasted_iota(jnp.int32, (size, 128), 1)
         first = jnp.sum(grad, axis=1, keepdims=True)
         second = jnp.sum(grad * normed_of(rows), axis=1, keepdims=True)
@@ -1248,7 +1389,7 @@
         for k in range(C - 1):
             both += stats_in[k, :, rows]
         columns = jnp.concatenate([both, jnp.zeros((120, size), F32)], axis=0).T * (1.0 / D)
-        grad = da[rows, :] - columns[:, 0:1] - normed_of(rows) * columns[:, 1:2]
+        grad = grad_of(rows) - columns[:, 0:1] - normed_of(rows) * columns[:, 1:2]
         y_ref[rows, :] = (dh_ref[rows, :].astype(F32) + r_ref[rows, :] * grad).astype(BF)
         return carry
 
@@ -1259,18 +1400,19 @@
         moves(step).wait_send()
 
 
-def input_terms(R, C, dq, dk, dv, w_qkv, a, tokens, dh, mu, r, grad):
+def input_terms(R, C, dq, dk, dv, w_qkv, a, tokens, dh, mu, r, grad, os):
     T, width = dq.shape
     D = w_qkv.shape[1]
     half, low = R // 2, D // R
     depth, columns = grad.shape[1:]
+    assert R == 2 * C
     return pl.pallas_call(
         functools.partial(input_terms_kernel, R, C),
-        in_specs=[VMEM_SPEC] * 3 + [ANY] * 7,
-        out_specs=[VMEM_SPEC] * 5,
+        in_specs=[VMEM_SPEC] * 3 + [ANY] * 8,
+        out_specs=[VMEM_SPEC] * 6,
         out_shape=[struct((T, width), BF)]
         + [struct((low, width), F32)] * 3
-        + [struct((depth, columns), F32)],
+        + [struct((depth, columns), F32), struct((width, low), F32)],
         scratch_shapes=[
             pltpu.VMEM((T, 1), F32),
             pltpu.VMEM((T, 1), F32),
@@ -1278,9 +1420,11 @@
             pltpu.VMEM((T, D), BF),
             pltpu.VMEM((T, width), BF),
             pltpu.VMEM((T, width), BF),
+            pltpu.VMEM((2, T, width), BF),
+            pltpu.VMEM((low, width), BF),
+            pltpu.VMEM((low, width), BF),
             pltpu.VMEM((C, T, width), BF),
             pltpu.VMEM((C - 1, T, width), BF),
-            pltpu.VMEM((T, width), F32),
             pltpu.VMEM((8, T), F32),
             pltpu.VMEM((C - 1, 8, T), F32),
             pltpu.VMEM((half, depth, columns), BF),
@@ -1288,6 +1432,8 @@
         + row_sum_buffers(R, depth, columns)
         + [pltpu.VMEM((half, 2, low, 3 * width), BF)]
         + row_sum_buffers(R, low, 3 * width)
+        + [pltpu.VMEM((half, 2, low, width), BF)]
+        + row_sum_buffers(R, low, width)
         + [
             DMA((C - 1,)),
             DMA((C - 1,)),
@@ -1296,13 +1442,17 @@
             DMA((C,)),
             DMA((5,)),
             DMA((half,)),
+            DMA((2, os.shape[1])),
+            DMA((1,)),
+            DMA((1,)),
         ]
+        + row_sum_semaphores(R)
         + row_sum_semaphores(R)
         + row_sum_semaphores(R),
         compiler_params=comm_params(6, 63),
         cost_estimate=cost(8e10, 20 * MIB),
         name="input_terms",
-    )(dq, dk, dv, mu, r, w_qkv, a, tokens, dh, grad)
+    )(dq, dk, dv, mu, r, w_qkv, a, tokens, dh, grad, os)
 
 
 def on_device(R, C, tokens, cotangent, segments, w_query, w_key, w_value, w_out, w_gate, w_up, w_down):
@@ -1310,27 +1460,22 @@
     D = width * C
     gathered = lambda w: lax.all_gather(w, "row", axis=0, tiled=True)
 
-    gate_w, up_w, down_w = gathered(w_gate), gathered(w_up), gathered(w_down.T)
+    gate_w, up_w = gathered(w_gate), gathered(w_up)
     seg_column, seg_row = segments.reshape(T, 1), segments.reshape(1, T)
     xs, w_qkv, cos_table, sin_table = first_gather(R, C, seg_column, seg_row, tokens, w_query, w_key, w_value)
     w_qkv = w_qkv.reshape(3, D, width)
-    act_one, q, k, v, mu_one, r_one, out_part = norm_and_project(xs, w_qkv, cos_table, sin_table, w_out)
-    os, log_total, out_w = attend(R, C, q, k, v, seg_column, seg_row, out_part.reshape(D, -1))
-    h_full, act_two, hidden, slope, silu, dys = feed_forward(
-        C, os, out_w, xs, gate_w, up_w, cotangent
-    )
-    dg, du = hidden_back(dys, down_w, slope, silu)
-    total, grad_gate, grad_up, grad_down, out_terms = norm_terms(
-        C, dg, du, hidden, gate_w, up_w, down_w, act_two, dys
+    act_one, q, k, v, mu_one, r_one, out_part = norm_and_project(xs, w_qkv, cos_table, sin_table, w_out.T)
+    os, log_total, out_w = attend(R, C, q, k, v, seg_column, seg_row, out_part)
+    h_full, act_two, dg, du, dys, grad_down, _, output = feed_forward(
+        R, C, os, out_w, xs, gate_w, up_w, w_down.T, cotangent
     )
     by_row = lambda values: values.reshape(R, D // R, -1)
-    grad_heads, grad_resid, grad_down = resid_back(R, total, h_full, dys, out_w, by_row(grad_down))
-    dq, dk, dv, output, grad_up, grad_out = attend_back(
-        R, q, k, v, grad_heads, log_total, seg_column, seg_row, cos_table, sin_table, out_terms, h_full,
-        by_row(grad_up), grad_resid, os,
+    total, grad_gate, grad_up, grad_down = norm_terms(R, C, dg, du, gate_w, up_w, act_two, by_row(grad_down))
+    dq, dk, dv, grad_gate, dh = attend_back(
+        R, total, log_total, seg_column, seg_row, cos_table, sin_table, q, k, v, h_full, dys, out_w, by_row(grad_gate)
     )
-    grad_tokens, grad_query, grad_key, grad_value, grad_gate = input_terms(
-        R, C, dq, dk, dv, w_qkv, act_one, tokens, grad_resid, mu_one, r_one, by_row(grad_gate)
+    grad_tokens, grad_query, grad_key, grad_value, grad_up, grad_out = input_terms(
+        R, C, dq, dk, dv, w_qkv, act_one, tokens, dh, mu_one, r_one, by_row(grad_up), os
     )
     return (output, grad_tokens, grad_query, grad_key, grad_value, grad_out, grad_gate, grad_up, grad_down)
 

time: 642 us -> 601 us (0.936)
  Pallas kernels: 601 us -> 557 us
    pallas_call x1, Pallas kernels: 91.5 us -> 59 us  [attend_back(): pl.pallas_call(functools.partial(attend_back_kernel, R, C), in_specs=[VME...]
    pallas_call x4 -> x2, Pallas kernels: 239 us -> 214 us  [the longest x1 134 us: feed_forward(): pl.pallas_call(functools.partial(feed_kernel, R, C), in_specs=[ANY] * 7,...]
    pallas_call x1, Pallas kernels: 90 us -> 103 us  [input_terms(): pl.pallas_call(functools.partial(input_terms_kernel, R, C), in_specs=[VME...]
    unnamed x26 -> x25, local copies, waits for them, and re-layouts: 14.1 us -> 15.9 us
  transfers between devices with their start and end apart: 3 -> 2, of which waited for: 0 -> 0; matrix products, arithmetic and copies ran while one was open for 1% -> 1% of each run, Pallas kernels for 41% -> 31%
where the time goes in v6:
time: 601 us; the launch traced here: 591 us
  Pallas kernels  557 us (93%)
  local copies, waits for them, and re-layouts  17.6 us (3%)
  between operations  14.4 us (2%)
    pallas_call x1, Pallas kernels, feed_forward(): pl.pallas_call(functools.partial(feed_kernel, R, C), in_specs=[ANY] * 7,...  134 us
    pallas_call x1, Pallas kernels, input_terms(): pl.pallas_call(functools.partial(input_terms_kernel, R, C), in_specs=[VME...  103 us
    pallas_call x1, Pallas kernels, norm_terms(): pl.pallas_call(functools.partial(norm_terms_kernel, R, C), in_specs=[ANY]...  79.9 us
    pallas_call x1, Pallas kernels, attend(): pl.pallas_call(functools.partial(attend_kernel, R, C), in_specs=[VMEM_SPE...  77.6 us
    pallas_call x1, Pallas kernels, first_gather(): pl.pallas_call(functools.partial(gather_kernel, R, C), in_specs=[VMEM_SPE...  77.4 us
    pallas_call x1, Pallas kernels, attend_back(): pl.pallas_call(functools.partial(attend_back_kernel, R, C), in_specs=[VME...  59 us
    pallas_call x1, Pallas kernels, norm_and_project(): pl.pallas_call(functools.partial(qkv_kernel, C), grid=(T // bt,), in_spec...  25.9 us
    unnamed x25, local copies, waits for them, and re-layouts  15.9 us
  transfers between devices with their start and end apart: 2, of which 0 were waited for; matrix products, arithmetic and copies ran while one was open for 1% of the time, Pallas kernels for 31%

profile of v6, /device:TPU:8, one launch (start us, length us, event | category | flops | bytes accessed | tf_op | source)
XLA Modules:
  0.0 591.1 jit_solution(4725503960602864777)
XLA Ops:
  7.2 0.0 all-gather.3.cloned.1.call-start
  7.2 0.7 all-gather.3.cloned.1.call-update
  7.9 0.0 all-gather.5.cloned.1.call-start
  8.0 0.7 all-gather.5.cloned.1.call-update
  8.7 1.8 copy.22
  10.5 1.7 copy.21.segk_ref
  12.2 2.3 copy.24
  14.4 0.6 maximum_bitcast_fusion.rate_ref
  15.0 77.4 %first_gather.1 = (bf16[4,1024,512]{2,1,0:T(8,128)(2,1)}, bf16[3,8,256,512]{3,2,1,0:T(8,128)(2,1)}, f32[1024,128]{1,0:T(8,128)}, f32[1024,128]{1,0:T(8,128)}) custom-call(s32[1024,1]{1,0:T(8,128)} %copy.21.segk_ref, s32[1,1024]{1,0:T(1,128)} %bitcast.13, f32[1,128]{1,0:T(1,128)} %maximum_bitcast_fusion.rate_ref, bf16[1024,512]{1,0:T(8,128)(2,1)} %x_hbm.1, ...), custom_call_target="tpu_custom_call" | custom-call | flops 60000002048 | bytes 14680064 | tf_op jit(solution)/shard_map/first_gather/pallas_call | solution.py:167
  92.4 25.9 %norm_and_project.1 = (bf16[1024,2048]{1,0:T(8,128)(2,1)}, bf16[1024,512]{1,0:T(8,128)(2,1)}, bf16[1024,512]{1,0:T(8,128)(2,1)}, bf16[1024,512]{1,0:T(8,128)(2,1...) custom-call(bf16[4,1024,512]{2,1,0:T(8,128)(2,1)} %get-tuple-element.45.xs_ref.xs_hbm, ...), custom_call_target="tpu_custom_call" | custom-call | flops 20000000000 | bytes 14680064 | tf_op jit(solution)/shard_map/norm_and_project/pallas_call | solution.py:253
  118.3 77.6 %attend.1 = (bf16[4,4,1024,128]{3,2,1,0:T(8,128)(2,1)}, f32[4,1,1024]{2,1,0:T(1,128)}, bf16[8,4,256,512]{3,2,1,0:T(8,128)(2,1)}) custom-call(bf16[1024,512]{1,0:T(8,128)(2,1)} %get-tuple-element.49.q_ref.q_hbm, bf16[1024,512]{1,0:T(8,128)(2,1)} %get-tuple-element.50.k_ref.k_hbm, bf16[1024,512]{1,0:T(8,128)(2,1)} %get-tuple-element.51.v_ref.v_hbm, ...), custom_call_target="tpu_custom_call" | custom-call | flops 70000001024 | bytes 14680064 | tf_op jit(solution)/shard_map/attend/pallas_call | solution.py:356
  195.9 0.0 all-gather.3.cloned.1.call-done.wg_hbm
  196.0 0.0 all-gather.5.cloned.1.call-done.wu_hbm
  196.0 133.9 %feed_forward.1 = (f32[1024,2048]{1,0:T(8,128)}, bf16[1024,2048]{1,0:T(8,128)(2,1)}, bf16[1024,2048]{1,0:T(8,128)(2,1)}, bf16[1024,2048]{1,0:T(8,128)(2,1)}, bf1...) custom-call(bf16[4,4,1024,128]{3,2,1,0:T(8,128)(2,1)} %get-tuple-ele, ...), custom_call_target="tpu_custom_call" | custom-call | flops 120000004096 | bytes 94371840 | tf_op jit(solution)/shard_map/feed_forward/pallas_call | solution.py:868
  329.9 79.9 %norm_terms.1 = (f32[256,2048]{1,0:T(8,128)}, bf16[2048,2048]{1,0:T(8,128)(2,1)}, bf16[2048,2048]{1,0:T(8,128)(2,1)}, f32[2048,256]{1,0:T(8,128)}) custom-call(bf16[1024,2048]{1,0:T(8,128)(2,1)} %get-tuple-element.56.dg_hbm, bf16[1024,2048]{1,0:T(8,128)(2,1)} %get-tuple-element.57.du_hbm, bf16[2048,2048]{1,0:T(8,128)(2,1)} %all-gather.3.cloned.1.call-done.wg_hbm, ...), custom_call_target="tpu_custom_call" | custom-call | flops 89999998976 | bytes 73400320 | tf_op jit(solution)/shard_map/norm_terms/pallas_call | solution.py:1034
  409.8 59.0 %attend_back.1 = (bf16[1024,512]{1,0:T(8,128)(2,1)}, bf16[1024,512]{1,0:T(8,128)(2,1)}, bf16[1024,512]{1,0:T(8,128)(2,1)}, f32[256,2048]{1,0:T(8,128)}, bf16[1024,512]{1,0:T(8,128)(2,1)}) custom-call(f32[256,2048]{1,0:T(8,128)} %get-tuple-element.60.sum_ref, f32[4,1,1024]{2,1,0:T(1,128)} %get-tuple-element.61.log_ref, s32[1024,1]{1,0:T(8,128)} %copy.21.segk_ref, ...), custom_call_target="tpu_custom_call" | custom-call | flops 49999998976 | bytes 31457280 | tf_op jit(solution)/shard_map/attend_back/pallas_call | solution.py:1173
  468.8 103.4 %input_terms.1 = (bf16[1024,512]{1,0:T(8,128)(2,1)}, f32[256,512]{1,0:T(8,128)}, f32[256,512]{1,0:T(8,128)}, f32[256,512]{1,0:T(8,128)}, f32[256,2048]{1,0:T(8,128)}, /*index=5*/f32[512,256]{1,0:T(8,128)}) custom-call(bf16[1024,512]{1,0:T(8,128)(2,1)} %get-tuple-element.65.dq_ref, bf16[1024,512]{1,0:T(8,128)(2,1)} %get-tuple-element.66.dk_ref, ...), custom_call_target="tpu_custom_call" | custom-call | flops 80000000000 | bytes 20971520 | tf_op jit(solution)/shard_map/input_terms/pallas_call | solution.py:1409
  572.2 0.0 copy-start.6
  572.2 0.0 copy-start.5
  572.2 0.0 copy-start.4
  572.2 0.0 copy-start.3
  572.2 0.0 copy-start.1
  572.2 2.4 copy.35
  574.6 2.3 copy.36
  576.9 0.0 copy-done.6
  576.9 0.0 copy-start.2
  576.9 0.8 copy.37
  577.7 0.0 copy-done.5
  577.7 0.8 copy.38
  578.5 0.0 copy-done.4
  578.5 0.8 copy.39
  579.3 0.0 copy-done.3
  579.3 0.8 copy.40
  580.1 0.0 copy-done.1
  580.1 0.0 copy-start
  580.1 1.3 copy.41
  581.4 0.0 copy-done.2
  581.4 1.3 copy.42
  582.7 0.0 copy-done
  582.7 1.3 copy.43
  (1 shorter events, 0.0 us)
Async XLA Ops:
  7.2 188.8 %all-gather.3.cloned.1.call-start = ((), (), s32[]{:S(2)}) async-start(), calls=%async_computation | async-start | bytes 9437184 | tf_op jit(solution)/shard_map/all_gather | solution.py:1461
  7.9 188.1 %all-gather.5.cloned.1.call-start = ((), (), s32[]{:S(2)}) async-start(), calls=%async_computation.1 | async-start | bytes 9437184 | tf_op jit(solution)/shard_map/all_gather | solution.py:1461
  572.2 4.7 copy-start.6
  572.2 5.5 copy-start.5
  572.2 6.3 %copy-start.4 = (f32[256,512]{1,0:T(8,128)S(1)}, f32[256,512]{1,0:T(8,128)}, u32[]{:S(2)}) copy-start(f32[256,512]{1,0:T(8,128)} %get-tuple-element.94) | copy-start | bytes 1572868
  572.2 7.1 %copy-start.3 = (f32[512,256]{1,0:T(8,128)S(1)}, f32[512,256]{1,0:T(8,128)}, u32[]{:S(2)}) copy-start(f32[512,256]{1,0:T(8,128)} %get-tuple-element.95) | copy-start | bytes 1572868
  572.2 7.9 %copy-start.1 = (f32[256,2048]{1,0:T(8,128)S(1)}, f32[256,2048]{1,0:T(8,128)}, u32[]{:S(2)}) copy-start(f32[256,2048]{1,0:T(8,128)} %get-tuple-element.96) | copy-start | bytes 6291460
  576.9 4.5 copy-start.2
  580.1 2.6 copy-start
Sparse Core Ops, SparseCore 0:
  9.9 79.3 all-gather.2
  91.1 101.4 all-gather.4

commit v7 on v6

--- a/solution.py
+++ b/solution.py
@@ -1208,20 +1208,18 @@
 
 
 def input_terms_kernel(
-    R, C, dq_ref, dk_ref, dv_ref, mu_hbm, r_hbm, w_hbm, a_hbm, x_hbm, dh_hbm, grad_hbm, os_hbm,
-    y_ref, gq_ref, gk_ref, gv_ref, total_ref, out_ref,
-    mu_ref, r_ref, w_ref, a_ref, x_ref, dh_ref, block, mine, theirs,
-    terms, held, stats, stats_in, own, exchanged, arrived, tiles, q_exchanged, q_arrived, o_tiles, o_exchanged, o_arrived,
-    send, recv, s_send, s_recv, w_load, late_load, load, block_load, own_send, own_recv, *semaphores,
+    R, C, dq_ref, dk_ref, dv_ref, mu_hbm, r_hbm, w_hbm, a_hbm, x_hbm, dh_hbm, os_hbm,
+    y_ref, gq_ref, gk_ref, gv_ref, out_ref,
+    mu_ref, r_ref, w_ref, a_ref, x_ref, dh_ref, block, product, mine, by_column, by_row,
+    terms, held, stats, stats_in, tiles, q_exchanged, q_arrived, o_tiles, o_exchanged, o_arrived,
+    send, recv, s_send, s_recv, w_load, late_load, block_load, c_send, c_recv, r_send, r_recv, local, *semaphores,
 ):
     me, right, left = ring_places(C)
     T, width = dq_ref.shape
     D = width * C
     heads = (dq_ref, dk_ref, dv_ref)
-    side_row = lax.rem(lax.axis_index("row"), 2)
-    partner = {"row": 2 * me + side_row, "col": lax.div(lax.axis_index("row"), 2)}
-    direct = [{"col": lax.rem(me + k, C)} for k in range(1, C)]
-    apart = partner["col"] != me
+    row = lax.axis_index("row")
+    thin = width // R
 
     def cut_of(s):
         return pl.ds(pl.multiple_of(lax.rem(me + 2 * C - 1 - s, C) * width, width), width)
@@ -1240,37 +1238,28 @@
     for copy in late:
         copy.start()
     depth = tiles.shape[2]
-    sums, loads = held_row_sum(R, grad_hbm, own, exchanged, arrived, load, semaphores[:4])
     side = lax.rem(lax.axis_index("row"), 2)
     q_sums = RowSum(
-        R, lambda i: tiles.at[i, side], lambda i: tiles.at[i, 1 - side], q_exchanged, q_arrived, semaphores[4:8]
+        R, lambda i: tiles.at[i, side], lambda i: tiles.at[i, 1 - side], q_exchanged, q_arrived, semaphores[:4]
     )
     o_sums = RowSum(
-        R, lambda i: o_tiles.at[i, side], lambda i: o_tiles.at[i, 1 - side], o_exchanged, o_arrived, semaphores[8:]
+        R, lambda i: o_tiles.at[i, side], lambda i: o_tiles.at[i, 1 - side], o_exchanged, o_arrived, semaphores[4:]
     )
 
     def block_in(i):
-        chip = lax.div(o_sums.places(o_sums.order()[i]), 2)
         return [
             pltpu.make_async_copy(
-                os_hbm.at[chip, n], block.at[i % 2, :, pl.ds(n * HEAD_DIM, HEAD_DIM)], block_load.at[i % 2, n]
+                os_hbm.at[i, n], block.at[i % 2, :, pl.ds(n * HEAD_DIM, HEAD_DIM)], block_load.at[i % 2, n]
             )
             for n in range(os_hbm.shape[1])
         ]
 
-    for copy in loads + block_in(0) + block_in(1):
-        copy.start()
-
-    @pl.when(apart)
-    def _():
-        greet(direct + sums.peers + [partner], C + len(sums.peers))
-
-    @pl.when(jnp.logical_not(apart))
-    def _():
-        greet(direct + sums.peers, C - 1 + len(sums.peers))
-
-    for slot in sums.order():
-        sums.exchange(slot).start()
+    for copy in block_in(0) + block_in(1):
+        copy.start()
+    greet(
+        [{"col": lax.rem(me + k, C)} for k in range(1, C)] + [{"row": lax.rem(row + k, R)} for k in range(1, R)],
+        C + R - 2,
+    )
 
     def moves(step):
         return ring_step(step, C, right, terms.at[0], held, send, recv)
@@ -1295,10 +1284,25 @@
         compute(s)
         return carry
 
+    late[2].wait()
+    for j in range(C):
+        for copy in block_in(j):
+            copy.wait()
+        product[...] = dot_tn(block[j % 2], dh_ref[...]).astype(BF)
+        for slot in range(R // 2):
+            for place in range(2):
+                rows = 2 * lax.div(o_sums.places(slot), 2) + place
+                o_tiles[slot, place, j * thin : (j + 1) * thin] = product[pl.ds(pl.multiple_of(rows * thin, thin), thin), :]
+        if j + 2 < C:
+            for copy in block_in(j + 2):
+                copy.start()
+    for slot in o_sums.order():
+        o_sums.exchange(slot).start()
+    o_sums.relay()
     lax.fori_loop(1, C, body, 0)
-    for copy in late:
-        copy.wait()
-    sums.relay(lambda slot: loads[slot].wait())
+    for i, copy in enumerate(late):
+        if i != 2:
+            copy.wait()
     for slot in q_sums.order():
         start = pl.multiple_of(lax.div(q_sums.places(slot), 2) * 2 * depth, 2 * depth)
         left_tile = a_ref[:, pl.ds(start, 2 * depth)]
@@ -1307,70 +1311,36 @@
             tiles[slot, 0, :, i * width : (i + 1) * width] = product[:depth]
             tiles[slot, 1, :, i * width : (i + 1) * width] = product[depth:]
         q_sums.exchange(slot).start()
+    o_sums.relay_again()
     pass_on(1)
     q_sums.relay()
-    for i, slot in enumerate(o_sums.order()):
-        for copy in block_in(i):
-            copy.wait()
-        product = dot_tn(dh_ref[...], block[i % 2]).astype(BF)
-        o_tiles[slot, 0] = product[:depth]
-        o_tiles[slot, 1] = product[depth:]
-        o_sums.exchange(slot).start()
-        if i + 2 < R // 2:
-            for copy in block_in(i + 2):
-                copy.start()
-    sums.relay_again()
-    o_sums.relay()
-    q_sums.relay_again()
-    for step in range(2, C - 1):
-        pass_on(step)
-
-    def write(part, values):
-        total_ref[part, :] = values
-
-    def write_qkv(part, values):
-        for i, target in enumerate((gq_ref, gk_ref, gv_ref)):
-            target[part, :] = values[:, i * width : (i + 1) * width]
 
     def write_out(part, values):
         mine[part, :] = values.astype(BF)
 
-    o_sums.relay_again()
     o_sums.finish(write_out)
-    handed = remote(mine, theirs, own_send.at[0], own_recv.at[0], **partner)
-
-    @pl.when(apart)
-    def _():
-        handed.start()
-
-    sums.finish(write)
-    q_sums.finish(write_qkv)
-
-    @pl.when(apart)
-    def _():
-        handed.wait()
-        out_ref[...] = theirs[...].astype(F32).T
-
-    @pl.when(jnp.logical_not(apart))
-    def _():
-        out_ref[...] = mine[...].astype(F32).T
-
-    moves(C - 2).wait_recv()
+    columns_out = []
+    for k in range(1, C):
+        place = lax.rem(me + k, C)
+        rows = pl.ds(pl.multiple_of(place * thin, thin), thin)
+        columns_out.append(remote(mine.at[rows, :], by_column.at[me], c_send.at[k - 1], c_recv.at[k - 1], col=place))
+    stay = pltpu.make_async_copy(
+        mine.at[pl.ds(pl.multiple_of(me * thin, thin), thin), :], by_column.at[me], local.at[0]
+    )
+    for copy in columns_out + [stay]:
+        copy.start()
     size = 128
-
-    def grad_of(rows):
-        return held[C - 2, rows, :].astype(F32) + terms[C - 1, rows, :].astype(F32)
-
-    def normed_of(rows):
-        return (x_ref[rows, :].astype(F32) - mu_ref[rows, :]) * r_ref[rows, :]
 
     def sum_rows(i, carry):
         rows = pl.ds(pl.multiple_of(i * size, size), size)
-        grad = grad_of(rows)
         lane = lax.broadcasted_iota(jnp.int32, (size, 128), 1)
-        first = jnp.sum(grad, axis=1, keepdims=True)
-        second = jnp.sum(grad * normed_of(rows), axis=1, keepdims=True)
-        packed = jnp.where(lane == 0, first, jnp.where(lane == 1, second, 0.0))
+        total = jnp.zeros((size, 1), F32)
+        second = jnp.zeros((size, 1), F32)
+        for s in range(C):
+            grad = terms[s, rows, :].astype(F32)
+            total += jnp.sum(grad, axis=1, keepdims=True)
+            second += jnp.sum(grad * a_ref[rows, cut_of(s)].astype(F32), axis=1, keepdims=True)
+        packed = jnp.where(lane == 0, total, jnp.where(lane == 1, second, 0.0))
         stats[:, rows] = packed.T[:8]
         return carry
 
@@ -1380,8 +1350,37 @@
     ]
     for copy in exchanges:
         copy.start()
+    for copy in columns_out:
+        copy.wait_recv()
+    stay.wait()
+
+    def piece_of(place):
+        return by_column.at[lax.div(place * C, R), :, pl.ds(pl.multiple_of(lax.rem(place, R // C) * depth, depth), depth)]
+
+    rows_out = []
+    for k in range(1, R):
+        place = lax.rem(row + k, R)
+        rows_out.append(remote(piece_of(place), by_row.at[row], r_send.at[k - 1], r_recv.at[k - 1], row=place))
+    keep = pltpu.make_async_copy(piece_of(row), by_row.at[row], local.at[1])
+    for copy in rows_out + [keep]:
+        copy.start()
+    for step in range(2, C - 1):
+        pass_on(step)
+    q_sums.relay_again()
+    for copy in rows_out:
+        copy.wait_recv()
+    keep.wait()
+    for n in range(R):
+        out_ref[n * thin : (n + 1) * thin, :] = by_row[n].astype(F32)
+
+    def write_qkv(part, values):
+        for i, target in enumerate((gq_ref, gk_ref, gv_ref)):
+            target[part, :] = values[:, i * width : (i + 1) * width]
+
+    q_sums.finish(write_qkv)
     for copy in exchanges:
         copy.wait_recv()
+    moves(C - 2).wait_recv()
 
     def last_rows(i, carry):
         rows = pl.ds(pl.multiple_of(i * size, size), size)
@@ -1389,30 +1388,31 @@
         for k in range(C - 1):
             both += stats_in[k, :, rows]
         columns = jnp.concatenate([both, jnp.zeros((120, size), F32)], axis=0).T * (1.0 / D)
-        grad = grad_of(rows) - columns[:, 0:1] - normed_of(rows) * columns[:, 1:2]
+        normed = (x_ref[rows, :].astype(F32) - mu_ref[rows, :]) * r_ref[rows, :]
+        grad = held[C - 2, rows, :].astype(F32) + terms[C - 1, rows, :].astype(F32)
+        grad = grad - columns[:, 0:1] - normed * columns[:, 1:2]
         y_ref[rows, :] = (dh_ref[rows, :].astype(F32) + r_ref[rows, :] * grad).astype(BF)
         return carry
 
     lax.fori_loop(0, T // size, last_rows, 0)
-    for copy in exchanges:
+    for copy in exchanges + columns_out + rows_out:
         copy.wait_send()
     for step in range(C - 1):
         moves(step).wait_send()
 
 
-def input_terms(R, C, dq, dk, dv, w_qkv, a, tokens, dh, mu, r, grad, os):
+def input_terms(R, C, dq, dk, dv, w_qkv, a, tokens, dh, mu, r, os):
     T, width = dq.shape
     D = w_qkv.shape[1]
     half, low = R // 2, D // R
-    depth, columns = grad.shape[1:]
-    assert R == 2 * C
+    thin = width // R
     return pl.pallas_call(
         functools.partial(input_terms_kernel, R, C),
-        in_specs=[VMEM_SPEC] * 3 + [ANY] * 8,
-        out_specs=[VMEM_SPEC] * 6,
+        in_specs=[VMEM_SPEC] * 3 + [ANY] * 7,
+        out_specs=[VMEM_SPEC] * 5,
         out_shape=[struct((T, width), BF)]
         + [struct((low, width), F32)] * 3
-        + [struct((depth, columns), F32), struct((width, low), F32)],
+        + [struct((width, low), F32)],
         scratch_shapes=[
             pltpu.VMEM((T, 1), F32),
             pltpu.VMEM((T, 1), F32),
@@ -1421,19 +1421,19 @@
             pltpu.VMEM((T, width), BF),
             pltpu.VMEM((T, width), BF),
             pltpu.VMEM((2, T, width), BF),
-            pltpu.VMEM((low, width), BF),
-            pltpu.VMEM((low, width), BF),
+            pltpu.VMEM((width, width), BF),
+            pltpu.VMEM((C * thin, width), BF),
+            pltpu.VMEM((C, thin, width), BF),
+            pltpu.VMEM((R, thin, low), BF),
             pltpu.VMEM((C, T, width), BF),
             pltpu.VMEM((C - 1, T, width), BF),
             pltpu.VMEM((8, T), F32),
             pltpu.VMEM((C - 1, 8, T), F32),
-            pltpu.VMEM((half, depth, columns), BF),
+            pltpu.VMEM((half, 2, low, 3 * width), BF),
         ]
-        + row_sum_buffers(R, depth, columns)
-        + [pltpu.VMEM((half, 2, low, 3 * width), BF)]
         + row_sum_buffers(R, low, 3 * width)
-        + [pltpu.VMEM((half, 2, low, width), BF)]
-        + row_sum_buffers(R, low, width)
+        + [pltpu.VMEM((half, 2, C * thin, width), BF)]
+        + row_sum_buffers(R, C * thin, width)
         + [
             DMA((C - 1,)),
             DMA((C - 1,)),
@@ -1441,18 +1441,19 @@
             DMA((C - 1,)),
             DMA((C,)),
             DMA((5,)),
-            DMA((half,)),
             DMA((2, os.shape[1])),
-            DMA((1,)),
-            DMA((1,)),
+            DMA((C - 1,)),
+            DMA((C - 1,)),
+            DMA((R - 1,)),
+            DMA((R - 1,)),
+            DMA((2,)),
         ]
-        + row_sum_semaphores(R)
         + row_sum_semaphores(R)
         + row_sum_semaphores(R),
         compiler_params=comm_params(6, 63),
         cost_estimate=cost(8e10, 20 * MIB),
         name="input_terms",
-    )(dq, dk, dv, mu, r, w_qkv, a, tokens, dh, grad, os)
+    )(dq, dk, dv, mu, r, w_qkv, a, tokens, dh, os)
 
 
 def on_device(R, C, tokens, cotangent, segments, w_query, w_key, w_value, w_out, w_gate, w_up, w_down):
@@ -1471,11 +1472,12 @@
     )
     by_row = lambda values: values.reshape(R, D // R, -1)
     total, grad_gate, grad_up, grad_down = norm_terms(R, C, dg, du, gate_w, up_w, act_two, by_row(grad_down))
+    grad_up = lax.psum_scatter(grad_up, "row", scatter_dimension=0, tiled=True).astype(F32)
     dq, dk, dv, grad_gate, dh = attend_back(
         R, total, log_total, seg_column, seg_row, cos_table, sin_table, q, k, v, h_full, dys, out_w, by_row(grad_gate)
     )
-    grad_tokens, grad_query, grad_key, grad_value, grad_up, grad_out = input_terms(
-        R, C, dq, dk, dv, w_qkv, act_one, tokens, dh, mu_one, r_one, by_row(grad_up), os
+    grad_tokens, grad_query, grad_key, grad_value, grad_out = input_terms(
+        R, C, dq, dk, dv, w_qkv, act_one, tokens, dh, mu_one, r_one, os
     )
     return (output, grad_tokens, grad_query, grad_key, grad_value, grad_out, grad_gate, grad_up, grad_down)
 

time: 601 us -> 610 us (1.015)
  the two profiles are of different devices: /device:TPU:8 before, /device:TPU:18 now
where the time goes in v7:
time: 610 us; the launch traced here: 605 us
  Pallas kernels  571 us (94%)
  local copies, waits for them, and re-layouts  15 us (2%)
  between operations  14.1 us (2%)
    pallas_call x1, Pallas kernels, feed_forward(): pl.pallas_call(functools.partial(feed_kernel, R, C), in_specs=[ANY] * 7,...  133 us
    pallas_call x1, Pallas kernels, input_terms(): pl.pallas_call(functools.partial(input_terms_kernel, R, C), in_specs=[VME...  112 us
    pallas_call x1, Pallas kernels, norm_terms(): pl.pallas_call(functools.partial(norm_terms_kernel, R, C), in_specs=[ANY]...  80.5 us
    pallas_call x1, Pallas kernels, first_gather(): pl.pallas_call(functools.partial(gather_kernel, R, C), in_specs=[VMEM_SPE...  76.4 us
    pallas_call x1, Pallas kernels, attend(): pl.pallas_call(functools.partial(attend_kernel, R, C), in_specs=[VMEM_SPE...  74.8 us
    pallas_call x1, Pallas kernels, attend_back(): pl.pallas_call(functools.partial(attend_back_kernel, R, C), in_specs=[VME...  67.2 us
    pallas_call x1, Pallas kernels, norm_and_project(): pl.pallas_call(functools.partial(qkv_kernel, C), grid=(T // bt,), in_spec...  26.9 us
    unnamed x24, local copies, waits for them, and re-layouts  13.3 us
  transfers between devices with their start and end apart: 3, of which 0 were waited for; matrix products, arithmetic and copies ran while one was open for 1% of the time, Pallas kernels for 59%

profile of v7, /device:TPU:18, one launch (start us, length us, event | category | flops | bytes accessed | tf_op | source)
XLA Modules:
  0.0 605.1 jit_solution(8118033063161889445)
XLA Ops:
  7.2 0.0 all-gather.3.cloned.1.call-start
  7.2 0.7 all-gather.3.cloned.1.call-update
  7.9 0.0 all-gather.5.cloned.1.call-start
  8.0 0.7 all-gather.5.cloned.1.call-update
  8.7 0.0 reduce-scatter.2.cloned.1.call-start
  8.7 1.8 copy.22
  10.5 1.7 copy.21.segk_ref
  12.2 2.3 copy.24
  14.5 0.6 maximum_bitcast_fusion.rate_ref
  15.1 76.4 %first_gather.1 = (bf16[4,1024,512]{2,1,0:T(8,128)(2,1)}, bf16[3,8,256,512]{3,2,1,0:T(8,128)(2,1)}, f32[1024,128]{1,0:T(8,128)}, f32[1024,128]{1,0:T(8,128)}) custom-call(s32[1024,1]{1,0:T(8,128)} %copy.21.segk_ref, s32[1,1024]{1,0:T(1,128)} %bitcast.12, f32[1,128]{1,0:T(1,128)} %maximum_bitcast_fusion.rate_ref, bf16[1024,512]{1,0:T(8,128)(2,1)} %x_hbm.1, ...), custom_call_target="tpu_custom_call" | custom-call | flops 60000002048 | bytes 14680064 | tf_op jit(solution)/shard_map/first_gather/pallas_call | solution.py:167
  91.5 26.9 %norm_and_project.1 = (bf16[1024,2048]{1,0:T(8,128)(2,1)}, bf16[1024,512]{1,0:T(8,128)(2,1)}, bf16[1024,512]{1,0:T(8,128)(2,1)}, bf16[1024,512]{1,0:T(8,128)(2,1...) custom-call(bf16[4,1024,512]{2,1,0:T(8,128)(2,1)} %get-tuple-element.44.xs_ref.xs_hbm, ...), custom_call_target="tpu_custom_call" | custom-call | flops 20000000000 | bytes 14680064 | tf_op jit(solution)/shard_map/norm_and_project/pallas_call | solution.py:253
  118.4 74.8 %attend.1 = (bf16[4,4,1024,128]{3,2,1,0:T(8,128)(2,1)}, f32[4,1,1024]{2,1,0:T(1,128)}, bf16[8,4,256,512]{3,2,1,0:T(8,128)(2,1)}) custom-call(bf16[1024,512]{1,0:T(8,128)(2,1)} %get-tuple-element.48.q_ref.q_hbm, bf16[1024,512]{1,0:T(8,128)(2,1)} %get-tuple-element.49.k_ref.k_hbm, bf16[1024,512]{1,0:T(8,128)(2,1)} %get-tuple-element.50.v_ref.v_hbm, ...), custom_call_target="tpu_custom_call" | custom-call | flops 70000001024 | bytes 14680064 | tf_op jit(solution)/shard_map/attend/pallas_call | solution.py:356
  193.2 0.0 all-gather.3.cloned.1.call-done.wg_hbm
  193.2 0.0 all-gather.5.cloned.1.call-done.wu_hbm
  193.2 133.2 %feed_forward.1 = (f32[1024,2048]{1,0:T(8,128)}, bf16[1024,2048]{1,0:T(8,128)(2,1)}, bf16[1024,2048]{1,0:T(8,128)(2,1)}, bf16[1024,2048]{1,0:T(8,128)(2,1)}, bf1...) custom-call(bf16[4,4,1024,128]{3,2,1,0:T(8,128)(2,1)} %get-tuple-ele, ...), custom_call_target="tpu_custom_call" | custom-call | flops 120000004096 | bytes 94371840 | tf_op jit(solution)/shard_map/feed_forward/pallas_call | solution.py:868
  326.4 80.5 %norm_terms.1 = (f32[256,2048]{1,0:T(8,128)}, bf16[2048,2048]{1,0:T(8,128)(2,1)}, bf16[2048,2048]{1,0:T(8,128)(2,1)}, f32[2048,256]{1,0:T(8,128)}) custom-call(bf16[1024,2048]{1,0:T(8,128)(2,1)} %get-tuple-element.55.dg_hbm, bf16[1024,2048]{1,0:T(8,128)(2,1)} %get-tuple-element.56.du_hbm, bf16[2048,2048]{1,0:T(8,128)(2,1)} %all-gather.3.cloned.1.call-done.wg_hbm, ...), custom_call_target="tpu_custom_call" | custom-call | flops 89999998976 | bytes 73400320 | tf_op jit(solution)/shard_map/norm_terms/pallas_call | solution.py:1034
  406.9 0.0 reduce-scatter.2.cloned.1.call-update
  407.0 67.2 %attend_back.1 = (bf16[1024,512]{1,0:T(8,128)(2,1)}, bf16[1024,512]{1,0:T(8,128)(2,1)}, bf16[1024,512]{1,0:T(8,128)(2,1)}, f32[256,2048]{1,0:T(8,128)}, bf16[1024,512]{1,0:T(8,128)(2,1)}) custom-call(f32[256,2048]{1,0:T(8,128)} %get-tuple-element.59.sum_ref, f32[4,1,1024]{2,1,0:T(1,128)} %get-tuple-element.60.log_ref, s32[1024,1]{1,0:T(8,128)} %copy.21.segk_ref, ...), custom_call_target="tpu_custom_call" | custom-call | flops 49999998976 | bytes 31457280 | tf_op jit(solution)/shard_map/attend_back/pallas_call | solution.py:1173
  474.2 111.9 %input_terms.1 = (bf16[1024,512]{1,0:T(8,128)(2,1)}, f32[256,512]{1,0:T(8,128)}, f32[256,512]{1,0:T(8,128)}, f32[256,512]{1,0:T(8,128)}, f32[512,256]{1,0:T(8,128)}) custom-call(bf16[1024,512]{1,0:T(8,128)(2,1)} %get-tuple-element.64.dq_ref, bf16[1024,512]{1,0:T(8,128)(2,1)} %get-tuple-element.65.dk_ref, bf16[1024,512]{1,0:T(8,128)(2,1)} %get-tuple-element.66.dv_ref, ...), custom_call_target="tpu_custom_call" | custom-call | flops 80000000000 | bytes 20971520 | tf_op jit(solution)/shard_map/input_terms/pallas_call | solution.py:1409
  586.1 0.0 copy-start.2
  586.1 0.0 copy-start.6
  586.2 0.0 copy-start.5
  586.2 0.0 copy-start.4
  586.2 0.0 reduce-scatter.2.cloned.1.call-done
  586.2 2.9 convert_element_type.3
  589.1 0.0 copy-start.3
  589.1 0.0 copy-start.1
  589.1 2.4 copy.34
  591.6 0.0 copy-done.2
  591.6 1.0 copy.35
  592.5 0.0 copy-done.6
  592.5 0.0 copy-start
  592.5 0.8 copy.36
  593.3 0.0 copy-done.5
  593.3 0.8 copy.37
  594.1 0.0 copy-done.4
  594.1 0.8 copy.38
  594.9 0.0 copy-done.3
  594.9 0.8 copy.39
  595.7 0.0 copy-done.1
  595.7 1.3 copy.40
  597.0 0.0 copy-done
  597.0 1.3 copy.41
  (1 shorter events, 0.0 us)
Async XLA Ops:
  7.2 186.0 %all-gather.3.cloned.1.call-start = ((), (), s32[]{:S(2)}) async-start(), calls=%async_computation.1 | async-start | bytes 9437184 | tf_op jit(solution)/shard_map/all_gather | solution.py:1462
  7.9 185.3 %all-gather.5.cloned.1.call-start = ((), (), s32[]{:S(2)}) async-start(), calls=%async_computation.2 | async-start | bytes 9437184 | tf_op jit(solution)/shard_map/all_gather | solution.py:1462
  8.7 577.5 %reduce-scatter.2.cloned.1.call-start = ((), (), s32[]{:S(2)}) async-start(), calls=%async_computation.3 | async-start | bytes 9437184 | tf_op jit(solution)/shard_map/reduce_scatter | solution.py:1475
  586.1 5.4 copy-start.2
  586.1 6.4 %copy-start.6 = (f32[256,512]{1,0:T(8,128)S(1)}, f32[256,512]{1,0:T(8,128)}, u32[]{:S(2)}) copy-start(f32[256,512]{1,0:T(8,128)} %get-tuple-element.90) | copy-start | bytes 1572868
  586.2 7.2 %copy-start.5 = (f32[256,512]{1,0:T(8,128)S(1)}, f32[256,512]{1,0:T(8,128)}, u32[]{:S(2)}) copy-start(f32[256,512]{1,0:T(8,128)} %get-tuple-element.91) | copy-start | bytes 1572868
  586.2 8.0 %copy-start.4 = (f32[256,512]{1,0:T(8,128)S(1)}, f32[256,512]{1,0:T(8,128)}, u32[]{:S(2)}) copy-start(f32[256,512]{1,0:T(8,128)} %get-tuple-element.92) | copy-start | bytes 1572868
  589.1 5.8 copy-start.3
  589.1 6.6 %copy-start.1 = (f32[256,2048]{1,0:T(8,128)S(1)}, f32[256,2048]{1,0:T(8,128)}, u32[]{:S(2)}) copy-start(f32[256,2048]{1,0:T(8,128)} %get-tuple-element.94) | copy-start | bytes 6291460
  592.5 4.5 copy-start
Sparse Core Ops, SparseCore 0:
  9.9 79.3 all-gather.2
  91.2 75.8 all-gather.4
  407.1 93.0 reduce-scatter.1

commit v8 on v7

--- a/solution.py
+++ b/solution.py
@@ -93,7 +93,8 @@
 
 
 def gather_kernel(
-    R, C, segk_ref, segq_ref, rate_ref, x_ref, wq_ref, wk_ref, wv_ref, xs_ref, w_ref, cos_ref, sin_ref,
+    R, C, segq_ref, rate_ref, wo_ref, wd_ref, x_ref, wq_ref, wk_ref, wv_ref,
+    xs_ref, w_ref, cos_ref, sin_ref, segk_ref, wo_turned, wd_turned,
     local, x_send, x_recv, w_send, w_recv, f_send, f_recv,
 ):
     me, right, left = ring_places(C)
@@ -126,10 +127,12 @@
     def table_rows(i, carry):
         rows = pl.ds(pl.multiple_of(i * size, size), size)
         first = SEQ * lax.div(i * size, SEQ)
+        here = jnp.broadcast_to(segq_ref[:, rows].astype(F32), (size, size)).T[:, :1]
+        segk_ref[rows, :] = here.astype(jnp.int32)
         shape = (size, T)
         queries = lax.broadcasted_iota(jnp.int32, shape, 0) + i * size
         keys = lax.broadcasted_iota(jnp.int32, shape, 1)
-        seen = (segk_ref[rows, :] == segq_ref[...]) & (keys <= queries) & (keys >= first)
+        seen = (here == segq_ref[...].astype(F32)) & (keys <= queries) & (keys >= first)
         place = jnp.sum(jnp.where(seen, 1.0, 0.0), axis=1, keepdims=True) - 1.0
         angles = place * rate_ref[...]
         lane = lax.broadcasted_iota(jnp.int32, angles.shape, 1)
@@ -139,6 +142,17 @@
         return carry
 
     lax.fori_loop(0, T // size, table_rows, 0)
+
+    def turn_rows(source, target):
+        def body(i, carry):
+            cut = pl.ds(pl.multiple_of(i * size, size), size)
+            target[:, cut] = source[cut, :].astype(F32).T.astype(BF)
+            return carry
+
+        lax.fori_loop(0, source.shape[0] // size, body, 0)
+
+    turn_rows(wo_ref, wo_turned)
+    turn_rows(wd_ref, wd_turned)
     for s in range(1, C - 1):
         x_copies[s - 1].wait_recv()
         x_copies[s].start()
@@ -158,7 +172,7 @@
         copy.wait()
 
 
-def first_gather(R, C, seg_column, seg_row, tokens, w_query, w_key, w_value):
+def first_gather(R, C, seg_row, tokens, w_query, w_key, w_value, w_out, w_down):
     depth, width = w_query.shape
     T = tokens.shape[0]
     half = R // 2
@@ -166,13 +180,16 @@
     rate = jnp.concatenate([rate, rate]).reshape(1, HEAD_DIM)
     return pl.pallas_call(
         functools.partial(gather_kernel, R, C),
-        in_specs=[VMEM_SPEC] * 3 + [ANY] * 4,
-        out_specs=[ANY] * 2 + [VMEM_SPEC] * 2,
+        in_specs=[VMEM_SPEC] * 4 + [ANY] * 4,
+        out_specs=[ANY] * 2 + [VMEM_SPEC] * 5,
         out_shape=[
             struct((C,) + tokens.shape, BF),
             struct((3, R, depth, width), BF),
             struct((T, HEAD_DIM), F32),
             struct((T, HEAD_DIM), F32),
+            struct((T, 1), jnp.int32),
+            struct(w_out.shape[::-1], BF),
+            struct(w_down.shape[::-1], BF),
         ],
         scratch_shapes=[
             DMA((4,)),
@@ -186,7 +203,7 @@
         compiler_params=comm_params(0),
         cost_estimate=cost(6e10, 14 * MIB),
         name="first_gather",
-    )(seg_column, seg_row, rate, tokens, w_query, w_key, w_value)
+    )(seg_row, rate, w_out, w_down, tokens, w_query, w_key, w_value)
 
 
 def norm_rows(x):
@@ -676,9 +693,9 @@
 
 def feed_kernel(
     R, C, os_hbm, w_hbm, xs_hbm, wg_hbm, wu_hbm, wd_hbm, dy_hbm,
-    h_hbm, b_hbm, dg_hbm, du_hbm, dys_hbm, grad_hbm, down_hbm, y_ref,
-    big, hidden, slope, silu, b, gates, ups, terms, rising, falling, dys, stage, h, h_mine,
-    load, block_load, tile_load, store, w_send, w_recv, f_send, f_recv, *semaphores,
+    h_hbm, b_hbm, dg_hbm, du_hbm, dys_hbm, down_hbm, y_ref, grad_ref,
+    big, hidden, slope, silu, b, gates, ups, terms, rising, falling, dys, h, exchanged, arrived,
+    load, block_load, tile_load, store, h_load, w_send, w_recv, f_send, f_recv, *semaphores,
 ):
     me = lax.axis_index("col")
     row, ahead, behind, other = row_places(R)
@@ -690,6 +707,11 @@
     up, down = semaphores[:2], semaphores[2:4]
     gather = LineGather(C, dy_hbm, dys, up, down)
     sums = LineSum(C, terms, rising, falling, semaphores[4:6], semaphores[6:8])
+    place = row_of(R)
+    row_sums = RowSum(
+        R, lambda i: big.at[place(i), :, pl.ds(0, F)], lambda i: big.at[place(i, True), :, pl.ds(0, F)],
+        exchanged, arrived, semaphores[8:],
+    )
 
     def began(source, target, semaphore):
         copy = pltpu.make_async_copy(source, target, semaphore)
@@ -754,13 +776,16 @@
             columns = slice(j * width, (j + 1) * width)
             right = big[j * group : (j + 1) * group, :, :D].reshape(width, D)
             h[:, columns] = slope[rows, columns].astype(F32) + dot_nt(left, right)
-        h_mine[rows, :] = h[:, mine]
         values = h[...]
         centre, inverse = norm_rows(values)
         b[rows, :] = ((values - centre) * inverse).astype(BF)
         stores.append(began(h, h_hbm.at[rows, :], store.at[0]))
     stores[-1].wait()
     b_out = began(b, b_hbm, store.at[1])
+    h_back = [
+        began(h_hbm.at[pl.ds(i * size, size), mine], h.at[:, pl.ds(i * width, width)], h_load.at[i])
+        for i in range(T // size)
+    ]
     for i in range(tiles):
         cut = slice(i * bf, (i + 1) * bf)
         for copy in tile_in(i):
@@ -819,38 +844,45 @@
     saved.append(began(slope.at[:, pl.ds(0, F)], dg_hbm, store.at[2]))
     saved.append(began(silu.at[:, pl.ds(0, F)], du_hbm, store.at[3]))
 
-    def grads(first, stop):
-        copies = []
-        for j in range(first, stop):
-            if len(copies) >= 2:
-                copies[-2].wait()
-            stage[j % 2] = dot_tn(dys[j], hidden[:, :F]).astype(BF)
-            copies.append(began(stage.at[j % 2], grad_hbm.at[pl.ds(j * width, width), :], load.at[j % 2]))
-        for copy in copies[-2:]:
-            copy.wait()
-
-    grads(0, C // 2)
+    for slot in row_sums.order():
+        chip = lax.div(place(slot), 2)
+        product = dot_tn(dys[chip], hidden[:, :F]).astype(BF)
+        for n in range(2):
+            big[2 * chip + n, :, :F] = product[n * depth : (n + 1) * depth]
+        row_sums.exchange(slot).start()
+    row_sums.relay()
     for t in range(2, C - 1):
         sums.level(t)
-    grads(C // 2, C)
+    row_sums.relay_again()
     sums.level(C - 1)
     last = C - 1
-    y_ref[...] = terms[me]
+    for copy in h_back:
+        copy.wait()
+
+    def result(more):
+        for i in range(T // size):
+            rows = pl.ds(i * size, size)
+            total = h[:, i * width : (i + 1) * width] + terms[me, rows, :].astype(F32)
+            for buffer, slot in more:
+                total += buffer[slot, rows, :].astype(F32)
+            y_ref[rows, :] = total.astype(BF)
 
     @pl.when(me == 0)
     def _():
-        y_ref[...] = (h_mine[...] + terms[me].astype(F32) + falling[0].astype(F32)).astype(BF)
+        result([(falling, 0)])
 
     @pl.when(me == last)
     def _():
-        y_ref[...] = (h_mine[...] + terms[me].astype(F32) + rising[0].astype(F32)).astype(BF)
+        result([(rising, 0)])
 
     @pl.when((me > 0) & (me < last))
     def _():
-        y_ref[...] = (
-            h_mine[...] + terms[me].astype(F32) + rising[last - me].astype(F32) + falling[me].astype(F32)
-        ).astype(BF)
-
+        result([(rising, last - me), (falling, me)])
+
+    def write(part, values):
+        grad_ref[:, part] = values.T
+
+    row_sums.finish(write, 128)
     sums.finish()
     gather.finish()
     for copy in spread + forward:
@@ -868,16 +900,16 @@
     return pl.pallas_call(
         functools.partial(feed_kernel, R, C),
         in_specs=[ANY] * 7,
-        out_specs=[ANY] * 7 + [VMEM_SPEC],
+        out_specs=[ANY] * 6 + [VMEM_SPEC] * 2,
         out_shape=[
             struct((T, D), F32),
             struct((T, D), BF),
             struct((T, F), BF),
             struct((T, F), BF),
             struct((C, T, width), BF),
-            struct((D, F), BF),
             struct((R, D // R, F), BF),
             struct((T, width), BF),
+            struct((F, D // R), F32),
         ],
         scratch_shapes=[
             pltpu.VMEM((R, D // R, most), BF),
@@ -891,20 +923,23 @@
             pltpu.VMEM((C - 1, T, width), BF),
             pltpu.VMEM((C - 1, T, width), BF),
             pltpu.VMEM((C, T, width), BF),
-            pltpu.VMEM((2, width, F), BF),
             pltpu.VMEM((256, D), F32),
-            pltpu.VMEM((T, width), F32),
+        ]
+        + row_sum_buffers(R, D // R, F)
+        + [
             DMA((R + 2,)),
             DMA((T // 256, C * heads + C)),
             DMA((2, 2)),
             DMA((4,)),
+            DMA((T // 256,)),
             DMA((R // 2,)),
             DMA((R // 2,)),
             DMA((R // 2,)),
             DMA((R // 2,)),
         ]
         + line_semaphores(C)
-        + line_semaphores(C),
+        + line_semaphores(C)
+        + row_sum_semaphores(R),
         compiler_params=comm_params(2, 63),
         cost_estimate=cost(1.2e11, 90 * MIB),
         name="feed_forward",
@@ -912,10 +947,10 @@
 
 
 def norm_terms_kernel(
-    R, C, dg_hbm, du_hbm, wg_hbm, wu_hbm, b_hbm, down_hbm,
-    sum_ref, gate_hbm, up_hbm, down_ref,
-    dg, du, wg, wu, b, terms, held, stage, own, exchanged, arrived,
-    load, tile_load, store, own_load, send, recv, *semaphores,
+    R, C, dg_hbm, du_hbm, wg_hbm, wu_hbm, b_hbm,
+    sum_ref, up_hbm, gate_ref,
+    dg, du, wg, wu, b, terms, held, stage, exchanged, arrived,
+    load, tile_load, store, send, recv, *semaphores,
 ):
     me, right, left = ring_places(C)
     D, F = wg.shape
@@ -945,12 +980,13 @@
                     (fetch(wg_hbm.at[cut, :], wg.at[cut, :], tile_load.at[2 * n]), fetch(wu_hbm.at[cut, :], wu.at[cut, :], tile_load.at[2 * n + 1]))
                 )
     b_in = fetch(b_hbm, b, load.at[2 * C])
-    sums, own_loads = held_row_sum(R, down_hbm, own, exchanged, arrived, own_load, semaphores)
-    for copy in own_loads:
-        copy.start()
+    place, depth = row_of(R), D // R
+
+    def block(places):
+        return wu.at[pl.ds(pl.multiple_of(places * depth, depth), depth), :]
+
+    sums = RowSum(R, lambda i: block(place(i)), lambda i: block(place(i, True)), exchanged, arrived, semaphores)
     greet([{"col": left}] + sums.peers, 1 + len(sums.peers))
-    for slot in sums.order():
-        sums.exchange(slot).start()
 
     def term_tile(s, part, n):
         cut = pl.ds(pl.multiple_of(n * width, width), width)
@@ -975,7 +1011,6 @@
                     copy.wait()
                 term_tile(s, part, n)
             moves(0).start()
-            sums.relay(lambda slot: own_loads[slot].wait())
         else:
 
             def body(n, carry):
@@ -1010,32 +1045,35 @@
     for step in range(1, middle + 1):
         if step < C - 1:
             pass_on(step)
-    product(dg, gate_hbm)
-    sums.relay_again()
+    for slot in sums.order():
+        cut = pl.ds(pl.multiple_of(lax.div(place(slot), 2) * 2 * depth, 2 * depth), 2 * depth)
+        wu[cut, :] = dot_tn(b[:, cut], dg[...]).astype(BF)
+        sums.exchange(slot).start()
+    sums.relay()
     product(du, up_hbm)
     for step in range(middle + 1, C - 1):
         pass_on(step)
+    sums.relay_again()
 
     def write(part, values):
-        down_ref[:, part] = values.T
-
-    sums.finish(write, 128)
+        gate_ref[part, :] = values
+
+    sums.finish(write)
     moves(C - 2).wait_recv()
     sum_ref[...] = held[C - 2].astype(F32) + terms[C - 1].astype(F32)
     for step in range(C - 1):
         moves(step).wait_send()
 
 
-def norm_terms(R, C, dg, du, w_gate, w_up, b, grad_down):
+def norm_terms(R, C, dg, du, w_gate, w_up, b):
     T, F = dg.shape
     D = w_gate.shape[0]
     rows, width = T // C, D // C
-    depth, columns = grad_down.shape[1:]
     return pl.pallas_call(
         functools.partial(norm_terms_kernel, R, C),
-        in_specs=[ANY] * 6,
-        out_specs=[VMEM_SPEC, ANY, ANY, VMEM_SPEC],
-        out_shape=[struct((rows, D), F32), struct((D, F), BF), struct((D, F), BF), struct((columns, depth), F32)],
+        in_specs=[ANY] * 5,
+        out_specs=[VMEM_SPEC, ANY, VMEM_SPEC],
+        out_shape=[struct((rows, D), F32), struct((D, F), BF), struct((D // R, F), F32)],
         scratch_shapes=[
             pltpu.VMEM((T, F), BF),
             pltpu.VMEM((T, F), BF),
@@ -1045,14 +1083,12 @@
             pltpu.VMEM((C, rows, D), BF),
             pltpu.VMEM((C - 1, rows, D), BF),
             pltpu.VMEM((2, width, F), BF),
-            pltpu.VMEM((R // 2, depth, columns), BF),
         ]
-        + row_sum_buffers(R, depth, columns)
+        + row_sum_buffers(R, D // R, F)
         + [
             DMA((2 * C + 1,)),
             DMA((2 * C,)),
             DMA((2,)),
-            DMA((R // 2,)),
             DMA((C - 1,)),
             DMA((C - 1,)),
         ]
@@ -1060,7 +1096,7 @@
         compiler_params=comm_params(3, 63),
         cost_estimate=cost(9e10, 70 * MIB),
         name="norm_terms",
-    )(dg, du, w_gate, w_up, b, grad_down)
+    )(dg, du, w_gate, w_up, b)
 
 
 def attend_back_kernel(
@@ -1462,19 +1498,20 @@
     gathered = lambda w: lax.all_gather(w, "row", axis=0, tiled=True)
 
     gate_w, up_w = gathered(w_gate), gathered(w_up)
-    seg_column, seg_row = segments.reshape(T, 1), segments.reshape(1, T)
-    xs, w_qkv, cos_table, sin_table = first_gather(R, C, seg_column, seg_row, tokens, w_query, w_key, w_value)
+    seg_row = segments.reshape(1, T)
+    xs, w_qkv, cos_table, sin_table, seg_column, out_part, down_part = first_gather(
+        R, C, seg_row, tokens, w_query, w_key, w_value, w_out, w_down
+    )
     w_qkv = w_qkv.reshape(3, D, width)
-    act_one, q, k, v, mu_one, r_one, out_part = norm_and_project(xs, w_qkv, cos_table, sin_table, w_out.T)
+    act_one, q, k, v, mu_one, r_one, out_part = norm_and_project(xs, w_qkv, cos_table, sin_table, out_part)
     os, log_total, out_w = attend(R, C, q, k, v, seg_column, seg_row, out_part)
-    h_full, act_two, dg, du, dys, grad_down, _, output = feed_forward(
-        R, C, os, out_w, xs, gate_w, up_w, w_down.T, cotangent
+    h_full, act_two, dg, du, dys, _, output, grad_down = feed_forward(
+        R, C, os, out_w, xs, gate_w, up_w, down_part, cotangent
     )
-    by_row = lambda values: values.reshape(R, D // R, -1)
-    total, grad_gate, grad_up, grad_down = norm_terms(R, C, dg, du, gate_w, up_w, act_two, by_row(grad_down))
-    grad_up = lax.psum_scatter(grad_up, "row", scatter_dimension=0, tiled=True).astype(F32)
-    dq, dk, dv, grad_gate, dh = attend_back(
-        R, total, log_total, seg_column, seg_row, cos_table, sin_table, q, k, v, h_full, dys, out_w, by_row(grad_gate)
+    total, grad_up, grad_gate = norm_terms(R, C, dg, du, gate_w, up_w, act_two)
+    grad_up = grad_up.reshape(R, D // R, -1)
+    dq, dk, dv, grad_up, dh = attend_back(
+        R, total, log_total, seg_column, seg_row, cos_table, sin_table, q, k, v, h_full, dys, out_w, grad_up
     )
     grad_tokens, grad_query, grad_key, grad_value, grad_out = input_terms(
         R, C, dq, dk, dv, w_qkv, act_one, tokens, dh, mu_one, r_one, os

time: 610 us -> 601 us (0.985)
  the two profiles are of different devices: /device:TPU:18 before, /device:TPU:8 now
where the time goes in v8:
time: 601 us; the launch traced here: 594 us
  Pallas kernels  565 us (94%)
  between operations  14.4 us (2%)
  local copies, waits for them, and re-layouts  11.8 us (2%)
    pallas_call x1, Pallas kernels, feed_forward(): pl.pallas_call(functools.partial(feed_kernel, R, C), in_specs=[ANY] * 7,...  142 us
    pallas_call x1, Pallas kernels, input_terms(): pl.pallas_call(functools.partial(input_terms_kernel, R, C), in_specs=[VME...  101 us
    pallas_call x1, Pallas kernels, norm_terms(): pl.pallas_call(functools.partial(norm_terms_kernel, R, C), in_specs=[ANY]...  83.3 us
    pallas_call x1, Pallas kernels, first_gather(): pl.pallas_call(functools.partial(gather_kernel, R, C), in_specs=[VMEM_SPE...  78.3 us
    pallas_call x1, Pallas kernels, attend(): pl.pallas_call(functools.partial(attend_kernel, R, C), in_specs=[VMEM_SPE...  77.8 us
    pallas_call x1, Pallas kernels, attend_back(): pl.pallas_call(functools.partial(attend_back_kernel, R, C), in_specs=[VME...  57.5 us
    pallas_call x1, Pallas kernels, norm_and_project(): pl.pallas_call(functools.partial(qkv_kernel, C), grid=(T // bt,), in_spec...  25.7 us
  transfers between devices with their start and end apart: 2, of which 0 were waited for; matrix products, arithmetic and copies ran while one was open for 0% of the time, Pallas kernels for 31%

profile of v8, /device:TPU:8, one launch (start us, length us, event | category | flops | bytes accessed | tf_op | source)
XLA Modules:
  0.0 593.7 jit_solution(14929893918219255926)
XLA Ops:
  7.2 0.0 all-gather.3.cloned.1.call-start
  7.2 0.7 all-gather.3.cloned.1.call-update
  7.9 0.0 all-gather.5.cloned.1.call-start
  8.0 0.7 all-gather.5.cloned.1.call-update
  8.7 0.6 maximum_bitcast_fusion.rate_ref
  9.3 78.3 %first_gather.1 = (bf16[4,1024,512]{2,1,0:T(8,128)(2,1)}, bf16[3,8,256,512]{3,2,1,0:T(8,128)(2,1)}, f32[1024,128]{1,0:T(8,128)}, f32[1024,128]{1,0:T(8,128)}, s3...) custom-call(s32[1,1024]{1,0:T(1,128)} %bitcast.5, f32[1,128]{1,0:T(1,128)} %maximum_bitcast_fusion.rate_ref, ...), custom_call_target="tpu_custom_call" | custom-call | flops 60000002048 | bytes 14680064 | tf_op jit(solution)/shard_map/first_gather/pallas_call | solution.py:181
  87.6 25.7 %norm_and_project.1 = (bf16[1024,2048]{1,0:T(8,128)(2,1)}, bf16[1024,512]{1,0:T(8,128)(2,1)}, bf16[1024,512]{1,0:T(8,128)(2,1)}, bf16[1024,512]{1,0:T(8,128)(2,1...) custom-call(bf16[4,1024,512]{2,1,0:T(8,128)(2,1)} %get-tuple-element.46.xs_ref.xs_hbm, ...), custom_call_target="tpu_custom_call" | custom-call | flops 20000000000 | bytes 14680064 | tf_op jit(solution)/shard_map/norm_and_project/pallas_call | solution.py:270
  113.3 77.8 %attend.1 = (bf16[4,4,1024,128]{3,2,1,0:T(8,128)(2,1)}, f32[4,1,1024]{2,1,0:T(1,128)}, bf16[8,4,256,512]{3,2,1,0:T(8,128)(2,1)}) custom-call(bf16[1024,512]{1,0:T(8,128)(2,1)} %get-tuple-element.51.q_ref.q_hbm, bf16[1024,512]{1,0:T(8,128)(2,1)} %get-tuple-element.52.k_ref.k_hbm, bf16[1024,512]{1,0:T(8,128)(2,1)} %get-tuple-element.53.v_ref.v_hbm, ...), custom_call_target="tpu_custom_call" | custom-call | flops 70000001024 | bytes 14680064 | tf_op jit(solution)/shard_map/attend/pallas_call | solution.py:373
  191.2 0.0 all-gather.3.cloned.1.call-done.wg_hbm
  191.2 0.0 all-gather.5.cloned.1.call-done.wu_hbm
  191.2 142.0 %feed_forward.1 = (f32[1024,2048]{1,0:T(8,128)}, bf16[1024,2048]{1,0:T(8,128)(2,1)}, bf16[1024,2048]{1,0:T(8,128)(2,1)}, bf16[1024,2048]{1,0:T(8,128)(2,1)}, bf1...) custom-call(bf16[4,4,1024,128]{3,2,1,0:T(8,128)(2,1)} %get-tuple-ele, ...), custom_call_target="tpu_custom_call" | custom-call | flops 120000004096 | bytes 94371840 | tf_op jit(solution)/shard_map/feed_forward/pallas_call | solution.py:900
  333.2 83.3 %norm_terms.1 = (f32[256,2048]{1,0:T(8,128)}, bf16[2048,2048]{1,0:T(8,128)(2,1)}, f32[256,2048]{1,0:T(8,128)}) custom-call(bf16[1024,2048]{1,0:T(8,128)(2,1)} %get-tuple-element.60.dg_hbm, bf16[1024,2048]{1,0:T(8,128)(2,1)} %get-tuple-element.61.du_hbm, bf16[2048,2048]{1,0:T(8,128)(2,1)} %all-gather.3.cloned.1.call-done.wg_hbm, ...), custom_call_target="tpu_custom_call" | custom-call | flops 89999998976 | bytes 73400320 | tf_op jit(solution)/shard_map/norm_terms/pallas_call | solution.py:1072
  416.5 57.5 %attend_back.1 = (bf16[1024,512]{1,0:T(8,128)(2,1)}, bf16[1024,512]{1,0:T(8,128)(2,1)}, bf16[1024,512]{1,0:T(8,128)(2,1)}, f32[256,2048]{1,0:T(8,128)}, bf16[1024,512]{1,0:T(8,128)(2,1)}) custom-call(f32[256,2048]{1,0:T(8,128)} %get-tuple-element.63.sum_ref, f32[4,1,1024]{2,1,0:T(1,128)} %get-tuple-element.64.log_ref, s32[1024,1]{1,0:T(8,128)} %get-tuple-element.54.segk_ref, ...), custom_call_target="tpu_custom_call" | custom-call | flops 49999998976 | bytes 31457280 | tf_op jit(solution)/shard_map/attend_back/pallas_call | solution.py:1209
  474.1 100.6 %input_terms.1 = (bf16[1024,512]{1,0:T(8,128)(2,1)}, f32[256,512]{1,0:T(8,128)}, f32[256,512]{1,0:T(8,128)}, f32[256,512]{1,0:T(8,128)}, f32[512,256]{1,0:T(8,128)}) custom-call(bf16[1024,512]{1,0:T(8,128)(2,1)} %get-tuple-element.68.dq_ref, bf16[1024,512]{1,0:T(8,128)(2,1)} %get-tuple-element.69.dk_ref, bf16[1024,512]{1,0:T(8,128)(2,1)} %get-tuple-element.70.dv_ref, ...), custom_call_target="tpu_custom_call" | custom-call | flops 80000000000 | bytes 20971520 | tf_op jit(solution)/shard_map/input_terms/pallas_call | solution.py:1445
  574.7 0.0 copy-start.6
  574.7 0.0 copy-start.5
  574.7 0.0 copy-start.4
  574.7 0.0 copy-start.3
  574.7 0.0 copy-start.1
  574.7 2.4 copy.28
  577.2 2.3 copy.29
  579.4 0.0 copy-done.6
  579.4 0.0 copy-start.2
  579.4 0.8 copy.30
  580.2 0.0 copy-done.5
  580.2 0.8 copy.31
  581.0 0.0 copy-done.4
  581.0 0.8 copy.32
  581.8 0.0 copy-done.3
  581.8 0.8 copy.33
  582.6 0.0 copy-done.1
  582.6 0.0 copy-start
  582.6 1.3 copy.34
  583.9 0.0 copy-done.2
  583.9 1.3 copy.35
  585.2 0.0 copy-done
  585.3 1.3 copy.36
  (1 shorter events, 0.0 us)
Async XLA Ops:
  7.2 184.0 %all-gather.3.cloned.1.call-start = ((), (), s32[]{:S(2)}) async-start(), calls=%async_computation | async-start | bytes 9437184 | tf_op jit(solution)/shard_map/all_gather | solution.py:1498
  7.9 183.3 %all-gather.5.cloned.1.call-start = ((), (), s32[]{:S(2)}) async-start(), calls=%async_computation.1 | async-start | bytes 9437184 | tf_op jit(solution)/shard_map/all_gather | solution.py:1498
  574.7 4.7 copy-start.6
  574.7 5.5 copy-start.5
  574.7 6.3 %copy-start.4 = (f32[256,512]{1,0:T(8,128)S(1)}, f32[256,512]{1,0:T(8,128)}, u32[]{:S(2)}) copy-start(f32[256,512]{1,0:T(8,128)} %get-tuple-element.96) | copy-start | bytes 1572868
  574.7 7.1 %copy-start.3 = (f32[512,256]{1,0:T(8,128)S(1)}, f32[512,256]{1,0:T(8,128)}, u32[]{:S(2)}) copy-start(f32[512,256]{1,0:T(8,128)} %get-tuple-element.97) | copy-start | bytes 1572868
  574.7 7.9 %copy-start.1 = (f32[256,2048]{1,0:T(8,128)S(1)}, f32[256,2048]{1,0:T(8,128)}, u32[]{:S(2)}) copy-start(f32[256,2048]{1,0:T(8,128)} %get-tuple-element.98) | copy-start | bytes 6291460
  579.4 4.5 copy-start.2
  582.6 2.6 copy-start
Sparse Core Ops, SparseCore 0:
  9.9 77.2 all-gather.2
  89.1 99.5 all-gather.4

commit v9 on v8

--- a/solution.py
+++ b/solution.py
@@ -82,14 +82,40 @@
     return row, ahead, behind, other
 
 
-def gather_ring(C, source, whole, send, recv):
-    me, right, left = ring_places(C)
-    copies = []
-    for step in range(C - 1):
-        owner = lax.rem(me - step + C, C)
-        piece = source if step == 0 else whole.at[owner]
-        copies.append(remote(piece, whole.at[owner], send.at[step], recv.at[step], col=right))
-    return copies
+class GatherRing:
+    def __init__(self, C, source, whole, send, recv):
+        me, right, left = ring_places(C)
+        self.C = C
+        size = source.shape[0] // 2
+        self.copies = []
+        for step in range(C - 1):
+            owner = lax.rem(me - step + C, C)
+            pair = []
+            for half in range(2):
+                rows = pl.ds(half * size, size)
+                piece = source.at[rows, :] if step == 0 else whole.at[owner, rows, :]
+                pair.append(
+                    remote(piece, whole.at[owner, rows, :], send.at[step, half], recv.at[step, half], col=right)
+                )
+            self.copies.append(pair)
+
+    def start(self):
+        for copy in self.copies[0]:
+            copy.start()
+
+    def pass_on(self, step):
+        for half in range(2):
+            self.copies[step - 1][half].wait_recv()
+            self.copies[step][half].start()
+
+    def arrived(self):
+        for copy in self.copies[-1]:
+            copy.wait_recv()
+
+    def sent(self):
+        for pair in self.copies:
+            for copy in pair:
+                copy.wait_send()
 
 
 def gather_kernel(
@@ -110,8 +136,8 @@
         1 + R // 2,
     )
 
-    x_copies = gather_ring(C, x_ref, xs_ref, x_send, x_recv)
-    x_copies[0].start()
+    ring = GatherRing(C, x_ref, xs_ref, x_send, x_recv)
+    ring.start()
     spread, forward = [], []
     for i, w in enumerate(weights):
         for k in range(1, R // 2):
@@ -154,8 +180,7 @@
     turn_rows(wo_ref, wo_turned)
     turn_rows(wd_ref, wd_turned)
     for s in range(1, C - 1):
-        x_copies[s - 1].wait_recv()
-        x_copies[s].start()
+        ring.pass_on(s)
     for i in range(3):
         for k in range(1, R // 2):
             spread[i * (R // 2 - 1) + k - 1].wait_recv()
@@ -163,10 +188,11 @@
             copy = remote(block, block, f_send.at[i, k], f_recv.at[i, k], row=other)
             copy.start()
             forward.append(copy)
-    x_copies[-1].wait_recv()
+    ring.arrived()
     for copy in forward:
         copy.wait_recv()
-    for copy in x_copies + spread + forward:
+    ring.sent()
+    for copy in spread + forward:
         copy.wait_send()
     for copy in mine:
         copy.wait()
@@ -193,8 +219,8 @@
         ],
         scratch_shapes=[
             DMA((4,)),
-            DMA((C - 1,)),
-            DMA((C - 1,)),
+            DMA((C - 1, 2)),
+            DMA((C - 1, 2)),
             DMA((3, half)),
             DMA((3, half)),
             DMA((3, half)),
@@ -222,21 +248,18 @@
 ):
     step, steps = pl.program_id(0), pl.num_programs(0)
     me, right, left = ring_places(C)
-    copies = gather_ring(C, wo_ref, wos_ref, send, recv)
+    ring = GatherRing(C, wo_ref, wos_ref, send, recv)
     mine = pltpu.make_async_copy(wo_ref, wos_ref.at[me], local.at[0])
 
     @pl.when(step == 0)
     def _():
         mine.start()
         greet([{"col": left}], 1)
-        copies[0].start()
-
-    for s in range(1, C - 1):
-
-        @pl.when(step == jnp.minimum(2 * s, steps - 1))
-        def _():
-            copies[s - 1].wait_recv()
-            copies[s].start()
+        ring.start()
+
+    @pl.when(step == steps // 2)
+    def _():
+        ring.pass_on(1)
 
     x = beside(xs_ref).astype(F32)
     centre, inverse = norm_rows(x)
@@ -256,9 +279,10 @@
 
     @pl.when(step == steps - 1)
     def _():
-        copies[-1].wait_recv()
-        for copy in copies:
-            copy.wait_send()
+        for s in range(2, C - 1):
+            ring.pass_on(s)
+        ring.arrived()
+        ring.sent()
         mine.wait()
 
 
@@ -287,7 +311,7 @@
             struct((T, 1), F32),
             struct((C,) + w_out.shape, BF),
         ],
-        scratch_shapes=[DMA((1,)), DMA((C - 1,)), DMA((C - 1,))],
+        scratch_shapes=[DMA((1,)), DMA((C - 1, 2)), DMA((C - 1, 2))],
         compiler_params=comm_params(7),
         cost_estimate=cost(2e10, 14 * MIB),
         name="norm_and_project",
@@ -395,9 +419,39 @@
     )(q, k, v, seg_column, seg_row, w_part)
 
 
-def ring_step(step, C, right, first, held, send, recv):
-    source = first if step == 0 else held.at[step - 1]
-    return remote(source, held.at[step], send.at[step], recv.at[step], col=right)
+class SumRing:
+    def __init__(self, C, terms, held, send, recv):
+        me, right, left = ring_places(C)
+        self.C, self.terms, self.held, self.send, self.recv, self.right = C, terms, held, send, recv, right
+        self.size = held.shape[1] // 2
+
+    def part(self, ref, slot, half):
+        return ref.at[slot, pl.ds(half * self.size, self.size), :]
+
+    def copy(self, step, half):
+        source = self.part(self.terms, 0, half) if step == 0 else self.part(self.held, step - 1, half)
+        return remote(
+            source, self.part(self.held, step, half), self.send.at[step, half], self.recv.at[step, half], col=self.right
+        )
+
+    def start(self):
+        for half in range(2):
+            self.copy(0, half).start()
+
+    def pass_on(self, step):
+        for half in range(2):
+            self.copy(step - 1, half).wait_recv()
+            add_into(self.part(self.held, step - 1, half), self.part(self.terms, step, half))
+            self.copy(step, half).start()
+
+    def arrived(self):
+        for half in range(2):
+            self.copy(self.C - 2, half).wait_recv()
+
+    def sent(self):
+        for step in range(self.C - 1):
+            for half in range(2):
+                self.copy(step, half).wait_send()
 
 
 def add_into(held, terms):
@@ -880,7 +934,7 @@
         result([(rising, last - me), (falling, me)])
 
     def write(part, values):
-        grad_ref[:, part] = values.T
+        grad_ref[:, part] = values.T.astype(BF)
 
     row_sums.finish(write, 128)
     sums.finish()
@@ -909,7 +963,7 @@
             struct((C, T, width), BF),
             struct((R, D // R, F), BF),
             struct((T, width), BF),
-            struct((F, D // R), F32),
+            struct((F, D // R), BF),
         ],
         scratch_shapes=[
             pltpu.VMEM((R, D // R, most), BF),
@@ -993,13 +1047,7 @@
         total = dot_nt(dg[part, :], wg[cut, :]) + dot_nt(du[part, :], wu[cut, :])
         terms[s, :, cut] = total.astype(BF)
 
-    def moves(step):
-        return ring_step(step, C, right, terms.at[0], held, send, recv)
-
-    def pass_on(step):
-        moves(step - 1).wait_recv()
-        add_into(held.at[step - 1], terms.at[step])
-        moves(step).start()
+    ring = SumRing(C, terms, held, send, recv)
 
     for s in range(C):
         part = chunk(s)
@@ -1010,7 +1058,7 @@
                 for copy in weights_in[n]:
                     copy.wait()
                 term_tile(s, part, n)
-            moves(0).start()
+            ring.start()
         else:
 
             def body(n, carry):
@@ -1044,7 +1092,7 @@
     middle = max(1, (C - 1) // 2)
     for step in range(1, middle + 1):
         if step < C - 1:
-            pass_on(step)
+            ring.pass_on(step)
     for slot in sums.order():
         cut = pl.ds(pl.multiple_of(lax.div(place(slot), 2) * 2 * depth, 2 * depth), 2 * depth)
         wu[cut, :] = dot_tn(b[:, cut], dg[...]).astype(BF)
@@ -1052,17 +1100,16 @@
     sums.relay()
     product(du, up_hbm)
     for step in range(middle + 1, C - 1):
-        pass_on(step)
+        ring.pass_on(step)
     sums.relay_again()
 
     def write(part, values):
-        gate_ref[part, :] = values
+        gate_ref[part, :] = values.astype(BF)
 
     sums.finish(write)
-    moves(C - 2).wait_recv()
+    ring.arrived()
     sum_ref[...] = held[C - 2].astype(F32) + terms[C - 1].astype(F32)
-    for step in range(C - 1):
-        moves(step).wait_send()
+    ring.sent()
 
 
 def norm_terms(R, C, dg, du, w_gate, w_up, b):
@@ -1073,7 +1120,7 @@
         functools.partial(norm_terms_kernel, R, C),
         in_specs=[ANY] * 5,
         out_specs=[VMEM_SPEC, ANY, VMEM_SPEC],
-        out_shape=[struct((rows, D), F32), struct((D, F), BF), struct((D // R, F), F32)],
+        out_shape=[struct((rows, D), F32), struct((D, F), BF), struct((D // R, F), BF)],
         scratch_shapes=[
             pltpu.VMEM((T, F), BF),
             pltpu.VMEM((T, F), BF),
@@ -1089,8 +1136,8 @@
             DMA((2 * C + 1,)),
             DMA((2 * C,)),
             DMA((2,)),
-            DMA((C - 1,)),
-            DMA((C - 1,)),
+            DMA((C - 1, 2)),
+            DMA((C - 1, 2)),
         ]
         + row_sum_semaphores(R),
         compiler_params=comm_params(3, 63),
@@ -1192,7 +1239,7 @@
     lax.fori_loop(heads // 2, heads, one_head, 0)
 
     def write(part, values):
-        gate_ref[part, :] = values
+        gate_ref[part, :] = values.astype(BF)
 
     sums.finish(write)
     for copy in do_copies[:-1]:
@@ -1210,7 +1257,7 @@
         functools.partial(attend_back_kernel, R, C),
         in_specs=[VMEM_SPEC] * 6 + [ANY] * 7,
         out_specs=[VMEM_SPEC] * 4 + [ANY],
-        out_shape=[struct((T, width), BF)] * 3 + [struct((depth, columns), F32), struct((T, width), BF)],
+        out_shape=[struct((T, width), BF)] * 3 + [struct((depth, columns), BF), struct((T, width), BF)],
         scratch_shapes=[
             pltpu.VMEM((rows, D), F32),
             pltpu.VMEM((C, rows, width), BF),
@@ -1297,13 +1344,7 @@
         C + R - 2,
     )
 
-    def moves(step):
-        return ring_step(step, C, right, terms.at[0], held, send, recv)
-
-    def pass_on(step):
-        moves(step - 1).wait_recv()
-        add_into(held.at[step - 1], terms.at[step])
-        moves(step).start()
+    ring = SumRing(C, terms, held, send, recv)
 
     def compute(s):
         cut = cut_of(s)
@@ -1314,7 +1355,7 @@
         terms[s] = total.astype(BF)
 
     compute(0)
-    moves(0).start()
+    ring.start()
 
     def body(s, carry):
         compute(s)
@@ -1348,7 +1389,7 @@
             tiles[slot, 1, :, i * width : (i + 1) * width] = product[depth:]
         q_sums.exchange(slot).start()
     o_sums.relay_again()
-    pass_on(1)
+    ring.pass_on(1)
     q_sums.relay()
 
     def write_out(part, values):
@@ -1401,22 +1442,22 @@
     for copy in rows_out + [keep]:
         copy.start()
     for step in range(2, C - 1):
-        pass_on(step)
+        ring.pass_on(step)
     q_sums.relay_again()
     for copy in rows_out:
         copy.wait_recv()
     keep.wait()
     for n in range(R):
-        out_ref[n * thin : (n + 1) * thin, :] = by_row[n].astype(F32)
+        out_ref[n * thin : (n + 1) * thin, :] = by_row[n]
 
     def write_qkv(part, values):
         for i, target in enumerate((gq_ref, gk_ref, gv_ref)):
-            target[part, :] = values[:, i * width : (i + 1) * width]
+            target[part, :] = values[:, i * width : (i + 1) * width].astype(BF)
 
     q_sums.finish(write_qkv)
     for copy in exchanges:
         copy.wait_recv()
-    moves(C - 2).wait_recv()
+    ring.arrived()
 
     def last_rows(i, carry):
         rows = pl.ds(pl.multiple_of(i * size, size), size)
@@ -1433,8 +1474,7 @@
     lax.fori_loop(0, T // size, last_rows, 0)
     for copy in exchanges + columns_out + rows_out:
         copy.wait_send()
-    for step in range(C - 1):
-        moves(step).wait_send()
+    ring.sent()
 
 
 def input_terms(R, C, dq, dk, dv, w_qkv, a, tokens, dh, mu, r, os):
@@ -1447,8 +1487,8 @@
         in_specs=[VMEM_SPEC] * 3 + [ANY] * 7,
         out_specs=[VMEM_SPEC] * 5,
         out_shape=[struct((T, width), BF)]
-        + [struct((low, width), F32)] * 3
-        + [struct((width, low), F32)],
+        + [struct((low, width), BF)] * 3
+        + [struct((width, low), BF)],
         scratch_shapes=[
             pltpu.VMEM((T, 1), F32),
             pltpu.VMEM((T, 1), F32),
@@ -1471,8 +1511,8 @@
         + [pltpu.VMEM((half, 2, C * thin, width), BF)]
         + row_sum_buffers(R, C * thin, width)
         + [
-            DMA((C - 1,)),
-            DMA((C - 1,)),
+            DMA((C - 1, 2)),
+            DMA((C - 1, 2)),
             DMA((C - 1,)),
             DMA((C - 1,)),
             DMA((C,)),
@@ -1490,6 +1530,25 @@
         cost_estimate=cost(8e10, 20 * MIB),
         name="input_terms",
     )(dq, dk, dv, mu, r, w_qkv, a, tokens, dh, os)
+
+
+def results_kernel(*refs):
+    half = len(refs) // 2
+    for source, target in zip(refs[:half], refs[half:]):
+        target[...] = source[...].astype(target.dtype)
+
+
+def results(*values):
+    shapes = [struct(value.shape, BF if i < 2 else F32) for i, value in enumerate(values)]
+    return pl.pallas_call(
+        results_kernel,
+        in_specs=[VMEM_SPEC] * len(values),
+        out_specs=[VMEM_SPEC] * len(values),
+        out_shape=shapes,
+        compiler_params=params(),
+        cost_estimate=cost(1e6, 16 * MIB),
+        name="results",
+    )(*values)
 
 
 def on_device(R, C, tokens, cotangent, segments, w_query, w_key, w_value, w_out, w_gate, w_up, w_down):
@@ -1516,7 +1575,9 @@
     grad_tokens, grad_query, grad_key, grad_value, grad_out = input_terms(
         R, C, dq, dk, dv, w_qkv, act_one, tokens, dh, mu_one, r_one, os
     )
-    return (output, grad_tokens, grad_query, grad_key, grad_value, grad_out, grad_gate, grad_up, grad_down)
+    return tuple(
+        results(output, grad_tokens, grad_query, grad_key, grad_value, grad_out, grad_gate, grad_up, grad_down)
+    )
 
 
 def solution(mesh):

time: 601 us -> 603 us (level)
  Pallas kernels: 565 us -> 579 us
  local copies, waits for them, and re-layouts: 11.8 us -> 0 us
    unnamed x23 -> x0, local copies, waits for them, and re-layouts: 11.8 us -> none
    pallas_call x1, Pallas kernels: 101 us -> 111 us  [input_terms(): pl.pallas_call(functools.partial(input_terms_kernel, R, C), in_specs=[VME...]
    pallas_call x0 -> x1, Pallas kernels: none -> 6.85 us  [results(): pl.pallas_call(results_kernel, in_specs=[VMEM_SPEC] * len(values), out_sp...]
  transfers between devices with their start and end apart: 2 -> 2, of which waited for: 0 -> 0; matrix products, arithmetic and copies ran while one was open for 0% -> 0% of each run, Pallas kernels for 31% -> 30%
where the time goes in v9:
time: 603 us; the launch traced here: 596 us
  Pallas kernels  579 us (96%)
  between operations  14.4 us (2%)
    pallas_call x1, Pallas kernels, feed_forward(): pl.pallas_call(functools.partial(feed_kernel, R, C), in_specs=[ANY] * 7,...  142 us
    pallas_call x1, Pallas kernels, input_terms(): pl.pallas_call(functools.partial(input_terms_kernel, R, C), in_specs=[VME...  111 us
    pallas_call x1, Pallas kernels, norm_terms(): pl.pallas_call(functools.partial(norm_terms_kernel, R, C), in_specs=[ANY]...  81.3 us
    pallas_call x1, Pallas kernels, attend(): pl.pallas_call(functools.partial(attend_kernel, R, C), in_specs=[VMEM_SPE...  77.4 us
    pallas_call x1, Pallas kernels, first_gather(): pl.pallas_call(functools.partial(gather_kernel, R, C), in_specs=[VMEM_SPE...  74.6 us
    pallas_call x1, Pallas kernels, attend_back(): pl.pallas_call(functools.partial(attend_back_kernel, R, C), in_specs=[VME...  58.6 us
    pallas_call x1, Pallas kernels, norm_and_project(): pl.pallas_call(functools.partial(qkv_kernel, C), grid=(T // bt,), in_spec...  27.7 us
  transfers between devices with their start and end apart: 2, of which 0 were waited for; matrix products, arithmetic and copies ran while one was open for 0% of the time, Pallas kernels for 30%

profile of v9, /device:TPU:8, one launch (start us, length us, event | category | flops | bytes accessed | tf_op | source)
XLA Modules:
  0.0 595.7 jit_solution(5992481565220199170)
XLA Ops:
  7.2 0.0 all-gather.3.cloned.1.call-start
  7.2 0.7 all-gather.3.cloned.1.call-update
  7.9 0.0 all-gather.5.cloned.1.call-start
  8.0 0.7 all-gather.5.cloned.1.call-update
  8.7 0.6 maximum_bitcast_fusion.rate_ref
  9.3 74.6 %first_gather.1 = (bf16[4,1024,512]{2,1,0:T(8,128)(2,1)}, bf16[3,8,256,512]{3,2,1,0:T(8,128)(2,1)}, f32[1024,128]{1,0:T(8,128)}, f32[1024,128]{1,0:T(8,128)}, s3...) custom-call(s32[1,1024]{1,0:T(1,128)} %bitcast.5, f32[1,128]{1,0:T(1,128)} %maximum_bitcast_fusion.rate_ref, ...), custom_call_target="tpu_custom_call" | custom-call | flops 60000002048 | bytes 14680064 | tf_op jit(solution)/shard_map/first_gather/pallas_call | solution.py:207
  83.9 27.7 %norm_and_project.1 = (bf16[1024,2048]{1,0:T(8,128)(2,1)}, bf16[1024,512]{1,0:T(8,128)(2,1)}, bf16[1024,512]{1,0:T(8,128)(2,1)}, bf16[1024,512]{1,0:T(8,128)(2,1...) custom-call(bf16[4,1024,512]{2,1,0:T(8,128)(2,1)} %get-tuple-element.46.xs_ref.xs_hbm, ...), custom_call_target="tpu_custom_call" | custom-call | flops 20000000000 | bytes 14680064 | tf_op jit(solution)/shard_map/norm_and_project/pallas_call | solution.py:294
  111.6 77.4 %attend.1 = (bf16[4,4,1024,128]{3,2,1,0:T(8,128)(2,1)}, f32[4,1,1024]{2,1,0:T(1,128)}, bf16[8,4,256,512]{3,2,1,0:T(8,128)(2,1)}) custom-call(bf16[1024,512]{1,0:T(8,128)(2,1)} %get-tuple-element.51.q_ref.q_hbm, bf16[1024,512]{1,0:T(8,128)(2,1)} %get-tuple-element.52.k_ref.k_hbm, bf16[1024,512]{1,0:T(8,128)(2,1)} %get-tuple-element.53.v_ref.v_hbm, ...), custom_call_target="tpu_custom_call" | custom-call | flops 70000001024 | bytes 14680064 | tf_op jit(solution)/shard_map/attend/pallas_call | solution.py:397
  189.1 0.0 all-gather.3.cloned.1.call-done.wg_hbm
  189.1 0.0 all-gather.5.cloned.1.call-done.wu_hbm
  189.1 142.0 %feed_forward.1 = (f32[1024,2048]{1,0:T(8,128)}, bf16[1024,2048]{1,0:T(8,128)(2,1)}, bf16[1024,2048]{1,0:T(8,128)(2,1)}, bf16[1024,2048]{1,0:T(8,128)(2,1)}, bf1...) custom-call(bf16[4,4,1024,128]{3,2,1,0:T(8,128)(2,1)} %get-tuple-ele, ...), custom_call_target="tpu_custom_call" | custom-call | flops 120000004096 | bytes 94371840 | tf_op jit(solution)/shard_map/feed_forward/pallas_call | solution.py:954
  331.2 81.3 %norm_terms.1 = (f32[256,2048]{1,0:T(8,128)}, bf16[2048,2048]{1,0:T(8,128)(2,1)}, bf16[256,2048]{1,0:T(8,128)(2,1)}) custom-call(bf16[1024,2048]{1,0:T(8,128)(2,1)} %get-tuple-element.60.dg_hbm, bf16[1024,2048]{1,0:T(8,128)(2,1)} %get-tuple-element.61.du_hbm, bf16[2048,2048]{1,0:T(8,128)(2,1)} %all-gather.3.cloned.1.call-done.wg_hbm, ...), custom_call_target="tpu_custom_call" | custom-call | flops 89999998976 | bytes 73400320 | tf_op jit(solution)/shard_map/norm_terms/pallas_call | solution.py:1119
  412.5 58.6 %attend_back.1 = (bf16[1024,512]{1,0:T(8,128)(2,1)}, bf16[1024,512]{1,0:T(8,128)(2,1)}, bf16[1024,512]{1,0:T(8,128)(2,1)}, bf16[256,2048]{1,0:T(8,128)(2,1)}, bf16[1024,512]{1,0:T(8,128)(2,1)}) custom-call(f32[256,2048]{1,0:T(8,128)} %get-tuple-element.63.sum_ref, f32[4,1,1024]{2,1,0:T(1,128)} %get-tuple-element.64.log_ref, ...), custom_call_target="tpu_custom_call" | custom-call | flops 49999998976 | bytes 31457280 | tf_op jit(solution)/shard_map/attend_back/pallas_call | solution.py:1256
  471.1 110.6 %input_terms.1 = (bf16[1024,512]{1,0:T(8,128)(2,1)}, bf16[256,512]{1,0:T(8,128)(2,1)}, bf16[256,512]{1,0:T(8,128)(2,1)}, bf16[256,512]{1,0:T(8,128)(2,1)}, bf16[512,256]{1,0:T(8,128)(2,1)}) custom-call(bf16[1024,512]{1,0:T(8,128)(2,1)} %get-tuple-element.68.dq_ref, bf16[1024,512]{1,0:T(8,128)(2,1)} %get-tuple-element.69.dk_ref, ...), custom_call_target="tpu_custom_call" | custom-call | flops 80000000000 | bytes 20971520 | tf_op jit(solution)/shard_map/input_terms/pallas_call | solution.py:1485
  581.7 6.9 %results.1 = (bf16[1024,512]{1,0:T(8,128)(2,1)}, bf16[1024,512]{1,0:T(8,128)(2,1)}, f32[256,512]{1,0:T(8,128)}, f32[256,512]{1,0:T(8,128)}, f32[256,512]{1,0:T(8...) custom-call(bf16[1024,512]{1,0:T(8,128)(2,1)} %get-tuple-element.59.refs_0_, ...), custom_call_target="tpu_custom_call" | custom-call | flops 1000000 | bytes 16777216 | tf_op jit(solution)/shard_map/results/pallas_call | solution.py:1543
  (1 shorter events, 0.0 us)
Async XLA Ops:
  7.2 181.9 %all-gather.3.cloned.1.call-start = ((), (), s32[]{:S(2)}) async-start(), calls=%async_computation | async-start | bytes 9437184 | tf_op jit(solution)/shard_map/all_gather | solution.py:1557
  7.9 181.2 %all-gather.5.cloned.1.call-start = ((), (), s32[]{:S(2)}) async-start(), calls=%async_computation.1 | async-start | bytes 9437184 | tf_op jit(solution)/shard_map/all_gather | solution.py:1557
Sparse Core Ops, SparseCore 0:
  9.9 77.2 all-gather.2
  89.1 97.9 all-gather.4

commit v10 on v9

--- a/solution.py
+++ b/solution.py
@@ -423,35 +423,25 @@
     def __init__(self, C, terms, held, send, recv):
         me, right, left = ring_places(C)
         self.C, self.terms, self.held, self.send, self.recv, self.right = C, terms, held, send, recv, right
-        self.size = held.shape[1] // 2
-
-    def part(self, ref, slot, half):
-        return ref.at[slot, pl.ds(half * self.size, self.size), :]
-
-    def copy(self, step, half):
-        source = self.part(self.terms, 0, half) if step == 0 else self.part(self.held, step - 1, half)
-        return remote(
-            source, self.part(self.held, step, half), self.send.at[step, half], self.recv.at[step, half], col=self.right
-        )
+
+    def copy(self, step):
+        source = self.terms.at[0] if step == 0 else self.held.at[step - 1]
+        return remote(source, self.held.at[step], self.send.at[step], self.recv.at[step], col=self.right)
 
     def start(self):
-        for half in range(2):
-            self.copy(0, half).start()
+        self.copy(0).start()
 
     def pass_on(self, step):
-        for half in range(2):
-            self.copy(step - 1, half).wait_recv()
-            add_into(self.part(self.held, step - 1, half), self.part(self.terms, step, half))
-            self.copy(step, half).start()
+        self.copy(step - 1).wait_recv()
+        add_into(self.held.at[step - 1], self.terms.at[step])
+        self.copy(step).start()
 
     def arrived(self):
-        for half in range(2):
-            self.copy(self.C - 2, half).wait_recv()
+        self.copy(self.C - 2).wait_recv()
 
     def sent(self):
         for step in range(self.C - 1):
-            for half in range(2):
-                self.copy(step, half).wait_send()
+            self.copy(step).wait_send()
 
 
 def add_into(held, terms):
@@ -505,17 +495,29 @@
             [2 * dp + 1 for dp in range(1, self.P)] + [1] + [2 * dp for dp in range(1, self.P)] + [0]
         )
 
+    def relay_one(self, slot):
+        self.exchange(slot).wait_recv()
+        add_into(self.own(slot), self.exchanged.at[slot])
+        dp, dq = divmod(slot, 2)
+        if dq:
+            self.left_one(dp).start()
+        if dp:
+            self.right_one(dp, dq).start()
+
     def relay(self, before=None):
         for slot in self.order():
             if before is not None:
                 before(slot)
-            self.exchange(slot).wait_recv()
-            add_into(self.own(slot), self.exchanged.at[slot])
-            dp, dq = divmod(slot, 2)
-            if dq:
-                self.left_one(dp).start()
-            if dp:
-                self.right_one(dp, dq).start()
+            self.relay_one(slot)
+
+    def compute_and_relay(self, compute):
+        slots = self.order()
+        for i, slot in enumerate(slots):
+            compute(slot)
+            self.exchange(slot).start()
+            if i:
+                self.relay_one(slots[i - 1])
+        self.relay_one(slots[-1])
 
     def relay_again(self):
         for dp in range(1, self.P):
@@ -898,13 +900,14 @@
     saved.append(began(slope.at[:, pl.ds(0, F)], dg_hbm, store.at[2]))
     saved.append(began(silu.at[:, pl.ds(0, F)], du_hbm, store.at[3]))
 
-    for slot in row_sums.order():
+
+    def down_tile(slot):
         chip = lax.div(place(slot), 2)
         product = dot_tn(dys[chip], hidden[:, :F]).astype(BF)
         for n in range(2):
             big[2 * chip + n, :, :F] = product[n * depth : (n + 1) * depth]
-        row_sums.exchange(slot).start()
-    row_sums.relay()
+
+    row_sums.compute_and_relay(down_tile)
     for t in range(2, C - 1):
         sums.level(t)
     row_sums.relay_again()
@@ -1093,11 +1096,12 @@
     for step in range(1, middle + 1):
         if step < C - 1:
             ring.pass_on(step)
-    for slot in sums.order():
+
+    def gate_tile(slot):
         cut = pl.ds(pl.multiple_of(lax.div(place(slot), 2) * 2 * depth, 2 * depth), 2 * depth)
         wu[cut, :] = dot_tn(b[:, cut], dg[...]).astype(BF)
-        sums.exchange(slot).start()
-    sums.relay()
+
+    sums.compute_and_relay(gate_tile)
     product(du, up_hbm)
     for step in range(middle + 1, C - 1):
         ring.pass_on(step)
@@ -1136,8 +1140,8 @@
             DMA((2 * C + 1,)),
             DMA((2 * C,)),
             DMA((2,)),
-            DMA((C - 1, 2)),
-            DMA((C - 1, 2)),
+            DMA((C - 1,)),
+            DMA((C - 1,)),
         ]
         + row_sum_semaphores(R),
         compiler_params=comm_params(3, 63),
@@ -1380,17 +1384,18 @@
     for i, copy in enumerate(late):
         if i != 2:
             copy.wait()
-    for slot in q_sums.order():
+
+    def qkv_tile(slot):
         start = pl.multiple_of(lax.div(q_sums.places(slot), 2) * 2 * depth, 2 * depth)
         left_tile = a_ref[:, pl.ds(start, 2 * depth)]
         for i, right_side in enumerate(heads):
             product = dot_tn(left_tile, right_side[...]).astype(BF)
             tiles[slot, 0, :, i * width : (i + 1) * width] = product[:depth]
             tiles[slot, 1, :, i * width : (i + 1) * width] = product[depth:]
-        q_sums.exchange(slot).start()
+
+    q_sums.compute_and_relay(qkv_tile)
     o_sums.relay_again()
     ring.pass_on(1)
-    q_sums.relay()
 
     def write_out(part, values):
         mine[part, :] = values.astype(BF)
@@ -1427,6 +1432,8 @@
     ]
     for copy in exchanges:
         copy.start()
+    for step in range(2, C - 1):
+        ring.pass_on(step)
     for copy in columns_out:
         copy.wait_recv()
     stay.wait()
@@ -1441,8 +1448,6 @@
     keep = pltpu.make_async_copy(piece_of(row), by_row.at[row], local.at[1])
     for copy in rows_out + [keep]:
         copy.start()
-    for step in range(2, C - 1):
-        ring.pass_on(step)
     q_sums.relay_again()
     for copy in rows_out:
         copy.wait_recv()
@@ -1511,8 +1516,8 @@
         + [pltpu.VMEM((half, 2, C * thin, width), BF)]
         + row_sum_buffers(R, C * thin, width)
         + [
-            DMA((C - 1, 2)),
-            DMA((C - 1, 2)),
+            DMA((C - 1,)),
+            DMA((C - 1,)),
             DMA((C - 1,)),
             DMA((C - 1,)),
             DMA((C,)),

time: 603 us -> 588 us (0.975)
  Pallas kernels: 579 us -> 567 us
    pallas_call x1, Pallas kernels: 111 us -> 102 us  [input_terms(): pl.pallas_call(functools.partial(input_terms_kernel, R, C), in_specs=[VME...]
  transfers between devices with their start and end apart: 2 -> 2, of which waited for: 0 -> 0; matrix products, arithmetic and copies ran while one was open for 0% -> 0% of each run, Pallas kernels for 30% -> 31%
where the time goes in v10:
time: 588 us; the launch traced here: 583 us
  Pallas kernels  567 us (96%)
  between operations  14.4 us (2%)
    pallas_call x1, Pallas kernels, feed_forward(): pl.pallas_call(functools.partial(feed_kernel, R, C), in_specs=[ANY] * 7,...  139 us
    pallas_call x1, Pallas kernels, input_terms(): pl.pallas_call(functools.partial(input_terms_kernel, R, C), in_specs=[VME...  102 us
    pallas_call x1, Pallas kernels, norm_terms(): pl.pallas_call(functools.partial(norm_terms_kernel, R, C), in_specs=[ANY]...  83.5 us
    pallas_call x1, Pallas kernels, attend(): pl.pallas_call(functools.partial(attend_kernel, R, C), in_specs=[VMEM_SPE...  77.4 us
    pallas_call x1, Pallas kernels, first_gather(): pl.pallas_call(functools.partial(gather_kernel, R, C), in_specs=[VMEM_SPE...  74.6 us
    pallas_call x1, Pallas kernels, attend_back(): pl.pallas_call(functools.partial(attend_back_kernel, R, C), in_specs=[VME...  56.4 us
    pallas_call x1, Pallas kernels, norm_and_project(): pl.pallas_call(functools.partial(qkv_kernel, C), grid=(T // bt,), in_spec...  27.7 us
  transfers between devices with their start and end apart: 2, of which 0 were waited for; matrix products, arithmetic and copies ran while one was open for 0% of the time, Pallas kernels for 31%

profile of v10, /device:TPU:8, one launch (start us, length us, event | category | flops | bytes accessed | tf_op | source)
XLA Modules:
  0.0 583.3 jit_solution(13127293745175562773)
XLA Ops:
  7.2 0.0 all-gather.3.cloned.1.call-start
  7.2 0.7 all-gather.3.cloned.1.call-update
  7.9 0.0 all-gather.5.cloned.1.call-start
  8.0 0.7 all-gather.5.cloned.1.call-update
  8.7 0.6 maximum_bitcast_fusion.rate_ref
  9.3 74.6 %first_gather.1 = (bf16[4,1024,512]{2,1,0:T(8,128)(2,1)}, bf16[3,8,256,512]{3,2,1,0:T(8,128)(2,1)}, f32[1024,128]{1,0:T(8,128)}, f32[1024,128]{1,0:T(8,128)}, s3...) custom-call(s32[1,1024]{1,0:T(1,128)} %bitcast.5, f32[1,128]{1,0:T(1,128)} %maximum_bitcast_fusion.rate_ref, ...), custom_call_target="tpu_custom_call" | custom-call | flops 60000002048 | bytes 14680064 | tf_op jit(solution)/shard_map/first_gather/pallas_call | solution.py:207
  83.9 27.7 %norm_and_project.1 = (bf16[1024,2048]{1,0:T(8,128)(2,1)}, bf16[1024,512]{1,0:T(8,128)(2,1)}, bf16[1024,512]{1,0:T(8,128)(2,1)}, bf16[1024,512]{1,0:T(8,128)(2,1...) custom-call(bf16[4,1024,512]{2,1,0:T(8,128)(2,1)} %get-tuple-element.46.xs_ref.xs_hbm, ...), custom_call_target="tpu_custom_call" | custom-call | flops 20000000000 | bytes 14680064 | tf_op jit(solution)/shard_map/norm_and_project/pallas_call | solution.py:294
  111.6 77.4 %attend.1 = (bf16[4,4,1024,128]{3,2,1,0:T(8,128)(2,1)}, f32[4,1,1024]{2,1,0:T(1,128)}, bf16[8,4,256,512]{3,2,1,0:T(8,128)(2,1)}) custom-call(bf16[1024,512]{1,0:T(8,128)(2,1)} %get-tuple-element.51.q_ref.q_hbm, bf16[1024,512]{1,0:T(8,128)(2,1)} %get-tuple-element.52.k_ref.k_hbm, bf16[1024,512]{1,0:T(8,128)(2,1)} %get-tuple-element.53.v_ref.v_hbm, ...), custom_call_target="tpu_custom_call" | custom-call | flops 70000001024 | bytes 14680064 | tf_op jit(solution)/shard_map/attend/pallas_call | solution.py:397
  189.1 0.0 all-gather.3.cloned.1.call-done.wg_hbm
  189.1 0.0 all-gather.5.cloned.1.call-done.wu_hbm
  189.1 138.6 %feed_forward.1 = (f32[1024,2048]{1,0:T(8,128)}, bf16[1024,2048]{1,0:T(8,128)(2,1)}, bf16[1024,2048]{1,0:T(8,128)(2,1)}, bf16[1024,2048]{1,0:T(8,128)(2,1)}, bf1...) custom-call(bf16[4,4,1024,128]{3,2,1,0:T(8,128)(2,1)} %get-tuple-ele, ...), custom_call_target="tpu_custom_call" | custom-call | flops 120000004096 | bytes 94371840 | tf_op jit(solution)/shard_map/feed_forward/pallas_call | solution.py:957
  327.8 83.5 %norm_terms.1 = (f32[256,2048]{1,0:T(8,128)}, bf16[2048,2048]{1,0:T(8,128)(2,1)}, bf16[256,2048]{1,0:T(8,128)(2,1)}) custom-call(bf16[1024,2048]{1,0:T(8,128)(2,1)} %get-tuple-element.60.dg_hbm, bf16[1024,2048]{1,0:T(8,128)(2,1)} %get-tuple-element.61.du_hbm, bf16[2048,2048]{1,0:T(8,128)(2,1)} %all-gather.3.cloned.1.call-done.wg_hbm, ...), custom_call_target="tpu_custom_call" | custom-call | flops 89999998976 | bytes 73400320 | tf_op jit(solution)/shard_map/norm_terms/pallas_call | solution.py:1123
  411.3 56.4 %attend_back.1 = (bf16[1024,512]{1,0:T(8,128)(2,1)}, bf16[1024,512]{1,0:T(8,128)(2,1)}, bf16[1024,512]{1,0:T(8,128)(2,1)}, bf16[256,2048]{1,0:T(8,128)(2,1)}, bf16[1024,512]{1,0:T(8,128)(2,1)}) custom-call(f32[256,2048]{1,0:T(8,128)} %get-tuple-element.63.sum_ref, f32[4,1,1024]{2,1,0:T(1,128)} %get-tuple-element.64.log_ref, ...), custom_call_target="tpu_custom_call" | custom-call | flops 49999998976 | bytes 31457280 | tf_op jit(solution)/shard_map/attend_back/pallas_call | solution.py:1260
  467.7 101.6 %input_terms.1 = (bf16[1024,512]{1,0:T(8,128)(2,1)}, bf16[256,512]{1,0:T(8,128)(2,1)}, bf16[256,512]{1,0:T(8,128)(2,1)}, bf16[256,512]{1,0:T(8,128)(2,1)}, bf16[512,256]{1,0:T(8,128)(2,1)}) custom-call(bf16[1024,512]{1,0:T(8,128)(2,1)} %get-tuple-element.68.dq_ref, bf16[1024,512]{1,0:T(8,128)(2,1)} %get-tuple-element.69.dk_ref, ...), custom_call_target="tpu_custom_call" | custom-call | flops 80000000000 | bytes 20971520 | tf_op jit(solution)/shard_map/input_terms/pallas_call | solution.py:1490
  569.3 6.9 %results.1 = (bf16[1024,512]{1,0:T(8,128)(2,1)}, bf16[1024,512]{1,0:T(8,128)(2,1)}, f32[256,512]{1,0:T(8,128)}, f32[256,512]{1,0:T(8,128)}, f32[256,512]{1,0:T(8...) custom-call(bf16[1024,512]{1,0:T(8,128)(2,1)} %get-tuple-element.59.refs_0_, ...), custom_call_target="tpu_custom_call" | custom-call | flops 1000000 | bytes 16777216 | tf_op jit(solution)/shard_map/results/pallas_call | solution.py:1548
  (1 shorter events, 0.0 us)
Async XLA Ops:
  7.2 181.9 %all-gather.3.cloned.1.call-start = ((), (), s32[]{:S(2)}) async-start(), calls=%async_computation | async-start | bytes 9437184 | tf_op jit(solution)/shard_map/all_gather | solution.py:1562
  7.9 181.2 %all-gather.5.cloned.1.call-start = ((), (), s32[]{:S(2)}) async-start(), calls=%async_computation.1 | async-start | bytes 9437184 | tf_op jit(solution)/shard_map/all_gather | solution.py:1562
Sparse Core Ops, SparseCore 0:
  9.9 77.2 all-gather.2
  89.1 97.9 all-gather.4

commit v11 on v10

--- a/solution.py
+++ b/solution.py
@@ -1298,8 +1298,8 @@
     R, C, dq_ref, dk_ref, dv_ref, mu_hbm, r_hbm, w_hbm, a_hbm, x_hbm, dh_hbm, os_hbm,
     y_ref, gq_ref, gk_ref, gv_ref, out_ref,
     mu_ref, r_ref, w_ref, a_ref, x_ref, dh_ref, block, product, mine, by_column, by_row,
-    terms, held, stats, stats_in, tiles, q_exchanged, q_arrived, o_tiles, o_exchanged, o_arrived,
-    send, recv, s_send, s_recv, w_load, late_load, block_load, c_send, c_recv, r_send, r_recv, local, *semaphores,
+    terms, rising, falling, stats, stats_in, tiles, q_exchanged, q_arrived, o_tiles, o_exchanged, o_arrived,
+    s_send, s_recv, w_load, late_load, block_load, c_send, c_recv, r_send, r_recv, local, *semaphores,
 ):
     me, right, left = ring_places(C)
     T, width = dq_ref.shape
@@ -1308,8 +1308,13 @@
     row = lax.axis_index("row")
     thin = width // R
 
+    upper = lax.div(me, C // 2)
+
+    def column_of(s):
+        return (C - 1 - s) * (1 - upper) + s * upper
+
     def cut_of(s):
-        return pl.ds(pl.multiple_of(lax.rem(me + 2 * C - 1 - s, C) * width, width), width)
+        return pl.ds(pl.multiple_of(column_of(s) * width, width), width)
 
     def weight_in(s):
         return pltpu.make_async_copy(w_hbm.at[:, cut_of(s), :], w_ref.at[:, cut_of(s), :], w_load.at[s])
@@ -1330,7 +1335,7 @@
         R, lambda i: tiles.at[i, side], lambda i: tiles.at[i, 1 - side], q_exchanged, q_arrived, semaphores[:4]
     )
     o_sums = RowSum(
-        R, lambda i: o_tiles.at[i, side], lambda i: o_tiles.at[i, 1 - side], o_exchanged, o_arrived, semaphores[4:]
+        R, lambda i: o_tiles.at[i, side], lambda i: o_tiles.at[i, 1 - side], o_exchanged, o_arrived, semaphores[4:8]
     )
 
     def block_in(i):
@@ -1348,7 +1353,7 @@
         C + R - 2,
     )
 
-    ring = SumRing(C, terms, held, send, recv)
+    line = LineSum(C, terms, rising, falling, semaphores[8:10], semaphores[10:])
 
     def compute(s):
         cut = cut_of(s)
@@ -1356,10 +1361,10 @@
         total = dot_nt(dq_ref[...], w_ref[0, cut, :])
         total += dot_nt(dk_ref[...], w_ref[1, cut, :])
         total += dot_nt(dv_ref[...], w_ref[2, cut, :])
-        terms[s] = total.astype(BF)
+        terms[column_of(s)] = total.astype(BF)
 
     compute(0)
-    ring.start()
+    line.level(0)
 
     def body(s, carry):
         compute(s)
@@ -1395,7 +1400,7 @@
 
     q_sums.compute_and_relay(qkv_tile)
     o_sums.relay_again()
-    ring.pass_on(1)
+    line.level(1)
 
     def write_out(part, values):
         mine[part, :] = values.astype(BF)
@@ -1421,7 +1426,7 @@
         for s in range(C):
             grad = terms[s, rows, :].astype(F32)
             total += jnp.sum(grad, axis=1, keepdims=True)
-            second += jnp.sum(grad * a_ref[rows, cut_of(s)].astype(F32), axis=1, keepdims=True)
+            second += jnp.sum(grad * a_ref[rows, s * width : (s + 1) * width].astype(F32), axis=1, keepdims=True)
         packed = jnp.where(lane == 0, total, jnp.where(lane == 1, second, 0.0))
         stats[:, rows] = packed.T[:8]
         return carry
@@ -1433,7 +1438,7 @@
     for copy in exchanges:
         copy.start()
     for step in range(2, C - 1):
-        ring.pass_on(step)
+        line.level(step)
     for copy in columns_out:
         copy.wait_recv()
     stay.wait()
@@ -1462,24 +1467,40 @@
     q_sums.finish(write_qkv)
     for copy in exchanges:
         copy.wait_recv()
-    ring.arrived()
-
-    def last_rows(i, carry):
-        rows = pl.ds(pl.multiple_of(i * size, size), size)
-        both = stats[:, rows]
-        for k in range(C - 1):
-            both += stats_in[k, :, rows]
-        columns = jnp.concatenate([both, jnp.zeros((120, size), F32)], axis=0).T * (1.0 / D)
-        normed = (x_ref[rows, :].astype(F32) - mu_ref[rows, :]) * r_ref[rows, :]
-        grad = held[C - 2, rows, :].astype(F32) + terms[C - 1, rows, :].astype(F32)
-        grad = grad - columns[:, 0:1] - normed * columns[:, 1:2]
-        y_ref[rows, :] = (dh_ref[rows, :].astype(F32) + r_ref[rows, :] * grad).astype(BF)
-        return carry
-
-    lax.fori_loop(0, T // size, last_rows, 0)
+    line.level(C - 1)
+
+    def last_rows(more):
+        def body(i, carry):
+            rows = pl.ds(pl.multiple_of(i * size, size), size)
+            both = stats[:, rows]
+            for k in range(C - 1):
+                both += stats_in[k, :, rows]
+            columns = jnp.concatenate([both, jnp.zeros((120, size), F32)], axis=0).T * (1.0 / D)
+            normed = (x_ref[rows, :].astype(F32) - mu_ref[rows, :]) * r_ref[rows, :]
+            grad = terms[me, rows, :].astype(F32)
+            for buffer, slot in more:
+                grad += buffer[slot, rows, :].astype(F32)
+            grad = grad - columns[:, 0:1] - normed * columns[:, 1:2]
+            y_ref[rows, :] = (dh_ref[rows, :].astype(F32) + r_ref[rows, :] * grad).astype(BF)
+            return carry
+
+        lax.fori_loop(0, T // size, body, 0)
+
+    @pl.when(me == 0)
+    def _():
+        last_rows([(falling, 0)])
+
+    @pl.when(me == C - 1)
+    def _():
+        last_rows([(rising, 0)])
+
+    @pl.when((me > 0) & (me < C - 1))
+    def _():
+        last_rows([(rising, C - 1 - me), (falling, me)])
+
     for copy in exchanges + columns_out + rows_out:
         copy.wait_send()
-    ring.sent()
+    line.finish()
 
 
 def input_terms(R, C, dq, dk, dv, w_qkv, a, tokens, dh, mu, r, os):
@@ -1508,6 +1529,7 @@
             pltpu.VMEM((R, thin, low), BF),
             pltpu.VMEM((C, T, width), BF),
             pltpu.VMEM((C - 1, T, width), BF),
+            pltpu.VMEM((C - 1, T, width), BF),
             pltpu.VMEM((8, T), F32),
             pltpu.VMEM((C - 1, 8, T), F32),
             pltpu.VMEM((half, 2, low, 3 * width), BF),
@@ -1516,8 +1538,6 @@
         + [pltpu.VMEM((half, 2, C * thin, width), BF)]
         + row_sum_buffers(R, C * thin, width)
         + [
-            DMA((C - 1,)),
-            DMA((C - 1,)),
             DMA((C - 1,)),
             DMA((C - 1,)),
             DMA((C,)),
@@ -1530,7 +1550,8 @@
             DMA((2,)),
         ]
         + row_sum_semaphores(R)
-        + row_sum_semaphores(R),
+        + row_sum_semaphores(R)
+        + line_semaphores(C),
         compiler_params=comm_params(6, 63),
         cost_estimate=cost(8e10, 20 * MIB),
         name="input_terms",

time: 588 us -> 576 us (0.980)
  Pallas kernels: 567 us -> 554 us
    pallas_call x1, Pallas kernels: 102 us -> 89.2 us  [input_terms(): pl.pallas_call(functools.partial(input_terms_kernel, R, C), in_specs=[VME...]
where the time goes in v11:
time: 576 us; the launch traced here: 571 us
  Pallas kernels  554 us (96%)
  between operations  14.4 us (2%)
    pallas_call x1, Pallas kernels, feed_forward(): pl.pallas_call(functools.partial(feed_kernel, R, C), in_specs=[ANY] * 7,...  139 us
    pallas_call x1, Pallas kernels, input_terms(): pl.pallas_call(functools.partial(input_terms_kernel, R, C), in_specs=[VME...  89.2 us
    pallas_call x1, Pallas kernels, norm_terms(): pl.pallas_call(functools.partial(norm_terms_kernel, R, C), in_specs=[ANY]...  83.5 us
    pallas_call x1, Pallas kernels, attend(): pl.pallas_call(functools.partial(attend_kernel, R, C), in_specs=[VMEM_SPE...  77.4 us
    pallas_call x1, Pallas kernels, first_gather(): pl.pallas_call(functools.partial(gather_kernel, R, C), in_specs=[VMEM_SPE...  74.6 us
    pallas_call x1, Pallas kernels, attend_back(): pl.pallas_call(functools.partial(attend_back_kernel, R, C), in_specs=[VME...  56.4 us
    pallas_call x1, Pallas kernels, norm_and_project(): pl.pallas_call(functools.partial(qkv_kernel, C), grid=(T // bt,), in_spec...  27.7 us
  transfers between devices with their start and end apart: 2, of which 0 were waited for; matrix products, arithmetic and copies ran while one was open for 0% of the time, Pallas kernels for 31%

profile of v11, /device:TPU:8, one launch (start us, length us, event | category | flops | bytes accessed | tf_op | source)
XLA Modules:
  0.0 570.9 jit_solution(10562410468676100293)
XLA Ops:
  7.2 0.0 all-gather.3.cloned.1.call-start
  7.2 0.7 all-gather.3.cloned.1.call-update
  7.9 0.0 all-gather.5.cloned.1.call-start
  8.0 0.7 all-gather.5.cloned.1.call-update
  8.7 0.6 maximum_bitcast_fusion.rate_ref
  9.3 74.6 %first_gather.1 = (bf16[4,1024,512]{2,1,0:T(8,128)(2,1)}, bf16[3,8,256,512]{3,2,1,0:T(8,128)(2,1)}, f32[1024,128]{1,0:T(8,128)}, f32[1024,128]{1,0:T(8,128)}, s3...) custom-call(s32[1,1024]{1,0:T(1,128)} %bitcast.5, f32[1,128]{1,0:T(1,128)} %maximum_bitcast_fusion.rate_ref, ...), custom_call_target="tpu_custom_call" | custom-call | flops 60000002048 | bytes 14680064 | tf_op jit(solution)/shard_map/first_gather/pallas_call | solution.py:207
  83.9 27.7 %norm_and_project.1 = (bf16[1024,2048]{1,0:T(8,128)(2,1)}, bf16[1024,512]{1,0:T(8,128)(2,1)}, bf16[1024,512]{1,0:T(8,128)(2,1)}, bf16[1024,512]{1,0:T(8,128)(2,1...) custom-call(bf16[4,1024,512]{2,1,0:T(8,128)(2,1)} %get-tuple-element.46.xs_ref.xs_hbm, ...), custom_call_target="tpu_custom_call" | custom-call | flops 20000000000 | bytes 14680064 | tf_op jit(solution)/shard_map/norm_and_project/pallas_call | solution.py:294
  111.6 77.4 %attend.1 = (bf16[4,4,1024,128]{3,2,1,0:T(8,128)(2,1)}, f32[4,1,1024]{2,1,0:T(1,128)}, bf16[8,4,256,512]{3,2,1,0:T(8,128)(2,1)}) custom-call(bf16[1024,512]{1,0:T(8,128)(2,1)} %get-tuple-element.51.q_ref.q_hbm, bf16[1024,512]{1,0:T(8,128)(2,1)} %get-tuple-element.52.k_ref.k_hbm, bf16[1024,512]{1,0:T(8,128)(2,1)} %get-tuple-element.53.v_ref.v_hbm, ...), custom_call_target="tpu_custom_call" | custom-call | flops 70000001024 | bytes 14680064 | tf_op jit(solution)/shard_map/attend/pallas_call | solution.py:397
  189.1 0.0 all-gather.3.cloned.1.call-done.wg_hbm
  189.1 0.0 all-gather.5.cloned.1.call-done.wu_hbm
  189.1 138.6 %feed_forward.1 = (f32[1024,2048]{1,0:T(8,128)}, bf16[1024,2048]{1,0:T(8,128)(2,1)}, bf16[1024,2048]{1,0:T(8,128)(2,1)}, bf16[1024,2048]{1,0:T(8,128)(2,1)}, bf1...) custom-call(bf16[4,4,1024,128]{3,2,1,0:T(8,128)(2,1)} %get-tuple-ele, ...), custom_call_target="tpu_custom_call" | custom-call | flops 120000004096 | bytes 94371840 | tf_op jit(solution)/shard_map/feed_forward/pallas_call | solution.py:957
  327.8 83.5 %norm_terms.1 = (f32[256,2048]{1,0:T(8,128)}, bf16[2048,2048]{1,0:T(8,128)(2,1)}, bf16[256,2048]{1,0:T(8,128)(2,1)}) custom-call(bf16[1024,2048]{1,0:T(8,128)(2,1)} %get-tuple-element.60.dg_hbm, bf16[1024,2048]{1,0:T(8,128)(2,1)} %get-tuple-element.61.du_hbm, bf16[2048,2048]{1,0:T(8,128)(2,1)} %all-gather.3.cloned.1.call-done.wg_hbm, ...), custom_call_target="tpu_custom_call" | custom-call | flops 89999998976 | bytes 73400320 | tf_op jit(solution)/shard_map/norm_terms/pallas_call | solution.py:1123
  411.3 56.4 %attend_back.1 = (bf16[1024,512]{1,0:T(8,128)(2,1)}, bf16[1024,512]{1,0:T(8,128)(2,1)}, bf16[1024,512]{1,0:T(8,128)(2,1)}, bf16[256,2048]{1,0:T(8,128)(2,1)}, bf16[1024,512]{1,0:T(8,128)(2,1)}) custom-call(f32[256,2048]{1,0:T(8,128)} %get-tuple-element.63.sum_ref, f32[4,1,1024]{2,1,0:T(1,128)} %get-tuple-element.64.log_ref, ...), custom_call_target="tpu_custom_call" | custom-call | flops 49999998976 | bytes 31457280 | tf_op jit(solution)/shard_map/attend_back/pallas_call | solution.py:1260
  467.7 89.2 %input_terms.1 = (bf16[1024,512]{1,0:T(8,128)(2,1)}, bf16[256,512]{1,0:T(8,128)(2,1)}, bf16[256,512]{1,0:T(8,128)(2,1)}, bf16[256,512]{1,0:T(8,128)(2,1)}, bf16[512,256]{1,0:T(8,128)(2,1)}) custom-call(bf16[1024,512]{1,0:T(8,128)(2,1)} %get-tuple-element.68.dq_ref, bf16[1024,512]{1,0:T(8,128)(2,1)} %get-tuple-element.69.dk_ref, ...), custom_call_target="tpu_custom_call" | custom-call | flops 80000000000 | bytes 20971520 | tf_op jit(solution)/shard_map/input_terms/pallas_call | solution.py:1511
  556.9 6.9 %results.1 = (bf16[1024,512]{1,0:T(8,128)(2,1)}, bf16[1024,512]{1,0:T(8,128)(2,1)}, f32[256,512]{1,0:T(8,128)}, f32[256,512]{1,0:T(8,128)}, f32[256,512]{1,0:T(8...) custom-call(bf16[1024,512]{1,0:T(8,128)(2,1)} %get-tuple-element.59.refs_0_, ...), custom_call_target="tpu_custom_call" | custom-call | flops 1000000 | bytes 16777216 | tf_op jit(solution)/shard_map/results/pallas_call | solution.py:1569
  (1 shorter events, 0.0 us)
Async XLA Ops:
  7.2 181.9 %all-gather.3.cloned.1.call-start = ((), (), s32[]{:S(2)}) async-start(), calls=%async_computation | async-start | bytes 9437184 | tf_op jit(solution)/shard_map/all_gather | solution.py:1583
  7.9 181.2 %all-gather.5.cloned.1.call-start = ((), (), s32[]{:S(2)}) async-start(), calls=%async_computation.1 | async-start | bytes 9437184 | tf_op jit(solution)/shard_map/all_gather | solution.py:1583
Sparse Core Ops, SparseCore 0:
  9.9 77.2 all-gather.2
  89.1 97.9 all-gather.4
